TPU v7x, 256 devices: a whole 4x4x8 slice. The times are simulated.
256 devices in a mesh: dp: 64 (over z_hi, y, x), shard: 4 (over z_lo, core).
Axes of the slice: x: 4, y: 4, z: 8 (z_hi: 4, z_lo: 2; z = z_hi * 2 + z_lo), core: 2. Of those that a mesh axis runs over, the one named last changes fastest.
Arguments:
- context: bfloat16 [65536, 2048], P(('dp', 'shard')), may hold values from -6 to 6
- out_grad: bfloat16 [65536, 2048], P(('dp', 'shard')), may hold values from -6 to 6
- weight: bfloat16 [2048, 2048], P('shard'), may hold values from -0.125 to 0.125
- error: float32 [64, 2048, 2048], P('dp', 'shard'), may hold values from -6 to 6
- warm: bfloat16 [2048, 256], P('shard'), may hold values from -1 to 1
Outputs:
- in_grad: bfloat16 [65536, 2048], P(('dp', 'shard'))
- new_error: float32 [64, 2048, 2048], P('dp', 'shard')
- factor_q: float32 [2048, 256], P('shard')
All inputs are finite; a program needn't handle non-finite values.
Results may differ from a plain program's by a relative error of at most 0.0085.
Values may be sent and summed in bfloat16 or wider, within the bound.
No kernel may reach another device: no remote copies, remote signals or barrier semaphores. Data moves between devices by JAX's collectives and lax.ppermute only.
A program may use at most 128 MiB of HBM per device.

v0:
```python
import functools
import math

import jax
import jax.numpy as jnp
import numpy as np
from jax import lax
from jax.experimental import pallas as pl
from jax.experimental.pallas import tpu as pltpu
from jax.sharding import Mesh, PartitionSpec as P

BF16 = jnp.bfloat16
F32 = jnp.float32
HI = lax.Precision.HIGHEST
PART = 64
SUB = 8
AXES = ("zh", "y", "x", "zl", "core")
SIZES = (4, 4, 4, 2, 2)
ROWS = 512
RANK = 256
FEAT = 2048
TOK = 256
HALF = RANK // 2
CHUNKS, CHUNK_ROWS, CHUNK_COLS = 16, 16, 1024
VMEM = pl.BlockSpec(memory_space=pltpu.VMEM)
SMEM = pl.BlockSpec(memory_space=pltpu.SMEM)


def swap(x, axis):
    return lax.ppermute(x, axis, [(0, 1), (1, 0)])


def mm(a, b, ca, cb):
    return lax.dot_general(a, b, (((ca,), (cb,)), ((), ())), preferred_element_type=F32)


def two(x):
    high = x.astype(BF16)
    return high, (x - high.astype(F32)).astype(BF16)


def chunk_at(n):
    return n // 2 * CHUNK_ROWS, n % 2 * CHUNK_COLS


def split_halves(core, total, keep, send):
    for n in range(CHUNKS):
        row, col = chunk_at(n)
        cols = pl.ds(col, CHUNK_COLS)
        keep[n] = total[pl.ds(pl.multiple_of(core * HALF + row, CHUNK_ROWS), CHUNK_ROWS), cols]
        send[n] = total[
            pl.ds(pl.multiple_of((1 - core) * HALF + row, CHUNK_ROWS), CHUNK_ROWS), cols
        ].astype(send.dtype)


def join_halves(core, mine, other, whole):
    for n in range(CHUNKS):
        row, col = chunk_at(n)
        cols = pl.ds(col, CHUNK_COLS)
        whole[pl.ds(pl.multiple_of(core * HALF + row, CHUNK_ROWS), CHUNK_ROWS), cols] = mine[n]
        whole[pl.ds(pl.multiple_of((1 - core) * HALF + row, CHUNK_ROWS), CHUNK_ROWS), cols] = other[n]


def block(zl, core):
    return pl.ds(pl.multiple_of((zl * 2 + core) * ROWS, ROWS), ROWS)


def prepare_kernel(at, ctx, err, own, near, far, diag, high, low):
    zl, core = at[0], at[1]
    own[...] = ctx[:, block(zl, core)]
    near[...] = ctx[:, block(zl, 1 - core)]
    far[...] = ctx[:, block(1 - zl, core)]
    diag[...] = ctx[:, block(1 - zl, 1 - core)]
    high[...], low[...] = two(err[...])


def left_kernel(scale, at, og, ctx, high, low, w0, w1, w2, w3, keep, send, total):
    zl, core = at[0], at[1]
    where = ((zl, core), (zl, 1 - core), (1 - zl, core), (1 - zl, 1 - core))
    proj = jnp.zeros((TOK, RANK), F32)
    own = jnp.zeros((ROWS, RANK), F32)
    for (a, b), w in zip(where, (w0, w1, w2, w3)):
        cols = block(a, b)
        proj += mm(og[:, cols], w[...], 1, 0)
        own += mm(high[:, cols], w[...], 1, 0) + mm(low[:, cols], w[...], 1, 0)
    first, second = two(proj * scale)
    total[...] = mm(first, ctx[...], 0, 0) + mm(second, ctx[...], 0, 0)
    total[:, block(zl, core)] += own.T
    split_halves(core, total, keep, send)


def right_kernel(scale, at, ctx, og, high, low, mine, other, keep, send, left, total):
    zl, core = at[0], at[1]
    join_halves(core, mine, other, left)
    first, second = two(mm(ctx[...], left[...], 1, 1) * scale)
    total[...] = mm(first, og[...], 0, 0) + mm(second, og[...], 0, 0)
    own = left[:, block(zl, core)]
    total[...] += mm(own, high[...], 1, 0) + mm(own, low[...], 1, 0)
    split_halves(core, total, keep, send)


def add_kernel(keep, got, out):
    out[...] = (keep[...] + got[...].astype(F32)).astype(BF16)


def sum_kernel(parts, out):
    out[...] = parts[...].astype(F32).sum(0)


def spread_kernel(part, one, opposite, three, out):
    whole = ((part[...] + opposite[...]) + (one[...] + three[...])).astype(BF16)
    for n in range(CHUNKS):
        out[n] = whole


def row_of(x, k):
    return jnp.broadcast_to(x[k : k + 1, :], x.shape)


def factor_block(rows):
    shape = rows[0].shape
    sub = lax.broadcasted_iota(jnp.int32, shape, 0)
    for p in range(len(rows)):
        cols = [
            [jnp.broadcast_to(r[:, SUB * p + k : SUB * p + k + 1], shape) for k in range(SUB)]
            for r in rows[p:]
        ]
        for k in range(SUB):
            diagonal = row_of(cols[0][k], k)
            inv = lax.rsqrt(diagonal)
            inv = inv * (1.5 - 0.5 * diagonal * inv * inv)
            pivot = row_of(rows[p], k) * inv
            later = [row_of(cols[0][j], k) * inv for j in range(k + 1, SUB)]
            for g, col in enumerate(cols, p):
                times = col[k] * inv
                if g == p:
                    times = jnp.where(sub > k, times, 0.0)
                rows[g] = rows[g] - times * pivot
                if g == p:
                    rows[g] = jnp.where(sub == k, pivot, rows[g])
                for j, entry in zip(range(k + 1, SUB), later):
                    col[j] = col[j] - times * entry
    return rows


def dot_hi(a, b, ca, cb):
    return lax.dot_general(
        a, b, (((ca,), (cb,)), ((), ())), precision=HI, preferred_element_type=F32
    )


def eye(n):
    shape = (n, n)
    same = lax.broadcasted_iota(jnp.int32, shape, 0) == lax.broadcasted_iota(jnp.int32, shape, 1)
    return same.astype(F32)


def eliminate(start, a):
    stop = start + PART
    rows = jnp.concatenate([a[start:stop, start:stop], eye(PART)], 1)
    rows = factor_block([rows[n : n + SUB] for n in range(0, PART, SUB)])
    inverse = jnp.concatenate(rows, 0)[:, PART:]
    panel = dot_hi(inverse, a[start:stop, :], 1, 0)
    a[start:stop, :] = panel
    if stop < RANK:
        a[stop:, :] = a[stop:, :] - dot_hi(panel[:, stop:RANK], panel, 0, 0)


def gram_kernel(left, a):
    a[:, :RANK] = mm(left[...], left[...], 1, 1)
    a[:, RANK:] = eye(RANK)
    eliminate(0, a)


def step_kernel(start, a_in, a):
    eliminate(start, a)


def basis_kernel(at, a_in, left, inverse, basis, a):
    a[...] = a_in[...]
    eliminate(RANK - PART, a)
    inverse[...] = a[:, RANK:]
    first, second = two(a[:, RANK:])
    own = left[:, block(at[0], at[1])]
    basis[...] = (mm(first, own, 1, 0) + mm(second, own, 1, 0)).astype(BF16)


def grad_kernel(g0, g1, g2, g3, weight, o0, o1, o2, o3):
    for g, o in ((g0, o0), (g1, o1), (g2, o2), (g3, o3)):
        o[...] = mm(g[...], weight[...], 1, 1).astype(BF16)


def merge_kernel(scale, err, c0, c1, g0, g1, out):
    total = mm(c0[...], g0[...], 0, 0) + mm(c1[...], g1[...], 0, 0)
    out[...] = err[...] + total * scale


def last_kernel(
    share, at, mine, other, inverse, basis, merged, i0, i1, i2, i3, new_error, factor_q, in_grad, right
):
    step = pl.program_id(0)
    zl, core = at[0], at[1]

    @pl.when(step == 0)
    def _():
        join_halves(core, mine, other, right)

    cols = pl.ds(pl.multiple_of(step * ROWS, ROWS), ROWS)
    first, second = two(inverse[...])
    q = (mm(first, right[:, cols], 1, 0) + mm(second, right[:, cols], 1, 0)) * share
    new_error[...] = merged[...] - mm(basis[...], q.astype(BF16), 0, 0)
    at_zl, at_core = step // 2, step % 2

    @pl.when((at_zl == zl) & (at_core == core))
    def _():
        factor_q[...] = q.T
        in_grad[...] = i0[...]

    @pl.when((at_zl == zl) & (at_core != core))
    def _():
        in_grad[...] = i1[...]

    @pl.when((at_zl != zl) & (at_core == core))
    def _():
        in_grad[...] = i2[...]

    @pl.when((at_zl != zl) & (at_core != core))
    def _():
        in_grad[...] = i3[...]


def size(shape, dtype):
    return math.prod(shape) * jnp.dtype(dtype).itemsize


def call(kernel, outs, args, flops, name, scratch=(), alias=None, limit=16):
    moved = sum(size(a.shape, a.dtype) for a in args) + sum(size(s, d) for s, d in outs)
    return pl.pallas_call(
        kernel,
        out_shape=[jax.ShapeDtypeStruct(s, d) for s, d in outs],
        in_specs=[SMEM if a.dtype == jnp.int32 else VMEM for a in args],
        out_specs=[VMEM] * len(outs),
        scratch_shapes=[pltpu.VMEM(s, d) for s, d in scratch],
        input_output_aliases=alias or {},
        compiler_params=pltpu.CompilerParams(vmem_limit_bytes=limit * 2**20),
        cost_estimate=pl.CostEstimate(flops=flops, bytes_accessed=moved, transcendentals=0),
        name=name,
    )(*args)


CHUNKED = (CHUNKS, CHUNK_ROWS, CHUNK_COLS)
CHUNK = (CHUNK_ROWS, CHUNK_COLS)


def tied(x, *others):
    return lax.optimization_barrier((x,) + others)[0]


def across_plane(keep, send):
    got = swap(send, "core")
    (half,) = call(add_kernel, [(CHUNKED, BF16)], (keep, got), 1_000_000, "add")
    parts = lax.all_to_all(half, ("y", "x"), 0, 0)
    (part,) = call(sum_kernel, [(CHUNK, F32)], (parts,), 1_000_000, "sum")
    return part


def across_z(part, beside=()):
    far = tied(swap(part, "zl"), *beside)
    part = part + far
    return (part,) + tuple(
        lax.ppermute(part, "zh", [(i, (i + step) % 4) for i in range(4)]) for step in (1, 2, 3)
    )


def back_over_plane(part, one, opposite, three, beside=()):
    (whole,) = call(
        spread_kernel,
        [(CHUNKED, BF16)],
        (tied(part, *beside), one, opposite, three),
        1_000_000,
        "spread",
    )
    return lax.all_to_all(whole, ("y", "x"), 0, 0)


def on_device(context, out_grad, weight, error, warm):
    scale = 1.0 / math.sqrt(TOK * 4)
    core = lax.axis_index("core")
    zl = lax.axis_index("zl")
    at = jnp.stack([zl, core]).astype(jnp.int32)
    error = error[0]
    tokens = ((TOK, ROWS), BF16)

    warm_far = swap(warm, "zl")
    warm_near = swap(warm, "core")
    c_own, c_near, c_far, c_diag, high, low = call(
        prepare_kernel,
        [tokens] * 4 + [((ROWS, FEAT), BF16)] * 2,
        (at, context, error),
        4_000_000,
        "prepare",
    )
    warm_diag = swap(tied(warm_far, low), "core")

    keep, send = call(
        functools.partial(left_kernel, scale),
        [(CHUNKED, F32), (CHUNKED, BF16)],
        (at, out_grad, context, high, low, warm, warm_near, warm_far, warm_diag),
        2_000_000_000,
        "left",
        [((RANK, FEAT), F32)],
    )
    g_far = swap(tied(out_grad, warm_far), "zl")
    g_near = swap(tied(out_grad, warm_far), "core")
    part = across_plane(keep, send)
    g_diag = swap(g_far, "core")
    c_near = swap(c_near, "core")
    zs = across_z(tied(part, g_far, g_near))
    (merged,) = call(
        functools.partial(merge_kernel, scale),
        [((ROWS, FEAT), F32)],
        (error, c_own, c_near, out_grad, g_near),
        1_100_000_000,
        "merge",
    )
    c_far, c_diag = (tied(c, zs[1]) for c in (c_far, c_diag))
    c_far, c_diag = swap(c_far, "zl"), swap(c_diag, "zl")
    mine = back_over_plane(*zs, beside=(g_diag, merged))

    i_own, i_near, i_far, i_diag = call(
        grad_kernel, [tokens] * 4, (out_grad, g_near, g_far, g_diag, weight), 2_200_000_000, "grad"
    )
    mine = tied(mine, i_own)
    other = swap(mine, "core")
    i_diag = swap(i_diag, "zl")
    i_far = swap(i_far, "zl")
    i_near = swap(i_near, "core")

    keep, send, left = call(
        functools.partial(right_kernel, scale),
        [(CHUNKED, F32), (CHUNKED, BF16), ((RANK, FEAT), BF16)],
        (at, context, out_grad, high, low, mine, other),
        2_000_000_000,
        "right",
        [((RANK, FEAT), F32)],
    )
    part = across_plane(keep, send)

    table = ((RANK, 2 * RANK), F32)
    (a,) = call(gram_kernel, [table], (left,), 300_000_000, "gram")
    part = tied(part, a, c_far, c_diag, i_far, i_diag, i_near)
    i_diag = swap(i_diag, "core")
    c_diag = swap(c_diag, "core")
    (a,) = call(
        functools.partial(step_kernel, PART), [table], (a,), 300_000_000, "step", alias={0: 0}
    )
    zs = across_z(part, (a,))
    (a,) = call(
        functools.partial(step_kernel, 2 * PART), [table], (a,), 300_000_000, "step", alias={0: 0}
    )
    mine = back_over_plane(*zs, beside=(a, c_diag))
    inverse, basis = call(
        basis_kernel,
        [((RANK, RANK), F32), ((RANK, ROWS), BF16)],
        (at, a, left),
        300_000_000,
        "basis",
        [table],
    )
    (merged,) = call(
        functools.partial(merge_kernel, scale),
        [((ROWS, FEAT), F32)],
        (merged, c_far, c_diag, g_far, g_diag),
        1_100_000_000,
        "merge",
        alias={0: 0},
    )
    mine = tied(mine, merged, basis)
    other = swap(mine, "core")

    whole = lambda *shape: pl.BlockSpec(shape, lambda j: (0,) * len(shape))
    column = lambda rows: pl.BlockSpec((rows, ROWS), lambda j: (0, j))
    new_error, factor_q, in_grad = pl.pallas_call(
        functools.partial(last_kernel, 1.0 / (SIZES[0] * SIZES[1] * SIZES[2])),
        grid=(4,),
        out_shape=[
            jax.ShapeDtypeStruct((ROWS, FEAT), F32),
            jax.ShapeDtypeStruct((ROWS, RANK), F32),
            jax.ShapeDtypeStruct((TOK, FEAT), BF16),
        ],
        in_specs=[SMEM, VMEM, VMEM, VMEM, VMEM, column(ROWS)] + [VMEM] * 4,
        out_specs=[column(ROWS), whole(ROWS, RANK), column(TOK)],
        scratch_shapes=[pltpu.VMEM((RANK, FEAT), BF16)],
        compiler_params=pltpu.CompilerParams(vmem_limit_bytes=20 * 2**20),
        cost_estimate=pl.CostEstimate(
            flops=1_200_000_000, bytes_accessed=12_000_000, transcendentals=0
        ),
        name="last",
    )(at, mine, other, inverse, basis, merged, i_own, i_near, i_far, i_diag)
    return in_grad, new_error[None], factor_q


def solution(mesh):
    split = Mesh(np.asarray(mesh.devices).reshape(SIZES), AXES)
    every = ("zh", "y", "x", "zl", "core")
    shard = ("zl", "core")
    return jax.shard_map(
        on_device,
        mesh=split,
        in_specs=(
            P(every, None),
            P(every, None),
            P(shard, None),
            P(("zh", "y", "x"), shard, None),
            P(shard, None),
        ),
        out_specs=(P(every, None), P(("zh", "y", "x"), shard, None), P(shard, None)),
        check_vma=False,
    )
```

profile of v0, /device:TPU:1, one launch (start us, length us, event | category | flops | bytes accessed | tf_op | source)
XLA Modules:
  0.0 178.0 jit_solution(5262053904220276473)
XLA Ops:
  0.6 2.6 %collective-permute-start.1 = (bf16[512,256]{1,0:T(8,128)(2,1)}, bf16[512,256]{1,0:T(8,128)(2,1)S(1)}, u32[]{:S(2)}, u32[]{:S(2)}) collective-permute-start(bf16[512,256]{1,0:T(8,128)(2,1)} %w0.1), channel_id=1, source_target_pairs={{0,2},{2,0},{1,3},{3,1},{4,6},{6,4},{5,7},{7,5},{8,10},{10,8},{9,1... | collective-permute-start | bytes 786440 | tf_op jit(solution)/shard_map/ppermute | solution.py:30
  3.2 5.3 %collective-permute-done.1.w2 = bf16[512,256]{1,0:T(8,128)(2,1)S(1)} collective-permute-done((bf16[512,256]{1,0:T(8,128)(2,1)}, bf16[512,256]{1,0:T(8,128)(2,1)S(1)}, u32[]{:S(2)}, u32[]{:S(2)}) %collective-permute-start.1) | collective-permute-done | bytes 262176 | tf_op jit(solution)/shard_map/ppermute | solution.py:30
  8.5 2.1 %collective-permute-start.4 = (bf16[256,2048]{1,0:T(8,128)(2,1)}, bf16[256,2048]{1,0:T(8,128)(2,1)S(1)}, u32[]{:S(2)}, u32[]{:S(2)}) collective-permute-start(bf16[256,2048]{1,0:T(8,128)(2,1)} %og.3), channel_id=1, source_target_pairs={{0,2},{2,0},{1,3},{3,1},{4,6},{6,4},{5,7},{7,5},{8,10},{10,8},{9,1... | collective-permute-start | bytes 3145736 | tf_op jit(solution)/shard_map/ppermute | solution.py:30
  10.6 1.8 %collective-permute-start = (bf16[512,256]{1,0:T(8,128)(2,1)}, bf16[512,256]{1,0:T(8,128)(2,1)S(1)}, u32[]{:S(2)}, u32[]{:S(2)}) collective-permute-start(bf16[512,256]{1,0:T(8,128)(2,1)} %w0.1), channel_id=1, source_target_pairs={{0,1},{1,0},{2,3},{3,2},{4,5},{5,4},{6,7},{7,6},{8,9},{9,8},{10,11... | collective-permute-start | bytes 786440 | tf_op jit(solution)/shard_map/ppermute | solution.py:30
  12.5 2.2 %copy-done.4 = f32[1,512,2048]{2,1,0:T(8,128)S(1)} copy-done((f32[1,512,2048]{2,1,0:T(8,128)S(1)}, f32[1,512,2048]{2,1,0:T(8,128)}, u32[]{:S(2)}) %copy-start.4) | copy-done | bytes 4194328
  14.7 1.2 copy-done.6
  15.9 1.4 prepare.1
  19.2 1.0 collective-permute-done.2.w3
  20.2 3.0 %left.1 = (f32[16,16,1024]{2,1,0:T(8,128)S(1)}, bf16[16,16,1024]{2,1,0:T(8,128)(2,1)S(1)}) custom-call(s32[2]{0:T(128)S(1)} %pad_add_fusion.at, bf16[256,2048]{1,0:T(8,128)(2,1)S(1)} %copy-done.8, bf16[256,2048]{1,0:T(8,128)(2,1)S(1)} %copy-done.6, bf16[512,2048]{1,0:T(8,128)(2,1)S(1)} %get-tuple-element.34.high, ...), custom_call_target="tpu_custom_call" | custom-call | flops 2000000000 | bytes 8912904 | tf_op jit(solution)/shard_map/left/pallas_call | solution.py:238
  23.4 9.0 %collective-permute-done.4.g2.g0 = bf16[256,2048]{1,0:T(8,128)(2,1)S(1)} collective-permute-done((bf16[256,2048]{1,0:T(8,128)(2,1)}, bf16[256,2048]{1,0:T(8,128)(2,1)S(1)}, u32[]{:S(2)}, u32[]{:S(2)}) %collective-permute-start.4) | collective-permute-done | bytes 1048608 | tf_op jit(solution)/shard_map/ppermute | solution.py:30
  32.4 2.5 %collective-permute-start.7 = (bf16[256,2048]{1,0:T(8,128)(2,1)S(1)}, bf16[256,2048]{1,0:T(8,128)(2,1)}, u32[]{:S(2)}, u32[]{:S(2)}) collective-permute-start(bf16[256,2048]{1,0:T(8,128)(2,1)S(1)} %collective-permute-done.4.g2.g0), channel_id=1, source_target_pairs={{0,1},{1,0},{2,3},{3,2},{4,5},{5,4},{6,7},{7,6},{8,9},{9,8},{10,11... | collective-permute-start | bytes 3145736 | tf_op jit(solution)/shard_map/ppermute | solution.py:30
  34.9 0.9 add.12
  35.8 7.0 %all-to-all-start = ((bf16[16,16,1024]{2,1,0:T(8,128)(2,1)}), bf16[16,16,1024]{2,1,0:T(8,128)(2,1)S(1)}, u32[]{:S(2)}, u32[]{:S(2)}) async-start(bf16[16,16,1024]{2,1,0:T(8,128)(2,1)} %add.12), calls=%async_computation | async-start | bytes 1048576 | tf_op jit(solution)/shard_map/all_to_all | solution.py:262
  43.3 10.4 %all-to-all-done.parts = bf16[16,16,1024]{2,1,0:T(8,128)(2,1)S(1)} async-done(((bf16[16,16,1024]{2,1,0:T(8,128)(2,1)}), bf16[16,16,1024]{2,1,0:T(8,128)(2,1)S(1)}, u32[]{:S(2)}, u32[]{:S(2)}) %all-to-all-start) | async-done | bytes 524320 | tf_op jit(solution)/shard_map/all_to_all | solution.py:262
  53.8 1.3 collective-permute-start.6
  55.1 1.9 %collective-permute-done.6 = f32[16,1024]{1,0:T(8,128)S(1)} collective-permute-done((f32[16,1024]{1,0:T(8,128)S(1)}, f32[16,1024]{1,0:T(8,128)S(1)}, u32[]{:S(2)}, u32[]{:S(2)}) %collective-permute-start.6) | collective-permute-done | bytes 65568 | tf_op jit(solution)/shard_map/ppermute | solution.py:30
  57.0 6.6 %collective-permute-start.10 = (f32[16,1024]{1,0:T(8,128)S(1)}, f32[16,1024]{1,0:T(8,128)S(1)}, u32[]{:S(2)}, u32[]{:S(2)}) collective-permute-start(f32[16,1024]{1,0:T(8,128)S(1)} %add.8.part), channel_id=1, source_target_pairs={{0,128},{64,192},{128,0},{192,64},{1,129},{65,193},{129,1},{193,65... | collective-permute-start | bytes 196616 | tf_op jit(solution)/shard_map/ppermute | solution.py:271
  63.6 2.4 %collective-permute-start.9 = (f32[16,1024]{1,0:T(8,128)S(1)}, f32[16,1024]{1,0:T(8,128)S(1)}, u32[]{:S(2)}, u32[]{:S(2)}) collective-permute-start(f32[16,1024]{1,0:T(8,128)S(1)} %add.8.part), channel_id=1, source_target_pairs={{0,64},{64,128},{128,192},{192,0},{1,65},{65,129},{129,193},{193,1... | collective-permute-start | bytes 196616 | tf_op jit(solution)/shard_map/ppermute | solution.py:271
  66.0 2.2 %copy-done.5 = f32[1,512,2048]{2,1,0:T(8,128)S(1)} copy-done((f32[1,512,2048]{2,1,0:T(8,128)S(1)}, f32[1,512,2048]{2,1,0:T(8,128)}, u32[]{:S(2)}) %copy-start.5) | copy-done | bytes 4194328
  68.1 2.6 %merge.2.err = f32[512,2048]{1,0:T(8,128)S(1)} custom-call(f32[512,2048]{1,0:T(8,128)S(1)} %bitcast.5, bf16[256,512]{1,0:T(8,128)(2,1)S(1)} %get-tuple-element.41.c0, bf16[256,512]{1,0:T(8,128)(2,1)S(1)} %collective-permute-done.8.c1, bf16[256,2048]{1,0:T(8,128)(2,1)S(1)} %copy-done.8, bf16[256,2048]{1,0:T(8,128)(2,1)} %collective-permute-done.5.g1), custom_call_target="tpu_custom_call" | custom-call | flops 1100000000 | bytes 11010048 | tf_op jit(solution)/shard_map/merge/pallas_call | solution.py:238
  70.8 2.0 %copy-done = f32[512,2048]{1,0:T(8,128)} copy-done((f32[512,2048]{1,0:T(8,128)}, f32[512,2048]{1,0:T(8,128)S(1)}, u32[]{:S(2)}) %copy-start) | copy-done | bytes 4194328
  72.8 0.9 spread.2
  73.6 3.8 %all-to-all-start.1 = ((bf16[16,16,1024]{2,1,0:T(8,128)(2,1)}), bf16[16,16,1024]{2,1,0:T(8,128)(2,1)S(1)}, u32[]{:S(2)}, u32[]{:S(2)}) async-start(bf16[16,16,1024]{2,1,0:T(8,128)(2,1)} %spread.2), calls=%async_computation.1 | async-start | bytes 1048576 | tf_op jit(solution)/shard_map/all_to_all | solution.py:283
  77.4 1.2 copy-done.10
  78.6 1.6 copy-done.14
  80.2 4.0 %grad.1 = (bf16[256,512]{1,0:T(8,128)(2,1)S(1)}, bf16[256,512]{1,0:T(8,128)(2,1)S(1)}, bf16[256,512]{1,0:T(8,128)(2,1)S(1)}, bf16[256,512]{1,0:T(8,128)(2,1)S(1)}) custom-call(bf16[256,2048]{1,0:T(8,128)(2,1)S(1)} %copy-done.8, bf16[256,2048]{1,0:T(8,128)(2,1)} %collective-permute-done.5.g1, bf16[256,2048]{1,0:T(8,128)(2,1)S(1)} %copy-done.10, ...), custom_call_target="tpu_custom_call" | custom-call | flops 2200000000 | bytes 7340032 | tf_op jit(solution)/shard_map/grad/pallas_call | solution.py:238
  84.2 0.7 copy-done.22
  85.0 0.7 copy-done.23
  86.5 4.7 %collective-permute-start.12 = (bf16[16,16,1024]{2,1,0:T(8,128)(2,1)S(1)}, bf16[16,16,1024]{2,1,0:T(8,128)(2,1)S(1)}, u32[]{:S(2)}, u32[]{:S(2)}) collective-permute-start(bf16[16,16,1024]{2,1,0:T(8,128)(2,1)S(1)} %all-to-all-done.1.mine), channel_id=1, source_target_pairs={{0,1},{1,0},{2,3},{3,2},{4,5},{5,4},{6,7},{7,6},{8,9},{9,8},{10,11... | collective-permute-start | bytes 1572872 | tf_op jit(solution)/shard_map/ppermute | solution.py:30
  91.2 0.8 copy-done.12
  92.0 0.7 collective-permute-done.12.other
  92.8 1.0 copy-done.13
  93.8 1.6 copy-done.16
  95.4 1.6 copy-done.18
  97.0 3.0 %right.1 = (f32[16,16,1024]{2,1,0:T(8,128)S(1)}, bf16[16,16,1024]{2,1,0:T(8,128)(2,1)S(1)}, bf16[256,2048]{1,0:T(8,128)(2,1)S(1)}) custom-call(s32[2]{0:T(128)S(1)} %pad_add_fusion.at, bf16[256,2048]{1,0:T(8,128)(2,1)S(1)} %copy-done.7, bf16[256,2048]{1,0:T(8,128)(2,1)S(1)} %copy-done.8, bf16[512,2048]{1,0:T(8,128)(2,1)S(1)} %copy-done.16, ...), custom_call_target="tpu_custom_call" | custom-call | flops 2000000000 | bytes 9961480 | tf_op jit(solution)/shard_map/right/pallas_call | solution.py:238
  100.5 1.5 collective-permute-done.13.got
  102.0 0.9 add.13
  102.9 5.9 %all-to-all-start.2 = ((bf16[16,16,1024]{2,1,0:T(8,128)(2,1)}), bf16[16,16,1024]{2,1,0:T(8,128)(2,1)S(1)}, u32[]{:S(2)}, u32[]{:S(2)}) async-start(bf16[16,16,1024]{2,1,0:T(8,128)(2,1)} %add.13), calls=%async_computation.2 | async-start | bytes 1048576 | tf_op jit(solution)/shard_map/all_to_all | solution.py:262
  108.7 0.8 collective-permute-start.15
  109.6 0.7 collective-permute-start.14
  110.3 0.7 collective-permute-start.16
  111.0 0.7 collective-permute-start.17
  111.8 1.8 collective-permute-start.18
  113.5 2.8 %collective-permute-done.15 = bf16[256,512]{1,0:T(8,128)(2,1)} collective-permute-done((bf16[256,512]{1,0:T(8,128)(2,1)}, bf16[256,512]{1,0:T(8,128)(2,1)}, u32[]{:S(2)}, u32[]{:S(2)}) %collective-permute-start.15) | collective-permute-done | bytes 262176 | tf_op jit(solution)/shard_map/ppermute | solution.py:30
  116.3 2.6 %collective-permute-start.20 = (bf16[256,512]{1,0:T(8,128)(2,1)}, bf16[256,512]{1,0:T(8,128)(2,1)}, u32[]{:S(2)}, u32[]{:S(2)}) collective-permute-start(bf16[256,512]{1,0:T(8,128)(2,1)} %collective-permute-done.15), channel_id=1, source_target_pairs={{0,1},{1,0},{2,3},{3,2},{4,5},{5,4},{6,7},{7,6},{8,9},{9,8},{10,11... | collective-permute-start | bytes 786440 | tf_op jit(solution)/shard_map/ppermute | solution.py:30
  119.0 4.0 %gram.1.a_in = f32[256,512]{1,0:T(8,128)S(1)} custom-call(bf16[256,2048]{1,0:T(8,128)(2,1)S(1)} %get-tuple-element.48.left), custom_call_target="tpu_custom_call" | custom-call | flops 300000000 | bytes 1572864 | tf_op jit(solution)/shard_map/gram/pallas_call | solution.py:238
  123.1 4.5 %collective-permute-done.16.i2 = bf16[256,512]{1,0:T(8,128)(2,1)} collective-permute-done((bf16[256,512]{1,0:T(8,128)(2,1)}, bf16[256,512]{1,0:T(8,128)(2,1)}, u32[]{:S(2)}, u32[]{:S(2)}) %collective-permute-start.16) | collective-permute-done | bytes 262176 | tf_op jit(solution)/shard_map/ppermute | solution.py:30
  127.6 5.6 %collective-permute-done.17 = bf16[256,512]{1,0:T(8,128)(2,1)} collective-permute-done((bf16[256,512]{1,0:T(8,128)(2,1)}, bf16[256,512]{1,0:T(8,128)(2,1)}, u32[]{:S(2)}, u32[]{:S(2)}) %collective-permute-start.17) | collective-permute-done | bytes 262176 | tf_op jit(solution)/shard_map/ppermute | solution.py:30
  133.2 0.7 collective-permute-start.19
  134.0 3.1 %step.2.a_in = f32[256,512]{1,0:T(8,128)S(1)} custom-call(f32[256,512]{1,0:T(8,128)S(1)} %gram.1.a_in), custom_call_target="tpu_custom_call", output_to_operand_aliasing={{}: (0, {})} | custom-call | flops 300000000 | bytes 1048576 | tf_op jit(solution)/shard_map/step/pallas_call | solution.py:238
  137.1 2.1 %collective-permute-start.21 = (f32[16,1024]{1,0:T(8,128)S(1)}, f32[16,1024]{1,0:T(8,128)S(1)}, u32[]{:S(2)}, u32[]{:S(2)}) collective-permute-start(f32[16,1024]{1,0:T(8,128)S(1)} %add.9.part), channel_id=1, source_target_pairs={{0,64},{64,128},{128,192},{192,0},{1,65},{65,129},{129,193},{193,1... | collective-permute-start | bytes 196616 | tf_op jit(solution)/shard_map/ppermute | solution.py:271
  139.2 1.2 collective-permute-start.22
  140.4 2.2 %collective-permute-start.23 = (f32[16,1024]{1,0:T(8,128)S(1)}, f32[16,1024]{1,0:T(8,128)S(1)}, u32[]{:S(2)}, u32[]{:S(2)}) collective-permute-start(f32[16,1024]{1,0:T(8,128)S(1)} %add.9.part), channel_id=1, source_target_pairs={{0,192},{64,0},{128,64},{192,128},{1,193},{65,1},{129,65},{193,129... | collective-permute-start | bytes 196616 | tf_op jit(solution)/shard_map/ppermute | solution.py:271
  142.6 3.0 %step.3.a_in = f32[256,512]{1,0:T(8,128)S(1)} custom-call(f32[256,512]{1,0:T(8,128)S(1)} %step.2.a_in), custom_call_target="tpu_custom_call", output_to_operand_aliasing={{}: (0, {})} | custom-call | flops 300000000 | bytes 1048576 | tf_op jit(solution)/shard_map/step/pallas_call | solution.py:238
  146.3 0.9 spread.3
  147.1 6.5 %all-to-all-start.3 = ((bf16[16,16,1024]{2,1,0:T(8,128)(2,1)}), bf16[16,16,1024]{2,1,0:T(8,128)(2,1)S(1)}, u32[]{:S(2)}, u32[]{:S(2)}) async-start(bf16[16,16,1024]{2,1,0:T(8,128)(2,1)} %spread.3), calls=%async_computation.3 | async-start | bytes 1048576 | tf_op jit(solution)/shard_map/all_to_all | solution.py:283
  153.6 2.2 %copy-done.1 = f32[512,2048]{1,0:T(8,128)S(1)} copy-done((f32[512,2048]{1,0:T(8,128)S(1)}, f32[512,2048]{1,0:T(8,128)}, u32[]{:S(2)}) %copy-start.1) | copy-done | bytes 4194328
  155.8 2.9 %merge.3.merged = f32[512,2048]{1,0:T(8,128)S(1)} custom-call(f32[512,2048]{1,0:T(8,128)S(1)} %copy-done.1, bf16[256,512]{1,0:T(8,128)(2,1)} %collective-permute-done.14.c0, bf16[256,512]{1,0:T(8,128)(2,1)} %collective-permute-done.20.c1, bf16[256,2048]{1,0:T(8,128)(2,1)S(1)} %copy-done.11, ...), custom_call_target="tpu_custom_call", output_to_operand_aliasing={{}: (0, {})} | custom-call | flops 1100000000 | bytes 11010048 | tf_op jit(solution)/shard_map/merge/pallas_call | solution.py:238
  158.7 2.0 %copy-done.2 = f32[512,2048]{1,0:T(8,128)} copy-done((f32[512,2048]{1,0:T(8,128)}, f32[512,2048]{1,0:T(8,128)S(1)}, u32[]{:S(2)}) %copy-start.2) | copy-done | bytes 4194328
  160.8 3.5 %basis.1 = (f32[256,256]{1,0:T(8,128)S(1)}, bf16[256,512]{1,0:T(8,128)(2,1)S(1)}) custom-call(s32[2]{0:T(128)S(1)} %pad_add_fusion.at, f32[256,512]{1,0:T(8,128)S(1)} %step.3.a_in, bf16[256,2048]{1,0:T(8,128)(2,1)S(1)} %get-tuple-element.48.left), custom_call_target="tpu_custom_call" | custom-call | flops 300000000 | bytes 2097160 | tf_op jit(solution)/shard_map/basis/pallas_call | solution.py:238
  164.3 3.8 %collective-permute-start.24 = (bf16[16,16,1024]{2,1,0:T(8,128)(2,1)S(1)}, bf16[16,16,1024]{2,1,0:T(8,128)(2,1)S(1)}, u32[]{:S(2)}, u32[]{:S(2)}) collective-permute-start(bf16[16,16,1024]{2,1,0:T(8,128)(2,1)S(1)} %all-to-all-done.3.mine), channel_id=1, source_target_pairs={{0,1},{1,0},{2,3},{3,2},{4,5},{5,4},{6,7},{7,6},{8,9},{9,8},{10,11... | collective-permute-start | bytes 1572872 | tf_op jit(solution)/shard_map/ppermute | solution.py:30
  168.2 2.0 %collective-permute-done.25.i3 = bf16[256,512]{1,0:T(8,128)(2,1)S(1)} collective-permute-done((bf16[256,512]{1,0:T(8,128)(2,1)}, bf16[256,512]{1,0:T(8,128)(2,1)S(1)}, u32[]{:S(2)}, u32[]{:S(2)}) %collective-permute-start.25) | collective-permute-done | bytes 262176 | tf_op jit(solution)/shard_map/ppermute | solution.py:30
  170.2 2.2 %copy-done.3 = f32[512,2048]{1,0:T(8,128)S(1)} copy-done((f32[512,2048]{1,0:T(8,128)S(1)}, f32[512,2048]{1,0:T(8,128)}, u32[]{:S(2)}) %copy-start.3) | copy-done | bytes 4194328
  172.4 5.6 %last.1 = (f32[512,2048]{1,0:T(8,128)}, f32[512,256]{1,0:T(8,128)}, bf16[256,2048]{1,0:T(8,128)(2,1)}) custom-call(s32[2]{0:T(128)S(1)} %pad_add_fusion.at, bf16[16,16,1024]{2,1,0:T(8,128)(2,1)S(1)} %all-to-all-done.3.mine, bf16[16,16,1024]{2,1,0:T(8,128)(2,1)S(1)} %collective-permute-done.24.other, f32[256,256]{1,0:T(8,128)S(1)} %get-tuple-element.61.inverse, ...), custom_call_target="tpu_custom_call" | custom-call | flops 1200000000 | bytes 12000000 | tf_op jit(solution)/shard_map/last/pallas_call | solution.py:383
  (66 shorter events, 5.0 us)
Async XLA Ops:
  0.6 7.8 %collective-permute-start.1 = (bf16[512,256]{1,0:T(8,128)(2,1)}, bf16[512,256]{1,0:T(8,128)(2,1)S(1)}, u32[]{:S(2)}, u32[]{:S(2)}) collective-permute-start(bf16[512,256]{1,0:T(8,128)(2,1)} %w0.1), channel_id=1, source_target_pairs={{0,2},{2,0},{1,3},{3,1},{4,6},{6,4},{5,7},{7,5},{8,10},{10,8},{9,1... | collective-permute-start | bytes 786440 | tf_op jit(solution)/shard_map/ppermute | solution.py:30
  8.5 23.9 %collective-permute-start.4 = (bf16[256,2048]{1,0:T(8,128)(2,1)}, bf16[256,2048]{1,0:T(8,128)(2,1)S(1)}, u32[]{:S(2)}, u32[]{:S(2)}) collective-permute-start(bf16[256,2048]{1,0:T(8,128)(2,1)} %og.3), channel_id=1, source_target_pairs={{0,2},{2,0},{1,3},{3,1},{4,6},{6,4},{5,7},{7,5},{8,10},{10,8},{9,1... | collective-permute-start | bytes 3145736 | tf_op jit(solution)/shard_map/ppermute | solution.py:30
  10.6 8.7 %collective-permute-start = (bf16[512,256]{1,0:T(8,128)(2,1)}, bf16[512,256]{1,0:T(8,128)(2,1)S(1)}, u32[]{:S(2)}, u32[]{:S(2)}) collective-permute-start(bf16[512,256]{1,0:T(8,128)(2,1)} %w0.1), channel_id=1, source_target_pairs={{0,1},{1,0},{2,3},{3,2},{4,5},{5,4},{6,7},{7,6},{8,9},{9,8},{10,11... | collective-permute-start | bytes 786440 | tf_op jit(solution)/shard_map/ppermute | solution.py:30
  12.5 2.2 %copy-start.4 = (f32[1,512,2048]{2,1,0:T(8,128)S(1)}, f32[1,512,2048]{2,1,0:T(8,128)}, u32[]{:S(2)}) copy-start(f32[1,512,2048]{2,1,0:T(8,128)} %param.8) | copy-start | bytes 12582916
  14.7 1.2 copy-start.6
  15.9 2.8 %copy-start.8 = (bf16[256,2048]{1,0:T(8,128)(2,1)S(1)}, bf16[256,2048]{1,0:T(8,128)(2,1)}, u32[]{:S(2)}) copy-start(bf16[256,2048]{1,0:T(8,128)(2,1)} %og.3) | copy-start | bytes 3145732
  15.9 4.4 %copy-start.19 = (bf16[512,256]{1,0:T(8,128)(2,1)S(1)}, bf16[512,256]{1,0:T(8,128)(2,1)}, u32[]{:S(2)}) copy-start(bf16[512,256]{1,0:T(8,128)(2,1)} %w0.1) | copy-start | bytes 786436
  17.3 0.7 copy-start.20
  18.0 0.7 copy-start.21
  18.7 16.2 %copy-start.15 = (bf16[512,2048]{1,0:T(8,128)(2,1)}, bf16[512,2048]{1,0:T(8,128)(2,1)S(1)}, u32[]{:S(2)}) copy-start(bf16[512,2048]{1,0:T(8,128)(2,1)S(1)} %get-tuple-element.34.high) | copy-start | bytes 6291460
  18.7 16.2 %copy-start.17 = (bf16[512,2048]{1,0:T(8,128)(2,1)}, bf16[512,2048]{1,0:T(8,128)(2,1)S(1)}, u32[]{:S(2)}) copy-start(bf16[512,2048]{1,0:T(8,128)(2,1)S(1)} %get-tuple-element.35.low) | copy-start | bytes 6291460
  18.7 1.5 collective-permute-start.2
  18.7 35.0 %collective-permute-start.5 = (bf16[256,2048]{1,0:T(8,128)(2,1)S(1)}, bf16[256,2048]{1,0:T(8,128)(2,1)}, u32[]{:S(2)}, u32[]{:S(2)}) collective-permute-start(bf16[256,2048]{1,0:T(8,128)(2,1)S(1)} %copy-done.8), channel_id=1, source_target_pairs={{0,1},{1,0},{2,3},{3,2},{4,5},{5,4},{6,7},{7,6},{8,9},{9,8},{10,11... | collective-permute-start | bytes 3145736 | tf_op jit(solution)/shard_map/ppermute | solution.py:30
  23.2 11.7 %collective-permute-start.3 = (bf16[16,16,1024]{2,1,0:T(8,128)(2,1)S(1)}, bf16[16,16,1024]{2,1,0:T(8,128)(2,1)S(1)}, u32[]{:S(2)}, u32[]{:S(2)}) collective-permute-start(bf16[16,16,1024]{2,1,0:T(8,128)(2,1)S(1)} %get-tuple-element.38), channel_id=1, source_target_pairs={{0,1},{1,0},{2,3},{3,2},{4,5},{5,4},{6,7},{7,6},{8,9},{9,8},{10,11... | collective-permute-start | bytes 1572872 | tf_op jit(solution)/shard_map/ppermute | solution.py:30
  32.4 38.3 %copy-start.9 = (bf16[256,2048]{1,0:T(8,128)(2,1)}, bf16[256,2048]{1,0:T(8,128)(2,1)S(1)}, u32[]{:S(2)}) copy-start(bf16[256,2048]{1,0:T(8,128)(2,1)S(1)} %collective-permute-done.4.g2.g0) | copy-start | bytes 3145732
  32.4 40.4 %collective-permute-start.7 = (bf16[256,2048]{1,0:T(8,128)(2,1)S(1)}, bf16[256,2048]{1,0:T(8,128)(2,1)}, u32[]{:S(2)}, u32[]{:S(2)}) collective-permute-start(bf16[256,2048]{1,0:T(8,128)(2,1)S(1)} %collective-permute-done.4.g2.g0), channel_id=1, source_target_pairs={{0,1},{1,0},{2,3},{3,2},{4,5},{5,4},{6,7},{7,6},{8,9},{9,8},{10,11... | collective-permute-start | bytes 3145736 | tf_op jit(solution)/shard_map/ppermute | solution.py:30
  35.8 17.9 %all-to-all-start = ((bf16[16,16,1024]{2,1,0:T(8,128)(2,1)}), bf16[16,16,1024]{2,1,0:T(8,128)(2,1)S(1)}, u32[]{:S(2)}, u32[]{:S(2)}) async-start(bf16[16,16,1024]{2,1,0:T(8,128)(2,1)} %add.12), calls=%async_computation | async-start | bytes 1048576 | tf_op jit(solution)/shard_map/all_to_all | solution.py:262
  42.8 23.2 %collective-permute-start.8 = (bf16[256,512]{1,0:T(8,128)(2,1)S(1)}, bf16[256,512]{1,0:T(8,128)(2,1)S(1)}, u32[]{:S(2)}, u32[]{:S(2)}) collective-permute-start(bf16[256,512]{1,0:T(8,128)(2,1)S(1)} %get-tuple-element.42), channel_id=1, source_target_pairs={{0,1},{1,0},{2,3},{3,2},{4,5},{5,4},{6,7},{7,6},{8,9},{9,8},{10,11... | collective-permute-start | bytes 786440 | tf_op jit(solution)/shard_map/ppermute | solution.py:30
  53.8 3.2 %collective-permute-start.6 = (f32[16,1024]{1,0:T(8,128)S(1)}, f32[16,1024]{1,0:T(8,128)S(1)}, u32[]{:S(2)}, u32[]{:S(2)}) collective-permute-start(f32[16,1024]{1,0:T(8,128)S(1)} %sum.2), channel_id=1, source_target_pairs={{0,2},{2,0},{1,3},{3,1},{4,6},{6,4},{5,7},{7,5},{8,10},{10,8},{9,1... | collective-permute-start | bytes 196616 | tf_op jit(solution)/shard_map/ppermute | solution.py:30
  57.0 15.8 %collective-permute-start.10 = (f32[16,1024]{1,0:T(8,128)S(1)}, f32[16,1024]{1,0:T(8,128)S(1)}, u32[]{:S(2)}, u32[]{:S(2)}) collective-permute-start(f32[16,1024]{1,0:T(8,128)S(1)} %add.8.part), channel_id=1, source_target_pairs={{0,128},{64,192},{128,0},{192,64},{1,129},{65,193},{129,1},{193,65... | collective-permute-start | bytes 196616 | tf_op jit(solution)/shard_map/ppermute | solution.py:271
  63.6 9.2 %collective-permute-start.11 = (f32[16,1024]{1,0:T(8,128)S(1)}, f32[16,1024]{1,0:T(8,128)S(1)}, u32[]{:S(2)}, u32[]{:S(2)}) collective-permute-start(f32[16,1024]{1,0:T(8,128)S(1)} %add.8.part), channel_id=1, source_target_pairs={{0,192},{64,0},{128,64},{192,128},{1,193},{65,1},{129,65},{193,129... | collective-permute-start | bytes 196616 | tf_op jit(solution)/shard_map/ppermute | solution.py:271
  63.6 9.2 %collective-permute-start.9 = (f32[16,1024]{1,0:T(8,128)S(1)}, f32[16,1024]{1,0:T(8,128)S(1)}, u32[]{:S(2)}, u32[]{:S(2)}) collective-permute-start(f32[16,1024]{1,0:T(8,128)S(1)} %add.8.part), channel_id=1, source_target_pairs={{0,64},{64,128},{128,192},{192,0},{1,65},{65,129},{129,193},{193,1... | collective-permute-start | bytes 196616 | tf_op jit(solution)/shard_map/ppermute | solution.py:271
  66.0 2.2 %copy-start.5 = (f32[1,512,2048]{2,1,0:T(8,128)S(1)}, f32[1,512,2048]{2,1,0:T(8,128)}, u32[]{:S(2)}) copy-start(f32[1,512,2048]{2,1,0:T(8,128)} %param.8) | copy-start | bytes 12582916
  70.8 2.0 %copy-start = (f32[512,2048]{1,0:T(8,128)}, f32[512,2048]{1,0:T(8,128)S(1)}, u32[]{:S(2)}) copy-start(f32[512,2048]{1,0:T(8,128)S(1)} %merge.2.err) | copy-start | bytes 12582916
  73.6 12.8 %all-to-all-start.1 = ((bf16[16,16,1024]{2,1,0:T(8,128)(2,1)}), bf16[16,16,1024]{2,1,0:T(8,128)(2,1)S(1)}, u32[]{:S(2)}, u32[]{:S(2)}) async-start(bf16[16,16,1024]{2,1,0:T(8,128)(2,1)} %spread.2), calls=%async_computation.1 | async-start | bytes 1048576 | tf_op jit(solution)/shard_map/all_to_all | solution.py:283
  77.4 1.2 copy-start.10
  78.6 1.6 copy-start.14
  80.2 12.5 %copy-start.7 = (bf16[256,2048]{1,0:T(8,128)(2,1)S(1)}, bf16[256,2048]{1,0:T(8,128)(2,1)}, u32[]{:S(2)}) copy-start(bf16[256,2048]{1,0:T(8,128)(2,1)} %ctx.5) | copy-start | bytes 3145732
  84.2 0.7 copy-start.22
  84.9 0.7 copy-start.23
  85.7 0.7 copy-start.24
  86.5 6.3 %collective-permute-start.12 = (bf16[16,16,1024]{2,1,0:T(8,128)(2,1)S(1)}, bf16[16,16,1024]{2,1,0:T(8,128)(2,1)S(1)}, u32[]{:S(2)}, u32[]{:S(2)}) collective-permute-start(bf16[16,16,1024]{2,1,0:T(8,128)(2,1)S(1)} %all-to-all-done.1.mine), channel_id=1, source_target_pairs={{0,1},{1,0},{2,3},{3,2},{4,5},{5,4},{6,7},{7,6},{8,9},{9,8},{10,11... | collective-permute-start | bytes 1572872 | tf_op jit(solution)/shard_map/ppermute | solution.py:30
  91.2 0.8 copy-start.12
  92.7 1.0 copy-start.13
  93.8 1.6 copy-start.16
  95.4 1.6 copy-start.18
  100.0 2.0 %collective-permute-start.13 = (bf16[16,16,1024]{2,1,0:T(8,128)(2,1)S(1)}, bf16[16,16,1024]{2,1,0:T(8,128)(2,1)S(1)}, u32[]{:S(2)}, u32[]{:S(2)}) collective-permute-start(bf16[16,16,1024]{2,1,0:T(8,128)(2,1)S(1)} %get-tuple-element.47), channel_id=1, source_target_pairs={{0,1},{1,0},{2,3},{3,2},{4,5},{5,4},{6,7},{7,6},{8,9},{9,8},{10,11... | collective-permute-start | bytes 1572872 | tf_op jit(solution)/shard_map/ppermute | solution.py:30
  102.9 50.8 %copy-start.11 = (bf16[256,2048]{1,0:T(8,128)(2,1)S(1)}, bf16[256,2048]{1,0:T(8,128)(2,1)}, u32[]{:S(2)}) copy-start(bf16[256,2048]{1,0:T(8,128)(2,1)} %copy-done.9) | copy-start | bytes 3145732
  102.9 20.1 %all-to-all-start.2 = ((bf16[16,16,1024]{2,1,0:T(8,128)(2,1)}), bf16[16,16,1024]{2,1,0:T(8,128)(2,1)S(1)}, u32[]{:S(2)}, u32[]{:S(2)}) async-start(bf16[16,16,1024]{2,1,0:T(8,128)(2,1)} %add.13), calls=%async_computation.2 | async-start | bytes 1048576 | tf_op jit(solution)/shard_map/all_to_all | solution.py:262
  108.7 7.6 %collective-permute-start.15 = (bf16[256,512]{1,0:T(8,128)(2,1)}, bf16[256,512]{1,0:T(8,128)(2,1)}, u32[]{:S(2)}, u32[]{:S(2)}) collective-permute-start(bf16[256,512]{1,0:T(8,128)(2,1)} %copy-done.21), channel_id=1, source_target_pairs={{0,2},{2,0},{1,3},{3,1},{4,6},{6,4},{5,7},{7,5},{8,10},{10,8},{9,1... | collective-permute-start | bytes 786440 | tf_op jit(solution)/shard_map/ppermute | solution.py:30
  109.6 13.5 %collective-permute-start.14 = (bf16[256,512]{1,0:T(8,128)(2,1)}, bf16[256,512]{1,0:T(8,128)(2,1)}, u32[]{:S(2)}, u32[]{:S(2)}) collective-permute-start(bf16[256,512]{1,0:T(8,128)(2,1)} %copy-done.20), channel_id=1, source_target_pairs={{0,2},{2,0},{1,3},{3,1},{4,6},{6,4},{5,7},{7,5},{8,10},{10,8},{9,1... | collective-permute-start | bytes 786440 | tf_op jit(solution)/shard_map/ppermute | solution.py:30
  110.3 17.3 %collective-permute-start.16 = (bf16[256,512]{1,0:T(8,128)(2,1)}, bf16[256,512]{1,0:T(8,128)(2,1)}, u32[]{:S(2)}, u32[]{:S(2)}) collective-permute-start(bf16[256,512]{1,0:T(8,128)(2,1)} %copy-done.24), channel_id=1, source_target_pairs={{0,2},{2,0},{1,3},{3,1},{4,6},{6,4},{5,7},{7,5},{8,10},{10,8},{9,1... | collective-permute-start | bytes 786440 | tf_op jit(solution)/shard_map/ppermute | solution.py:30
  111.0 22.2 %collective-permute-start.17 = (bf16[256,512]{1,0:T(8,128)(2,1)}, bf16[256,512]{1,0:T(8,128)(2,1)}, u32[]{:S(2)}, u32[]{:S(2)}) collective-permute-start(bf16[256,512]{1,0:T(8,128)(2,1)} %copy-done.23), channel_id=1, source_target_pairs={{0,2},{2,0},{1,3},{3,1},{4,6},{6,4},{5,7},{7,5},{8,10},{10,8},{9,1... | collective-permute-start | bytes 786440 | tf_op jit(solution)/shard_map/ppermute | solution.py:30
  111.8 21.4 %collective-permute-start.18 = (bf16[256,512]{1,0:T(8,128)(2,1)}, bf16[256,512]{1,0:T(8,128)(2,1)}, u32[]{:S(2)}, u32[]{:S(2)}) collective-permute-start(bf16[256,512]{1,0:T(8,128)(2,1)} %copy-done.22), channel_id=1, source_target_pairs={{0,1},{1,0},{2,3},{3,2},{4,5},{5,4},{6,7},{7,6},{8,9},{9,8},{10,11... | collective-permute-start | bytes 786440 | tf_op jit(solution)/shard_map/ppermute | solution.py:30
  116.3 29.3 %collective-permute-start.20 = (bf16[256,512]{1,0:T(8,128)(2,1)}, bf16[256,512]{1,0:T(8,128)(2,1)}, u32[]{:S(2)}, u32[]{:S(2)}) collective-permute-start(bf16[256,512]{1,0:T(8,128)(2,1)} %collective-permute-done.15), channel_id=1, source_target_pairs={{0,1},{1,0},{2,3},{3,2},{4,5},{5,4},{6,7},{7,6},{8,9},{9,8},{10,11... | collective-permute-start | bytes 786440 | tf_op jit(solution)/shard_map/ppermute | solution.py:30
  133.2 3.8 %collective-permute-start.19 = (f32[16,1024]{1,0:T(8,128)S(1)}, f32[16,1024]{1,0:T(8,128)S(1)}, u32[]{:S(2)}, u32[]{:S(2)}) collective-permute-start(f32[16,1024]{1,0:T(8,128)S(1)} %sum.3), channel_id=1, source_target_pairs={{0,2},{2,0},{1,3},{3,1},{4,6},{6,4},{5,7},{7,5},{8,10},{10,8},{9,1... | collective-permute-start | bytes 196616 | tf_op jit(solution)/shard_map/ppermute | solution.py:30
  137.1 8.6 %collective-permute-start.21 = (f32[16,1024]{1,0:T(8,128)S(1)}, f32[16,1024]{1,0:T(8,128)S(1)}, u32[]{:S(2)}, u32[]{:S(2)}) collective-permute-start(f32[16,1024]{1,0:T(8,128)S(1)} %add.9.part), channel_id=1, source_target_pairs={{0,64},{64,128},{128,192},{192,0},{1,65},{65,129},{129,193},{193,1... | collective-permute-start | bytes 196616 | tf_op jit(solution)/shard_map/ppermute | solution.py:271
  139.2 7.0 %collective-permute-start.22 = (f32[16,1024]{1,0:T(8,128)S(1)}, f32[16,1024]{1,0:T(8,128)S(1)}, u32[]{:S(2)}, u32[]{:S(2)}) collective-permute-start(f32[16,1024]{1,0:T(8,128)S(1)} %add.9.part), channel_id=1, source_target_pairs={{0,128},{64,192},{128,0},{192,64},{1,129},{65,193},{129,1},{193,65... | collective-permute-start | bytes 196616 | tf_op jit(solution)/shard_map/ppermute | solution.py:271
  140.4 5.9 %collective-permute-start.23 = (f32[16,1024]{1,0:T(8,128)S(1)}, f32[16,1024]{1,0:T(8,128)S(1)}, u32[]{:S(2)}, u32[]{:S(2)}) collective-permute-start(f32[16,1024]{1,0:T(8,128)S(1)} %add.9.part), channel_id=1, source_target_pairs={{0,192},{64,0},{128,64},{192,128},{1,193},{65,1},{129,65},{193,129... | collective-permute-start | bytes 196616 | tf_op jit(solution)/shard_map/ppermute | solution.py:271
  147.1 17.2 %all-to-all-start.3 = ((bf16[16,16,1024]{2,1,0:T(8,128)(2,1)}), bf16[16,16,1024]{2,1,0:T(8,128)(2,1)S(1)}, u32[]{:S(2)}, u32[]{:S(2)}) async-start(bf16[16,16,1024]{2,1,0:T(8,128)(2,1)} %spread.3), calls=%async_computation.3 | async-start | bytes 1048576 | tf_op jit(solution)/shard_map/all_to_all | solution.py:283
  153.6 2.2 %copy-start.1 = (f32[512,2048]{1,0:T(8,128)S(1)}, f32[512,2048]{1,0:T(8,128)}, u32[]{:S(2)}) copy-start(f32[512,2048]{1,0:T(8,128)} %copy-done) | copy-start | bytes 12582916
  158.7 2.0 %copy-start.2 = (f32[512,2048]{1,0:T(8,128)}, f32[512,2048]{1,0:T(8,128)S(1)}, u32[]{:S(2)}) copy-start(f32[512,2048]{1,0:T(8,128)S(1)} %merge.3.merged) | copy-start | bytes 12582916
  164.3 5.9 %collective-permute-start.24 = (bf16[16,16,1024]{2,1,0:T(8,128)(2,1)S(1)}, bf16[16,16,1024]{2,1,0:T(8,128)(2,1)S(1)}, u32[]{:S(2)}, u32[]{:S(2)}) collective-permute-start(bf16[16,16,1024]{2,1,0:T(8,128)(2,1)S(1)} %all-to-all-done.3.mine), channel_id=1, source_target_pairs={{0,1},{1,0},{2,3},{3,2},{4,5},{5,4},{6,7},{7,6},{8,9},{9,8},{10,11... | collective-permute-start | bytes 1572872 | tf_op jit(solution)/shard_map/ppermute | solution.py:30
  168.1 2.1 %collective-permute-start.25 = (bf16[256,512]{1,0:T(8,128)(2,1)}, bf16[256,512]{1,0:T(8,128)(2,1)S(1)}, u32[]{:S(2)}, u32[]{:S(2)}) collective-permute-start(bf16[256,512]{1,0:T(8,128)(2,1)} %collective-permute-done.17), channel_id=1, source_target_pairs={{0,1},{1,0},{2,3},{3,2},{4,5},{5,4},{6,7},{7,6},{8,9},{9,8},{10,11... | collective-permute-start | bytes 786440 | tf_op jit(solution)/shard_map/ppermute | solution.py:30
  170.2 2.2 %copy-start.3 = (f32[512,2048]{1,0:T(8,128)S(1)}, f32[512,2048]{1,0:T(8,128)}, u32[]{:S(2)}) copy-start(f32[512,2048]{1,0:T(8,128)} %copy-done.2) | copy-start | bytes 12582916
where the time goes:
time: 179 us; the launch traced here: 178 us
  starting transfers between devices  66.4 us (37%)
  waiting for transfers between devices  45.6 us (25%)
  Pallas kernels  39.7 us (22%)
  local copies, waits for them, and re-layouts  25.3 us (14%)
    ppermute x20, waiting for transfers between devices, swap(): return lax.ppermute(x, axis, [(0, 1), (1, 0)])  34.4 us
    pallas_call x16, Pallas kernels, call(): pl.pallas_call(kernel, out_shape=[jax.ShapeDtypeStruct(s, d) for s, d in...  34.1 us
    ppermute x20, starting transfers between devices, swap(): return lax.ppermute(x, axis, [(0, 1), (1, 0)])  28.8 us
    unnamed x50, local copies, waits for them, and re-layouts  25.3 us
    ppermute x6, starting transfers between devices, across_z(): lax.ppermute(part, 'zh', [(i, (i + step) % 4) for i in range(4)])  14.5 us
    all_to_all x2, starting transfers between devices, across_plane(): parts = lax.all_to_all(half, ('y', 'x'), 0, 0)  12.8 us
    all_to_all x2, waiting for transfers between devices, across_plane(): parts = lax.all_to_all(half, ('y', 'x'), 0, 0)  10.4 us
    all_to_all x2, starting transfers between devices, back_over_plane(): return lax.all_to_all(whole, ('y', 'x'), 0, 0)  10.3 us
  transfers between devices with their start and end apart: 30, of which 13 were waited for; matrix products, arithmetic and copies ran while one was open for 0% of the time, Pallas kernels for 16%

commit v1 on v0

--- a/solution.py
+++ b/solution.py
@@ -24,6 +24,7 @@
 CHUNKS, CHUNK_ROWS, CHUNK_COLS = 16, 16, 1024
 VMEM = pl.BlockSpec(memory_space=pltpu.VMEM)
 SMEM = pl.BlockSpec(memory_space=pltpu.SMEM)
+ANY = pl.BlockSpec(memory_space=pl.ANY)
 
 
 def swap(x, axis):
@@ -41,6 +42,15 @@
 
 def chunk_at(n):
     return n // 2 * CHUNK_ROWS, n % 2 * CHUNK_COLS
+
+
+def fetch(sources, targets, sems):
+    copies = [
+        pltpu.make_async_copy(src, dst, sems.at[n]) for n, (src, dst) in enumerate(zip(sources, targets))
+    ]
+    for copy in copies:
+        copy.start()
+    return copies
 
 
 def split_halves(core, total, keep, send):
@@ -65,36 +75,50 @@
     return pl.ds(pl.multiple_of((zl * 2 + core) * ROWS, ROWS), ROWS)
 
 
-def prepare_kernel(at, ctx, err, own, near, far, diag, high, low):
+def prepare_kernel(at, ctx, err, own, near, far, high, low):
     zl, core = at[0], at[1]
     own[...] = ctx[:, block(zl, core)]
     near[...] = ctx[:, block(zl, 1 - core)]
-    far[...] = ctx[:, block(1 - zl, core)]
-    diag[...] = ctx[:, block(1 - zl, 1 - core)]
+    far[0] = ctx[:, block(1 - zl, core)]
+    far[1] = ctx[:, block(1 - zl, 1 - core)]
     high[...], low[...] = two(err[...])
 
 
-def left_kernel(scale, at, og, ctx, high, low, w0, w1, w2, w3, keep, send, total):
+def left_kernel(
+    scale, at, og, ctx, high_hbm, low_hbm, w0, w1, w2, w3, keep, send, total, high, low, sems
+):
     zl, core = at[0], at[1]
+    copies = fetch((high_hbm, low_hbm), (high, low), sems)
     where = ((zl, core), (zl, 1 - core), (1 - zl, core), (1 - zl, 1 - core))
     proj = jnp.zeros((TOK, RANK), F32)
+    for (a, b), w in zip(where, (w0, w1, w2, w3)):
+        proj += mm(og[:, block(a, b)], w[...], 1, 0)
+    first, second = two(proj * scale)
+    total[...] = mm(first, ctx[...], 0, 0) + mm(second, ctx[...], 0, 0)
+    for copy in copies:
+        copy.wait()
     own = jnp.zeros((ROWS, RANK), F32)
     for (a, b), w in zip(where, (w0, w1, w2, w3)):
         cols = block(a, b)
-        proj += mm(og[:, cols], w[...], 1, 0)
         own += mm(high[:, cols], w[...], 1, 0) + mm(low[:, cols], w[...], 1, 0)
-    first, second = two(proj * scale)
-    total[...] = mm(first, ctx[...], 0, 0) + mm(second, ctx[...], 0, 0)
     total[:, block(zl, core)] += own.T
     split_halves(core, total, keep, send)
 
 
-def right_kernel(scale, at, ctx, og, high, low, mine, other, keep, send, left, total):
+def right_kernel(
+    scale, at, ctx, og, high_hbm, low_hbm, mine_hbm, other_hbm,
+    keep, send, left, total, high, low, mine, other, sems,
+):
     zl, core = at[0], at[1]
+    copies = fetch((mine_hbm, other_hbm, high_hbm, low_hbm), (mine, other, high, low), sems)
+    copies[0].wait()
+    copies[1].wait()
     join_halves(core, mine, other, left)
     first, second = two(mm(ctx[...], left[...], 1, 1) * scale)
     total[...] = mm(first, og[...], 0, 0) + mm(second, og[...], 0, 0)
     own = left[:, block(zl, core)]
+    copies[2].wait()
+    copies[3].wait()
     total[...] += mm(own, high[...], 1, 0) + mm(own, low[...], 1, 0)
     split_halves(core, total, keep, send)
 
@@ -185,8 +209,11 @@
     basis[...] = (mm(first, own, 1, 0) + mm(second, own, 1, 0)).astype(BF16)
 
 
-def grad_kernel(g0, g1, g2, g3, weight, o0, o1, o2, o3):
-    for g, o in ((g0, o0), (g1, o1), (g2, o2), (g3, o3)):
+def grad_kernel(h0, h1, h2, h3, weight_hbm, o0, o1, far, weight, g0, g1, g2, g3, sems):
+    copies = fetch((weight_hbm, h0, h1, h2, h3), (weight, g0, g1, g2, g3), sems)
+    copies[0].wait()
+    for g, o, copy in zip((g0, g1, g2, g3), (o0, o1, far.at[0], far.at[1]), copies[1:]):
+        copy.wait()
         o[...] = mm(g[...], weight[...], 1, 1).astype(BF16)
 
 
@@ -196,19 +223,24 @@
 
 
 def last_kernel(
-    share, at, mine, other, inverse, basis, merged, i0, i1, i2, i3, new_error, factor_q, in_grad, right
+    share, scale, at, mine_hbm, other_hbm, inverse, basis, merged, c2, c3, g2, g3, i0, i1, i2, i3,
+    new_error, factor_q, in_grad, right, mine, other, sems,
 ):
     step = pl.program_id(0)
     zl, core = at[0], at[1]
 
     @pl.when(step == 0)
     def _():
+        copies = fetch((mine_hbm, other_hbm), (mine, other), sems)
+        copies[0].wait()
+        copies[1].wait()
         join_halves(core, mine, other, right)
 
     cols = pl.ds(pl.multiple_of(step * ROWS, ROWS), ROWS)
     first, second = two(inverse[...])
     q = (mm(first, right[:, cols], 1, 0) + mm(second, right[:, cols], 1, 0)) * share
-    new_error[...] = merged[...] - mm(basis[...], q.astype(BF16), 0, 0)
+    total = mm(c2[...], g2[...], 0, 0) + mm(c3[...], g3[...], 0, 0)
+    new_error[...] = merged[...] + total * scale - mm(basis[...], q.astype(BF16), 0, 0)
     at_zl, at_core = step // 2, step % 2
 
     @pl.when((at_zl == zl) & (at_core == core))
@@ -233,14 +265,27 @@
     return math.prod(shape) * jnp.dtype(dtype).itemsize
 
 
-def call(kernel, outs, args, flops, name, scratch=(), alias=None, limit=16):
+def in_hbm(x):
+    return pltpu.with_memory_space_constraint(x, pltpu.HBM)
+
+
+def call(
+    kernel, outs, args, flops, name, scratch=(), alias=None, limit=20, loose=(), held=(), free=False, sems=0
+):
+    args = [in_hbm(a) if n in held else a for n, a in enumerate(args)]
     moved = sum(size(a.shape, a.dtype) for a in args) + sum(size(s, d) for s, d in outs)
+    scratch = [pltpu.VMEM(s, d) for s, d in scratch]
+    if sems:
+        scratch.append(pltpu.SemaphoreType.DMA((sems,)))
     return pl.pallas_call(
         kernel,
-        out_shape=[jax.ShapeDtypeStruct(s, d) for s, d in outs],
-        in_specs=[SMEM if a.dtype == jnp.int32 else VMEM for a in args],
-        out_specs=[VMEM] * len(outs),
-        scratch_shapes=[pltpu.VMEM(s, d) for s, d in scratch],
+        out_shape=[(pltpu.HBM if free else jax.ShapeDtypeStruct)(s, d) for s, d in outs],
+        in_specs=[
+            SMEM if a.dtype == jnp.int32 else ANY if n in loose or n in held else VMEM
+            for n, a in enumerate(args)
+        ],
+        out_specs=[pl.BlockSpec(s, lambda s=s: (0,) * len(s)) if free else VMEM for s, _ in outs],
+        scratch_shapes=scratch,
         input_output_aliases=alias or {},
         compiler_params=pltpu.CompilerParams(vmem_limit_bytes=limit * 2**20),
         cost_estimate=pl.CostEstimate(flops=flops, bytes_accessed=moved, transcendentals=0),
@@ -248,6 +293,37 @@
     )(*args)
 
 
+def call_grid(kernel, steps, outs, ins, args, flops, name, scratch=(), sems=0, limit=24):
+    args = [a if spec in (SMEM, ANY, VMEM) else in_hbm(a) for a, spec in zip(args, ins)]
+    moved = sum(size(a.shape, a.dtype) for a in args) + sum(size(s, d) for s, d, _ in outs)
+    scratch = [pltpu.VMEM(s, d) for s, d in scratch]
+    if sems:
+        scratch.append(pltpu.SemaphoreType.DMA((sems,)))
+    return pl.pallas_call(
+        kernel,
+        grid=(steps,),
+        out_shape=[pltpu.HBM(s, d) for s, d, _ in outs],
+        in_specs=ins,
+        out_specs=[spec for _, _, spec in outs],
+        scratch_shapes=scratch,
+        compiler_params=pltpu.CompilerParams(vmem_limit_bytes=limit * 2**20),
+        cost_estimate=pl.CostEstimate(flops=flops, bytes_accessed=moved, transcendentals=0),
+        name=name,
+    )(*args)
+
+
+def whole(*shape):
+    return pl.BlockSpec(shape, lambda j: (0,) * len(shape))
+
+
+def column(rows):
+    return pl.BlockSpec((rows, ROWS), lambda j: (0, j))
+
+
+def rows_of(rows, cols):
+    return pl.BlockSpec((rows, cols), lambda j: (j, 0))
+
+
 CHUNKED = (CHUNKS, CHUNK_ROWS, CHUNK_COLS)
 CHUNK = (CHUNK_ROWS, CHUNK_COLS)
 
@@ -256,9 +332,9 @@
     return lax.optimization_barrier((x,) + others)[0]
 
 
-def across_plane(keep, send):
+def across_plane(keep, send, beside=()):
     got = swap(send, "core")
-    (half,) = call(add_kernel, [(CHUNKED, BF16)], (keep, got), 1_000_000, "add")
+    (half,) = call(add_kernel, [(CHUNKED, BF16)], (keep, tied(got, *beside)), 1_000_000, "add")
     parts = lax.all_to_all(half, ("y", "x"), 0, 0)
     (part,) = call(sum_kernel, [(CHUNK, F32)], (parts,), 1_000_000, "sum")
     return part
@@ -290,49 +366,66 @@
     at = jnp.stack([zl, core]).astype(jnp.int32)
     error = error[0]
     tokens = ((TOK, ROWS), BF16)
+    pair = ((2, TOK, ROWS), BF16)
 
     warm_far = swap(warm, "zl")
     warm_near = swap(warm, "core")
-    c_own, c_near, c_far, c_diag, high, low = call(
+    quarter = rows_of(TOK // 4, ROWS)
+    strip = rows_of(ROWS // 4, FEAT)
+    c_own, c_near, c_far, high, low = call_grid(
         prepare_kernel,
-        [tokens] * 4 + [((ROWS, FEAT), BF16)] * 2,
+        4,
+        [tokens + (quarter,)] * 2
+        + [pair + (pl.BlockSpec((2, TOK // 4, ROWS), lambda j: (0, j, 0)),)]
+        + [((ROWS, FEAT), BF16, strip)] * 2,
+        [SMEM, rows_of(TOK // 4, FEAT), strip],
         (at, context, error),
         4_000_000,
         "prepare",
     )
     warm_diag = swap(tied(warm_far, low), "core")
 
+    big = ((ROWS, FEAT), BF16)
     keep, send = call(
         functools.partial(left_kernel, scale),
         [(CHUNKED, F32), (CHUNKED, BF16)],
         (at, out_grad, context, high, low, warm, warm_near, warm_far, warm_diag),
         2_000_000_000,
         "left",
-        [((RANK, FEAT), F32)],
-    )
-    g_far = swap(tied(out_grad, warm_far), "zl")
-    g_near = swap(tied(out_grad, warm_far), "core")
+        [((RANK, FEAT), F32), big, big],
+        held=(3, 4),
+        sems=2,
+    )
+    g_far = swap(tied(out_grad, warm_far, low), "zl")
+    g_near = swap(tied(out_grad, warm_far, low), "core")
     part = across_plane(keep, send)
-    g_diag = swap(g_far, "core")
+    g_diag = swap(tied(g_far, part), "core")
     c_near = swap(c_near, "core")
     zs = across_z(tied(part, g_far, g_near))
-    (merged,) = call(
+    (merged,) = call_grid(
         functools.partial(merge_kernel, scale),
-        [((ROWS, FEAT), F32)],
+        4,
+        [((ROWS, FEAT), F32, column(ROWS))],
+        [column(ROWS), whole(TOK, ROWS), whole(TOK, ROWS), column(TOK), column(TOK)],
         (error, c_own, c_near, out_grad, g_near),
         1_100_000_000,
         "merge",
     )
-    c_far, c_diag = (tied(c, zs[1]) for c in (c_far, c_diag))
-    c_far, c_diag = swap(c_far, "zl"), swap(c_diag, "zl")
+    c_far = swap(tied(c_far, zs[1]), "zl")
     mine = back_over_plane(*zs, beside=(g_diag, merged))
 
-    i_own, i_near, i_far, i_diag = call(
-        grad_kernel, [tokens] * 4, (out_grad, g_near, g_far, g_diag, weight), 2_200_000_000, "grad"
-    )
-    mine = tied(mine, i_own)
-    other = swap(mine, "core")
-    i_diag = swap(i_diag, "zl")
+    i_own, i_near, i_far = call(
+        grad_kernel,
+        [tokens] * 2 + [pair],
+        (out_grad, g_near, g_far, g_diag, weight),
+        2_200_000_000,
+        "grad",
+        [big] + [((TOK, FEAT), BF16)] * 4,
+        held=range(5),
+        free=True,
+        sems=5,
+    )
+    other = swap(tied(mine, i_own, c_far), "core")
     i_far = swap(i_far, "zl")
     i_near = swap(i_near, "core")
 
@@ -342,15 +435,18 @@
         (at, context, out_grad, high, low, mine, other),
         2_000_000_000,
         "right",
-        [((RANK, FEAT), F32)],
+        [((RANK, FEAT), F32), big, big, (CHUNKED, BF16), (CHUNKED, BF16)],
+        loose=(6,),
+        held=(3, 4, 5),
+        sems=4,
     )
     part = across_plane(keep, send)
 
     table = ((RANK, 2 * RANK), F32)
     (a,) = call(gram_kernel, [table], (left,), 300_000_000, "gram")
-    part = tied(part, a, c_far, c_diag, i_far, i_diag, i_near)
-    i_diag = swap(i_diag, "core")
-    c_diag = swap(c_diag, "core")
+    part = tied(part, a, i_far, i_near)
+    i_diag = swap(tied(i_far, part)[1], "core")
+    c_diag = swap(c_far[1], "core")
     (a,) = call(
         functools.partial(step_kernel, PART), [table], (a,), 300_000_000, "step", alias={0: 0}
     )
@@ -358,7 +454,7 @@
     (a,) = call(
         functools.partial(step_kernel, 2 * PART), [table], (a,), 300_000_000, "step", alias={0: 0}
     )
-    mine = back_over_plane(*zs, beside=(a, c_diag))
+    mine = back_over_plane(*zs, beside=(a, c_diag, i_diag))
     inverse, basis = call(
         basis_kernel,
         [((RANK, RANK), F32), ((RANK, ROWS), BF16)],
@@ -367,36 +463,29 @@
         "basis",
         [table],
     )
-    (merged,) = call(
-        functools.partial(merge_kernel, scale),
-        [((ROWS, FEAT), F32)],
-        (merged, c_far, c_diag, g_far, g_diag),
-        1_100_000_000,
-        "merge",
-        alias={0: 0},
-    )
-    mine = tied(mine, merged, basis)
-    other = swap(mine, "core")
-
-    whole = lambda *shape: pl.BlockSpec(shape, lambda j: (0,) * len(shape))
-    column = lambda rows: pl.BlockSpec((rows, ROWS), lambda j: (0, j))
-    new_error, factor_q, in_grad = pl.pallas_call(
-        functools.partial(last_kernel, 1.0 / (SIZES[0] * SIZES[1] * SIZES[2])),
-        grid=(4,),
-        out_shape=[
-            jax.ShapeDtypeStruct((ROWS, FEAT), F32),
-            jax.ShapeDtypeStruct((ROWS, RANK), F32),
-            jax.ShapeDtypeStruct((TOK, FEAT), BF16),
+    other = swap(tied(mine, basis), "core")
+
+    block_in = whole(TOK, ROWS)
+    first = pl.BlockSpec((None, TOK, ROWS), lambda j: (0, 0, 0))
+    new_error, factor_q, in_grad = call_grid(
+        functools.partial(last_kernel, 1.0 / (SIZES[0] * SIZES[1] * SIZES[2]), scale),
+        4,
+        [
+            ((ROWS, FEAT), F32, column(ROWS)),
+            ((ROWS, RANK), F32, whole(ROWS, RANK)),
+            ((TOK, FEAT), BF16, column(TOK)),
         ],
-        in_specs=[SMEM, VMEM, VMEM, VMEM, VMEM, column(ROWS)] + [VMEM] * 4,
-        out_specs=[column(ROWS), whole(ROWS, RANK), column(TOK)],
-        scratch_shapes=[pltpu.VMEM((RANK, FEAT), BF16)],
-        compiler_params=pltpu.CompilerParams(vmem_limit_bytes=20 * 2**20),
-        cost_estimate=pl.CostEstimate(
-            flops=1_200_000_000, bytes_accessed=12_000_000, transcendentals=0
+        [SMEM, ANY, ANY, VMEM, VMEM, column(ROWS), first, block_in, column(TOK), column(TOK)]
+        + [block_in, block_in, first, block_in],
+        (
+            at, mine, other, inverse, basis, merged, c_far, c_diag, g_far, g_diag,
+            i_own, i_near, i_far, i_diag,
         ),
-        name="last",
-    )(at, mine, other, inverse, basis, merged, i_own, i_near, i_far, i_diag)
+        2_300_000_000,
+        "last",
+        [((RANK, FEAT), BF16), (CHUNKED, BF16), (CHUNKED, BF16)],
+        sems=2,
+    )
     return in_grad, new_error[None], factor_q
 
 

time: 179 us -> 150 us (0.84)
  local copies, waits for them, and re-layouts: 25.3 us -> 2.75 us
  Pallas kernels: 39.7 us -> 54.6 us
  starting transfers between devices: 66.4 us -> 55.7 us
  waiting for transfers between devices: 45.6 us -> 34.9 us
    ppermute x20 -> x18, waiting for transfers between devices: 34.4 us -> 7.54 us  [swap(): return lax.ppermute(x, axis, [(0, 1), (1, 0)])]
    unnamed x50 -> x26, local copies, waits for them, and re-layouts: 25.3 us -> 1.76 us
    pallas_call x17 -> x16, Pallas kernels: 39.7 us -> 54.6 us  [the longest x13 35.1 us: call(): pl.pallas_call(kernel, out_shape=[(pltpu.HBM if free else jax.ShapeDtypeS...]
    all_to_all x2, waiting for transfers between devices: 0.13 us -> 9.79 us  [back_over_plane(): return lax.all_to_all(whole, ('y', 'x'), 0, 0)]
    ppermute x20 -> x18, starting transfers between devices: 28.8 us -> 20.4 us  [swap(): return lax.ppermute(x, axis, [(0, 1), (1, 0)])]
    all_to_all x2, waiting for transfers between devices: 10.4 us -> 15.4 us  [across_plane(): parts = lax.all_to_all(half, ('y', 'x'), 0, 0)]
    ppermute x6, starting transfers between devices: 14.5 us -> 17.7 us  [across_z(): lax.ppermute(part, 'zh', [(i, (i + step) % 4) for i in range(4)])]
    all_to_all x2, starting transfers between devices: 10.3 us -> 7.33 us  [back_over_plane(): return lax.all_to_all(whole, ('y', 'x'), 0, 0)]
  transfers between devices with their start and end apart: 30 -> 28, of which waited for: 13 -> 10; matrix products, arithmetic and copies ran while one was open for 0% -> 1% of each run, Pallas kernels for 16% -> 27%
where the time goes in v1:
time: 150 us; the launch traced here: 149 us
  starting transfers between devices  55.7 us (37%)
  Pallas kernels  54.6 us (36%)
  waiting for transfers between devices  34.9 us (23%)
  local copies, waits for them, and re-layouts  2.75 us (2%)
    pallas_call x13, Pallas kernels, call(): pl.pallas_call(kernel, out_shape=[(pltpu.HBM if free else jax.ShapeDtypeS...  35.1 us
    ppermute x18, starting transfers between devices, swap(): return lax.ppermute(x, axis, [(0, 1), (1, 0)])  20.4 us
    pallas_call x3, Pallas kernels, call_grid(): pl.pallas_call(kernel, grid=(steps,), out_shape=[pltpu.HBM(s, d) for s, d...  19.4 us
    ppermute x6, starting transfers between devices, across_z(): lax.ppermute(part, 'zh', [(i, (i + step) % 4) for i in range(4)])  17.7 us
    all_to_all x2, waiting for transfers between devices, across_plane(): parts = lax.all_to_all(half, ('y', 'x'), 0, 0)  15.4 us
    all_to_all x2, starting transfers between devices, across_plane(): parts = lax.all_to_all(half, ('y', 'x'), 0, 0)  10.3 us
    all_to_all x2, waiting for transfers between devices, back_over_plane(): return lax.all_to_all(whole, ('y', 'x'), 0, 0)  9.79 us
    ppermute x18, waiting for transfers between devices, swap(): return lax.ppermute(x, axis, [(0, 1), (1, 0)])  7.54 us
  transfers between devices with their start and end apart: 28, of which 10 were waited for; matrix products, arithmetic and copies ran while one was open for 1% of the time, Pallas kernels for 27%

profile of v1, /device:TPU:1, one launch (start us, length us, event | category | flops | bytes accessed | tf_op | source)
XLA Modules:
  0.0 149.2 jit_solution(5884458654750625526)
XLA Ops:
  0.6 0.0 copy-start
  0.7 0.0 copy-start.1
  0.7 2.6 %collective-permute-start.1 = (bf16[512,256]{1,0:T(8,128)(2,1)}, bf16[512,256]{1,0:T(8,128)(2,1)S(1)}, u32[]{:S(2)}, u32[]{:S(2)}) collective-permute-start(bf16[512,256]{1,0:T(8,128)(2,1)} %w0.1), channel_id=1, source_target_pairs={{0,2},{2,0},{1,3},{3,1},{4,6},{6,4},{5,7},{7,5},{8,10},{10,8},{9,1... | collective-permute-start | bytes 786440 | tf_op jit(solution)/shard_map/ppermute | solution.py:31
  3.2 1.0 collective-permute-start
  4.2 0.1 pad_add_fusion.at
  4.2 5.4 %prepare.1 = (bf16[256,512]{1,0:T(8,128)(2,1)}, bf16[256,512]{1,0:T(8,128)(2,1)}, bf16[2,256,512]{2,1,0:T(8,128)(2,1)}, bf16[512,2048]{1,0:T(8,128)(2,1)}, bf16[512,2048]{1,0:T(8,128)(2,1)}) custom-call(s32[2]{0:T(128)S(1)} %pad_add_fusion.at, bf16[256,2048]{1,0:T(8,128)(2,1)} %ctx.5, f32[512,2048]{1,0:T(8,128)} %bitcast.8), custom_call_target="tpu_custom_call" | custom-call | flops 4000000 | bytes 10485768 | tf_op jit(solution)/shard_map/prepare/pallas_call | solution.py:302
  9.6 1.1 collective-permute-start.2
  10.7 1.5 collective-permute-start.4
  12.2 0.0 collective-permute-done.w1
  12.2 0.0 collective-permute-done.2.w3
  12.2 5.7 %left.1 = (f32[16,16,1024]{2,1,0:T(8,128)S(1)}, bf16[16,16,1024]{2,1,0:T(8,128)(2,1)S(1)}) custom-call(s32[2]{0:T(128)S(1)} %pad_add_fusion.at, bf16[256,2048]{1,0:T(8,128)(2,1)S(1)} %copy-done.1, bf16[256,2048]{1,0:T(8,128)(2,1)S(1)} %copy-done, bf16[512,2048]{1,0:T(8,128)(2,1)} %get-tuple-element.33.high_hbm, bf16[512,2048]{1,0:T(8,128)(2,1)} %get-tuple-element.34.low_hbm, ...), custom_call_target="tpu_custom_call" | custom-call | flops 2000000000 | bytes 8912904 | tf_op jit(solution)/shard_map/left/pallas_call | solution.py:280
  17.9 0.4 collective-permute-start.3
  18.2 1.6 %collective-permute-done.3.got = bf16[16,16,1024]{2,1,0:T(8,128)(2,1)S(1)} collective-permute-done((bf16[16,16,1024]{2,1,0:T(8,128)(2,1)S(1)}, bf16[16,16,1024]{2,1,0:T(8,128)(2,1)S(1)}, u32[]{:S(2)}, u32[]{:S(2)}) %collective-permute-start.3) | collective-permute-done | bytes 524320 | tf_op jit(solution)/shard_map/ppermute | solution.py:31
  19.9 0.9 add.12
  20.8 6.8 %all-to-all-start = ((bf16[16,16,1024]{2,1,0:T(8,128)(2,1)}), bf16[16,16,1024]{2,1,0:T(8,128)(2,1)S(1)}, u32[]{:S(2)}, u32[]{:S(2)}) async-start(bf16[16,16,1024]{2,1,0:T(8,128)(2,1)} %add.12), calls=%async_computation | async-start | bytes 1048576 | tf_op jit(solution)/shard_map/all_to_all | solution.py:338
  27.5 0.6 collective-permute-start.5
  28.2 10.2 %all-to-all-done.parts = bf16[16,16,1024]{2,1,0:T(8,128)(2,1)S(1)} async-done(((bf16[16,16,1024]{2,1,0:T(8,128)(2,1)}), bf16[16,16,1024]{2,1,0:T(8,128)(2,1)S(1)}, u32[]{:S(2)}, u32[]{:S(2)}) %all-to-all-start) | async-done | bytes 524320 | tf_op jit(solution)/shard_map/all_to_all | solution.py:338
  38.3 0.1 sum.2
  38.4 0.0 collective-permute-done.4.h2.g2
  38.4 1.7 %collective-permute-start.7 = (bf16[256,2048]{1,0:T(8,128)(2,1)}, bf16[256,2048]{1,0:T(8,128)(2,1)S(1)}, u32[]{:S(2)}, u32[]{:S(2)}) collective-permute-start(bf16[256,2048]{1,0:T(8,128)(2,1)} %collective-permute-done.4.h2.g2), channel_id=1, source_target_pairs={{0,1},{1,0},{2,3},{3,2},{4,5},{5,4},{6,7},{7,6},{8,9},{9,8},{10,11... | collective-permute-start | bytes 3145736 | tf_op jit(solution)/shard_map/ppermute | solution.py:31
  40.2 0.1 collective-permute-start.8
  40.3 1.1 collective-permute-start.6
  41.4 2.0 %collective-permute-done.6 = f32[16,1024]{1,0:T(8,128)S(1)} collective-permute-done((f32[16,1024]{1,0:T(8,128)S(1)}, f32[16,1024]{1,0:T(8,128)S(1)}, u32[]{:S(2)}, u32[]{:S(2)}) %collective-permute-start.6) | collective-permute-done | bytes 65568 | tf_op jit(solution)/shard_map/ppermute | solution.py:31
  43.4 3.1 %collective-permute-start.9 = (f32[16,1024]{1,0:T(8,128)S(1)}, f32[16,1024]{1,0:T(8,128)S(1)}, u32[]{:S(2)}, u32[]{:S(2)}) collective-permute-start(f32[16,1024]{1,0:T(8,128)S(1)} %add.8.part), channel_id=1, source_target_pairs={{0,64},{64,128},{128,192},{192,0},{1,65},{65,129},{129,193},{193,1... | collective-permute-start | bytes 196616 | tf_op jit(solution)/shard_map/ppermute | solution.py:347
  46.5 4.6 %collective-permute-start.10 = (f32[16,1024]{1,0:T(8,128)S(1)}, f32[16,1024]{1,0:T(8,128)S(1)}, u32[]{:S(2)}, u32[]{:S(2)}) collective-permute-start(f32[16,1024]{1,0:T(8,128)S(1)} %add.8.part), channel_id=1, source_target_pairs={{0,128},{64,192},{128,0},{192,64},{1,129},{65,193},{129,1},{193,65... | collective-permute-start | bytes 196616 | tf_op jit(solution)/shard_map/ppermute | solution.py:347
  51.1 2.4 %collective-permute-start.11 = (f32[16,1024]{1,0:T(8,128)S(1)}, f32[16,1024]{1,0:T(8,128)S(1)}, u32[]{:S(2)}, u32[]{:S(2)}) collective-permute-start(f32[16,1024]{1,0:T(8,128)S(1)} %add.8.part), channel_id=1, source_target_pairs={{0,192},{64,0},{128,64},{192,128},{1,193},{65,1},{129,65},{193,129... | collective-permute-start | bytes 196616 | tf_op jit(solution)/shard_map/ppermute | solution.py:347
  53.5 0.7 collective-permute-start.12
  54.2 0.7 copy-done.11
  54.9 6.2 %merge.1.merged = f32[512,2048]{1,0:T(8,128)} custom-call(f32[512,2048]{1,0:T(8,128)} %bitcast.9, bf16[256,512]{1,0:T(8,128)(2,1)} %get-tuple-element.41.c0, bf16[256,512]{1,0:T(8,128)(2,1)} %copy-done.11, bf16[256,2048]{1,0:T(8,128)(2,1)} %og.3, bf16[256,2048]{1,0:T(8,128)(2,1)} %collective-permute-done.5.g1.h1), custom_call_target="tpu_custom_call" | custom-call | flops 1100000000 | bytes 11010048 | tf_op jit(solution)/shard_map/merge/pallas_call | solution.py:302
  61.2 1.0 copy-done.6
  62.2 0.9 spread.2
  63.0 3.8 %all-to-all-start.1 = ((bf16[16,16,1024]{2,1,0:T(8,128)(2,1)}), bf16[16,16,1024]{2,1,0:T(8,128)(2,1)S(1)}, u32[]{:S(2)}, u32[]{:S(2)}) async-start(bf16[16,16,1024]{2,1,0:T(8,128)(2,1)} %spread.2), calls=%async_computation.1 | async-start | bytes 1048576 | tf_op jit(solution)/shard_map/all_to_all | solution.py:359
  66.8 0.0 copy-start.2
  66.8 6.4 %grad.1 = (bf16[256,512]{1,0:T(8,128)(2,1)}, bf16[256,512]{1,0:T(8,128)(2,1)}, bf16[2,256,512]{2,1,0:T(8,128)(2,1)}) custom-call(bf16[256,2048]{1,0:T(8,128)(2,1)} %og.3, bf16[256,2048]{1,0:T(8,128)(2,1)} %collective-permute-done.5.g1.h1, bf16[256,2048]{1,0:T(8,128)(2,1)} %collective-permute-done.4.h2.g2, bf16[256,2048]{1,0:T(8,128)(2,1)} %copy-done.6, ...), custom_call_target="tpu_custom_call" | custom-call | flops 2200000000 | bytes 7340032 | tf_op jit(solution)/shard_map/grad/pallas_call | solution.py:280
  73.2 2.5 %all-to-all-done.1.mine_hbm = bf16[16,16,1024]{2,1,0:T(8,128)(2,1)S(1)} async-done(((bf16[16,16,1024]{2,1,0:T(8,128)(2,1)}), bf16[16,16,1024]{2,1,0:T(8,128)(2,1)S(1)}, u32[]{:S(2)}, u32[]{:S(2)}) %all-to-all-start.1) | async-done | bytes 524320 | tf_op jit(solution)/shard_map/all_to_all | solution.py:359
  75.7 3.7 %collective-permute-start.13 = (bf16[16,16,1024]{2,1,0:T(8,128)(2,1)S(1)}, bf16[16,16,1024]{2,1,0:T(8,128)(2,1)S(1)}, u32[]{:S(2)}, u32[]{:S(2)}) collective-permute-start(bf16[16,16,1024]{2,1,0:T(8,128)(2,1)S(1)} %all-to-all-done.1.mine_hbm), channel_id=1, source_target_pairs={{0,1},{1,0},{2,3},{3,2},{4,5},{5,4},{6,7},{7,6},{8,9},{9,8},{10,11... | collective-permute-start | bytes 1572872 | tf_op jit(solution)/shard_map/ppermute | solution.py:31
  79.4 1.5 %collective-permute-done.13.other_hbm = bf16[16,16,1024]{2,1,0:T(8,128)(2,1)S(1)} collective-permute-done((bf16[16,16,1024]{2,1,0:T(8,128)(2,1)S(1)}, bf16[16,16,1024]{2,1,0:T(8,128)(2,1)S(1)}, u32[]{:S(2)}, u32[]{:S(2)}) %collective-permute-start.13) | collective-permute-done | bytes 524320 | tf_op jit(solution)/shard_map/ppermute | solution.py:31
  80.9 5.9 %right.1 = (f32[16,16,1024]{2,1,0:T(8,128)S(1)}, bf16[16,16,1024]{2,1,0:T(8,128)(2,1)S(1)}, bf16[256,2048]{1,0:T(8,128)(2,1)S(1)}) custom-call(s32[2]{0:T(128)S(1)} %pad_add_fusion.at, bf16[256,2048]{1,0:T(8,128)(2,1)S(1)} %copy-done, bf16[256,2048]{1,0:T(8,128)(2,1)S(1)} %copy-done.2, bf16[512,2048]{1,0:T(8,128)(2,1)} %get-tuple-element.33.high_hbm, ...), custom_call_target="tpu_custom_call" | custom-call | flops 2000000000 | bytes 9961480 | tf_op jit(solution)/shard_map/right/pallas_call | solution.py:280
  86.8 0.5 collective-permute-start.14
  87.3 0.7 collective-permute-start.15
  88.0 0.8 collective-permute-done.14.got
  88.8 0.9 add.13
  89.7 3.6 %all-to-all-start.2 = ((bf16[16,16,1024]{2,1,0:T(8,128)(2,1)}), bf16[16,16,1024]{2,1,0:T(8,128)(2,1)S(1)}, u32[]{:S(2)}, u32[]{:S(2)}) async-start(bf16[16,16,1024]{2,1,0:T(8,128)(2,1)} %add.13), calls=%async_computation.2 | async-start | bytes 1048576 | tf_op jit(solution)/shard_map/all_to_all | solution.py:338
  93.3 0.5 collective-permute-start.16
  93.8 1.0 slice_bitcast_fusion
  94.8 0.2 collective-permute-start.18
  94.9 4.0 %gram.1.a_in = f32[256,512]{1,0:T(8,128)S(1)} custom-call(bf16[256,2048]{1,0:T(8,128)(2,1)S(1)} %get-tuple-element.50.left), custom_call_target="tpu_custom_call" | custom-call | flops 300000000 | bytes 1572864 | tf_op jit(solution)/shard_map/gram/pallas_call | solution.py:280
  98.9 5.2 %all-to-all-done.2.parts = bf16[16,16,1024]{2,1,0:T(8,128)(2,1)S(1)} async-done(((bf16[16,16,1024]{2,1,0:T(8,128)(2,1)}), bf16[16,16,1024]{2,1,0:T(8,128)(2,1)S(1)}, u32[]{:S(2)}, u32[]{:S(2)}) %all-to-all-start.2) | async-done | bytes 524320 | tf_op jit(solution)/shard_map/all_to_all | solution.py:338
  104.2 0.1 sum.3
  104.3 1.7 %collective-permute-start.19 = (bf16[256,512]{1,0:T(8,128)(2,1)S(1)}, bf16[256,512]{1,0:T(8,128)(2,1)S(1)}, u32[]{:S(2)}, u32[]{:S(2)}) collective-permute-start(bf16[256,512]{1,0:T(8,128)(2,1)S(1)} %slice_bitcast_fusion.1), channel_id=1, source_target_pairs={{0,1},{1,0},{2,3},{3,2},{4,5},{5,4},{6,7},{7,6},{8,9},{9,8},{10,11... | collective-permute-start | bytes 786440 | tf_op jit(solution)/shard_map/ppermute | solution.py:31
  106.0 0.7 collective-permute-start.17
  106.7 3.1 %step.2.a_in = f32[256,512]{1,0:T(8,128)S(1)} custom-call(f32[256,512]{1,0:T(8,128)S(1)} %gram.1.a_in), custom_call_target="tpu_custom_call", output_to_operand_aliasing={{}: (0, {})} | custom-call | flops 300000000 | bytes 1048576 | tf_op jit(solution)/shard_map/step/pallas_call | solution.py:280
  109.8 0.1 collective-permute-start.20
  109.9 4.1 %collective-permute-start.21 = (f32[16,1024]{1,0:T(8,128)S(1)}, f32[16,1024]{1,0:T(8,128)S(1)}, u32[]{:S(2)}, u32[]{:S(2)}) collective-permute-start(f32[16,1024]{1,0:T(8,128)S(1)} %add.9.part), channel_id=1, source_target_pairs={{0,128},{64,192},{128,0},{192,64},{1,129},{65,193},{129,1},{193,65... | collective-permute-start | bytes 196616 | tf_op jit(solution)/shard_map/ppermute | solution.py:347
  114.0 3.5 %collective-permute-start.22 = (f32[16,1024]{1,0:T(8,128)S(1)}, f32[16,1024]{1,0:T(8,128)S(1)}, u32[]{:S(2)}, u32[]{:S(2)}) collective-permute-start(f32[16,1024]{1,0:T(8,128)S(1)} %add.9.part), channel_id=1, source_target_pairs={{0,192},{64,0},{128,64},{192,128},{1,193},{65,1},{129,65},{193,129... | collective-permute-start | bytes 196616 | tf_op jit(solution)/shard_map/ppermute | solution.py:347
  117.5 3.0 %step.3.a_in = f32[256,512]{1,0:T(8,128)S(1)} custom-call(f32[256,512]{1,0:T(8,128)S(1)} %step.2.a_in), custom_call_target="tpu_custom_call", output_to_operand_aliasing={{}: (0, {})} | custom-call | flops 300000000 | bytes 1048576 | tf_op jit(solution)/shard_map/step/pallas_call | solution.py:280
  120.5 2.2 %collective-permute-done.22.three = f32[16,1024]{1,0:T(8,128)S(1)} collective-permute-done((f32[16,1024]{1,0:T(8,128)S(1)}, f32[16,1024]{1,0:T(8,128)S(1)}, u32[]{:S(2)}, u32[]{:S(2)}) %collective-permute-start.22) | collective-permute-done | bytes 65568 | tf_op jit(solution)/shard_map/ppermute | solution.py:347
  122.7 0.9 spread.3
  123.6 3.6 %all-to-all-start.3 = ((bf16[16,16,1024]{2,1,0:T(8,128)(2,1)}), bf16[16,16,1024]{2,1,0:T(8,128)(2,1)S(1)}, u32[]{:S(2)}, u32[]{:S(2)}) async-start(bf16[16,16,1024]{2,1,0:T(8,128)(2,1)} %spread.3), calls=%async_computation.3 | async-start | bytes 1048576 | tf_op jit(solution)/shard_map/all_to_all | solution.py:359
  127.2 3.5 %basis.1 = (f32[256,256]{1,0:T(8,128)S(1)}, bf16[256,512]{1,0:T(8,128)(2,1)S(1)}) custom-call(s32[2]{0:T(128)S(1)} %pad_add_fusion.at, f32[256,512]{1,0:T(8,128)S(1)} %step.3.a_in, bf16[256,2048]{1,0:T(8,128)(2,1)S(1)} %get-tuple-element.50.left), custom_call_target="tpu_custom_call" | custom-call | flops 300000000 | bytes 2097160 | tf_op jit(solution)/shard_map/basis/pallas_call | solution.py:280
  130.7 7.3 %all-to-all-done.3.mine_hbm = bf16[16,16,1024]{2,1,0:T(8,128)(2,1)S(1)} async-done(((bf16[16,16,1024]{2,1,0:T(8,128)(2,1)}), bf16[16,16,1024]{2,1,0:T(8,128)(2,1)S(1)}, u32[]{:S(2)}, u32[]{:S(2)}) %all-to-all-start.3) | async-done | bytes 524320 | tf_op jit(solution)/shard_map/all_to_all | solution.py:359
  138.0 1.6 %collective-permute-start.23 = (bf16[16,16,1024]{2,1,0:T(8,128)(2,1)S(1)}, bf16[16,16,1024]{2,1,0:T(8,128)(2,1)S(1)}, u32[]{:S(2)}, u32[]{:S(2)}) collective-permute-start(bf16[16,16,1024]{2,1,0:T(8,128)(2,1)S(1)} %all-to-all-done.3.mine_hbm), channel_id=1, source_target_pairs={{0,1},{1,0},{2,3},{3,2},{4,5},{5,4},{6,7},{7,6},{8,9},{9,8},{10,11... | collective-permute-start | bytes 1572872 | tf_op jit(solution)/shard_map/ppermute | solution.py:31
  139.6 1.5 %collective-permute-done.23.other_hbm = bf16[16,16,1024]{2,1,0:T(8,128)(2,1)S(1)} collective-permute-done((bf16[16,16,1024]{2,1,0:T(8,128)(2,1)S(1)}, bf16[16,16,1024]{2,1,0:T(8,128)(2,1)S(1)}, u32[]{:S(2)}, u32[]{:S(2)}) %collective-permute-start.23) | collective-permute-done | bytes 524320 | tf_op jit(solution)/shard_map/ppermute | solution.py:31
  141.2 7.9 %last.1 = (f32[512,2048]{1,0:T(8,128)}, f32[512,256]{1,0:T(8,128)}, bf16[256,2048]{1,0:T(8,128)(2,1)}) custom-call(s32[2]{0:T(128)S(1)} %pad_add_fusion.at, bf16[16,16,1024]{2,1,0:T(8,128)(2,1)S(1)} %all-to-all-done.3.mine_hbm, bf16[16,16,1024]{2,1,0:T(8,128)(2,1)S(1)} %collective-permute-done.23.other_hbm, f32[256,256]{1,0:T(8,128)S(1)} %get-tuple-element.59.inverse, ...), custom_call_target="tpu_custom_call" | custom-call | flops 2300000000 | bytes 15728648 | tf_op jit(solution)/shard_map/last/pallas_call | solution.py:302
  (39 shorter events, 0.1 us)
Async XLA Ops:
  0.6 11.5 %copy-start.3 = (bf16[512,256]{1,0:T(8,128)(2,1)S(1)}, bf16[512,256]{1,0:T(8,128)(2,1)}, u32[]{:S(2)}) copy-start(bf16[512,256]{1,0:T(8,128)(2,1)} %w0.1) | copy-start | bytes 786436
  0.6 11.5 %copy-start = (bf16[256,2048]{1,0:T(8,128)(2,1)S(1)}, bf16[256,2048]{1,0:T(8,128)(2,1)}, u32[]{:S(2)}) copy-start(bf16[256,2048]{1,0:T(8,128)(2,1)} %ctx.5) | copy-start | bytes 3145732
  0.7 10.0 %copy-start.1 = (bf16[256,2048]{1,0:T(8,128)(2,1)S(1)}, bf16[256,2048]{1,0:T(8,128)(2,1)}, u32[]{:S(2)}) copy-start(bf16[256,2048]{1,0:T(8,128)(2,1)} %og.3) | copy-start | bytes 3145732
  0.7 8.9 %collective-permute-start.1 = (bf16[512,256]{1,0:T(8,128)(2,1)}, bf16[512,256]{1,0:T(8,128)(2,1)S(1)}, u32[]{:S(2)}, u32[]{:S(2)}) collective-permute-start(bf16[512,256]{1,0:T(8,128)(2,1)} %w0.1), channel_id=1, source_target_pairs={{0,2},{2,0},{1,3},{3,1},{4,6},{6,4},{5,7},{7,5},{8,10},{10,8},{9,1... | collective-permute-start | bytes 786440 | tf_op jit(solution)/shard_map/ppermute | solution.py:31
  3.2 8.9 %collective-permute-start = (bf16[512,256]{1,0:T(8,128)(2,1)}, bf16[512,256]{1,0:T(8,128)(2,1)S(1)}, u32[]{:S(2)}, u32[]{:S(2)}) collective-permute-start(bf16[512,256]{1,0:T(8,128)(2,1)} %w0.1), channel_id=1, source_target_pairs={{0,1},{1,0},{2,3},{3,2},{4,5},{5,4},{6,7},{7,6},{8,9},{9,8},{10,11... | collective-permute-start | bytes 786440 | tf_op jit(solution)/shard_map/ppermute | solution.py:31
  9.6 2.6 %collective-permute-start.2 = (bf16[512,256]{1,0:T(8,128)(2,1)S(1)}, bf16[512,256]{1,0:T(8,128)(2,1)S(1)}, u32[]{:S(2)}, u32[]{:S(2)}) collective-permute-start(bf16[512,256]{1,0:T(8,128)(2,1)S(1)} %collective-permute-done.1.w2), channel_id=1, source_target_pairs={{0,1},{1,0},{2,3},{3,2},{4,5},{5,4},{6,7},{7,6},{8,9},{9,8},{10,11... | collective-permute-start | bytes 786440 | tf_op jit(solution)/shard_map/ppermute | solution.py:31
  10.7 27.7 %collective-permute-start.4 = (bf16[256,2048]{1,0:T(8,128)(2,1)S(1)}, bf16[256,2048]{1,0:T(8,128)(2,1)}, u32[]{:S(2)}, u32[]{:S(2)}) collective-permute-start(bf16[256,2048]{1,0:T(8,128)(2,1)S(1)} %copy-done.1), channel_id=1, source_target_pairs={{0,2},{2,0},{1,3},{3,1},{4,6},{6,4},{5,7},{7,5},{8,10},{10,8},{9,1... | collective-permute-start | bytes 3145736 | tf_op jit(solution)/shard_map/ppermute | solution.py:31
  12.2 28.0 %copy-start.12 = (bf16[256,512]{1,0:T(8,128)(2,1)S(1)}, bf16[256,512]{1,0:T(8,128)(2,1)}, u32[]{:S(2)}) copy-start(bf16[256,512]{1,0:T(8,128)(2,1)} %get-tuple-element.42) | copy-start | bytes 786436
  17.9 2.0 %collective-permute-start.3 = (bf16[16,16,1024]{2,1,0:T(8,128)(2,1)S(1)}, bf16[16,16,1024]{2,1,0:T(8,128)(2,1)S(1)}, u32[]{:S(2)}, u32[]{:S(2)}) collective-permute-start(bf16[16,16,1024]{2,1,0:T(8,128)(2,1)S(1)} %get-tuple-element.37), channel_id=1, source_target_pairs={{0,1},{1,0},{2,3},{3,2},{4,5},{5,4},{6,7},{7,6},{8,9},{9,8},{10,11... | collective-permute-start | bytes 1572872 | tf_op jit(solution)/shard_map/ppermute | solution.py:31
  20.8 17.6 %all-to-all-start = ((bf16[16,16,1024]{2,1,0:T(8,128)(2,1)}), bf16[16,16,1024]{2,1,0:T(8,128)(2,1)S(1)}, u32[]{:S(2)}, u32[]{:S(2)}) async-start(bf16[16,16,1024]{2,1,0:T(8,128)(2,1)} %add.12), calls=%async_computation | async-start | bytes 1048576 | tf_op jit(solution)/shard_map/all_to_all | solution.py:338
  27.5 12.8 %collective-permute-start.5 = (bf16[256,2048]{1,0:T(8,128)(2,1)S(1)}, bf16[256,2048]{1,0:T(8,128)(2,1)}, u32[]{:S(2)}, u32[]{:S(2)}) collective-permute-start(bf16[256,2048]{1,0:T(8,128)(2,1)S(1)} %copy-done.1), channel_id=1, source_target_pairs={{0,1},{1,0},{2,3},{3,2},{4,5},{5,4},{6,7},{7,6},{8,9},{9,8},{10,11... | collective-permute-start | bytes 3145736 | tf_op jit(solution)/shard_map/ppermute | solution.py:31
  38.4 22.7 %collective-permute-start.7 = (bf16[256,2048]{1,0:T(8,128)(2,1)}, bf16[256,2048]{1,0:T(8,128)(2,1)S(1)}, u32[]{:S(2)}, u32[]{:S(2)}) collective-permute-start(bf16[256,2048]{1,0:T(8,128)(2,1)} %collective-permute-done.4.h2.g2), channel_id=1, source_target_pairs={{0,1},{1,0},{2,3},{3,2},{4,5},{5,4},{6,7},{7,6},{8,9},{9,8},{10,11... | collective-permute-start | bytes 3145736 | tf_op jit(solution)/shard_map/ppermute | solution.py:31
  40.2 14.0 %collective-permute-start.8 = (bf16[256,512]{1,0:T(8,128)(2,1)S(1)}, bf16[256,512]{1,0:T(8,128)(2,1)S(1)}, u32[]{:S(2)}, u32[]{:S(2)}) collective-permute-start(bf16[256,512]{1,0:T(8,128)(2,1)S(1)} %copy-done.12), channel_id=1, source_target_pairs={{0,1},{1,0},{2,3},{3,2},{4,5},{5,4},{6,7},{7,6},{8,9},{9,8},{10,11... | collective-permute-start | bytes 786440 | tf_op jit(solution)/shard_map/ppermute | solution.py:31
  40.3 3.1 %collective-permute-start.6 = (f32[16,1024]{1,0:T(8,128)S(1)}, f32[16,1024]{1,0:T(8,128)S(1)}, u32[]{:S(2)}, u32[]{:S(2)}) collective-permute-start(f32[16,1024]{1,0:T(8,128)S(1)} %sum.2), channel_id=1, source_target_pairs={{0,2},{2,0},{1,3},{3,1},{4,6},{6,4},{5,7},{7,5},{8,10},{10,8},{9,1... | collective-permute-start | bytes 196616 | tf_op jit(solution)/shard_map/ppermute | solution.py:31
  43.4 10.1 %collective-permute-start.9 = (f32[16,1024]{1,0:T(8,128)S(1)}, f32[16,1024]{1,0:T(8,128)S(1)}, u32[]{:S(2)}, u32[]{:S(2)}) collective-permute-start(f32[16,1024]{1,0:T(8,128)S(1)} %add.8.part), channel_id=1, source_target_pairs={{0,64},{64,128},{128,192},{192,0},{1,65},{65,129},{129,193},{193,1... | collective-permute-start | bytes 196616 | tf_op jit(solution)/shard_map/ppermute | solution.py:347
  46.5 14.7 %collective-permute-start.10 = (f32[16,1024]{1,0:T(8,128)S(1)}, f32[16,1024]{1,0:T(8,128)S(1)}, u32[]{:S(2)}, u32[]{:S(2)}) collective-permute-start(f32[16,1024]{1,0:T(8,128)S(1)} %add.8.part), channel_id=1, source_target_pairs={{0,128},{64,192},{128,0},{192,64},{1,129},{65,193},{129,1},{193,65... | collective-permute-start | bytes 196616 | tf_op jit(solution)/shard_map/ppermute | solution.py:347
  51.1 10.1 %collective-permute-start.11 = (f32[16,1024]{1,0:T(8,128)S(1)}, f32[16,1024]{1,0:T(8,128)S(1)}, u32[]{:S(2)}, u32[]{:S(2)}) collective-permute-start(f32[16,1024]{1,0:T(8,128)S(1)} %add.8.part), channel_id=1, source_target_pairs={{0,192},{64,0},{128,64},{192,128},{1,193},{65,1},{129,65},{193,129... | collective-permute-start | bytes 196616 | tf_op jit(solution)/shard_map/ppermute | solution.py:347
  53.5 19.7 %collective-permute-start.12 = (bf16[2,256,512]{2,1,0:T(8,128)(2,1)}, bf16[2,256,512]{2,1,0:T(8,128)(2,1)S(1)}, u32[]{:S(2)}, u32[]{:S(2)}) collective-permute-start(bf16[2,256,512]{2,1,0:T(8,128)(2,1)} %get-tuple-element.46), channel_id=1, source_target_pairs={{0,2},{2,0},{1,3},{3,1},{4,6},{6,4},{5,7},{7,5},{8,10},{10,8},{9,1... | collective-permute-start | bytes 1572872 | tf_op jit(solution)/shard_map/ppermute | solution.py:31
  54.2 0.7 copy-start.11
  61.1 1.0 copy-start.6
  63.0 12.7 %all-to-all-start.1 = ((bf16[16,16,1024]{2,1,0:T(8,128)(2,1)}), bf16[16,16,1024]{2,1,0:T(8,128)(2,1)S(1)}, u32[]{:S(2)}, u32[]{:S(2)}) async-start(bf16[16,16,1024]{2,1,0:T(8,128)(2,1)} %spread.2), calls=%async_computation.1 | async-start | bytes 1048576 | tf_op jit(solution)/shard_map/all_to_all | solution.py:359
  66.8 14.2 %copy-start.2 = (bf16[256,2048]{1,0:T(8,128)(2,1)S(1)}, bf16[256,2048]{1,0:T(8,128)(2,1)}, u32[]{:S(2)}) copy-start(bf16[256,2048]{1,0:T(8,128)(2,1)} %og.3) | copy-start | bytes 3145732
  73.2 6.2 %copy-start.4 = (bf16[2,256,512]{2,1,0:T(8,128)(2,1)}, bf16[2,256,512]{2,1,0:T(8,128)(2,1)S(1)}, u32[]{:S(2)}) copy-start(bf16[2,256,512]{2,1,0:T(8,128)(2,1)S(1)} %collective-permute-done.12.c2) | copy-start | bytes 1572868
  75.7 3.7 %copy-start.7 = (bf16[16,16,1024]{2,1,0:T(8,128)(2,1)}, bf16[16,16,1024]{2,1,0:T(8,128)(2,1)S(1)}, u32[]{:S(2)}) copy-start(bf16[16,16,1024]{2,1,0:T(8,128)(2,1)S(1)} %all-to-all-done.1.mine_hbm) | copy-start | bytes 1572868
  75.7 5.2 %collective-permute-start.13 = (bf16[16,16,1024]{2,1,0:T(8,128)(2,1)S(1)}, bf16[16,16,1024]{2,1,0:T(8,128)(2,1)S(1)}, u32[]{:S(2)}, u32[]{:S(2)}) collective-permute-start(bf16[16,16,1024]{2,1,0:T(8,128)(2,1)S(1)} %all-to-all-done.1.mine_hbm), channel_id=1, source_target_pairs={{0,1},{1,0},{2,3},{3,2},{4,5},{5,4},{6,7},{7,6},{8,9},{9,8},{10,11... | collective-permute-start | bytes 1572872 | tf_op jit(solution)/shard_map/ppermute | solution.py:31
  86.8 2.0 %collective-permute-start.14 = (bf16[16,16,1024]{2,1,0:T(8,128)(2,1)S(1)}, bf16[16,16,1024]{2,1,0:T(8,128)(2,1)S(1)}, u32[]{:S(2)}, u32[]{:S(2)}) collective-permute-start(bf16[16,16,1024]{2,1,0:T(8,128)(2,1)S(1)} %get-tuple-element.49), channel_id=1, source_target_pairs={{0,1},{1,0},{2,3},{3,2},{4,5},{5,4},{6,7},{7,6},{8,9},{9,8},{10,11... | collective-permute-start | bytes 1572872 | tf_op jit(solution)/shard_map/ppermute | solution.py:31
  87.3 17.0 %collective-permute-start.15 = (bf16[2,256,512]{2,1,0:T(8,128)(2,1)}, bf16[2,256,512]{2,1,0:T(8,128)(2,1)S(1)}, u32[]{:S(2)}, u32[]{:S(2)}) collective-permute-start(bf16[2,256,512]{2,1,0:T(8,128)(2,1)} %get-tuple-element.51), channel_id=1, source_target_pairs={{0,2},{2,0},{1,3},{3,1},{4,6},{6,4},{5,7},{7,5},{8,10},{10,8},{9,1... | collective-permute-start | bytes 1572872 | tf_op jit(solution)/shard_map/ppermute | solution.py:31
  89.7 14.5 %all-to-all-start.2 = ((bf16[16,16,1024]{2,1,0:T(8,128)(2,1)}), bf16[16,16,1024]{2,1,0:T(8,128)(2,1)S(1)}, u32[]{:S(2)}, u32[]{:S(2)}) async-start(bf16[16,16,1024]{2,1,0:T(8,128)(2,1)} %add.13), calls=%async_computation.2 | async-start | bytes 1048576 | tf_op jit(solution)/shard_map/all_to_all | solution.py:338
  93.3 10.9 %collective-permute-start.16 = (bf16[256,512]{1,0:T(8,128)(2,1)}, bf16[256,512]{1,0:T(8,128)(2,1)S(1)}, u32[]{:S(2)}, u32[]{:S(2)}) collective-permute-start(bf16[256,512]{1,0:T(8,128)(2,1)} %get-tuple-element.52), channel_id=1, source_target_pairs={{0,1},{1,0},{2,3},{3,2},{4,5},{5,4},{6,7},{7,6},{8,9},{9,8},{10,11... | collective-permute-start | bytes 786440 | tf_op jit(solution)/shard_map/ppermute | solution.py:31
  94.8 25.7 %collective-permute-start.18 = (bf16[256,512]{1,0:T(8,128)(2,1)S(1)}, bf16[256,512]{1,0:T(8,128)(2,1)S(1)}, u32[]{:S(2)}, u32[]{:S(2)}) collective-permute-start(bf16[256,512]{1,0:T(8,128)(2,1)S(1)} %slice_bitcast_fusion), channel_id=1, source_target_pairs={{0,1},{1,0},{2,3},{3,2},{4,5},{5,4},{6,7},{7,6},{8,9},{9,8},{10,11... | collective-permute-start | bytes 786440 | tf_op jit(solution)/shard_map/ppermute | solution.py:31
  104.2 36.9 %copy-start.8 = (bf16[256,512]{1,0:T(8,128)(2,1)}, bf16[256,512]{1,0:T(8,128)(2,1)S(1)}, u32[]{:S(2)}) copy-start(bf16[256,512]{1,0:T(8,128)(2,1)S(1)} %collective-permute-done.16.i1) | copy-start | bytes 786436
  104.3 36.9 %copy-start.5 = (bf16[2,256,512]{2,1,0:T(8,128)(2,1)}, bf16[2,256,512]{2,1,0:T(8,128)(2,1)S(1)}, u32[]{:S(2)}) copy-start(bf16[2,256,512]{2,1,0:T(8,128)(2,1)S(1)} %collective-permute-done.15.i2) | copy-start | bytes 1572868
  104.3 16.2 %collective-permute-start.19 = (bf16[256,512]{1,0:T(8,128)(2,1)S(1)}, bf16[256,512]{1,0:T(8,128)(2,1)S(1)}, u32[]{:S(2)}, u32[]{:S(2)}) collective-permute-start(bf16[256,512]{1,0:T(8,128)(2,1)S(1)} %slice_bitcast_fusion.1), channel_id=1, source_target_pairs={{0,1},{1,0},{2,3},{3,2},{4,5},{5,4},{6,7},{7,6},{8,9},{9,8},{10,11... | collective-permute-start | bytes 786440 | tf_op jit(solution)/shard_map/ppermute | solution.py:31
  106.0 3.8 %collective-permute-start.17 = (f32[16,1024]{1,0:T(8,128)S(1)}, f32[16,1024]{1,0:T(8,128)S(1)}, u32[]{:S(2)}, u32[]{:S(2)}) collective-permute-start(f32[16,1024]{1,0:T(8,128)S(1)} %sum.3), channel_id=1, source_target_pairs={{0,2},{2,0},{1,3},{3,1},{4,6},{6,4},{5,7},{7,5},{8,10},{10,8},{9,1... | collective-permute-start | bytes 196616 | tf_op jit(solution)/shard_map/ppermute | solution.py:31
  109.8 10.7 %collective-permute-start.20 = (f32[16,1024]{1,0:T(8,128)S(1)}, f32[16,1024]{1,0:T(8,128)S(1)}, u32[]{:S(2)}, u32[]{:S(2)}) collective-permute-start(f32[16,1024]{1,0:T(8,128)S(1)} %add.9.part), channel_id=1, source_target_pairs={{0,64},{64,128},{128,192},{192,0},{1,65},{65,129},{129,193},{193,1... | collective-permute-start | bytes 196616 | tf_op jit(solution)/shard_map/ppermute | solution.py:347
  109.9 10.7 %collective-permute-start.21 = (f32[16,1024]{1,0:T(8,128)S(1)}, f32[16,1024]{1,0:T(8,128)S(1)}, u32[]{:S(2)}, u32[]{:S(2)}) collective-permute-start(f32[16,1024]{1,0:T(8,128)S(1)} %add.9.part), channel_id=1, source_target_pairs={{0,128},{64,192},{128,0},{192,64},{1,129},{65,193},{129,1},{193,65... | collective-permute-start | bytes 196616 | tf_op jit(solution)/shard_map/ppermute | solution.py:347
  114.0 8.8 %collective-permute-start.22 = (f32[16,1024]{1,0:T(8,128)S(1)}, f32[16,1024]{1,0:T(8,128)S(1)}, u32[]{:S(2)}, u32[]{:S(2)}) collective-permute-start(f32[16,1024]{1,0:T(8,128)S(1)} %add.9.part), channel_id=1, source_target_pairs={{0,192},{64,0},{128,64},{192,128},{1,193},{65,1},{129,65},{193,129... | collective-permute-start | bytes 196616 | tf_op jit(solution)/shard_map/ppermute | solution.py:347
  120.5 3.1 %copy-start.9 = (bf16[256,512]{1,0:T(8,128)(2,1)}, bf16[256,512]{1,0:T(8,128)(2,1)S(1)}, u32[]{:S(2)}) copy-start(bf16[256,512]{1,0:T(8,128)(2,1)S(1)} %collective-permute-done.18.c3) | copy-start | bytes 786436
  120.5 3.1 %copy-start.10 = (bf16[256,512]{1,0:T(8,128)(2,1)}, bf16[256,512]{1,0:T(8,128)(2,1)S(1)}, u32[]{:S(2)}) copy-start(bf16[256,512]{1,0:T(8,128)(2,1)S(1)} %collective-permute-done.19.i3) | copy-start | bytes 786436
  123.6 14.4 %all-to-all-start.3 = ((bf16[16,16,1024]{2,1,0:T(8,128)(2,1)}), bf16[16,16,1024]{2,1,0:T(8,128)(2,1)S(1)}, u32[]{:S(2)}, u32[]{:S(2)}) async-start(bf16[16,16,1024]{2,1,0:T(8,128)(2,1)} %spread.3), calls=%async_computation.3 | async-start | bytes 1048576 | tf_op jit(solution)/shard_map/all_to_all | solution.py:359
  138.0 3.2 %collective-permute-start.23 = (bf16[16,16,1024]{2,1,0:T(8,128)(2,1)S(1)}, bf16[16,16,1024]{2,1,0:T(8,128)(2,1)S(1)}, u32[]{:S(2)}, u32[]{:S(2)}) collective-permute-start(bf16[16,16,1024]{2,1,0:T(8,128)(2,1)S(1)} %all-to-all-done.3.mine_hbm), channel_id=1, source_target_pairs={{0,1},{1,0},{2,3},{3,2},{4,5},{5,4},{6,7},{7,6},{8,9},{9,8},{10,11... | collective-permute-start | bytes 1572872 | tf_op jit(solution)/shard_map/ppermute | solution.py:31

commit v2 on v1

--- a/solution.py
+++ b/solution.py
@@ -75,42 +75,37 @@
     return pl.ds(pl.multiple_of((zl * 2 + core) * ROWS, ROWS), ROWS)
 
 
-def prepare_kernel(at, ctx, err, own, near, far, high, low):
+def prepare_kernel(at, ctx, err, own, near, far, low):
     zl, core = at[0], at[1]
     own[...] = ctx[:, block(zl, core)]
     near[...] = ctx[:, block(zl, 1 - core)]
     far[0] = ctx[:, block(1 - zl, core)]
     far[1] = ctx[:, block(1 - zl, 1 - core)]
-    high[...], low[...] = two(err[...])
-
-
-def left_kernel(
-    scale, at, og, ctx, high_hbm, low_hbm, w0, w1, w2, w3, keep, send, total, high, low, sems
-):
+    rows = err.shape[0]
+    low[pl.ds(pl.multiple_of(pl.program_id(0) * rows, rows), rows), :] = err[...].astype(BF16)
+
+
+def left_kernel(scale, at, og, ctx, low, w0, w1, w2, w3, keep, send, total):
     zl, core = at[0], at[1]
-    copies = fetch((high_hbm, low_hbm), (high, low), sems)
     where = ((zl, core), (zl, 1 - core), (1 - zl, core), (1 - zl, 1 - core))
     proj = jnp.zeros((TOK, RANK), F32)
-    for (a, b), w in zip(where, (w0, w1, w2, w3)):
-        proj += mm(og[:, block(a, b)], w[...], 1, 0)
-    first, second = two(proj * scale)
-    total[...] = mm(first, ctx[...], 0, 0) + mm(second, ctx[...], 0, 0)
-    for copy in copies:
-        copy.wait()
     own = jnp.zeros((ROWS, RANK), F32)
     for (a, b), w in zip(where, (w0, w1, w2, w3)):
         cols = block(a, b)
-        own += mm(high[:, cols], w[...], 1, 0) + mm(low[:, cols], w[...], 1, 0)
+        proj += mm(og[:, cols], w[...], 1, 0)
+        own += mm(low[:, cols], w[...], 1, 0)
+    first, second = two(proj * scale)
+    total[...] = mm(first, ctx[...], 0, 0) + mm(second, ctx[...], 0, 0)
     total[:, block(zl, core)] += own.T
     split_halves(core, total, keep, send)
 
 
 def right_kernel(
-    scale, at, ctx, og, high_hbm, low_hbm, mine_hbm, other_hbm,
-    keep, send, left, total, high, low, mine, other, sems,
+    scale, at, ctx, og, low_hbm, mine_hbm, other_hbm,
+    keep, send, left, total, low, mine, other, sems,
 ):
     zl, core = at[0], at[1]
-    copies = fetch((mine_hbm, other_hbm, high_hbm, low_hbm), (mine, other, high, low), sems)
+    copies = fetch((mine_hbm, other_hbm, low_hbm), (mine, other, low), sems)
     copies[0].wait()
     copies[1].wait()
     join_halves(core, mine, other, left)
@@ -118,8 +113,7 @@
     total[...] = mm(first, og[...], 0, 0) + mm(second, og[...], 0, 0)
     own = left[:, block(zl, core)]
     copies[2].wait()
-    copies[3].wait()
-    total[...] += mm(own, high[...], 1, 0) + mm(own, low[...], 1, 0)
+    total[...] += mm(own, low[...], 1, 0)
     split_halves(core, total, keep, send)
 
 
@@ -217,13 +211,18 @@
         o[...] = mm(g[...], weight[...], 1, 1).astype(BF16)
 
 
-def merge_kernel(scale, err, c0, c1, g0, g1, out):
-    total = mm(c0[...], g0[...], 0, 0) + mm(c1[...], g1[...], 0, 0)
+def merge_kernel(scale, err, c0, c1, g0, g1, out, t0, t1):
+    @pl.when(pl.program_id(0) == 0)
+    def _():
+        t0[...] = c0[...].T
+        t1[...] = c1[...].T
+
+    total = mm(t0[...], g0[...], 1, 0) + mm(t1[...], g1[...], 1, 0)
     out[...] = err[...] + total * scale
 
 
 def last_kernel(
-    share, scale, at, mine_hbm, other_hbm, inverse, basis, merged, c2, c3, g2, g3, i0, i1, i2, i3,
+    share, at, mine_hbm, other_hbm, inverse, basis, merged, i0, i1, i2, i3,
     new_error, factor_q, in_grad, right, mine, other, sems,
 ):
     step = pl.program_id(0)
@@ -239,8 +238,7 @@
     cols = pl.ds(pl.multiple_of(step * ROWS, ROWS), ROWS)
     first, second = two(inverse[...])
     q = (mm(first, right[:, cols], 1, 0) + mm(second, right[:, cols], 1, 0)) * share
-    total = mm(c2[...], g2[...], 0, 0) + mm(c3[...], g3[...], 0, 0)
-    new_error[...] = merged[...] + total * scale - mm(basis[...], q.astype(BF16), 0, 0)
+    new_error[...] = merged[...] - mm(basis[...], q.astype(BF16), 0, 0)
     at_zl, at_core = step // 2, step % 2
 
     @pl.when((at_zl == zl) & (at_core == core))
@@ -293,8 +291,11 @@
     )(*args)
 
 
-def call_grid(kernel, steps, outs, ins, args, flops, name, scratch=(), sems=0, limit=24):
-    args = [a if spec in (SMEM, ANY, VMEM) else in_hbm(a) for a, spec in zip(args, ins)]
+def call_grid(kernel, steps, outs, ins, args, flops, name, scratch=(), sems=0, limit=24, loose=()):
+    args = [
+        a if spec in (SMEM, ANY, VMEM) or n in loose else in_hbm(a)
+        for n, (a, spec) in enumerate(zip(args, ins))
+    ]
     moved = sum(size(a.shape, a.dtype) for a in args) + sum(size(s, d) for s, d, _ in outs)
     scratch = [pltpu.VMEM(s, d) for s, d in scratch]
     if sems:
@@ -302,7 +303,9 @@
     return pl.pallas_call(
         kernel,
         grid=(steps,),
-        out_shape=[pltpu.HBM(s, d) for s, d, _ in outs],
+        out_shape=[
+            (jax.ShapeDtypeStruct if spec is VMEM else pltpu.HBM)(s, d) for s, d, spec in outs
+        ],
         in_specs=ins,
         out_specs=[spec for _, _, spec in outs],
         scratch_shapes=scratch,
@@ -334,8 +337,8 @@
 
 def across_plane(keep, send, beside=()):
     got = swap(send, "core")
-    (half,) = call(add_kernel, [(CHUNKED, BF16)], (keep, tied(got, *beside)), 1_000_000, "add")
-    parts = lax.all_to_all(half, ("y", "x"), 0, 0)
+    (half,) = call(add_kernel, [(CHUNKED, BF16)], (keep, got), 1_000_000, "add")
+    parts = tied(lax.all_to_all(half, ("y", "x"), 0, 0), *beside)
     (part,) = call(sum_kernel, [(CHUNK, F32)], (parts,), 1_000_000, "sum")
     return part
 
@@ -372,12 +375,12 @@
     warm_near = swap(warm, "core")
     quarter = rows_of(TOK // 4, ROWS)
     strip = rows_of(ROWS // 4, FEAT)
-    c_own, c_near, c_far, high, low = call_grid(
+    c_own, c_near, c_far, low = call_grid(
         prepare_kernel,
         4,
         [tokens + (quarter,)] * 2
         + [pair + (pl.BlockSpec((2, TOK // 4, ROWS), lambda j: (0, j, 0)),)]
-        + [((ROWS, FEAT), BF16, strip)] * 2,
+        + [((ROWS, FEAT), BF16, VMEM)],
         [SMEM, rows_of(TOK // 4, FEAT), strip],
         (at, context, error),
         4_000_000,
@@ -389,30 +392,31 @@
     keep, send = call(
         functools.partial(left_kernel, scale),
         [(CHUNKED, F32), (CHUNKED, BF16)],
-        (at, out_grad, context, high, low, warm, warm_near, warm_far, warm_diag),
+        (at, out_grad, context, low, warm, warm_near, warm_far, warm_diag),
         2_000_000_000,
         "left",
-        [((RANK, FEAT), F32), big, big],
-        held=(3, 4),
-        sems=2,
+        [((RANK, FEAT), F32)],
     )
     g_far = swap(tied(out_grad, warm_far, low), "zl")
     g_near = swap(tied(out_grad, warm_far, low), "core")
-    part = across_plane(keep, send)
-    g_diag = swap(tied(g_far, part), "core")
     c_near = swap(c_near, "core")
-    zs = across_z(tied(part, g_far, g_near))
+    turned = [((ROWS, TOK), BF16)] * 2
     (merged,) = call_grid(
         functools.partial(merge_kernel, scale),
         4,
         [((ROWS, FEAT), F32, column(ROWS))],
-        [column(ROWS), whole(TOK, ROWS), whole(TOK, ROWS), column(TOK), column(TOK)],
+        [column(ROWS), VMEM, VMEM, column(TOK), column(TOK)],
         (error, c_own, c_near, out_grad, g_near),
         1_100_000_000,
         "merge",
-    )
+        turned,
+        loose=(3, 4),
+    )
+    part = across_plane(keep, send, (merged,))
+    g_diag = swap(tied(g_far, part), "core")
+    zs = across_z(tied(part, g_far))
     c_far = swap(tied(c_far, zs[1]), "zl")
-    mine = back_over_plane(*zs, beside=(g_diag, merged))
+    mine = back_over_plane(*zs)
 
     i_own, i_near, i_far = call(
         grad_kernel,
@@ -432,25 +436,25 @@
     keep, send, left = call(
         functools.partial(right_kernel, scale),
         [(CHUNKED, F32), (CHUNKED, BF16), ((RANK, FEAT), BF16)],
-        (at, context, out_grad, high, low, mine, other),
+        (at, context, out_grad, low, mine, other),
         2_000_000_000,
         "right",
-        [((RANK, FEAT), F32), big, big, (CHUNKED, BF16), (CHUNKED, BF16)],
-        loose=(6,),
-        held=(3, 4, 5),
-        sems=4,
-    )
-    part = across_plane(keep, send)
+        [((RANK, FEAT), F32), big, (CHUNKED, BF16), (CHUNKED, BF16)],
+        loose=(5,),
+        held=(3, 4),
+        sems=3,
+    )
 
     table = ((RANK, 2 * RANK), F32)
     (a,) = call(gram_kernel, [table], (left,), 300_000_000, "gram")
-    part = tied(part, a, i_far, i_near)
-    i_diag = swap(tied(i_far, part)[1], "core")
-    c_diag = swap(c_far[1], "core")
+    c_diag = swap(c_far, "core")
     (a,) = call(
         functools.partial(step_kernel, PART), [table], (a,), 300_000_000, "step", alias={0: 0}
     )
-    zs = across_z(part, (a,))
+    part = across_plane(keep, send, (a,))
+    part = tied(part, i_far, i_near)
+    zs = across_z(part)
+    i_diag = swap(tied(i_far, zs[0]), "core")
     (a,) = call(
         functools.partial(step_kernel, 2 * PART), [table], (a,), 300_000_000, "step", alias={0: 0}
     )
@@ -463,25 +467,33 @@
         "basis",
         [table],
     )
-    other = swap(tied(mine, basis), "core")
-
     block_in = whole(TOK, ROWS)
     first = pl.BlockSpec((None, TOK, ROWS), lambda j: (0, 0, 0))
+    second = pl.BlockSpec((None, TOK, ROWS), lambda j: (1, 0, 0))
+    (merged,) = call_grid(
+        functools.partial(merge_kernel, scale),
+        4,
+        [((ROWS, FEAT), F32, column(ROWS))],
+        [column(ROWS), first, second, column(TOK), column(TOK)],
+        (merged, c_far, c_diag, g_far, g_diag),
+        1_100_000_000,
+        "merge",
+        turned,
+    )
+    other = swap(tied(mine, basis, merged), "core")
+
     new_error, factor_q, in_grad = call_grid(
-        functools.partial(last_kernel, 1.0 / (SIZES[0] * SIZES[1] * SIZES[2]), scale),
+        functools.partial(last_kernel, 1.0 / (SIZES[0] * SIZES[1] * SIZES[2])),
         4,
         [
             ((ROWS, FEAT), F32, column(ROWS)),
             ((ROWS, RANK), F32, whole(ROWS, RANK)),
             ((TOK, FEAT), BF16, column(TOK)),
         ],
-        [SMEM, ANY, ANY, VMEM, VMEM, column(ROWS), first, block_in, column(TOK), column(TOK)]
-        + [block_in, block_in, first, block_in],
-        (
-            at, mine, other, inverse, basis, merged, c_far, c_diag, g_far, g_diag,
-            i_own, i_near, i_far, i_diag,
-        ),
-        2_300_000_000,
+        [SMEM, ANY, ANY, VMEM, VMEM, column(ROWS)]
+        + [block_in, block_in, first, second],
+        (at, mine, other, inverse, basis, merged, i_own, i_near, i_far, i_diag),
+        1_200_000_000,
         "last",
         [((RANK, FEAT), BF16), (CHUNKED, BF16), (CHUNKED, BF16)],
         sems=2,

time: 150 us -> 144 us (0.960)
  waiting for transfers between devices: 34.9 us -> 30.4 us
  local copies, waits for them, and re-layouts: 2.75 us -> 0.07 us
  starting transfers between devices: 55.7 us -> 57.8 us
    all_to_all x2, waiting for transfers between devices: 15.4 us -> 6.42 us  [across_plane(): parts = tied(lax.all_to_all(half, ('y', 'x'), 0, 0), *beside)]
    ppermute x6, waiting for transfers between devices: 2.2 us -> 7.38 us  [across_z(): lax.ppermute(part, 'zh', [(i, (i + step) % 4) for i in range(4)])]
    all_to_all x2, waiting for transfers between devices: 9.79 us -> 5.09 us  [back_over_plane(): return lax.all_to_all(whole, ('y', 'x'), 0, 0)]
    pallas_call x13, Pallas kernels: 35.1 us -> 30.6 us  [call(): pl.pallas_call(kernel, out_shape=[(pltpu.HBM if free else jax.ShapeDtypeS...]
    ppermute x18, waiting for transfers between devices: 7.54 us -> 11.5 us  [swap(): return lax.ppermute(x, axis, [(0, 1), (1, 0)])]
    pallas_call x3 -> x4, Pallas kernels: 19.4 us -> 23.2 us  [call_grid(): pl.pallas_call(kernel, grid=(steps,), out_shape=[(jax.ShapeDtypeStruct if...]
    all_to_all x2, starting transfers between devices: 7.33 us -> 10.3 us  [back_over_plane(): return lax.all_to_all(whole, ('y', 'x'), 0, 0)]
    ppermute x6, starting transfers between devices: 17.7 us -> 15.9 us  [across_z(): lax.ppermute(part, 'zh', [(i, (i + step) % 4) for i in range(4)])]
  transfers between devices with their start and end apart: 28 -> 28, of which waited for: 10 -> 14; matrix products, arithmetic and copies ran while one was open for 1% -> 0% of each run, Pallas kernels for 27% -> 29%
where the time goes in v2:
time: 144 us; the launch traced here: 143 us
  starting transfers between devices  57.8 us (40%)
  Pallas kernels  53.8 us (37%)
  waiting for transfers between devices  30.4 us (21%)
    pallas_call x13, Pallas kernels, call(): pl.pallas_call(kernel, out_shape=[(pltpu.HBM if free else jax.ShapeDtypeS...  30.6 us
    pallas_call x4, Pallas kernels, call_grid(): pl.pallas_call(kernel, grid=(steps,), out_shape=[(jax.ShapeDtypeStruct if...  23.2 us
    ppermute x18, starting transfers between devices, swap(): return lax.ppermute(x, axis, [(0, 1), (1, 0)])  21.3 us
    ppermute x6, starting transfers between devices, across_z(): lax.ppermute(part, 'zh', [(i, (i + step) % 4) for i in range(4)])  15.9 us
    ppermute x18, waiting for transfers between devices, swap(): return lax.ppermute(x, axis, [(0, 1), (1, 0)])  11.5 us
    all_to_all x2, starting transfers between devices, across_plane(): parts = tied(lax.all_to_all(half, ('y', 'x'), 0, 0), *beside)  10.3 us
    all_to_all x2, starting transfers between devices, back_over_plane(): return lax.all_to_all(whole, ('y', 'x'), 0, 0)  10.3 us
    ppermute x6, waiting for transfers between devices, across_z(): lax.ppermute(part, 'zh', [(i, (i + step) % 4) for i in range(4)])  7.38 us
  transfers between devices with their start and end apart: 28, of which 14 were waited for; matrix products, arithmetic and copies ran while one was open for 0% of the time, Pallas kernels for 29%

profile of v2, /device:TPU:1, one launch (start us, length us, event | category | flops | bytes accessed | tf_op | source)
XLA Modules:
  0.0 143.3 jit_solution(18173527951629735008)
XLA Ops:
  0.6 0.0 copy-start
  0.7 0.0 copy-start.1
  0.7 2.6 %collective-permute-start.1 = (bf16[512,256]{1,0:T(8,128)(2,1)}, bf16[512,256]{1,0:T(8,128)(2,1)S(1)}, u32[]{:S(2)}, u32[]{:S(2)}) collective-permute-start(bf16[512,256]{1,0:T(8,128)(2,1)} %w0.1), channel_id=1, source_target_pairs={{0,2},{2,0},{1,3},{3,1},{4,6},{6,4},{5,7},{7,5},{8,10},{10,8},{9,1... | collective-permute-start | bytes 786440 | tf_op jit(solution)/shard_map/ppermute | solution.py:31
  3.2 1.0 collective-permute-start
  4.2 0.1 pad_add_fusion.at
  4.2 4.3 %prepare.1 = (bf16[256,512]{1,0:T(8,128)(2,1)}, bf16[256,512]{1,0:T(8,128)(2,1)}, bf16[2,256,512]{2,1,0:T(8,128)(2,1)}, bf16[512,2048]{1,0:T(8,128)(2,1)S(1)}) custom-call(s32[2]{0:T(128)S(1)} %pad_add_fusion.at, bf16[256,2048]{1,0:T(8,128)(2,1)} %ctx.5, f32[512,2048]{1,0:T(8,128)} %bitcast.4), custom_call_target="tpu_custom_call" | custom-call | flops 4000000 | bytes 8388616 | tf_op jit(solution)/shard_map/prepare/pallas_call | solution.py:303
  8.5 0.0 copy-start.3
  8.5 2.1 %collective-permute-start.2 = (bf16[512,256]{1,0:T(8,128)(2,1)S(1)}, bf16[512,256]{1,0:T(8,128)(2,1)S(1)}, u32[]{:S(2)}, u32[]{:S(2)}) collective-permute-start(bf16[512,256]{1,0:T(8,128)(2,1)S(1)} %collective-permute-done.1.w2), channel_id=1, source_target_pairs={{0,1},{1,0},{2,3},{3,2},{4,5},{5,4},{6,7},{7,6},{8,9},{9,8},{10,11... | collective-permute-start | bytes 786440 | tf_op jit(solution)/shard_map/ppermute | solution.py:31
  10.7 0.1 collective-permute-start.5
  10.8 1.5 %collective-permute-start.6 = (bf16[256,2048]{1,0:T(8,128)(2,1)S(1)}, bf16[256,2048]{1,0:T(8,128)(2,1)}, u32[]{:S(2)}, u32[]{:S(2)}) collective-permute-start(bf16[256,2048]{1,0:T(8,128)(2,1)S(1)} %copy-done.1), channel_id=1, source_target_pairs={{0,2},{2,0},{1,3},{3,1},{4,6},{6,4},{5,7},{7,5},{8,10},{10,8},{9,1... | collective-permute-start | bytes 3145736 | tf_op jit(solution)/shard_map/ppermute | solution.py:31
  12.3 2.4 %left.1 = (f32[16,16,1024]{2,1,0:T(8,128)S(1)}, bf16[16,16,1024]{2,1,0:T(8,128)(2,1)S(1)}) custom-call(s32[2]{0:T(128)S(1)} %pad_add_fusion.at, bf16[256,2048]{1,0:T(8,128)(2,1)S(1)} %copy-done.1, bf16[256,2048]{1,0:T(8,128)(2,1)S(1)} %copy-done, bf16[512,2048]{1,0:T(8,128)(2,1)S(1)} %get-tuple-element.32.low.low_hbm, bf16[512,256]{1,0:T(8,128)(2,1)S(1)} %copy-done.5, ...), custom_call_target="tpu_custom_call" | custom-call | flops 2000000000 | bytes 6815752 | tf_op jit(solution)/shard_map/left/pallas_call | solution.py:278
  14.7 0.8 collective-permute-start.3
  15.5 1.5 %collective-permute-done.3.got = bf16[16,16,1024]{2,1,0:T(8,128)(2,1)S(1)} collective-permute-done((bf16[16,16,1024]{2,1,0:T(8,128)(2,1)S(1)}, bf16[16,16,1024]{2,1,0:T(8,128)(2,1)S(1)}, u32[]{:S(2)}, u32[]{:S(2)}) %collective-permute-start.3) | collective-permute-done | bytes 524320 | tf_op jit(solution)/shard_map/ppermute | solution.py:31
  17.0 0.9 add.12
  17.9 6.8 %all-to-all-start = ((bf16[16,16,1024]{2,1,0:T(8,128)(2,1)}), bf16[16,16,1024]{2,1,0:T(8,128)(2,1)S(1)}, u32[]{:S(2)}, u32[]{:S(2)}) async-start(bf16[16,16,1024]{2,1,0:T(8,128)(2,1)} %add.12), calls=%async_computation | async-start | bytes 1048576 | tf_op jit(solution)/shard_map/all_to_all | solution.py:341
  24.7 0.7 collective-permute-start.4
  25.4 1.2 collective-permute-done.4.c1
  26.6 5.8 %merge.2.err = f32[512,2048]{1,0:T(8,128)} custom-call(f32[512,2048]{1,0:T(8,128)} %bitcast.5, bf16[256,512]{1,0:T(8,128)(2,1)S(1)} %copy-done.3, bf16[256,512]{1,0:T(8,128)(2,1)S(1)} %collective-permute-done.4.c1, bf16[256,2048]{1,0:T(8,128)(2,1)S(1)} %copy-done.1, bf16[256,2048]{1,0:T(8,128)(2,1)} %collective-permute-done.5.g1.h1), custom_call_target="tpu_custom_call" | custom-call | flops 1100000000 | bytes 11010048 | tf_op jit(solution)/shard_map/merge/pallas_call | solution.py:303
  32.4 3.0 %all-to-all-done.parts = bf16[16,16,1024]{2,1,0:T(8,128)(2,1)S(1)} async-done(((bf16[16,16,1024]{2,1,0:T(8,128)(2,1)}), bf16[16,16,1024]{2,1,0:T(8,128)(2,1)S(1)}, u32[]{:S(2)}, u32[]{:S(2)}) %all-to-all-start) | async-done | bytes 524320 | tf_op jit(solution)/shard_map/all_to_all | solution.py:341
  35.4 0.1 sum.2
  35.5 1.9 %collective-permute-start.11 = (bf16[256,2048]{1,0:T(8,128)(2,1)}, bf16[256,2048]{1,0:T(8,128)(2,1)}, u32[]{:S(2)}, u32[]{:S(2)}) collective-permute-start(bf16[256,2048]{1,0:T(8,128)(2,1)} %collective-permute-done.6.h2.g0), channel_id=1, source_target_pairs={{0,1},{1,0},{2,3},{3,2},{4,5},{5,4},{6,7},{7,6},{8,9},{9,8},{10,11... | collective-permute-start | bytes 3145736 | tf_op jit(solution)/shard_map/ppermute | solution.py:31
  37.3 0.7 collective-permute-start.7
  38.1 2.9 %collective-permute-done.7 = f32[16,1024]{1,0:T(8,128)S(1)} collective-permute-done((f32[16,1024]{1,0:T(8,128)S(1)}, f32[16,1024]{1,0:T(8,128)S(1)}, u32[]{:S(2)}, u32[]{:S(2)}) %collective-permute-start.7) | collective-permute-done | bytes 65568 | tf_op jit(solution)/shard_map/ppermute | solution.py:31
  41.0 3.1 %collective-permute-start.8 = (f32[16,1024]{1,0:T(8,128)S(1)}, f32[16,1024]{1,0:T(8,128)S(1)}, u32[]{:S(2)}, u32[]{:S(2)}) collective-permute-start(f32[16,1024]{1,0:T(8,128)S(1)} %add.8.part), channel_id=1, source_target_pairs={{0,64},{64,128},{128,192},{192,0},{1,65},{65,129},{129,193},{193,1... | collective-permute-start | bytes 196616 | tf_op jit(solution)/shard_map/ppermute | solution.py:350
  44.1 4.2 %collective-permute-start.9 = (f32[16,1024]{1,0:T(8,128)S(1)}, f32[16,1024]{1,0:T(8,128)S(1)}, u32[]{:S(2)}, u32[]{:S(2)}) collective-permute-start(f32[16,1024]{1,0:T(8,128)S(1)} %add.8.part), channel_id=1, source_target_pairs={{0,128},{64,192},{128,0},{192,64},{1,129},{65,193},{129,1},{193,65... | collective-permute-start | bytes 196616 | tf_op jit(solution)/shard_map/ppermute | solution.py:350
  48.3 2.4 %collective-permute-start.10 = (f32[16,1024]{1,0:T(8,128)S(1)}, f32[16,1024]{1,0:T(8,128)S(1)}, u32[]{:S(2)}, u32[]{:S(2)}) collective-permute-start(f32[16,1024]{1,0:T(8,128)S(1)} %add.8.part), channel_id=1, source_target_pairs={{0,192},{64,0},{128,64},{192,128},{1,193},{65,1},{129,65},{193,129... | collective-permute-start | bytes 196616 | tf_op jit(solution)/shard_map/ppermute | solution.py:350
  50.7 0.7 collective-permute-start.12
  51.4 0.9 collective-permute-done.9.opposite
  52.3 3.6 %collective-permute-done.10.three = f32[16,1024]{1,0:T(8,128)S(1)} collective-permute-done((f32[16,1024]{1,0:T(8,128)S(1)}, f32[16,1024]{1,0:T(8,128)S(1)}, u32[]{:S(2)}, u32[]{:S(2)}) %collective-permute-start.10) | collective-permute-done | bytes 65568 | tf_op jit(solution)/shard_map/ppermute | solution.py:350
  55.9 0.9 spread.2
  56.8 6.7 %all-to-all-start.1 = ((bf16[16,16,1024]{2,1,0:T(8,128)(2,1)}), bf16[16,16,1024]{2,1,0:T(8,128)(2,1)S(1)}, u32[]{:S(2)}, u32[]{:S(2)}) async-start(bf16[16,16,1024]{2,1,0:T(8,128)(2,1)} %spread.2), calls=%async_computation.1 | async-start | bytes 1048576 | tf_op jit(solution)/shard_map/all_to_all | solution.py:362
  63.5 0.0 copy-start.2
  63.5 6.4 %grad.1 = (bf16[256,512]{1,0:T(8,128)(2,1)}, bf16[256,512]{1,0:T(8,128)(2,1)}, bf16[2,256,512]{2,1,0:T(8,128)(2,1)}) custom-call(bf16[256,2048]{1,0:T(8,128)(2,1)} %og.3, bf16[256,2048]{1,0:T(8,128)(2,1)} %collective-permute-done.5.g1.h1, bf16[256,2048]{1,0:T(8,128)(2,1)} %collective-permute-done.6.h2.g0, bf16[256,2048]{1,0:T(8,128)(2,1)} %collective-permute-done.11.h3.g1, ...), custom_call_target="tpu_custom_call" | custom-call | flops 2200000000 | bytes 7340032 | tf_op jit(solution)/shard_map/grad/pallas_call | solution.py:278
  69.9 4.2 %all-to-all-done.1.mine_hbm = bf16[16,16,1024]{2,1,0:T(8,128)(2,1)S(1)} async-done(((bf16[16,16,1024]{2,1,0:T(8,128)(2,1)}), bf16[16,16,1024]{2,1,0:T(8,128)(2,1)S(1)}, u32[]{:S(2)}, u32[]{:S(2)}) %all-to-all-start.1) | async-done | bytes 524320 | tf_op jit(solution)/shard_map/all_to_all | solution.py:362
  74.1 2.0 %collective-permute-start.13 = (bf16[16,16,1024]{2,1,0:T(8,128)(2,1)S(1)}, bf16[16,16,1024]{2,1,0:T(8,128)(2,1)S(1)}, u32[]{:S(2)}, u32[]{:S(2)}) collective-permute-start(bf16[16,16,1024]{2,1,0:T(8,128)(2,1)S(1)} %all-to-all-done.1.mine_hbm), channel_id=1, source_target_pairs={{0,1},{1,0},{2,3},{3,2},{4,5},{5,4},{6,7},{7,6},{8,9},{9,8},{10,11... | collective-permute-start | bytes 1572872 | tf_op jit(solution)/shard_map/ppermute | solution.py:31
  76.1 1.5 %collective-permute-done.13.other_hbm = bf16[16,16,1024]{2,1,0:T(8,128)(2,1)S(1)} collective-permute-done((bf16[16,16,1024]{2,1,0:T(8,128)(2,1)S(1)}, bf16[16,16,1024]{2,1,0:T(8,128)(2,1)S(1)}, u32[]{:S(2)}, u32[]{:S(2)}) %collective-permute-start.13) | collective-permute-done | bytes 524320 | tf_op jit(solution)/shard_map/ppermute | solution.py:31
  77.6 4.6 %right.1 = (f32[16,16,1024]{2,1,0:T(8,128)S(1)}, bf16[16,16,1024]{2,1,0:T(8,128)(2,1)S(1)}, bf16[256,2048]{1,0:T(8,128)(2,1)S(1)}) custom-call(s32[2]{0:T(128)S(1)} %pad_add_fusion.at, bf16[256,2048]{1,0:T(8,128)(2,1)S(1)} %copy-done, bf16[256,2048]{1,0:T(8,128)(2,1)S(1)} %copy-done.2, bf16[512,2048]{1,0:T(8,128)(2,1)} %copy-done.4, ...), custom_call_target="tpu_custom_call" | custom-call | flops 2000000000 | bytes 7864328 | tf_op jit(solution)/shard_map/right/pallas_call | solution.py:278
  82.3 0.5 collective-permute-start.14
  82.7 1.5 %collective-permute-done.14.got = bf16[16,16,1024]{2,1,0:T(8,128)(2,1)S(1)} collective-permute-done((bf16[16,16,1024]{2,1,0:T(8,128)(2,1)S(1)}, bf16[16,16,1024]{2,1,0:T(8,128)(2,1)S(1)}, u32[]{:S(2)}, u32[]{:S(2)}) %collective-permute-start.14) | collective-permute-done | bytes 524320 | tf_op jit(solution)/shard_map/ppermute | solution.py:31
  84.3 0.9 add.13
  85.2 3.6 %all-to-all-start.2 = ((bf16[16,16,1024]{2,1,0:T(8,128)(2,1)}), bf16[16,16,1024]{2,1,0:T(8,128)(2,1)S(1)}, u32[]{:S(2)}, u32[]{:S(2)}) async-start(bf16[16,16,1024]{2,1,0:T(8,128)(2,1)} %add.13), calls=%async_computation.2 | async-start | bytes 1048576 | tf_op jit(solution)/shard_map/all_to_all | solution.py:341
  88.7 0.5 collective-permute-start.16
  89.2 4.0 %gram.1.a_in = f32[256,512]{1,0:T(8,128)S(1)} custom-call(bf16[256,2048]{1,0:T(8,128)(2,1)S(1)} %get-tuple-element.48.left), custom_call_target="tpu_custom_call" | custom-call | flops 300000000 | bytes 1572864 | tf_op jit(solution)/shard_map/gram/pallas_call | solution.py:278
  93.2 3.1 %step.2.a_in = f32[256,512]{1,0:T(8,128)S(1)} custom-call(f32[256,512]{1,0:T(8,128)S(1)} %gram.1.a_in), custom_call_target="tpu_custom_call", output_to_operand_aliasing={{}: (0, {})} | custom-call | flops 300000000 | bytes 1048576 | tf_op jit(solution)/shard_map/step/pallas_call | solution.py:278
  96.3 3.4 %all-to-all-done.2.parts = bf16[16,16,1024]{2,1,0:T(8,128)(2,1)S(1)} async-done(((bf16[16,16,1024]{2,1,0:T(8,128)(2,1)}), bf16[16,16,1024]{2,1,0:T(8,128)(2,1)S(1)}, u32[]{:S(2)}, u32[]{:S(2)}) %all-to-all-start.2) | async-done | bytes 524320 | tf_op jit(solution)/shard_map/all_to_all | solution.py:341
  99.7 0.1 sum.3
  99.8 0.1 collective-permute-start.17
  99.9 1.8 %collective-permute-start.18 = (bf16[2,256,512]{2,1,0:T(8,128)(2,1)S(1)}, bf16[2,256,512]{2,1,0:T(8,128)(2,1)S(1)}, u32[]{:S(2)}, u32[]{:S(2)}) collective-permute-start(bf16[2,256,512]{2,1,0:T(8,128)(2,1)S(1)} %copy-done.7), channel_id=1, source_target_pairs={{0,1},{1,0},{2,3},{3,2},{4,5},{5,4},{6,7},{7,6},{8,9},{9,8},{10,11... | collective-permute-start | bytes 1572872 | tf_op jit(solution)/shard_map/ppermute | solution.py:31
  101.7 1.3 collective-permute-done.17
  103.0 2.7 %collective-permute-start.19 = (bf16[2,256,512]{2,1,0:T(8,128)(2,1)S(1)}, bf16[2,256,512]{2,1,0:T(8,128)(2,1)S(1)}, u32[]{:S(2)}, u32[]{:S(2)}) collective-permute-start(bf16[2,256,512]{2,1,0:T(8,128)(2,1)S(1)} %collective-permute-done.15.i2), channel_id=1, source_target_pairs={{0,1},{1,0},{2,3},{3,2},{4,5},{5,4},{6,7},{7,6},{8,9},{9,8},{10,11... | collective-permute-start | bytes 1572872 | tf_op jit(solution)/shard_map/ppermute | solution.py:31
  105.8 0.6 collective-permute-start.20
  106.4 4.2 %collective-permute-start.21 = (f32[16,1024]{1,0:T(8,128)S(1)}, f32[16,1024]{1,0:T(8,128)S(1)}, u32[]{:S(2)}, u32[]{:S(2)}) collective-permute-start(f32[16,1024]{1,0:T(8,128)S(1)} %add.9.part), channel_id=1, source_target_pairs={{0,128},{64,192},{128,0},{192,64},{1,129},{65,193},{129,1},{193,65... | collective-permute-start | bytes 196616 | tf_op jit(solution)/shard_map/ppermute | solution.py:350
  110.5 1.5 %collective-permute-start.22 = (f32[16,1024]{1,0:T(8,128)S(1)}, f32[16,1024]{1,0:T(8,128)S(1)}, u32[]{:S(2)}, u32[]{:S(2)}) collective-permute-start(f32[16,1024]{1,0:T(8,128)S(1)} %add.9.part), channel_id=1, source_target_pairs={{0,192},{64,0},{128,64},{192,128},{1,193},{65,1},{129,65},{193,129... | collective-permute-start | bytes 196616 | tf_op jit(solution)/shard_map/ppermute | solution.py:350
  112.0 3.0 %step.3.a_in = f32[256,512]{1,0:T(8,128)S(1)} custom-call(f32[256,512]{1,0:T(8,128)S(1)} %step.2.a_in), custom_call_target="tpu_custom_call", output_to_operand_aliasing={{}: (0, {})} | custom-call | flops 300000000 | bytes 1048576 | tf_op jit(solution)/shard_map/step/pallas_call | solution.py:278
  115.1 0.0 copy-start.8
  115.1 2.8 %collective-permute-done.22.three = f32[16,1024]{1,0:T(8,128)S(1)} collective-permute-done((f32[16,1024]{1,0:T(8,128)S(1)}, f32[16,1024]{1,0:T(8,128)S(1)}, u32[]{:S(2)}, u32[]{:S(2)}) %collective-permute-start.22) | collective-permute-done | bytes 65568 | tf_op jit(solution)/shard_map/ppermute | solution.py:350
  118.0 0.9 spread.3
  118.8 3.6 %all-to-all-start.3 = ((bf16[16,16,1024]{2,1,0:T(8,128)(2,1)}), bf16[16,16,1024]{2,1,0:T(8,128)(2,1)S(1)}, u32[]{:S(2)}, u32[]{:S(2)}) async-start(bf16[16,16,1024]{2,1,0:T(8,128)(2,1)} %spread.3), calls=%async_computation.3 | async-start | bytes 1048576 | tf_op jit(solution)/shard_map/all_to_all | solution.py:362
  122.4 6.4 %merge.3.merged = f32[512,2048]{1,0:T(8,128)} custom-call(f32[512,2048]{1,0:T(8,128)} %merge.2.err, bf16[2,256,512]{2,1,0:T(8,128)(2,1)} %copy-done.6, bf16[2,256,512]{2,1,0:T(8,128)(2,1)} %copy-done.8, bf16[256,2048]{1,0:T(8,128)(2,1)} %collective-permute-done.6.h2.g0, bf16[256,2048]{1,0:T(8,128)(2,1)} %collective-permute-done.11.h3.g1), custom_call_target="tpu_custom_call" | custom-call | flops 1100000000 | bytes 11534336 | tf_op jit(solution)/shard_map/merge/pallas_call | solution.py:303
  128.8 3.5 %basis.1 = (f32[256,256]{1,0:T(8,128)S(1)}, bf16[256,512]{1,0:T(8,128)(2,1)S(1)}) custom-call(s32[2]{0:T(128)S(1)} %pad_add_fusion.at, f32[256,512]{1,0:T(8,128)S(1)} %step.3.a_in, bf16[256,2048]{1,0:T(8,128)(2,1)S(1)} %get-tuple-element.48.left), custom_call_target="tpu_custom_call" | custom-call | flops 300000000 | bytes 2097160 | tf_op jit(solution)/shard_map/basis/pallas_call | solution.py:278
  132.3 0.9 all-to-all-done.3.mine_hbm
  133.2 1.6 %collective-permute-start.23 = (bf16[16,16,1024]{2,1,0:T(8,128)(2,1)S(1)}, bf16[16,16,1024]{2,1,0:T(8,128)(2,1)S(1)}, u32[]{:S(2)}, u32[]{:S(2)}) collective-permute-start(bf16[16,16,1024]{2,1,0:T(8,128)(2,1)S(1)} %all-to-all-done.3.mine_hbm), channel_id=1, source_target_pairs={{0,1},{1,0},{2,3},{3,2},{4,5},{5,4},{6,7},{7,6},{8,9},{9,8},{10,11... | collective-permute-start | bytes 1572872 | tf_op jit(solution)/shard_map/ppermute | solution.py:31
  134.8 1.5 %collective-permute-done.23.other_hbm = bf16[16,16,1024]{2,1,0:T(8,128)(2,1)S(1)} collective-permute-done((bf16[16,16,1024]{2,1,0:T(8,128)(2,1)S(1)}, bf16[16,16,1024]{2,1,0:T(8,128)(2,1)S(1)}, u32[]{:S(2)}, u32[]{:S(2)}) %collective-permute-start.23) | collective-permute-done | bytes 524320 | tf_op jit(solution)/shard_map/ppermute | solution.py:31
  136.4 6.8 %last.1 = (f32[512,2048]{1,0:T(8,128)}, f32[512,256]{1,0:T(8,128)}, bf16[256,2048]{1,0:T(8,128)(2,1)}) custom-call(s32[2]{0:T(128)S(1)} %pad_add_fusion.at, bf16[16,16,1024]{2,1,0:T(8,128)(2,1)S(1)} %all-to-all-done.3.mine_hbm, bf16[16,16,1024]{2,1,0:T(8,128)(2,1)S(1)} %collective-permute-done.23.other_hbm, f32[256,256]{1,0:T(8,128)S(1)} %get-tuple-element.57.inverse, ...), custom_call_target="tpu_custom_call" | custom-call | flops 1200000000 | bytes 13107208 | tf_op jit(solution)/shard_map/last/pallas_call | solution.py:303
  (40 shorter events, 0.1 us)
Async XLA Ops:
  0.6 11.6 %copy-start.5 = (bf16[512,256]{1,0:T(8,128)(2,1)S(1)}, bf16[512,256]{1,0:T(8,128)(2,1)}, u32[]{:S(2)}) copy-start(bf16[512,256]{1,0:T(8,128)(2,1)} %w0.1) | copy-start | bytes 786436
  0.6 11.6 %copy-start = (bf16[256,2048]{1,0:T(8,128)(2,1)S(1)}, bf16[256,2048]{1,0:T(8,128)(2,1)}, u32[]{:S(2)}) copy-start(bf16[256,2048]{1,0:T(8,128)(2,1)} %ctx.5) | copy-start | bytes 3145732
  0.7 10.0 %copy-start.1 = (bf16[256,2048]{1,0:T(8,128)(2,1)S(1)}, bf16[256,2048]{1,0:T(8,128)(2,1)}, u32[]{:S(2)}) copy-start(bf16[256,2048]{1,0:T(8,128)(2,1)} %og.3) | copy-start | bytes 3145732
  0.7 7.9 %collective-permute-start.1 = (bf16[512,256]{1,0:T(8,128)(2,1)}, bf16[512,256]{1,0:T(8,128)(2,1)S(1)}, u32[]{:S(2)}, u32[]{:S(2)}) collective-permute-start(bf16[512,256]{1,0:T(8,128)(2,1)} %w0.1), channel_id=1, source_target_pairs={{0,2},{2,0},{1,3},{3,1},{4,6},{6,4},{5,7},{7,5},{8,10},{10,8},{9,1... | collective-permute-start | bytes 786440 | tf_op jit(solution)/shard_map/ppermute | solution.py:31
  3.2 9.0 %collective-permute-start = (bf16[512,256]{1,0:T(8,128)(2,1)}, bf16[512,256]{1,0:T(8,128)(2,1)S(1)}, u32[]{:S(2)}, u32[]{:S(2)}) collective-permute-start(bf16[512,256]{1,0:T(8,128)(2,1)} %w0.1), channel_id=1, source_target_pairs={{0,1},{1,0},{2,3},{3,2},{4,5},{5,4},{6,7},{7,6},{8,9},{9,8},{10,11... | collective-permute-start | bytes 786440 | tf_op jit(solution)/shard_map/ppermute | solution.py:31
  8.5 8.5 %copy-start.4 = (bf16[512,2048]{1,0:T(8,128)(2,1)}, bf16[512,2048]{1,0:T(8,128)(2,1)S(1)}, u32[]{:S(2)}) copy-start(bf16[512,2048]{1,0:T(8,128)(2,1)S(1)} %get-tuple-element.32.low.low_hbm) | copy-start | bytes 6291460
  8.5 16.2 %copy-start.13 = (bf16[256,512]{1,0:T(8,128)(2,1)S(1)}, bf16[256,512]{1,0:T(8,128)(2,1)}, u32[]{:S(2)}) copy-start(bf16[256,512]{1,0:T(8,128)(2,1)} %get-tuple-element.37) | copy-start | bytes 786436
  8.5 18.1 %copy-start.3 = (bf16[256,512]{1,0:T(8,128)(2,1)S(1)}, bf16[256,512]{1,0:T(8,128)(2,1)}, u32[]{:S(2)}) copy-start(bf16[256,512]{1,0:T(8,128)(2,1)} %get-tuple-element.36.c0) | copy-start | bytes 786436
  8.5 3.7 %collective-permute-start.2 = (bf16[512,256]{1,0:T(8,128)(2,1)S(1)}, bf16[512,256]{1,0:T(8,128)(2,1)S(1)}, u32[]{:S(2)}, u32[]{:S(2)}) collective-permute-start(bf16[512,256]{1,0:T(8,128)(2,1)S(1)} %collective-permute-done.1.w2), channel_id=1, source_target_pairs={{0,1},{1,0},{2,3},{3,2},{4,5},{5,4},{6,7},{7,6},{8,9},{9,8},{10,11... | collective-permute-start | bytes 786440 | tf_op jit(solution)/shard_map/ppermute | solution.py:31
  10.7 15.9 %collective-permute-start.5 = (bf16[256,2048]{1,0:T(8,128)(2,1)S(1)}, bf16[256,2048]{1,0:T(8,128)(2,1)}, u32[]{:S(2)}, u32[]{:S(2)}) collective-permute-start(bf16[256,2048]{1,0:T(8,128)(2,1)S(1)} %copy-done.1), channel_id=1, source_target_pairs={{0,1},{1,0},{2,3},{3,2},{4,5},{5,4},{6,7},{7,6},{8,9},{9,8},{10,11... | collective-permute-start | bytes 3145736 | tf_op jit(solution)/shard_map/ppermute | solution.py:31
  10.8 24.7 %collective-permute-start.6 = (bf16[256,2048]{1,0:T(8,128)(2,1)S(1)}, bf16[256,2048]{1,0:T(8,128)(2,1)}, u32[]{:S(2)}, u32[]{:S(2)}) collective-permute-start(bf16[256,2048]{1,0:T(8,128)(2,1)S(1)} %copy-done.1), channel_id=1, source_target_pairs={{0,2},{2,0},{1,3},{3,1},{4,6},{6,4},{5,7},{7,5},{8,10},{10,8},{9,1... | collective-permute-start | bytes 3145736 | tf_op jit(solution)/shard_map/ppermute | solution.py:31
  14.7 2.3 %collective-permute-start.3 = (bf16[16,16,1024]{2,1,0:T(8,128)(2,1)S(1)}, bf16[16,16,1024]{2,1,0:T(8,128)(2,1)S(1)}, u32[]{:S(2)}, u32[]{:S(2)}) collective-permute-start(bf16[16,16,1024]{2,1,0:T(8,128)(2,1)S(1)} %get-tuple-element.35), channel_id=1, source_target_pairs={{0,1},{1,0},{2,3},{3,2},{4,5},{5,4},{6,7},{7,6},{8,9},{9,8},{10,11... | collective-permute-start | bytes 1572872 | tf_op jit(solution)/shard_map/ppermute | solution.py:31
  17.9 17.5 %all-to-all-start = ((bf16[16,16,1024]{2,1,0:T(8,128)(2,1)}), bf16[16,16,1024]{2,1,0:T(8,128)(2,1)S(1)}, u32[]{:S(2)}, u32[]{:S(2)}) async-start(bf16[16,16,1024]{2,1,0:T(8,128)(2,1)} %add.12), calls=%async_computation | async-start | bytes 1048576 | tf_op jit(solution)/shard_map/all_to_all | solution.py:341
  24.7 1.9 %collective-permute-start.4 = (bf16[256,512]{1,0:T(8,128)(2,1)S(1)}, bf16[256,512]{1,0:T(8,128)(2,1)S(1)}, u32[]{:S(2)}, u32[]{:S(2)}) collective-permute-start(bf16[256,512]{1,0:T(8,128)(2,1)S(1)} %copy-done.13), channel_id=1, source_target_pairs={{0,1},{1,0},{2,3},{3,2},{4,5},{5,4},{6,7},{7,6},{8,9},{9,8},{10,11... | collective-permute-start | bytes 786440 | tf_op jit(solution)/shard_map/ppermute | solution.py:31
  35.5 28.0 %collective-permute-start.11 = (bf16[256,2048]{1,0:T(8,128)(2,1)}, bf16[256,2048]{1,0:T(8,128)(2,1)}, u32[]{:S(2)}, u32[]{:S(2)}) collective-permute-start(bf16[256,2048]{1,0:T(8,128)(2,1)} %collective-permute-done.6.h2.g0), channel_id=1, source_target_pairs={{0,1},{1,0},{2,3},{3,2},{4,5},{5,4},{6,7},{7,6},{8,9},{9,8},{10,11... | collective-permute-start | bytes 3145736 | tf_op jit(solution)/shard_map/ppermute | solution.py:31
  37.3 3.7 %collective-permute-start.7 = (f32[16,1024]{1,0:T(8,128)S(1)}, f32[16,1024]{1,0:T(8,128)S(1)}, u32[]{:S(2)}, u32[]{:S(2)}) collective-permute-start(f32[16,1024]{1,0:T(8,128)S(1)} %sum.2), channel_id=1, source_target_pairs={{0,2},{2,0},{1,3},{3,1},{4,6},{6,4},{5,7},{7,5},{8,10},{10,8},{9,1... | collective-permute-start | bytes 196616 | tf_op jit(solution)/shard_map/ppermute | solution.py:31
  41.0 9.7 %collective-permute-start.8 = (f32[16,1024]{1,0:T(8,128)S(1)}, f32[16,1024]{1,0:T(8,128)S(1)}, u32[]{:S(2)}, u32[]{:S(2)}) collective-permute-start(f32[16,1024]{1,0:T(8,128)S(1)} %add.8.part), channel_id=1, source_target_pairs={{0,64},{64,128},{128,192},{192,0},{1,65},{65,129},{129,193},{193,1... | collective-permute-start | bytes 196616 | tf_op jit(solution)/shard_map/ppermute | solution.py:350
  44.1 8.3 %collective-permute-start.9 = (f32[16,1024]{1,0:T(8,128)S(1)}, f32[16,1024]{1,0:T(8,128)S(1)}, u32[]{:S(2)}, u32[]{:S(2)}) collective-permute-start(f32[16,1024]{1,0:T(8,128)S(1)} %add.8.part), channel_id=1, source_target_pairs={{0,128},{64,192},{128,0},{192,64},{1,129},{65,193},{129,1},{193,65... | collective-permute-start | bytes 196616 | tf_op jit(solution)/shard_map/ppermute | solution.py:350
  48.3 7.6 %collective-permute-start.10 = (f32[16,1024]{1,0:T(8,128)S(1)}, f32[16,1024]{1,0:T(8,128)S(1)}, u32[]{:S(2)}, u32[]{:S(2)}) collective-permute-start(f32[16,1024]{1,0:T(8,128)S(1)} %add.8.part), channel_id=1, source_target_pairs={{0,192},{64,0},{128,64},{192,128},{1,193},{65,1},{129,65},{193,129... | collective-permute-start | bytes 196616 | tf_op jit(solution)/shard_map/ppermute | solution.py:350
  50.7 23.4 %collective-permute-start.12 = (bf16[2,256,512]{2,1,0:T(8,128)(2,1)}, bf16[2,256,512]{2,1,0:T(8,128)(2,1)S(1)}, u32[]{:S(2)}, u32[]{:S(2)}) collective-permute-start(bf16[2,256,512]{2,1,0:T(8,128)(2,1)} %get-tuple-element.44), channel_id=1, source_target_pairs={{0,2},{2,0},{1,3},{3,1},{4,6},{6,4},{5,7},{7,5},{8,10},{10,8},{9,1... | collective-permute-start | bytes 1572872 | tf_op jit(solution)/shard_map/ppermute | solution.py:31
  56.8 17.3 %all-to-all-start.1 = ((bf16[16,16,1024]{2,1,0:T(8,128)(2,1)}), bf16[16,16,1024]{2,1,0:T(8,128)(2,1)S(1)}, u32[]{:S(2)}, u32[]{:S(2)}) async-start(bf16[16,16,1024]{2,1,0:T(8,128)(2,1)} %spread.2), calls=%async_computation.1 | async-start | bytes 1048576 | tf_op jit(solution)/shard_map/all_to_all | solution.py:362
  63.5 14.1 %copy-start.2 = (bf16[256,2048]{1,0:T(8,128)(2,1)S(1)}, bf16[256,2048]{1,0:T(8,128)(2,1)}, u32[]{:S(2)}) copy-start(bf16[256,2048]{1,0:T(8,128)(2,1)} %og.3) | copy-start | bytes 3145732
  74.1 2.0 %copy-start.9 = (bf16[16,16,1024]{2,1,0:T(8,128)(2,1)}, bf16[16,16,1024]{2,1,0:T(8,128)(2,1)S(1)}, u32[]{:S(2)}) copy-start(bf16[16,16,1024]{2,1,0:T(8,128)(2,1)S(1)} %all-to-all-done.1.mine_hbm) | copy-start | bytes 1572868
  74.1 2.0 %copy-start.6 = (bf16[2,256,512]{2,1,0:T(8,128)(2,1)}, bf16[2,256,512]{2,1,0:T(8,128)(2,1)S(1)}, u32[]{:S(2)}) copy-start(bf16[2,256,512]{2,1,0:T(8,128)(2,1)S(1)} %collective-permute-done.12.c0) | copy-start | bytes 1572868
  74.1 3.5 %collective-permute-start.13 = (bf16[16,16,1024]{2,1,0:T(8,128)(2,1)S(1)}, bf16[16,16,1024]{2,1,0:T(8,128)(2,1)S(1)}, u32[]{:S(2)}, u32[]{:S(2)}) collective-permute-start(bf16[16,16,1024]{2,1,0:T(8,128)(2,1)S(1)} %all-to-all-done.1.mine_hbm), channel_id=1, source_target_pairs={{0,1},{1,0},{2,3},{3,2},{4,5},{5,4},{6,7},{7,6},{8,9},{9,8},{10,11... | collective-permute-start | bytes 1572872 | tf_op jit(solution)/shard_map/ppermute | solution.py:31
  82.3 17.6 %copy-start.7 = (bf16[2,256,512]{2,1,0:T(8,128)(2,1)S(1)}, bf16[2,256,512]{2,1,0:T(8,128)(2,1)}, u32[]{:S(2)}) copy-start(bf16[2,256,512]{2,1,0:T(8,128)(2,1)} %copy-done.6) | copy-start | bytes 1572868
  82.3 2.0 %collective-permute-start.14 = (bf16[16,16,1024]{2,1,0:T(8,128)(2,1)S(1)}, bf16[16,16,1024]{2,1,0:T(8,128)(2,1)S(1)}, u32[]{:S(2)}, u32[]{:S(2)}) collective-permute-start(bf16[16,16,1024]{2,1,0:T(8,128)(2,1)S(1)} %get-tuple-element.47), channel_id=1, source_target_pairs={{0,1},{1,0},{2,3},{3,2},{4,5},{5,4},{6,7},{7,6},{8,9},{9,8},{10,11... | collective-permute-start | bytes 1572872 | tf_op jit(solution)/shard_map/ppermute | solution.py:31
  82.7 17.1 %collective-permute-start.15 = (bf16[2,256,512]{2,1,0:T(8,128)(2,1)}, bf16[2,256,512]{2,1,0:T(8,128)(2,1)S(1)}, u32[]{:S(2)}, u32[]{:S(2)}) collective-permute-start(bf16[2,256,512]{2,1,0:T(8,128)(2,1)} %get-tuple-element.50), channel_id=1, source_target_pairs={{0,2},{2,0},{1,3},{3,1},{4,6},{6,4},{5,7},{7,5},{8,10},{10,8},{9,1... | collective-permute-start | bytes 1572872 | tf_op jit(solution)/shard_map/ppermute | solution.py:31
  85.2 14.5 %all-to-all-start.2 = ((bf16[16,16,1024]{2,1,0:T(8,128)(2,1)}), bf16[16,16,1024]{2,1,0:T(8,128)(2,1)S(1)}, u32[]{:S(2)}, u32[]{:S(2)}) async-start(bf16[16,16,1024]{2,1,0:T(8,128)(2,1)} %add.13), calls=%async_computation.2 | async-start | bytes 1048576 | tf_op jit(solution)/shard_map/all_to_all | solution.py:341
  88.7 11.0 %collective-permute-start.16 = (bf16[256,512]{1,0:T(8,128)(2,1)}, bf16[256,512]{1,0:T(8,128)(2,1)S(1)}, u32[]{:S(2)}, u32[]{:S(2)}) collective-permute-start(bf16[256,512]{1,0:T(8,128)(2,1)} %get-tuple-element.51), channel_id=1, source_target_pairs={{0,1},{1,0},{2,3},{3,2},{4,5},{5,4},{6,7},{7,6},{8,9},{9,8},{10,11... | collective-permute-start | bytes 786440 | tf_op jit(solution)/shard_map/ppermute | solution.py:31
  99.8 29.0 %copy-start.12 = (bf16[256,512]{1,0:T(8,128)(2,1)}, bf16[256,512]{1,0:T(8,128)(2,1)S(1)}, u32[]{:S(2)}) copy-start(bf16[256,512]{1,0:T(8,128)(2,1)S(1)} %collective-permute-done.16.i1) | copy-start | bytes 786436
  99.8 36.6 %copy-start.10 = (bf16[2,256,512]{2,1,0:T(8,128)(2,1)}, bf16[2,256,512]{2,1,0:T(8,128)(2,1)S(1)}, u32[]{:S(2)}) copy-start(bf16[2,256,512]{2,1,0:T(8,128)(2,1)S(1)} %collective-permute-done.15.i2) | copy-start | bytes 1572868
  99.8 3.2 %collective-permute-start.17 = (f32[16,1024]{1,0:T(8,128)S(1)}, f32[16,1024]{1,0:T(8,128)S(1)}, u32[]{:S(2)}, u32[]{:S(2)}) collective-permute-start(f32[16,1024]{1,0:T(8,128)S(1)} %sum.3), channel_id=1, source_target_pairs={{0,2},{2,0},{1,3},{3,1},{4,6},{6,4},{5,7},{7,5},{8,10},{10,8},{9,1... | collective-permute-start | bytes 196616 | tf_op jit(solution)/shard_map/ppermute | solution.py:31
  99.9 15.1 %collective-permute-start.18 = (bf16[2,256,512]{2,1,0:T(8,128)(2,1)S(1)}, bf16[2,256,512]{2,1,0:T(8,128)(2,1)S(1)}, u32[]{:S(2)}, u32[]{:S(2)}) collective-permute-start(bf16[2,256,512]{2,1,0:T(8,128)(2,1)S(1)} %copy-done.7), channel_id=1, source_target_pairs={{0,1},{1,0},{2,3},{3,2},{4,5},{5,4},{6,7},{7,6},{8,9},{9,8},{10,11... | collective-permute-start | bytes 1572872 | tf_op jit(solution)/shard_map/ppermute | solution.py:31
  103.0 12.0 %collective-permute-start.19 = (bf16[2,256,512]{2,1,0:T(8,128)(2,1)S(1)}, bf16[2,256,512]{2,1,0:T(8,128)(2,1)S(1)}, u32[]{:S(2)}, u32[]{:S(2)}) collective-permute-start(bf16[2,256,512]{2,1,0:T(8,128)(2,1)S(1)} %collective-permute-done.15.i2), channel_id=1, source_target_pairs={{0,1},{1,0},{2,3},{3,2},{4,5},{5,4},{6,7},{7,6},{8,9},{9,8},{10,11... | collective-permute-start | bytes 1572872 | tf_op jit(solution)/shard_map/ppermute | solution.py:31
  105.8 9.3 %collective-permute-start.20 = (f32[16,1024]{1,0:T(8,128)S(1)}, f32[16,1024]{1,0:T(8,128)S(1)}, u32[]{:S(2)}, u32[]{:S(2)}) collective-permute-start(f32[16,1024]{1,0:T(8,128)S(1)} %add.9.part), channel_id=1, source_target_pairs={{0,64},{64,128},{128,192},{192,0},{1,65},{65,129},{129,193},{193,1... | collective-permute-start | bytes 196616 | tf_op jit(solution)/shard_map/ppermute | solution.py:350
  106.4 8.8 %collective-permute-start.21 = (f32[16,1024]{1,0:T(8,128)S(1)}, f32[16,1024]{1,0:T(8,128)S(1)}, u32[]{:S(2)}, u32[]{:S(2)}) collective-permute-start(f32[16,1024]{1,0:T(8,128)S(1)} %add.9.part), channel_id=1, source_target_pairs={{0,128},{64,192},{128,0},{192,64},{1,129},{65,193},{129,1},{193,65... | collective-permute-start | bytes 196616 | tf_op jit(solution)/shard_map/ppermute | solution.py:350
  110.5 7.4 %collective-permute-start.22 = (f32[16,1024]{1,0:T(8,128)S(1)}, f32[16,1024]{1,0:T(8,128)S(1)}, u32[]{:S(2)}, u32[]{:S(2)}) collective-permute-start(f32[16,1024]{1,0:T(8,128)S(1)} %add.9.part), channel_id=1, source_target_pairs={{0,192},{64,0},{128,64},{192,128},{1,193},{65,1},{129,65},{193,129... | collective-permute-start | bytes 196616 | tf_op jit(solution)/shard_map/ppermute | solution.py:350
  115.1 7.3 %copy-start.8 = (bf16[2,256,512]{2,1,0:T(8,128)(2,1)}, bf16[2,256,512]{2,1,0:T(8,128)(2,1)S(1)}, u32[]{:S(2)}) copy-start(bf16[2,256,512]{2,1,0:T(8,128)(2,1)S(1)} %collective-permute-done.18.c1) | copy-start | bytes 1572868
  115.1 2.9 %copy-start.11 = (bf16[2,256,512]{2,1,0:T(8,128)(2,1)}, bf16[2,256,512]{2,1,0:T(8,128)(2,1)S(1)}, u32[]{:S(2)}) copy-start(bf16[2,256,512]{2,1,0:T(8,128)(2,1)S(1)} %collective-permute-done.19.i3) | copy-start | bytes 1572868
  118.8 14.4 %all-to-all-start.3 = ((bf16[16,16,1024]{2,1,0:T(8,128)(2,1)}), bf16[16,16,1024]{2,1,0:T(8,128)(2,1)S(1)}, u32[]{:S(2)}, u32[]{:S(2)}) async-start(bf16[16,16,1024]{2,1,0:T(8,128)(2,1)} %spread.3), calls=%async_computation.3 | async-start | bytes 1048576 | tf_op jit(solution)/shard_map/all_to_all | solution.py:362
  133.2 3.2 %collective-permute-start.23 = (bf16[16,16,1024]{2,1,0:T(8,128)(2,1)S(1)}, bf16[16,16,1024]{2,1,0:T(8,128)(2,1)S(1)}, u32[]{:S(2)}, u32[]{:S(2)}) collective-permute-start(bf16[16,16,1024]{2,1,0:T(8,128)(2,1)S(1)} %all-to-all-done.3.mine_hbm), channel_id=1, source_target_pairs={{0,1},{1,0},{2,3},{3,2},{4,5},{5,4},{6,7},{7,6},{8,9},{9,8},{10,11... | collective-permute-start | bytes 1572872 | tf_op jit(solution)/shard_map/ppermute | solution.py:31

commit v3 on v2

--- a/solution.py
+++ b/solution.py
@@ -63,26 +63,19 @@
         ].astype(send.dtype)
 
 
-def join_halves(core, mine, other, whole):
-    for n in range(CHUNKS):
-        row, col = chunk_at(n)
-        cols = pl.ds(col, CHUNK_COLS)
-        whole[pl.ds(pl.multiple_of(core * HALF + row, CHUNK_ROWS), CHUNK_ROWS), cols] = mine[n]
-        whole[pl.ds(pl.multiple_of((1 - core) * HALF + row, CHUNK_ROWS), CHUNK_ROWS), cols] = other[n]
-
-
 def block(zl, core):
     return pl.ds(pl.multiple_of((zl * 2 + core) * ROWS, ROWS), ROWS)
 
 
-def prepare_kernel(at, ctx, err, own, near, far, low):
+def prepare_kernel(at, ctx, err, own, near, far, low, kept):
     zl, core = at[0], at[1]
     own[...] = ctx[:, block(zl, core)]
     near[...] = ctx[:, block(zl, 1 - core)]
     far[0] = ctx[:, block(1 - zl, core)]
     far[1] = ctx[:, block(1 - zl, 1 - core)]
     rows = err.shape[0]
-    low[pl.ds(pl.multiple_of(pl.program_id(0) * rows, rows), rows), :] = err[...].astype(BF16)
+    kept[...] = err[...].astype(BF16)
+    low[pl.ds(pl.multiple_of(pl.program_id(0) * rows, rows), rows), :] = kept[...]
 
 
 def left_kernel(scale, at, og, ctx, low, w0, w1, w2, w3, keep, send, total):
@@ -100,21 +93,27 @@
     split_halves(core, total, keep, send)
 
 
-def right_kernel(
-    scale, at, ctx, og, low_hbm, mine_hbm, other_hbm,
-    keep, send, left, total, low, mine, other, sems,
-):
-    zl, core = at[0], at[1]
-    copies = fetch((mine_hbm, other_hbm, low_hbm), (mine, other, low), sems)
-    copies[0].wait()
-    copies[1].wait()
-    join_halves(core, mine, other, left)
-    first, second = two(mm(ctx[...], left[...], 1, 1) * scale)
-    total[...] = mm(first, og[...], 0, 0) + mm(second, og[...], 0, 0)
-    own = left[:, block(zl, core)]
-    copies[2].wait()
+def unchunk(chunks, half):
+    for n in range(CHUNKS):
+        row, col = chunk_at(n)
+        half[row : row + CHUNK_ROWS, col : col + CHUNK_COLS] = chunks[n]
+
+
+def right_kernel(scale, at, ctx, og, chunks, low_hbm, out, half_hbm, low, half, total, sems):
+    copy = pltpu.make_async_copy(low_hbm, low, sems.at[0])
+    copy.start()
+    unchunk(chunks, half)
+    back = pltpu.make_async_copy(half, half_hbm, sems.at[1])
+    back.start()
+    first, second = two(mm(half[...], ctx[...], 1, 1) * scale)
+    total[...] = mm(first, og[...], 1, 0) + mm(second, og[...], 1, 0)
+    own = half[:, block(at[0], at[1])]
+    copy.wait()
     total[...] += mm(own, low[...], 1, 0)
-    split_halves(core, total, keep, send)
+    for n in range(CHUNKS):
+        row, col = chunk_at(n)
+        out[n] = total[row : row + CHUNK_ROWS, col : col + CHUNK_COLS].astype(out.dtype)
+    back.wait()
 
 
 def add_kernel(keep, got, out):
@@ -184,7 +183,12 @@
         a[stop:, :] = a[stop:, :] - dot_hi(panel[:, stop:RANK], panel, 0, 0)
 
 
-def gram_kernel(left, a):
+def gram_kernel(at, mine_hbm, other_hbm, a, left, sems):
+    core = at[1]
+    mine = left.at[pl.ds(pl.multiple_of(core * HALF, HALF), HALF), :]
+    other = left.at[pl.ds(pl.multiple_of((1 - core) * HALF, HALF), HALF), :]
+    for copy in fetch((mine_hbm, other_hbm), (mine, other), sems):
+        copy.wait()
     a[:, :RANK] = mm(left[...], left[...], 1, 1)
     a[:, RANK:] = eye(RANK)
     eliminate(0, a)
@@ -200,7 +204,7 @@
     inverse[...] = a[:, RANK:]
     first, second = two(a[:, RANK:])
     own = left[:, block(at[0], at[1])]
-    basis[...] = (mm(first, own, 1, 0) + mm(second, own, 1, 0)).astype(BF16)
+    basis[...] = (mm(first, own, 1, 0) + mm(second, own, 1, 0)).astype(BF16).T
 
 
 def grad_kernel(h0, h1, h2, h3, weight_hbm, o0, o1, far, weight, g0, g1, g2, g3, sems):
@@ -212,7 +216,9 @@
 
 
 def merge_kernel(scale, err, c0, c1, g0, g1, out, t0, t1):
-    @pl.when(pl.program_id(0) == 0)
+    step = pl.program_id(0)
+
+    @pl.when(step == 0)
     def _():
         t0[...] = c0[...].T
         t1[...] = c1[...].T
@@ -221,24 +227,35 @@
     out[...] = err[...] + total * scale
 
 
+def columns_of(inverse, half):
+    return inverse[:, pl.ds(pl.multiple_of(half * HALF, HALF), HALF)]
+
+
+def begin_kernel(at, chunks, inverse, c2, c3, out, t2, t3, half):
+    t2[...] = c2[0].T
+    t3[...] = c3[1].T
+    unchunk(chunks, half)
+    first, second = two(columns_of(inverse, at[1]))
+    out[...] = mm(first, half[...], 1, 0) + mm(second, half[...], 1, 0)
+
+
 def last_kernel(
-    share, at, mine_hbm, other_hbm, inverse, basis, merged, i0, i1, i2, i3,
-    new_error, factor_q, in_grad, right, mine, other, sems,
+    share, scale, at, other, inverse, basis, begun, t2, t3, merged, g2, g3, i0, i1, i2, i3,
+    new_error, factor_q, in_grad, half,
 ):
     step = pl.program_id(0)
     zl, core = at[0], at[1]
 
     @pl.when(step == 0)
     def _():
-        copies = fetch((mine_hbm, other_hbm), (mine, other), sems)
-        copies[0].wait()
-        copies[1].wait()
-        join_halves(core, mine, other, right)
+        unchunk(other, half)
 
     cols = pl.ds(pl.multiple_of(step * ROWS, ROWS), ROWS)
-    first, second = two(inverse[...])
-    q = (mm(first, right[:, cols], 1, 0) + mm(second, right[:, cols], 1, 0)) * share
-    new_error[...] = merged[...] - mm(basis[...], q.astype(BF16), 0, 0)
+    first, second = two(columns_of(inverse, 1 - core))
+    q = mm(first, half[:, cols], 1, 0) + mm(second, half[:, cols], 1, 0)
+    q = (begun[:, cols] + q) * share
+    total = mm(t2[...], g2[...], 1, 0) + mm(t3[...], g3[...], 1, 0)
+    new_error[...] = merged[...] + total * scale - mm(basis[...], q.astype(BF16), 1, 0)
     at_zl, at_core = step // 2, step % 2
 
     @pl.when((at_zl == zl) & (at_core == core))
@@ -291,7 +308,7 @@
     )(*args)
 
 
-def call_grid(kernel, steps, outs, ins, args, flops, name, scratch=(), sems=0, limit=24, loose=()):
+def call_grid(kernel, steps, outs, ins, args, flops, name, scratch=(), sems=0, limit=24, loose=(), alias=None):
     args = [
         a if spec in (SMEM, ANY, VMEM) or n in loose else in_hbm(a)
         for n, (a, spec) in enumerate(zip(args, ins))
@@ -309,6 +326,7 @@
         in_specs=ins,
         out_specs=[spec for _, _, spec in outs],
         scratch_shapes=scratch,
+        input_output_aliases=alias or {},
         compiler_params=pltpu.CompilerParams(vmem_limit_bytes=limit * 2**20),
         cost_estimate=pl.CostEstimate(flops=flops, bytes_accessed=moved, transcendentals=0),
         name=name,
@@ -375,12 +393,12 @@
     warm_near = swap(warm, "core")
     quarter = rows_of(TOK // 4, ROWS)
     strip = rows_of(ROWS // 4, FEAT)
-    c_own, c_near, c_far, low = call_grid(
+    c_own, c_near, c_far, low, kept = call_grid(
         prepare_kernel,
         4,
         [tokens + (quarter,)] * 2
         + [pair + (pl.BlockSpec((2, TOK // 4, ROWS), lambda j: (0, j, 0)),)]
-        + [((ROWS, FEAT), BF16, VMEM)],
+        + [((ROWS, FEAT), BF16, VMEM), ((ROWS, FEAT), BF16, strip)],
         [SMEM, rows_of(TOK // 4, FEAT), strip],
         (at, context, error),
         4_000_000,
@@ -415,7 +433,7 @@
     part = across_plane(keep, send, (merged,))
     g_diag = swap(tied(g_far, part), "core")
     zs = across_z(tied(part, g_far))
-    c_far = swap(tied(c_far, zs[1]), "zl")
+    c_far = swap(tied(c_far, *zs[1:]), "zl")
     mine = back_over_plane(*zs)
 
     i_own, i_near, i_far = call(
@@ -433,35 +451,49 @@
     i_far = swap(i_far, "zl")
     i_near = swap(i_near, "core")
 
-    keep, send, left = call(
-        functools.partial(right_kernel, scale),
-        [(CHUNKED, F32), (CHUNKED, BF16), ((RANK, FEAT), BF16)],
-        (at, context, out_grad, low, mine, other),
-        2_000_000_000,
-        "right",
-        [((RANK, FEAT), F32), big, (CHUNKED, BF16), (CHUNKED, BF16)],
-        loose=(5,),
-        held=(3, 4),
-        sems=3,
-    )
+    half = ((HALF, FEAT), BF16)
+
+    def right(chunks, dtype):
+        return call_grid(
+            functools.partial(right_kernel, scale),
+            1,
+            [(CHUNKED, dtype, VMEM), half + (ANY,)],
+            [SMEM, VMEM, VMEM, VMEM, ANY],
+            (at, context, out_grad, chunks, in_hbm(kept)),
+            1_000_000_000,
+            "right",
+            [big, half, ((HALF, FEAT), F32)],
+            sems=2,
+        )
+
+    keep, mine_half = right(mine, F32)
+    send, other_half = right(tied(other, keep), BF16)
 
     table = ((RANK, 2 * RANK), F32)
-    (a,) = call(gram_kernel, [table], (left,), 300_000_000, "gram")
-    c_diag = swap(c_far, "core")
+    a, left = call(
+        gram_kernel,
+        [table, ((RANK, FEAT), BF16)],
+        (at, mine_half, other_half),
+        300_000_000,
+        "gram",
+        held=(1, 2),
+        sems=2,
+    )
     (a,) = call(
         functools.partial(step_kernel, PART), [table], (a,), 300_000_000, "step", alias={0: 0}
     )
     part = across_plane(keep, send, (a,))
     part = tied(part, i_far, i_near)
     zs = across_z(part)
-    i_diag = swap(tied(i_far, zs[0]), "core")
     (a,) = call(
         functools.partial(step_kernel, 2 * PART), [table], (a,), 300_000_000, "step", alias={0: 0}
     )
-    mine = back_over_plane(*zs, beside=(a, c_diag, i_diag))
+    mine = back_over_plane(*zs, beside=(a,))
+    c_diag = swap(tied(c_far, *zs[1:]), "core")
+    i_diag = swap(tied(i_far, *zs[1:]), "core")
     inverse, basis = call(
         basis_kernel,
-        [((RANK, RANK), F32), ((RANK, ROWS), BF16)],
+        [((RANK, RANK), F32), ((ROWS, RANK), BF16)],
         (at, a, left),
         300_000_000,
         "basis",
@@ -470,33 +502,34 @@
     block_in = whole(TOK, ROWS)
     first = pl.BlockSpec((None, TOK, ROWS), lambda j: (0, 0, 0))
     second = pl.BlockSpec((None, TOK, ROWS), lambda j: (1, 0, 0))
-    (merged,) = call_grid(
-        functools.partial(merge_kernel, scale),
-        4,
-        [((ROWS, FEAT), F32, column(ROWS))],
-        [column(ROWS), first, second, column(TOK), column(TOK)],
-        (merged, c_far, c_diag, g_far, g_diag),
-        1_100_000_000,
-        "merge",
-        turned,
-    )
-    other = swap(tied(mine, basis, merged), "core")
+    other = swap(tied(mine, basis, c_diag, i_diag), "core")
+    begun, t2, t3 = call(
+        begin_kernel,
+        [((RANK, FEAT), F32)] + turned,
+        (at, mine, inverse, c_far, c_diag),
+        300_000_000,
+        "begin",
+        [((HALF, FEAT), BF16)],
+    )
+    other = tied(other, begun)
 
     new_error, factor_q, in_grad = call_grid(
-        functools.partial(last_kernel, 1.0 / (SIZES[0] * SIZES[1] * SIZES[2])),
+        functools.partial(last_kernel, 1.0 / (SIZES[0] * SIZES[1] * SIZES[2]), scale),
         4,
         [
             ((ROWS, FEAT), F32, column(ROWS)),
             ((ROWS, RANK), F32, whole(ROWS, RANK)),
             ((TOK, FEAT), BF16, column(TOK)),
         ],
-        [SMEM, ANY, ANY, VMEM, VMEM, column(ROWS)]
+        [SMEM] + [VMEM] * 6 + [column(ROWS), column(TOK), column(TOK)]
         + [block_in, block_in, first, second],
-        (at, mine, other, inverse, basis, merged, i_own, i_near, i_far, i_diag),
-        1_200_000_000,
+        (
+            at, other, inverse, basis, begun, t2, t3, merged, g_far, g_diag,
+            i_own, i_near, i_far, i_diag,
+        ),
+        2_000_000_000,
         "last",
-        [((RANK, FEAT), BF16), (CHUNKED, BF16), (CHUNKED, BF16)],
-        sems=2,
+        [((HALF, FEAT), BF16)],
     )
     return in_grad, new_error[None], factor_q
 

time: 144 us -> 150 us (1.042)
  starting transfers between devices: 57.8 us -> 60 us
  Pallas kernels: 53.8 us -> 55.8 us
  waiting for transfers between devices: 30.4 us -> 32.3 us
    all_to_all x2, waiting for transfers between devices: 5.09 us -> 9.5 us  [back_over_plane(): return lax.all_to_all(whole, ('y', 'x'), 0, 0)]
    pallas_call x4 -> x5, Pallas kernels: 23.2 us -> 26.2 us  [call_grid(): pl.pallas_call(kernel, grid=(steps,), out_shape=[(jax.ShapeDtypeStruct if...]
    ppermute x18, waiting for transfers between devices: 11.5 us -> 9.25 us  [swap(): return lax.ppermute(x, axis, [(0, 1), (1, 0)])]
    ppermute x18, starting transfers between devices: 21.3 us -> 23.1 us  [swap(): return lax.ppermute(x, axis, [(0, 1), (1, 0)])]
  transfers between devices with their start and end apart: 28 -> 28, of which waited for: 14 -> 14; matrix products, arithmetic and copies ran while one was open for 0% -> 0% of each run, Pallas kernels for 29% -> 30%
where the time goes in v3:
time: 150 us; the launch traced here: 149 us
  starting transfers between devices  60 us (40%)
  Pallas kernels  55.8 us (37%)
  waiting for transfers between devices  32.3 us (22%)
    pallas_call x13, Pallas kernels, call(): pl.pallas_call(kernel, out_shape=[(pltpu.HBM if free else jax.ShapeDtypeS...  29.6 us
    pallas_call x5, Pallas kernels, call_grid(): pl.pallas_call(kernel, grid=(steps,), out_shape=[(jax.ShapeDtypeStruct if...  26.2 us
    ppermute x18, starting transfers between devices, swap(): return lax.ppermute(x, axis, [(0, 1), (1, 0)])  23.1 us
    ppermute x6, starting transfers between devices, across_z(): lax.ppermute(part, 'zh', [(i, (i + step) % 4) for i in range(4)])  16 us
    all_to_all x2, starting transfers between devices, back_over_plane(): return lax.all_to_all(whole, ('y', 'x'), 0, 0)  10.6 us
    all_to_all x2, starting transfers between devices, across_plane(): parts = tied(lax.all_to_all(half, ('y', 'x'), 0, 0), *beside)  10.3 us
    all_to_all x2, waiting for transfers between devices, back_over_plane(): return lax.all_to_all(whole, ('y', 'x'), 0, 0)  9.5 us
    ppermute x18, waiting for transfers between devices, swap(): return lax.ppermute(x, axis, [(0, 1), (1, 0)])  9.25 us
  transfers between devices with their start and end apart: 28, of which 14 were waited for; matrix products, arithmetic and copies ran while one was open for 0% of the time, Pallas kernels for 30%

profile of v3, /device:TPU:1, one launch (start us, length us, event | category | flops | bytes accessed | tf_op | source)
XLA Modules:
  0.0 149.2 jit_solution(10168229811322678586)
XLA Ops:
  0.6 2.6 %collective-permute-start.1 = (bf16[512,256]{1,0:T(8,128)(2,1)}, bf16[512,256]{1,0:T(8,128)(2,1)S(1)}, u32[]{:S(2)}, u32[]{:S(2)}) collective-permute-start(bf16[512,256]{1,0:T(8,128)(2,1)} %w0.1), channel_id=1, source_target_pairs={{0,2},{2,0},{1,3},{3,1},{4,6},{6,4},{5,7},{7,5},{8,10},{10,8},{9,1... | collective-permute-start | bytes 786440 | tf_op jit(solution)/shard_map/ppermute | solution.py:31
  3.2 1.0 collective-permute-start
  4.1 0.1 pad_add_fusion.at
  4.2 4.9 %prepare.1 = (bf16[256,512]{1,0:T(8,128)(2,1)}, bf16[256,512]{1,0:T(8,128)(2,1)}, bf16[2,256,512]{2,1,0:T(8,128)(2,1)}, bf16[512,2048]{1,0:T(8,128)(2,1)S(1)}, bf16[512,2048]{1,0:T(8,128)(2,1)}) custom-call(s32[2]{0:T(128)S(1)} %pad_add_fusion.at, bf16[256,2048]{1,0:T(8,128)(2,1)} %ctx.7, f32[512,2048]{1,0:T(8,128)} %bitcast.4), custom_call_target="tpu_custom_call" | custom-call | flops 4000000 | bytes 10485768 | tf_op jit(solution)/shard_map/prepare/pallas_call | solution.py:320
  9.1 0.0 collective-permute-done.1.w2
  9.1 1.6 %collective-permute-start.2 = (bf16[512,256]{1,0:T(8,128)(2,1)S(1)}, bf16[512,256]{1,0:T(8,128)(2,1)S(1)}, u32[]{:S(2)}, u32[]{:S(2)}) collective-permute-start(bf16[512,256]{1,0:T(8,128)(2,1)S(1)} %collective-permute-done.1.w2), channel_id=1, source_target_pairs={{0,1},{1,0},{2,3},{3,2},{4,5},{5,4},{6,7},{7,6},{8,9},{9,8},{10,11... | collective-permute-start | bytes 786440 | tf_op jit(solution)/shard_map/ppermute | solution.py:31
  10.7 1.5 collective-permute-start.6
  12.1 0.3 collective-permute-start.5
  12.4 0.0 collective-permute-done.w1
  12.4 2.4 %left.1 = (f32[16,16,1024]{2,1,0:T(8,128)S(1)}, bf16[16,16,1024]{2,1,0:T(8,128)(2,1)S(1)}) custom-call(s32[2]{0:T(128)S(1)} %pad_add_fusion.at, bf16[256,2048]{1,0:T(8,128)(2,1)S(1)} %copy-done.1, bf16[256,2048]{1,0:T(8,128)(2,1)S(1)} %copy-done, bf16[512,2048]{1,0:T(8,128)(2,1)S(1)} %get-tuple-element.42.low, bf16[512,256]{1,0:T(8,128)(2,1)S(1)} %copy-done.4, ...), custom_call_target="tpu_custom_call" | custom-call | flops 2000000000 | bytes 6815752 | tf_op jit(solution)/shard_map/left/pallas_call | solution.py:295
  14.9 0.3 collective-permute-start.3
  15.2 1.7 %collective-permute-done.3.got = bf16[16,16,1024]{2,1,0:T(8,128)(2,1)S(1)} collective-permute-done((bf16[16,16,1024]{2,1,0:T(8,128)(2,1)S(1)}, bf16[16,16,1024]{2,1,0:T(8,128)(2,1)S(1)}, u32[]{:S(2)}, u32[]{:S(2)}) %collective-permute-start.3) | collective-permute-done | bytes 524320 | tf_op jit(solution)/shard_map/ppermute | solution.py:31
  16.9 0.9 add.12
  17.8 6.8 %all-to-all-start = ((bf16[16,16,1024]{2,1,0:T(8,128)(2,1)}), bf16[16,16,1024]{2,1,0:T(8,128)(2,1)S(1)}, u32[]{:S(2)}, u32[]{:S(2)}) async-start(bf16[16,16,1024]{2,1,0:T(8,128)(2,1)} %add.12), calls=%async_computation | async-start | bytes 1048576 | tf_op jit(solution)/shard_map/all_to_all | solution.py:359
  24.5 0.6 collective-permute-start.4
  25.1 1.2 collective-permute-done.4.c1
  26.3 5.9 %merge.1.merged = f32[512,2048]{1,0:T(8,128)} custom-call(f32[512,2048]{1,0:T(8,128)} %bitcast.5, bf16[256,512]{1,0:T(8,128)(2,1)S(1)} %copy-done.3, bf16[256,512]{1,0:T(8,128)(2,1)S(1)} %collective-permute-done.4.c1, bf16[256,2048]{1,0:T(8,128)(2,1)S(1)} %copy-done.1, bf16[256,2048]{1,0:T(8,128)(2,1)} %collective-permute-done.5.g1.h1), custom_call_target="tpu_custom_call" | custom-call | flops 1100000000 | bytes 11010048 | tf_op jit(solution)/shard_map/merge/pallas_call | solution.py:320
  32.2 3.2 %all-to-all-done.parts = bf16[16,16,1024]{2,1,0:T(8,128)(2,1)S(1)} async-done(((bf16[16,16,1024]{2,1,0:T(8,128)(2,1)}), bf16[16,16,1024]{2,1,0:T(8,128)(2,1)S(1)}, u32[]{:S(2)}, u32[]{:S(2)}) %all-to-all-start) | async-done | bytes 524320 | tf_op jit(solution)/shard_map/all_to_all | solution.py:359
  35.4 0.1 sum.2
  35.4 0.1 collective-permute-done.6.h2.g2
  35.6 1.6 %collective-permute-start.11 = (bf16[256,2048]{1,0:T(8,128)(2,1)}, bf16[256,2048]{1,0:T(8,128)(2,1)}, u32[]{:S(2)}, u32[]{:S(2)}) collective-permute-start(bf16[256,2048]{1,0:T(8,128)(2,1)} %collective-permute-done.6.h2.g2), channel_id=1, source_target_pairs={{0,1},{1,0},{2,3},{3,2},{4,5},{5,4},{6,7},{7,6},{8,9},{9,8},{10,11... | collective-permute-start | bytes 3145736 | tf_op jit(solution)/shard_map/ppermute | solution.py:31
  37.2 0.9 collective-permute-start.7
  38.1 2.8 %collective-permute-done.7 = f32[16,1024]{1,0:T(8,128)S(1)} collective-permute-done((f32[16,1024]{1,0:T(8,128)S(1)}, f32[16,1024]{1,0:T(8,128)S(1)}, u32[]{:S(2)}, u32[]{:S(2)}) %collective-permute-start.7) | collective-permute-done | bytes 65568 | tf_op jit(solution)/shard_map/ppermute | solution.py:31
  40.8 5.3 %collective-permute-start.10 = (f32[16,1024]{1,0:T(8,128)S(1)}, f32[16,1024]{1,0:T(8,128)S(1)}, u32[]{:S(2)}, u32[]{:S(2)}) collective-permute-start(f32[16,1024]{1,0:T(8,128)S(1)} %add.8.part), channel_id=1, source_target_pairs={{0,192},{64,0},{128,64},{192,128},{1,193},{65,1},{129,65},{193,129... | collective-permute-start | bytes 196616 | tf_op jit(solution)/shard_map/ppermute | solution.py:368
  46.2 1.0 collective-permute-start.9
  47.2 2.2 %collective-permute-start.8 = (f32[16,1024]{1,0:T(8,128)S(1)}, f32[16,1024]{1,0:T(8,128)S(1)}, u32[]{:S(2)}, u32[]{:S(2)}) collective-permute-start(f32[16,1024]{1,0:T(8,128)S(1)} %add.8.part), channel_id=1, source_target_pairs={{0,64},{64,128},{128,192},{192,0},{1,65},{65,129},{129,193},{193,1... | collective-permute-start | bytes 196616 | tf_op jit(solution)/shard_map/ppermute | solution.py:368
  49.4 4.0 %collective-permute-done.9.opposite = f32[16,1024]{1,0:T(8,128)S(1)} collective-permute-done((f32[16,1024]{1,0:T(8,128)S(1)}, f32[16,1024]{1,0:T(8,128)S(1)}, u32[]{:S(2)}, u32[]{:S(2)}) %collective-permute-start.9) | collective-permute-done | bytes 65568 | tf_op jit(solution)/shard_map/ppermute | solution.py:368
  53.4 0.3 collective-permute-done.8.one
  53.7 0.9 collective-permute-start.12
  54.6 0.8 spread.2
  55.4 6.7 %all-to-all-start.1 = ((bf16[16,16,1024]{2,1,0:T(8,128)(2,1)}), bf16[16,16,1024]{2,1,0:T(8,128)(2,1)S(1)}, u32[]{:S(2)}, u32[]{:S(2)}) async-start(bf16[16,16,1024]{2,1,0:T(8,128)(2,1)} %spread.2), calls=%async_computation.1 | async-start | bytes 1048576 | tf_op jit(solution)/shard_map/all_to_all | solution.py:380
  62.1 0.0 copy-start.2
  62.1 6.4 %grad.1 = (bf16[256,512]{1,0:T(8,128)(2,1)}, bf16[256,512]{1,0:T(8,128)(2,1)}, bf16[2,256,512]{2,1,0:T(8,128)(2,1)}) custom-call(bf16[256,2048]{1,0:T(8,128)(2,1)} %og.5, bf16[256,2048]{1,0:T(8,128)(2,1)} %collective-permute-done.5.g1.h1, bf16[256,2048]{1,0:T(8,128)(2,1)} %collective-permute-done.6.h2.g2, bf16[256,2048]{1,0:T(8,128)(2,1)} %collective-permute-done.11.h3.g3, ...), custom_call_target="tpu_custom_call" | custom-call | flops 2200000000 | bytes 7340032 | tf_op jit(solution)/shard_map/grad/pallas_call | solution.py:295
  68.6 2.5 %all-to-all-done.1.chunks = bf16[16,16,1024]{2,1,0:T(8,128)(2,1)S(1)} async-done(((bf16[16,16,1024]{2,1,0:T(8,128)(2,1)}), bf16[16,16,1024]{2,1,0:T(8,128)(2,1)S(1)}, u32[]{:S(2)}, u32[]{:S(2)}) %all-to-all-start.1) | async-done | bytes 524320 | tf_op jit(solution)/shard_map/all_to_all | solution.py:380
  71.1 4.3 %collective-permute-start.13 = (bf16[16,16,1024]{2,1,0:T(8,128)(2,1)S(1)}, bf16[16,16,1024]{2,1,0:T(8,128)(2,1)S(1)}, u32[]{:S(2)}, u32[]{:S(2)}) collective-permute-start(bf16[16,16,1024]{2,1,0:T(8,128)(2,1)S(1)} %all-to-all-done.1.chunks), channel_id=1, source_target_pairs={{0,1},{1,0},{2,3},{3,2},{4,5},{5,4},{6,7},{7,6},{8,9},{9,8},{10,11... | collective-permute-start | bytes 1572872 | tf_op jit(solution)/shard_map/ppermute | solution.py:31
  75.4 4.0 %right.2 = (f32[16,16,1024]{2,1,0:T(8,128)S(1)}, bf16[128,2048]{1,0:T(8,128)(2,1)}) custom-call(s32[2]{0:T(128)S(1)} %pad_add_fusion.at, bf16[256,2048]{1,0:T(8,128)(2,1)S(1)} %copy-done, bf16[256,2048]{1,0:T(8,128)(2,1)S(1)} %copy-done.2, bf16[16,16,1024]{2,1,0:T(8,128)(2,1)S(1)} %all-to-all-done.1.chunks, bf16[512,2048]{1,0:T(8,128)(2,1)} %get-tuple-element.51.low_hbm), custom_call_target="tpu_custom_call" | custom-call | flops 1000000000 | bytes 6291464 | tf_op jit(solution)/shard_map/right/pallas_call | solution.py:320
  79.4 4.0 %right.3 = (bf16[16,16,1024]{2,1,0:T(8,128)(2,1)S(1)}, bf16[128,2048]{1,0:T(8,128)(2,1)}) custom-call(s32[2]{0:T(128)S(1)} %pad_add_fusion.at, bf16[256,2048]{1,0:T(8,128)(2,1)S(1)} %copy-done, bf16[256,2048]{1,0:T(8,128)(2,1)S(1)} %copy-done.2, bf16[16,16,1024]{2,1,0:T(8,128)(2,1)S(1)} %collective-permute-done.13.chunks, ...), custom_call_target="tpu_custom_call" | custom-call | flops 1000000000 | bytes 5767176 | tf_op jit(solution)/shard_map/right/pallas_call | solution.py:320
  83.4 0.1 collective-permute-start.14
  83.5 0.8 collective-permute-start.15
  84.3 1.1 collective-permute-done.14.got
  85.4 0.9 add.13
  86.2 3.6 %all-to-all-start.2 = ((bf16[16,16,1024]{2,1,0:T(8,128)(2,1)}), bf16[16,16,1024]{2,1,0:T(8,128)(2,1)S(1)}, u32[]{:S(2)}, u32[]{:S(2)}) async-start(bf16[16,16,1024]{2,1,0:T(8,128)(2,1)} %add.13), calls=%async_computation.2 | async-start | bytes 1048576 | tf_op jit(solution)/shard_map/all_to_all | solution.py:359
  89.8 0.3 collective-permute-start.16
  90.1 5.7 %gram.1 = (f32[256,512]{1,0:T(8,128)S(1)}, bf16[256,2048]{1,0:T(8,128)(2,1)S(1)}) custom-call(s32[2]{0:T(128)S(1)} %pad_add_fusion.at, bf16[128,2048]{1,0:T(8,128)(2,1)} %get-tuple-element.60.mine_hbm, bf16[128,2048]{1,0:T(8,128)(2,1)} %get-tuple-element.61.other_hbm), custom_call_target="tpu_custom_call" | custom-call | flops 300000000 | bytes 2621448 | tf_op jit(solution)/shard_map/gram/pallas_call | solution.py:295
  95.9 3.1 %step.2.a_in = f32[256,512]{1,0:T(8,128)S(1)} custom-call(f32[256,512]{1,0:T(8,128)S(1)} %get-tuple-element.62.a_in), custom_call_target="tpu_custom_call", output_to_operand_aliasing={{}: (0, {})} | custom-call | flops 300000000 | bytes 1048576 | tf_op jit(solution)/shard_map/step/pallas_call | solution.py:295
  98.9 2.0 %all-to-all-done.2.parts = bf16[16,16,1024]{2,1,0:T(8,128)(2,1)S(1)} async-done(((bf16[16,16,1024]{2,1,0:T(8,128)(2,1)}), bf16[16,16,1024]{2,1,0:T(8,128)(2,1)S(1)}, u32[]{:S(2)}, u32[]{:S(2)}) %all-to-all-start.2) | async-done | bytes 524320 | tf_op jit(solution)/shard_map/all_to_all | solution.py:359
  100.9 0.1 sum.3
  101.0 0.8 collective-permute-start.17
  101.8 2.4 %collective-permute-done.17 = f32[16,1024]{1,0:T(8,128)S(1)} collective-permute-done((f32[16,1024]{1,0:T(8,128)S(1)}, f32[16,1024]{1,0:T(8,128)S(1)}, u32[]{:S(2)}, u32[]{:S(2)}) %collective-permute-start.17) | collective-permute-done | bytes 65568 | tf_op jit(solution)/shard_map/ppermute | solution.py:31
  104.2 3.8 %collective-permute-start.20 = (f32[16,1024]{1,0:T(8,128)S(1)}, f32[16,1024]{1,0:T(8,128)S(1)}, u32[]{:S(2)}, u32[]{:S(2)}) collective-permute-start(f32[16,1024]{1,0:T(8,128)S(1)} %add.9.part), channel_id=1, source_target_pairs={{0,192},{64,0},{128,64},{192,128},{1,193},{65,1},{129,65},{193,129... | collective-permute-start | bytes 196616 | tf_op jit(solution)/shard_map/ppermute | solution.py:368
  108.0 1.5 %collective-permute-start.19 = (f32[16,1024]{1,0:T(8,128)S(1)}, f32[16,1024]{1,0:T(8,128)S(1)}, u32[]{:S(2)}, u32[]{:S(2)}) collective-permute-start(f32[16,1024]{1,0:T(8,128)S(1)} %add.9.part), channel_id=1, source_target_pairs={{0,128},{64,192},{128,0},{192,64},{1,129},{65,193},{129,1},{193,65... | collective-permute-start | bytes 196616 | tf_op jit(solution)/shard_map/ppermute | solution.py:368
  109.5 2.1 %collective-permute-start.18 = (f32[16,1024]{1,0:T(8,128)S(1)}, f32[16,1024]{1,0:T(8,128)S(1)}, u32[]{:S(2)}, u32[]{:S(2)}) collective-permute-start(f32[16,1024]{1,0:T(8,128)S(1)} %add.9.part), channel_id=1, source_target_pairs={{0,64},{64,128},{128,192},{192,0},{1,65},{65,129},{129,193},{193,1... | collective-permute-start | bytes 196616 | tf_op jit(solution)/shard_map/ppermute | solution.py:368
  111.6 3.5 %collective-permute-done.19.opposite = f32[16,1024]{1,0:T(8,128)S(1)} collective-permute-done((f32[16,1024]{1,0:T(8,128)S(1)}, f32[16,1024]{1,0:T(8,128)S(1)}, u32[]{:S(2)}, u32[]{:S(2)}) %collective-permute-start.19) | collective-permute-done | bytes 65568 | tf_op jit(solution)/shard_map/ppermute | solution.py:368
  115.1 0.7 collective-permute-done.18.one
  115.8 3.7 %collective-permute-start.21 = (bf16[2,256,512]{2,1,0:T(8,128)(2,1)S(1)}, bf16[2,256,512]{2,1,0:T(8,128)(2,1)}, u32[]{:S(2)}, u32[]{:S(2)}) collective-permute-start(bf16[2,256,512]{2,1,0:T(8,128)(2,1)S(1)} %collective-permute-done.12.c2), channel_id=1, source_target_pairs={{0,1},{1,0},{2,3},{3,2},{4,5},{5,4},{6,7},{7,6},{8,9},{9,8},{10,11... | collective-permute-start | bytes 1572872 | tf_op jit(solution)/shard_map/ppermute | solution.py:31
  119.6 0.0 collective-permute-start.22
  119.6 3.0 %step.3.a_in = f32[256,512]{1,0:T(8,128)S(1)} custom-call(f32[256,512]{1,0:T(8,128)S(1)} %step.2.a_in), custom_call_target="tpu_custom_call", output_to_operand_aliasing={{}: (0, {})} | custom-call | flops 300000000 | bytes 1048576 | tf_op jit(solution)/shard_map/step/pallas_call | solution.py:295
  122.6 0.9 spread.3
  123.4 3.9 %all-to-all-start.3 = ((bf16[16,16,1024]{2,1,0:T(8,128)(2,1)}), bf16[16,16,1024]{2,1,0:T(8,128)(2,1)S(1)}, u32[]{:S(2)}, u32[]{:S(2)}) async-start(bf16[16,16,1024]{2,1,0:T(8,128)(2,1)} %spread.3), calls=%async_computation.3 | async-start | bytes 1048576 | tf_op jit(solution)/shard_map/all_to_all | solution.py:380
  127.3 3.6 %basis.1 = (f32[256,256]{1,0:T(8,128)S(1)}, bf16[512,256]{1,0:T(8,128)(2,1)S(1)}) custom-call(s32[2]{0:T(128)S(1)} %pad_add_fusion.at, f32[256,512]{1,0:T(8,128)S(1)} %step.3.a_in, bf16[256,2048]{1,0:T(8,128)(2,1)S(1)} %get-tuple-element.68.left), custom_call_target="tpu_custom_call" | custom-call | flops 300000000 | bytes 2097160 | tf_op jit(solution)/shard_map/basis/pallas_call | solution.py:295
  130.9 7.0 %all-to-all-done.3.chunks = bf16[16,16,1024]{2,1,0:T(8,128)(2,1)S(1)} async-done(((bf16[16,16,1024]{2,1,0:T(8,128)(2,1)}), bf16[16,16,1024]{2,1,0:T(8,128)(2,1)S(1)}, u32[]{:S(2)}, u32[]{:S(2)}) %all-to-all-start.3) | async-done | bytes 524320 | tf_op jit(solution)/shard_map/all_to_all | solution.py:380
  137.9 1.9 %collective-permute-start.23 = (bf16[16,16,1024]{2,1,0:T(8,128)(2,1)S(1)}, bf16[16,16,1024]{2,1,0:T(8,128)(2,1)S(1)}, u32[]{:S(2)}, u32[]{:S(2)}) collective-permute-start(bf16[16,16,1024]{2,1,0:T(8,128)(2,1)S(1)} %all-to-all-done.3.chunks), channel_id=1, source_target_pairs={{0,1},{1,0},{2,3},{3,2},{4,5},{5,4},{6,7},{7,6},{8,9},{9,8},{10,11... | collective-permute-start | bytes 1572872 | tf_op jit(solution)/shard_map/ppermute | solution.py:31
  139.8 1.7 %begin.1 = (f32[256,2048]{1,0:T(8,128)S(1)}, bf16[512,256]{1,0:T(8,128)(2,1)S(1)}, bf16[512,256]{1,0:T(8,128)(2,1)S(1)}) custom-call(s32[2]{0:T(128)S(1)} %pad_add_fusion.at, bf16[16,16,1024]{2,1,0:T(8,128)(2,1)S(1)} %all-to-all-done.3.chunks, f32[256,256]{1,0:T(8,128)S(1)} %get-tuple-element.73.inverse, ...), custom_call_target="tpu_custom_call" | custom-call | flops 300000000 | bytes 4456456 | tf_op jit(solution)/shard_map/begin/pallas_call | solution.py:295
  141.6 7.5 %last.1 = (f32[512,2048]{1,0:T(8,128)}, f32[512,256]{1,0:T(8,128)}, bf16[256,2048]{1,0:T(8,128)(2,1)}) custom-call(s32[2]{0:T(128)S(1)} %pad_add_fusion.at, bf16[16,16,1024]{2,1,0:T(8,128)(2,1)S(1)} %collective-permute-done.23.other, f32[256,256]{1,0:T(8,128)S(1)} %get-tuple-element.73.inverse, bf16[512,256]{1,0:T(8,128)(2,1)S(1)} %get-tuple-element.69.basis, ...), custom_call_target="tpu_custom_call" | custom-call | flops 2000000000 | bytes 17301512 | tf_op jit(solution)/shard_map/last/pallas_call | solution.py:320
  (29 shorter events, 0.1 us)
Async XLA Ops:
  0.6 8.5 %collective-permute-start.1 = (bf16[512,256]{1,0:T(8,128)(2,1)}, bf16[512,256]{1,0:T(8,128)(2,1)S(1)}, u32[]{:S(2)}, u32[]{:S(2)}) collective-permute-start(bf16[512,256]{1,0:T(8,128)(2,1)} %w0.1), channel_id=1, source_target_pairs={{0,2},{2,0},{1,3},{3,1},{4,6},{6,4},{5,7},{7,5},{8,10},{10,8},{9,1... | collective-permute-start | bytes 786440 | tf_op jit(solution)/shard_map/ppermute | solution.py:31
  3.2 9.2 %collective-permute-start = (bf16[512,256]{1,0:T(8,128)(2,1)}, bf16[512,256]{1,0:T(8,128)(2,1)S(1)}, u32[]{:S(2)}, u32[]{:S(2)}) collective-permute-start(bf16[512,256]{1,0:T(8,128)(2,1)} %w0.1), channel_id=1, source_target_pairs={{0,1},{1,0},{2,3},{3,2},{4,5},{5,4},{6,7},{7,6},{8,9},{9,8},{10,11... | collective-permute-start | bytes 786440 | tf_op jit(solution)/shard_map/ppermute | solution.py:31
  4.2 6.4 %copy-start.1 = (bf16[256,2048]{1,0:T(8,128)(2,1)S(1)}, bf16[256,2048]{1,0:T(8,128)(2,1)}, u32[]{:S(2)}) copy-start(bf16[256,2048]{1,0:T(8,128)(2,1)} %og.5) | copy-start | bytes 3145732
  4.2 8.2 %copy-start = (bf16[256,2048]{1,0:T(8,128)(2,1)S(1)}, bf16[256,2048]{1,0:T(8,128)(2,1)}, u32[]{:S(2)}) copy-start(bf16[256,2048]{1,0:T(8,128)(2,1)} %ctx.7) | copy-start | bytes 3145732
  4.2 8.2 %copy-start.4 = (bf16[512,256]{1,0:T(8,128)(2,1)S(1)}, bf16[512,256]{1,0:T(8,128)(2,1)}, u32[]{:S(2)}) copy-start(bf16[512,256]{1,0:T(8,128)(2,1)} %w0.1) | copy-start | bytes 786436
  9.1 3.3 %collective-permute-start.2 = (bf16[512,256]{1,0:T(8,128)(2,1)S(1)}, bf16[512,256]{1,0:T(8,128)(2,1)S(1)}, u32[]{:S(2)}, u32[]{:S(2)}) collective-permute-start(bf16[512,256]{1,0:T(8,128)(2,1)S(1)} %collective-permute-done.1.w2), channel_id=1, source_target_pairs={{0,1},{1,0},{2,3},{3,2},{4,5},{5,4},{6,7},{7,6},{8,9},{9,8},{10,11... | collective-permute-start | bytes 786440 | tf_op jit(solution)/shard_map/ppermute | solution.py:31
  10.7 24.9 %collective-permute-start.6 = (bf16[256,2048]{1,0:T(8,128)(2,1)S(1)}, bf16[256,2048]{1,0:T(8,128)(2,1)}, u32[]{:S(2)}, u32[]{:S(2)}) collective-permute-start(bf16[256,2048]{1,0:T(8,128)(2,1)S(1)} %copy-done.1), channel_id=1, source_target_pairs={{0,2},{2,0},{1,3},{3,1},{4,6},{6,4},{5,7},{7,5},{8,10},{10,8},{9,1... | collective-permute-start | bytes 3145736 | tf_op jit(solution)/shard_map/ppermute | solution.py:31
  12.1 14.2 %collective-permute-start.5 = (bf16[256,2048]{1,0:T(8,128)(2,1)S(1)}, bf16[256,2048]{1,0:T(8,128)(2,1)}, u32[]{:S(2)}, u32[]{:S(2)}) collective-permute-start(bf16[256,2048]{1,0:T(8,128)(2,1)S(1)} %copy-done.1), channel_id=1, source_target_pairs={{0,1},{1,0},{2,3},{3,2},{4,5},{5,4},{6,7},{7,6},{8,9},{9,8},{10,11... | collective-permute-start | bytes 3145736 | tf_op jit(solution)/shard_map/ppermute | solution.py:31
  14.9 9.7 %copy-start.7 = (bf16[256,512]{1,0:T(8,128)(2,1)S(1)}, bf16[256,512]{1,0:T(8,128)(2,1)}, u32[]{:S(2)}) copy-start(bf16[256,512]{1,0:T(8,128)(2,1)} %get-tuple-element.47) | copy-start | bytes 786436
  14.9 11.4 %copy-start.3 = (bf16[256,512]{1,0:T(8,128)(2,1)S(1)}, bf16[256,512]{1,0:T(8,128)(2,1)}, u32[]{:S(2)}) copy-start(bf16[256,512]{1,0:T(8,128)(2,1)} %get-tuple-element.46.c0) | copy-start | bytes 786436
  14.9 2.0 %collective-permute-start.3 = (bf16[16,16,1024]{2,1,0:T(8,128)(2,1)S(1)}, bf16[16,16,1024]{2,1,0:T(8,128)(2,1)S(1)}, u32[]{:S(2)}, u32[]{:S(2)}) collective-permute-start(bf16[16,16,1024]{2,1,0:T(8,128)(2,1)S(1)} %get-tuple-element.45), channel_id=1, source_target_pairs={{0,1},{1,0},{2,3},{3,2},{4,5},{5,4},{6,7},{7,6},{8,9},{9,8},{10,11... | collective-permute-start | bytes 1572872 | tf_op jit(solution)/shard_map/ppermute | solution.py:31
  17.8 17.6 %all-to-all-start = ((bf16[16,16,1024]{2,1,0:T(8,128)(2,1)}), bf16[16,16,1024]{2,1,0:T(8,128)(2,1)S(1)}, u32[]{:S(2)}, u32[]{:S(2)}) async-start(bf16[16,16,1024]{2,1,0:T(8,128)(2,1)} %add.12), calls=%async_computation | async-start | bytes 1048576 | tf_op jit(solution)/shard_map/all_to_all | solution.py:359
  24.5 1.8 %collective-permute-start.4 = (bf16[256,512]{1,0:T(8,128)(2,1)S(1)}, bf16[256,512]{1,0:T(8,128)(2,1)S(1)}, u32[]{:S(2)}, u32[]{:S(2)}) collective-permute-start(bf16[256,512]{1,0:T(8,128)(2,1)S(1)} %copy-done.7), channel_id=1, source_target_pairs={{0,1},{1,0},{2,3},{3,2},{4,5},{5,4},{6,7},{7,6},{8,9},{9,8},{10,11... | collective-permute-start | bytes 786440 | tf_op jit(solution)/shard_map/ppermute | solution.py:31
  35.6 26.6 %collective-permute-start.11 = (bf16[256,2048]{1,0:T(8,128)(2,1)}, bf16[256,2048]{1,0:T(8,128)(2,1)}, u32[]{:S(2)}, u32[]{:S(2)}) collective-permute-start(bf16[256,2048]{1,0:T(8,128)(2,1)} %collective-permute-done.6.h2.g2), channel_id=1, source_target_pairs={{0,1},{1,0},{2,3},{3,2},{4,5},{5,4},{6,7},{7,6},{8,9},{9,8},{10,11... | collective-permute-start | bytes 3145736 | tf_op jit(solution)/shard_map/ppermute | solution.py:31
  37.2 3.7 %collective-permute-start.7 = (f32[16,1024]{1,0:T(8,128)S(1)}, f32[16,1024]{1,0:T(8,128)S(1)}, u32[]{:S(2)}, u32[]{:S(2)}) collective-permute-start(f32[16,1024]{1,0:T(8,128)S(1)} %sum.2), channel_id=1, source_target_pairs={{0,2},{2,0},{1,3},{3,1},{4,6},{6,4},{5,7},{7,5},{8,10},{10,8},{9,1... | collective-permute-start | bytes 196616 | tf_op jit(solution)/shard_map/ppermute | solution.py:31
  40.8 8.6 %collective-permute-start.10 = (f32[16,1024]{1,0:T(8,128)S(1)}, f32[16,1024]{1,0:T(8,128)S(1)}, u32[]{:S(2)}, u32[]{:S(2)}) collective-permute-start(f32[16,1024]{1,0:T(8,128)S(1)} %add.8.part), channel_id=1, source_target_pairs={{0,192},{64,0},{128,64},{192,128},{1,193},{65,1},{129,65},{193,129... | collective-permute-start | bytes 196616 | tf_op jit(solution)/shard_map/ppermute | solution.py:368
  46.2 7.2 %collective-permute-start.9 = (f32[16,1024]{1,0:T(8,128)S(1)}, f32[16,1024]{1,0:T(8,128)S(1)}, u32[]{:S(2)}, u32[]{:S(2)}) collective-permute-start(f32[16,1024]{1,0:T(8,128)S(1)} %add.8.part), channel_id=1, source_target_pairs={{0,128},{64,192},{128,0},{192,64},{1,129},{65,193},{129,1},{193,65... | collective-permute-start | bytes 196616 | tf_op jit(solution)/shard_map/ppermute | solution.py:368
  47.2 6.5 %collective-permute-start.8 = (f32[16,1024]{1,0:T(8,128)S(1)}, f32[16,1024]{1,0:T(8,128)S(1)}, u32[]{:S(2)}, u32[]{:S(2)}) collective-permute-start(f32[16,1024]{1,0:T(8,128)S(1)} %add.8.part), channel_id=1, source_target_pairs={{0,64},{64,128},{128,192},{192,0},{1,65},{65,129},{129,193},{193,1... | collective-permute-start | bytes 196616 | tf_op jit(solution)/shard_map/ppermute | solution.py:368
  53.7 17.4 %collective-permute-start.12 = (bf16[2,256,512]{2,1,0:T(8,128)(2,1)}, bf16[2,256,512]{2,1,0:T(8,128)(2,1)S(1)}, u32[]{:S(2)}, u32[]{:S(2)}) collective-permute-start(bf16[2,256,512]{2,1,0:T(8,128)(2,1)} %get-tuple-element.56), channel_id=1, source_target_pairs={{0,2},{2,0},{1,3},{3,1},{4,6},{6,4},{5,7},{7,5},{8,10},{10,8},{9,1... | collective-permute-start | bytes 1572872 | tf_op jit(solution)/shard_map/ppermute | solution.py:31
  55.4 15.6 %all-to-all-start.1 = ((bf16[16,16,1024]{2,1,0:T(8,128)(2,1)}), bf16[16,16,1024]{2,1,0:T(8,128)(2,1)S(1)}, u32[]{:S(2)}, u32[]{:S(2)}) async-start(bf16[16,16,1024]{2,1,0:T(8,128)(2,1)} %spread.2), calls=%async_computation.1 | async-start | bytes 1048576 | tf_op jit(solution)/shard_map/all_to_all | solution.py:380
  62.1 13.3 %copy-start.2 = (bf16[256,2048]{1,0:T(8,128)(2,1)S(1)}, bf16[256,2048]{1,0:T(8,128)(2,1)}, u32[]{:S(2)}) copy-start(bf16[256,2048]{1,0:T(8,128)(2,1)} %og.5) | copy-start | bytes 3145732
  71.1 8.3 %collective-permute-start.13 = (bf16[16,16,1024]{2,1,0:T(8,128)(2,1)S(1)}, bf16[16,16,1024]{2,1,0:T(8,128)(2,1)S(1)}, u32[]{:S(2)}, u32[]{:S(2)}) collective-permute-start(bf16[16,16,1024]{2,1,0:T(8,128)(2,1)S(1)} %all-to-all-done.1.chunks), channel_id=1, source_target_pairs={{0,1},{1,0},{2,3},{3,2},{4,5},{5,4},{6,7},{7,6},{8,9},{9,8},{10,11... | collective-permute-start | bytes 1572872 | tf_op jit(solution)/shard_map/ppermute | solution.py:31
  79.4 4.1 %copy-start.6 = (bf16[2,256,512]{2,1,0:T(8,128)(2,1)S(1)}, bf16[2,256,512]{2,1,0:T(8,128)(2,1)}, u32[]{:S(2)}) copy-start(bf16[2,256,512]{2,1,0:T(8,128)(2,1)} %get-tuple-element.64) | copy-start | bytes 1572868
  83.4 2.0 %collective-permute-start.14 = (bf16[16,16,1024]{2,1,0:T(8,128)(2,1)S(1)}, bf16[16,16,1024]{2,1,0:T(8,128)(2,1)S(1)}, u32[]{:S(2)}, u32[]{:S(2)}) collective-permute-start(bf16[16,16,1024]{2,1,0:T(8,128)(2,1)S(1)} %get-tuple-element.59), channel_id=1, source_target_pairs={{0,1},{1,0},{2,3},{3,2},{4,5},{5,4},{6,7},{7,6},{8,9},{9,8},{10,11... | collective-permute-start | bytes 1572872 | tf_op jit(solution)/shard_map/ppermute | solution.py:31
  83.5 17.5 %collective-permute-start.15 = (bf16[2,256,512]{2,1,0:T(8,128)(2,1)S(1)}, bf16[2,256,512]{2,1,0:T(8,128)(2,1)}, u32[]{:S(2)}, u32[]{:S(2)}) collective-permute-start(bf16[2,256,512]{2,1,0:T(8,128)(2,1)S(1)} %copy-done.6), channel_id=1, source_target_pairs={{0,2},{2,0},{1,3},{3,1},{4,6},{6,4},{5,7},{7,5},{8,10},{10,8},{9,1... | collective-permute-start | bytes 1572872 | tf_op jit(solution)/shard_map/ppermute | solution.py:31
  86.2 14.7 %all-to-all-start.2 = ((bf16[16,16,1024]{2,1,0:T(8,128)(2,1)}), bf16[16,16,1024]{2,1,0:T(8,128)(2,1)S(1)}, u32[]{:S(2)}, u32[]{:S(2)}) async-start(bf16[16,16,1024]{2,1,0:T(8,128)(2,1)} %add.13), calls=%async_computation.2 | async-start | bytes 1048576 | tf_op jit(solution)/shard_map/all_to_all | solution.py:359
  89.8 11.2 %collective-permute-start.16 = (bf16[256,512]{1,0:T(8,128)(2,1)}, bf16[256,512]{1,0:T(8,128)(2,1)S(1)}, u32[]{:S(2)}, u32[]{:S(2)}) collective-permute-start(bf16[256,512]{1,0:T(8,128)(2,1)} %get-tuple-element.65), channel_id=1, source_target_pairs={{0,1},{1,0},{2,3},{3,2},{4,5},{5,4},{6,7},{7,6},{8,9},{9,8},{10,11... | collective-permute-start | bytes 786440 | tf_op jit(solution)/shard_map/ppermute | solution.py:31
  101.0 29.9 %copy-start.5 = (bf16[256,512]{1,0:T(8,128)(2,1)}, bf16[256,512]{1,0:T(8,128)(2,1)S(1)}, u32[]{:S(2)}) copy-start(bf16[256,512]{1,0:T(8,128)(2,1)S(1)} %collective-permute-done.16.i1) | copy-start | bytes 786436
  101.0 3.2 %collective-permute-start.17 = (f32[16,1024]{1,0:T(8,128)S(1)}, f32[16,1024]{1,0:T(8,128)S(1)}, u32[]{:S(2)}, u32[]{:S(2)}) collective-permute-start(f32[16,1024]{1,0:T(8,128)S(1)} %sum.3), channel_id=1, source_target_pairs={{0,2},{2,0},{1,3},{3,1},{4,6},{6,4},{5,7},{7,5},{8,10},{10,8},{9,1... | collective-permute-start | bytes 196616 | tf_op jit(solution)/shard_map/ppermute | solution.py:31
  104.2 7.4 %collective-permute-start.20 = (f32[16,1024]{1,0:T(8,128)S(1)}, f32[16,1024]{1,0:T(8,128)S(1)}, u32[]{:S(2)}, u32[]{:S(2)}) collective-permute-start(f32[16,1024]{1,0:T(8,128)S(1)} %add.9.part), channel_id=1, source_target_pairs={{0,192},{64,0},{128,64},{192,128},{1,193},{65,1},{129,65},{193,129... | collective-permute-start | bytes 196616 | tf_op jit(solution)/shard_map/ppermute | solution.py:368
  108.0 7.1 %collective-permute-start.19 = (f32[16,1024]{1,0:T(8,128)S(1)}, f32[16,1024]{1,0:T(8,128)S(1)}, u32[]{:S(2)}, u32[]{:S(2)}) collective-permute-start(f32[16,1024]{1,0:T(8,128)S(1)} %add.9.part), channel_id=1, source_target_pairs={{0,128},{64,192},{128,0},{192,64},{1,129},{65,193},{129,1},{193,65... | collective-permute-start | bytes 196616 | tf_op jit(solution)/shard_map/ppermute | solution.py:368
  109.5 6.3 %collective-permute-start.18 = (f32[16,1024]{1,0:T(8,128)S(1)}, f32[16,1024]{1,0:T(8,128)S(1)}, u32[]{:S(2)}, u32[]{:S(2)}) collective-permute-start(f32[16,1024]{1,0:T(8,128)S(1)} %add.9.part), channel_id=1, source_target_pairs={{0,64},{64,128},{128,192},{192,0},{1,65},{65,129},{129,193},{193,1... | collective-permute-start | bytes 196616 | tf_op jit(solution)/shard_map/ppermute | solution.py:368
  115.8 22.1 %collective-permute-start.21 = (bf16[2,256,512]{2,1,0:T(8,128)(2,1)S(1)}, bf16[2,256,512]{2,1,0:T(8,128)(2,1)}, u32[]{:S(2)}, u32[]{:S(2)}) collective-permute-start(bf16[2,256,512]{2,1,0:T(8,128)(2,1)S(1)} %collective-permute-done.12.c2), channel_id=1, source_target_pairs={{0,1},{1,0},{2,3},{3,2},{4,5},{5,4},{6,7},{7,6},{8,9},{9,8},{10,11... | collective-permute-start | bytes 1572872 | tf_op jit(solution)/shard_map/ppermute | solution.py:31
  119.6 18.4 %collective-permute-start.22 = (bf16[2,256,512]{2,1,0:T(8,128)(2,1)}, bf16[2,256,512]{2,1,0:T(8,128)(2,1)}, u32[]{:S(2)}, u32[]{:S(2)}) collective-permute-start(bf16[2,256,512]{2,1,0:T(8,128)(2,1)} %collective-permute-done.15.i2), channel_id=1, source_target_pairs={{0,1},{1,0},{2,3},{3,2},{4,5},{5,4},{6,7},{7,6},{8,9},{9,8},{10,11... | collective-permute-start | bytes 1572872 | tf_op jit(solution)/shard_map/ppermute | solution.py:31
  123.4 14.5 %all-to-all-start.3 = ((bf16[16,16,1024]{2,1,0:T(8,128)(2,1)}), bf16[16,16,1024]{2,1,0:T(8,128)(2,1)S(1)}, u32[]{:S(2)}, u32[]{:S(2)}) async-start(bf16[16,16,1024]{2,1,0:T(8,128)(2,1)} %spread.3), calls=%async_computation.3 | async-start | bytes 1048576 | tf_op jit(solution)/shard_map/all_to_all | solution.py:380
  137.9 3.7 %collective-permute-start.23 = (bf16[16,16,1024]{2,1,0:T(8,128)(2,1)S(1)}, bf16[16,16,1024]{2,1,0:T(8,128)(2,1)S(1)}, u32[]{:S(2)}, u32[]{:S(2)}) collective-permute-start(bf16[16,16,1024]{2,1,0:T(8,128)(2,1)S(1)} %all-to-all-done.3.chunks), channel_id=1, source_target_pairs={{0,1},{1,0},{2,3},{3,2},{4,5},{5,4},{6,7},{7,6},{8,9},{9,8},{10,11... | collective-permute-start | bytes 1572872 | tf_op jit(solution)/shard_map/ppermute | solution.py:31

commit v4 on v3

--- a/solution.py
+++ b/solution.py
@@ -99,21 +99,29 @@
         half[row : row + CHUNK_ROWS, col : col + CHUNK_COLS] = chunks[n]
 
 
-def right_kernel(scale, at, ctx, og, chunks, low_hbm, out, half_hbm, low, half, total, sems):
+def early_kernel(ctx, mine, half, proj):
+    unchunk(mine, half)
+    proj[...] = mm(half[...], ctx[...], 1, 1)
+
+
+def right_kernel(
+    scale, at, ctx, og, low_hbm, mine, proj_mine, other, keep, send, left, total, low, proj, sems
+):
+    zl, core = at[0], at[1]
     copy = pltpu.make_async_copy(low_hbm, low, sems.at[0])
     copy.start()
-    unchunk(chunks, half)
-    back = pltpu.make_async_copy(half, half_hbm, sems.at[1])
-    back.start()
-    first, second = two(mm(half[...], ctx[...], 1, 1) * scale)
+    here = pl.ds(pl.multiple_of(core * HALF, HALF), HALF)
+    there = pl.ds(pl.multiple_of((1 - core) * HALF, HALF), HALF)
+    unchunk(other, left.at[there, :])
+    left[here, :] = mine[...]
+    proj[here, :] = proj_mine[...]
+    proj[there, :] = mm(left[there, :], ctx[...], 1, 1)
+    first, second = two(proj[...] * scale)
     total[...] = mm(first, og[...], 1, 0) + mm(second, og[...], 1, 0)
-    own = half[:, block(at[0], at[1])]
+    own = left[:, block(zl, core)]
     copy.wait()
     total[...] += mm(own, low[...], 1, 0)
-    for n in range(CHUNKS):
-        row, col = chunk_at(n)
-        out[n] = total[row : row + CHUNK_ROWS, col : col + CHUNK_COLS].astype(out.dtype)
-    back.wait()
+    split_halves(core, total, keep, send)
 
 
 def add_kernel(keep, got, out):
@@ -125,7 +133,8 @@
 
 
 def spread_kernel(part, one, opposite, three, out):
-    whole = ((part[...] + opposite[...]) + (one[...] + three[...])).astype(BF16)
+    part, one, opposite, three = (x[...].astype(F32) for x in (part, one, opposite, three))
+    whole = ((part + opposite) + (one + three)).astype(BF16)
     for n in range(CHUNKS):
         out[n] = whole
 
@@ -183,12 +192,7 @@
         a[stop:, :] = a[stop:, :] - dot_hi(panel[:, stop:RANK], panel, 0, 0)
 
 
-def gram_kernel(at, mine_hbm, other_hbm, a, left, sems):
-    core = at[1]
-    mine = left.at[pl.ds(pl.multiple_of(core * HALF, HALF), HALF), :]
-    other = left.at[pl.ds(pl.multiple_of((1 - core) * HALF, HALF), HALF), :]
-    for copy in fetch((mine_hbm, other_hbm), (mine, other), sems):
-        copy.wait()
+def gram_kernel(left, a):
     a[:, :RANK] = mm(left[...], left[...], 1, 1)
     a[:, RANK:] = eye(RANK)
     eliminate(0, a)
@@ -227,6 +231,13 @@
     out[...] = err[...] + total * scale
 
 
+def place_kernel(at, own, near, far, diag, out, sems):
+    zl, core = at[0], at[1]
+    where = (block(zl, core), block(zl, 1 - core), block(1 - zl, core), block(1 - zl, 1 - core))
+    for copy in fetch((own, near, far.at[0], diag.at[1]), [out.at[:, cols] for cols in where], sems):
+        copy.wait()
+
+
 def columns_of(inverse, half):
     return inverse[:, pl.ds(pl.multiple_of(half * HALF, HALF), HALF)]
 
@@ -240,8 +251,8 @@
 
 
 def last_kernel(
-    share, scale, at, other, inverse, basis, begun, t2, t3, merged, g2, g3, i0, i1, i2, i3,
-    new_error, factor_q, in_grad, half,
+    share, scale, at, other, inverse, basis, begun, t2, t3, merged, g2, g3,
+    new_error, factor_q, half,
 ):
     step = pl.program_id(0)
     zl, core = at[0], at[1]
@@ -256,24 +267,10 @@
     q = (begun[:, cols] + q) * share
     total = mm(t2[...], g2[...], 1, 0) + mm(t3[...], g3[...], 1, 0)
     new_error[...] = merged[...] + total * scale - mm(basis[...], q.astype(BF16), 1, 0)
-    at_zl, at_core = step // 2, step % 2
-
-    @pl.when((at_zl == zl) & (at_core == core))
+
+    @pl.when(step == zl * 2 + core)
     def _():
         factor_q[...] = q.T
-        in_grad[...] = i0[...]
-
-    @pl.when((at_zl == zl) & (at_core != core))
-    def _():
-        in_grad[...] = i1[...]
-
-    @pl.when((at_zl != zl) & (at_core == core))
-    def _():
-        in_grad[...] = i2[...]
-
-    @pl.when((at_zl != zl) & (at_core != core))
-    def _():
-        in_grad[...] = i3[...]
 
 
 def size(shape, dtype):
@@ -285,7 +282,7 @@
 
 
 def call(
-    kernel, outs, args, flops, name, scratch=(), alias=None, limit=20, loose=(), held=(), free=False, sems=0
+    kernel, outs, args, flops, name, scratch=(), alias=None, limit=12, loose=(), held=(), free=False, sems=0
 ):
     args = [in_hbm(a) if n in held else a for n, a in enumerate(args)]
     moved = sum(size(a.shape, a.dtype) for a in args) + sum(size(s, d) for s, d in outs)
@@ -308,7 +305,7 @@
     )(*args)
 
 
-def call_grid(kernel, steps, outs, ins, args, flops, name, scratch=(), sems=0, limit=24, loose=(), alias=None):
+def call_grid(kernel, steps, outs, ins, args, flops, name, scratch=(), sems=0, limit=14, loose=(), alias=None):
     args = [
         a if spec in (SMEM, ANY, VMEM) or n in loose else in_hbm(a)
         for n, (a, spec) in enumerate(zip(args, ins))
@@ -363,7 +360,7 @@
 
 def across_z(part, beside=()):
     far = tied(swap(part, "zl"), *beside)
-    part = part + far
+    part = (part + far).astype(BF16)
     return (part,) + tuple(
         lax.ppermute(part, "zh", [(i, (i + step) % 4) for i in range(4)]) for step in (1, 2, 3)
     )
@@ -400,24 +397,24 @@
         + [pair + (pl.BlockSpec((2, TOK // 4, ROWS), lambda j: (0, j, 0)),)]
         + [((ROWS, FEAT), BF16, VMEM), ((ROWS, FEAT), BF16, strip)],
         [SMEM, rows_of(TOK // 4, FEAT), strip],
-        (at, context, error),
+        (tied(at, warm_near), context, error),
         4_000_000,
         "prepare",
     )
     warm_diag = swap(tied(warm_far, low), "core")
+    c_near = swap(c_near, "core")
 
     big = ((ROWS, FEAT), BF16)
     keep, send = call(
         functools.partial(left_kernel, scale),
         [(CHUNKED, F32), (CHUNKED, BF16)],
-        (at, out_grad, context, low, warm, warm_near, warm_far, warm_diag),
+        (at, out_grad, context, tied(low, c_near), warm, warm_near, warm_far, warm_diag),
         2_000_000_000,
         "left",
         [((RANK, FEAT), F32)],
     )
-    g_far = swap(tied(out_grad, warm_far, low), "zl")
+    g_far = swap(tied(out_grad, warm_near), "zl")
     g_near = swap(tied(out_grad, warm_far, low), "core")
-    c_near = swap(c_near, "core")
     turned = [((ROWS, TOK), BF16)] * 2
     (merged,) = call_grid(
         functools.partial(merge_kernel, scale),
@@ -451,46 +448,48 @@
     i_far = swap(i_far, "zl")
     i_near = swap(i_near, "core")
 
-    half = ((HALF, FEAT), BF16)
-
-    def right(chunks, dtype):
-        return call_grid(
-            functools.partial(right_kernel, scale),
-            1,
-            [(CHUNKED, dtype, VMEM), half + (ANY,)],
-            [SMEM, VMEM, VMEM, VMEM, ANY],
-            (at, context, out_grad, chunks, in_hbm(kept)),
-            1_000_000_000,
-            "right",
-            [big, half, ((HALF, FEAT), F32)],
-            sems=2,
-        )
-
-    keep, mine_half = right(mine, F32)
-    send, other_half = right(tied(other, keep), BF16)
+    mine_half, proj = call(
+        early_kernel,
+        [((HALF, FEAT), BF16), ((HALF, TOK), F32)],
+        (context, mine),
+        150_000_000,
+        "early",
+    )
+    other = tied(other, proj)
+    keep, send, left = call(
+        functools.partial(right_kernel, scale),
+        [(CHUNKED, F32), (CHUNKED, BF16), ((RANK, FEAT), BF16)],
+        (at, context, out_grad, kept, mine_half, proj, other),
+        2_000_000_000,
+        "right",
+        [((RANK, FEAT), F32), big, ((RANK, TOK), F32)],
+        held=(3,),
+        sems=1,
+    )
 
     table = ((RANK, 2 * RANK), F32)
-    a, left = call(
-        gram_kernel,
-        [table, ((RANK, FEAT), BF16)],
-        (at, mine_half, other_half),
-        300_000_000,
-        "gram",
-        held=(1, 2),
-        sems=2,
-    )
+    (a,) = call(gram_kernel, [table], (left,), 300_000_000, "gram")
     (a,) = call(
         functools.partial(step_kernel, PART), [table], (a,), 300_000_000, "step", alias={0: 0}
     )
     part = across_plane(keep, send, (a,))
     part = tied(part, i_far, i_near)
+    c_diag = swap(c_far, "core")
     zs = across_z(part)
+    i_diag = swap(tied(i_far, zs[0]), "core")
     (a,) = call(
         functools.partial(step_kernel, 2 * PART), [table], (a,), 300_000_000, "step", alias={0: 0}
     )
-    mine = back_over_plane(*zs, beside=(a,))
-    c_diag = swap(tied(c_far, *zs[1:]), "core")
-    i_diag = swap(tied(i_far, *zs[1:]), "core")
+    mine = back_over_plane(*zs, beside=(a, c_diag, i_diag))
+    in_grad = pl.pallas_call(
+        place_kernel,
+        out_shape=pltpu.HBM((TOK, FEAT), BF16),
+        in_specs=[SMEM] + [ANY] * 4,
+        out_specs=ANY,
+        scratch_shapes=[pltpu.SemaphoreType.DMA((4,))],
+        cost_estimate=pl.CostEstimate(flops=0, bytes_accessed=2**21, transcendentals=0),
+        name="place",
+    )(at, *(in_hbm(x) for x in (i_own, i_near, i_far, i_diag)))
     inverse, basis = call(
         basis_kernel,
         [((RANK, RANK), F32), ((ROWS, RANK), BF16)],
@@ -499,10 +498,7 @@
         "basis",
         [table],
     )
-    block_in = whole(TOK, ROWS)
-    first = pl.BlockSpec((None, TOK, ROWS), lambda j: (0, 0, 0))
-    second = pl.BlockSpec((None, TOK, ROWS), lambda j: (1, 0, 0))
-    other = swap(tied(mine, basis, c_diag, i_diag), "core")
+    other = swap(tied(mine, basis, in_grad), "core")
     begun, t2, t3 = call(
         begin_kernel,
         [((RANK, FEAT), F32)] + turned,
@@ -513,20 +509,16 @@
     )
     other = tied(other, begun)
 
-    new_error, factor_q, in_grad = call_grid(
+    new_error, factor_q = call_grid(
         functools.partial(last_kernel, 1.0 / (SIZES[0] * SIZES[1] * SIZES[2]), scale),
         4,
         [
             ((ROWS, FEAT), F32, column(ROWS)),
             ((ROWS, RANK), F32, whole(ROWS, RANK)),
-            ((TOK, FEAT), BF16, column(TOK)),
         ],
-        [SMEM] + [VMEM] * 6 + [column(ROWS), column(TOK), column(TOK)]
-        + [block_in, block_in, first, second],
-        (
-            at, other, inverse, basis, begun, t2, t3, merged, g_far, g_diag,
-            i_own, i_near, i_far, i_diag,
-        ),
+        [SMEM, VMEM, VMEM, whole(ROWS, RANK), VMEM, VMEM, VMEM]
+        + [column(ROWS), column(TOK), column(TOK)],
+        (at, other, inverse, basis, begun, t2, t3, merged, g_far, g_diag),
         2_000_000_000,
         "last",
         [((HALF, FEAT), BF16)],

time: 150 us -> 167 us (1.11)
  Pallas kernels: 55.8 us -> 83.6 us
  starting transfers between devices: 60 us -> 52.7 us
  waiting for transfers between devices: 32.3 us -> 27.5 us
    pallas_call x0 -> x1, Pallas kernels: none -> 33.7 us  [on_device(): pl.pallas_call(place_kernel, out_shape=pltpu.HBM((TOK, FEAT), BF16), in_s...]
    pallas_call x5 -> x3, Pallas kernels: 26.2 us -> 17.7 us  [call_grid(): pl.pallas_call(kernel, grid=(steps,), out_shape=[(jax.ShapeDtypeStruct if...]
    all_to_all x2, waiting for transfers between devices: 9.5 us -> 2.65 us  [back_over_plane(): return lax.all_to_all(whole, ('y', 'x'), 0, 0)]
    ppermute x6, waiting for transfers between devices: 8.44 us -> 3.43 us  [across_z(): lax.ppermute(part, 'zh', [(i, (i + step) % 4) for i in range(4)])]
    ppermute x18, starting transfers between devices: 23.1 us -> 19 us  [swap(): return lax.ppermute(x, axis, [(0, 1), (1, 0)])]
    ppermute x18, waiting for transfers between devices: 9.25 us -> 13.1 us  [swap(): return lax.ppermute(x, axis, [(0, 1), (1, 0)])]
    all_to_all x2, waiting for transfers between devices: 5.13 us -> 8.31 us  [across_plane(): parts = tied(lax.all_to_all(half, ('y', 'x'), 0, 0), *beside)]
    pallas_call x13 -> x15, Pallas kernels: 29.6 us -> 32.2 us  [call(): pl.pallas_call(kernel, out_shape=[(pltpu.HBM if free else jax.ShapeDtypeS...]
  transfers between devices with their start and end apart: 28 -> 28, of which waited for: 14 -> 14; matrix products, arithmetic and copies ran while one was open for 0% -> 0% of each run, Pallas kernels for 30% -> 43%
where the time goes in v4:
time: 167 us; the launch traced here: 166 us
  Pallas kernels  83.6 us (50%)
  starting transfers between devices  52.7 us (32%)
  waiting for transfers between devices  27.5 us (16%)
    pallas_call x1, Pallas kernels, on_device(): pl.pallas_call(place_kernel, out_shape=pltpu.HBM((TOK, FEAT), BF16), in_s...  33.7 us
    pallas_call x15, Pallas kernels, call(): pl.pallas_call(kernel, out_shape=[(pltpu.HBM if free else jax.ShapeDtypeS...  32.2 us
    ppermute x18, starting transfers between devices, swap(): return lax.ppermute(x, axis, [(0, 1), (1, 0)])  19 us
    pallas_call x3, Pallas kernels, call_grid(): pl.pallas_call(kernel, grid=(steps,), out_shape=[(jax.ShapeDtypeStruct if...  17.7 us
    ppermute x6, starting transfers between devices, across_z(): lax.ppermute(part, 'zh', [(i, (i + step) % 4) for i in range(4)])  14 us
    ppermute x18, waiting for transfers between devices, swap(): return lax.ppermute(x, axis, [(0, 1), (1, 0)])  13.1 us
    all_to_all x2, starting transfers between devices, back_over_plane(): return lax.all_to_all(whole, ('y', 'x'), 0, 0)  10.2 us
    all_to_all x2, starting transfers between devices, across_plane(): parts = tied(lax.all_to_all(half, ('y', 'x'), 0, 0), *beside)  9.49 us
  transfers between devices with their start and end apart: 28, of which 14 were waited for; matrix products, arithmetic and copies ran while one was open for 0% of the time, Pallas kernels for 43%

profile of v4, /device:TPU:1, one launch (start us, length us, event | category | flops | bytes accessed | tf_op | source)
XLA Modules:
  0.0 166.2 jit_solution(4285348970579327137)
XLA Ops:
  0.6 3.3 %collective-permute-start.1 = (bf16[512,256]{1,0:T(8,128)(2,1)}, bf16[512,256]{1,0:T(8,128)(2,1)S(1)}, u32[]{:S(2)}, u32[]{:S(2)}) collective-permute-start(bf16[512,256]{1,0:T(8,128)(2,1)} %w0.1), channel_id=1, source_target_pairs={{0,1},{1,0},{2,3},{3,2},{4,5},{5,4},{6,7},{7,6},{8,9},{9,8},{10,11... | collective-permute-start | bytes 786440 | tf_op jit(solution)/shard_map/ppermute | solution.py:31
  4.0 0.1 pad_add_fusion.at
  4.0 1.3 collective-permute-done.1.w1
  5.3 4.9 %prepare.1 = (bf16[256,512]{1,0:T(8,128)(2,1)}, bf16[256,512]{1,0:T(8,128)(2,1)}, bf16[2,256,512]{2,1,0:T(8,128)(2,1)}, bf16[512,2048]{1,0:T(8,128)(2,1)S(1)}, bf16[512,2048]{1,0:T(8,128)(2,1)}) custom-call(s32[2]{0:T(128)S(1)} %pad_add_fusion.at, bf16[256,2048]{1,0:T(8,128)(2,1)} %ctx.7, f32[512,2048]{1,0:T(8,128)} %bitcast.4), custom_call_target="tpu_custom_call" | custom-call | flops 4000000 | bytes 10485768 | tf_op jit(solution)/shard_map/prepare/pallas_call | solution.py:317
  10.2 0.4 collective-permute-start.4
  10.6 1.5 collective-permute-done.w2
  12.0 0.9 collective-permute-start.5
  12.9 0.3 collective-permute-start.2
  13.2 0.9 collective-permute-done.5.w3
  14.1 2.4 %left.1 = (f32[16,16,1024]{2,1,0:T(8,128)S(1)}, bf16[16,16,1024]{2,1,0:T(8,128)(2,1)S(1)}) custom-call(s32[2]{0:T(128)S(1)} %pad_add_fusion.at, bf16[256,2048]{1,0:T(8,128)(2,1)S(1)} %copy-done.1, bf16[256,2048]{1,0:T(8,128)(2,1)S(1)} %copy-done, bf16[512,2048]{1,0:T(8,128)(2,1)S(1)} %get-tuple-element.47.low, bf16[512,256]{1,0:T(8,128)(2,1)S(1)} %copy-done.9, ...), custom_call_target="tpu_custom_call" | custom-call | flops 2000000000 | bytes 6815752 | tf_op jit(solution)/shard_map/left/pallas_call | solution.py:292
  16.5 0.5 collective-permute-start.6
  17.0 1.5 collective-permute-done.6.got
  18.5 0.9 add.14
  19.4 5.8 %all-to-all-start = ((bf16[16,16,1024]{2,1,0:T(8,128)(2,1)}), bf16[16,16,1024]{2,1,0:T(8,128)(2,1)S(1)}, u32[]{:S(2)}, u32[]{:S(2)}) async-start(bf16[16,16,1024]{2,1,0:T(8,128)(2,1)} %add.14), calls=%async_computation | async-start | bytes 1048576 | tf_op jit(solution)/shard_map/all_to_all | solution.py:356
  25.2 5.9 %merge.1.merged = f32[512,2048]{1,0:T(8,128)} custom-call(f32[512,2048]{1,0:T(8,128)} %bitcast.5, bf16[256,512]{1,0:T(8,128)(2,1)S(1)} %copy-done.5, bf16[256,512]{1,0:T(8,128)(2,1)S(1)} %collective-permute-done.4.c1, bf16[256,2048]{1,0:T(8,128)(2,1)S(1)} %copy-done.1, bf16[256,2048]{1,0:T(8,128)(2,1)} %collective-permute-done.2.g1.h1), custom_call_target="tpu_custom_call" | custom-call | flops 1100000000 | bytes 11010048 | tf_op jit(solution)/shard_map/merge/pallas_call | solution.py:317
  31.1 4.9 %all-to-all-done.parts = bf16[16,16,1024]{2,1,0:T(8,128)(2,1)S(1)} async-done(((bf16[16,16,1024]{2,1,0:T(8,128)(2,1)}), bf16[16,16,1024]{2,1,0:T(8,128)(2,1)S(1)}, u32[]{:S(2)}, u32[]{:S(2)}) %all-to-all-start) | async-done | bytes 524320 | tf_op jit(solution)/shard_map/all_to_all | solution.py:356
  36.0 0.1 sum.2
  36.1 1.7 %collective-permute-done.3.h2.g2 = bf16[256,2048]{1,0:T(8,128)(2,1)} collective-permute-done((bf16[256,2048]{1,0:T(8,128)(2,1)S(1)}, bf16[256,2048]{1,0:T(8,128)(2,1)}, u32[]{:S(2)}, u32[]{:S(2)}) %collective-permute-start.3) | collective-permute-done | bytes 1048608 | tf_op jit(solution)/shard_map/ppermute | solution.py:31
  37.8 0.8 collective-permute-start.7
  38.6 0.2 collective-permute-start.10
  38.7 3.6 %collective-permute-done.10 = f32[16,1024]{1,0:T(8,128)S(1)} collective-permute-done((f32[16,1024]{1,0:T(8,128)S(1)}, f32[16,1024]{1,0:T(8,128)S(1)}, u32[]{:S(2)}, u32[]{:S(2)}) %collective-permute-start.10) | collective-permute-done | bytes 65568 | tf_op jit(solution)/shard_map/ppermute | solution.py:31
  42.3 4.5 %collective-permute-start.13 = (bf16[16,1024]{1,0:T(8,128)(2,1)S(1)}, bf16[16,1024]{1,0:T(8,128)(2,1)S(1)}, u32[]{:S(2)}, u32[]{:S(2)}) collective-permute-start(bf16[16,1024]{1,0:T(8,128)(2,1)S(1)} %add_convert_fusion.1.part), channel_id=1, source_target_pairs={{0,192},{64,0},{128,64},{192,128},{1,193},{65,1},{129,65},{193,129... | collective-permute-start | bytes 98312 | tf_op jit(solution)/shard_map/ppermute | solution.py:365
  46.9 1.0 collective-permute-start.12
  47.9 2.2 %collective-permute-start.11 = (bf16[16,1024]{1,0:T(8,128)(2,1)S(1)}, bf16[16,1024]{1,0:T(8,128)(2,1)S(1)}, u32[]{:S(2)}, u32[]{:S(2)}) collective-permute-start(bf16[16,1024]{1,0:T(8,128)(2,1)S(1)} %add_convert_fusion.1.part), channel_id=1, source_target_pairs={{0,64},{64,128},{128,192},{192,0},{1,65},{65,129},{129,193},{193,1... | collective-permute-start | bytes 98312 | tf_op jit(solution)/shard_map/ppermute | solution.py:365
  50.1 3.4 %collective-permute-done.12.opposite = bf16[16,1024]{1,0:T(8,128)(2,1)S(1)} collective-permute-done((bf16[16,1024]{1,0:T(8,128)(2,1)S(1)}, bf16[16,1024]{1,0:T(8,128)(2,1)S(1)}, u32[]{:S(2)}, u32[]{:S(2)}) %collective-permute-start.12) | collective-permute-done | bytes 32800 | tf_op jit(solution)/shard_map/ppermute | solution.py:365
  53.5 0.7 collective-permute-start.14
  54.3 0.9 spread.2
  55.2 6.6 %all-to-all-start.1 = ((bf16[16,16,1024]{2,1,0:T(8,128)(2,1)}), bf16[16,16,1024]{2,1,0:T(8,128)(2,1)S(1)}, u32[]{:S(2)}, u32[]{:S(2)}) async-start(bf16[16,16,1024]{2,1,0:T(8,128)(2,1)} %spread.2), calls=%async_computation.1 | async-start | bytes 1048576 | tf_op jit(solution)/shard_map/all_to_all | solution.py:377
  61.8 0.0 copy-start.2
  61.8 6.4 %grad.1 = (bf16[256,512]{1,0:T(8,128)(2,1)}, bf16[256,512]{1,0:T(8,128)(2,1)}, bf16[2,256,512]{2,1,0:T(8,128)(2,1)}) custom-call(bf16[256,2048]{1,0:T(8,128)(2,1)} %og.3, bf16[256,2048]{1,0:T(8,128)(2,1)} %collective-permute-done.2.g1.h1, bf16[256,2048]{1,0:T(8,128)(2,1)} %collective-permute-done.3.h2.g2, bf16[256,2048]{1,0:T(8,128)(2,1)} %collective-permute-done.7.h3.g3, ...), custom_call_target="tpu_custom_call" | custom-call | flops 2200000000 | bytes 7340032 | tf_op jit(solution)/shard_map/grad/pallas_call | solution.py:292
  68.2 2.7 %all-to-all-done.1.mine = bf16[16,16,1024]{2,1,0:T(8,128)(2,1)S(1)} async-done(((bf16[16,16,1024]{2,1,0:T(8,128)(2,1)}), bf16[16,16,1024]{2,1,0:T(8,128)(2,1)S(1)}, u32[]{:S(2)}, u32[]{:S(2)}) %all-to-all-start.1) | async-done | bytes 524320 | tf_op jit(solution)/shard_map/all_to_all | solution.py:377
  70.8 3.9 %collective-permute-start.15 = (bf16[16,16,1024]{2,1,0:T(8,128)(2,1)S(1)}, bf16[16,16,1024]{2,1,0:T(8,128)(2,1)S(1)}, u32[]{:S(2)}, u32[]{:S(2)}) collective-permute-start(bf16[16,16,1024]{2,1,0:T(8,128)(2,1)S(1)} %all-to-all-done.1.mine), channel_id=1, source_target_pairs={{0,1},{1,0},{2,3},{3,2},{4,5},{5,4},{6,7},{7,6},{8,9},{9,8},{10,11... | collective-permute-start | bytes 1572872 | tf_op jit(solution)/shard_map/ppermute | solution.py:31
  74.7 0.5 early.1
  75.2 1.0 collective-permute-done.15.other
  76.2 4.4 %right.1 = (f32[16,16,1024]{2,1,0:T(8,128)S(1)}, bf16[16,16,1024]{2,1,0:T(8,128)(2,1)S(1)}, bf16[256,2048]{1,0:T(8,128)(2,1)S(1)}) custom-call(s32[2]{0:T(128)S(1)} %pad_add_fusion.at, bf16[256,2048]{1,0:T(8,128)(2,1)S(1)} %copy-done, bf16[256,2048]{1,0:T(8,128)(2,1)S(1)} %copy-done.2, bf16[512,2048]{1,0:T(8,128)(2,1)} %get-tuple-element.57.low_hbm, ...), custom_call_target="tpu_custom_call" | custom-call | flops 2000000000 | bytes 7995400 | tf_op jit(solution)/shard_map/right/pallas_call | solution.py:292
  80.7 0.5 collective-permute-start.16
  81.1 0.8 collective-permute-start.9
  81.9 0.8 collective-permute-done.16.got
  82.7 0.9 add.15
  83.5 3.7 %all-to-all-start.2 = ((bf16[16,16,1024]{2,1,0:T(8,128)(2,1)}), bf16[16,16,1024]{2,1,0:T(8,128)(2,1)S(1)}, u32[]{:S(2)}, u32[]{:S(2)}) async-start(bf16[16,16,1024]{2,1,0:T(8,128)(2,1)} %add.15), calls=%async_computation.2 | async-start | bytes 1048576 | tf_op jit(solution)/shard_map/all_to_all | solution.py:356
  87.3 0.5 collective-permute-start.8
  87.7 4.0 %gram.1.a_in = f32[256,512]{1,0:T(8,128)S(1)} custom-call(bf16[256,2048]{1,0:T(8,128)(2,1)S(1)} %get-tuple-element.67.left), custom_call_target="tpu_custom_call" | custom-call | flops 300000000 | bytes 1572864 | tf_op jit(solution)/shard_map/gram/pallas_call | solution.py:292
  91.7 3.1 %step.2.a_in = f32[256,512]{1,0:T(8,128)S(1)} custom-call(f32[256,512]{1,0:T(8,128)S(1)} %gram.1.a_in), custom_call_target="tpu_custom_call", output_to_operand_aliasing={{}: (0, {})} | custom-call | flops 300000000 | bytes 1048576 | tf_op jit(solution)/shard_map/step/pallas_call | solution.py:292
  94.8 3.4 %all-to-all-done.2.parts = bf16[16,16,1024]{2,1,0:T(8,128)(2,1)S(1)} async-done(((bf16[16,16,1024]{2,1,0:T(8,128)(2,1)}), bf16[16,16,1024]{2,1,0:T(8,128)(2,1)S(1)}, u32[]{:S(2)}, u32[]{:S(2)}) %all-to-all-start.2) | async-done | bytes 524320 | tf_op jit(solution)/shard_map/all_to_all | solution.py:356
  98.1 0.1 sum.3
  98.3 0.0 copy-start.10
  98.3 0.9 collective-permute-start.17
  99.1 1.8 %collective-permute-start.19 = (bf16[2,256,512]{2,1,0:T(8,128)(2,1)S(1)}, bf16[2,256,512]{2,1,0:T(8,128)(2,1)S(1)}, u32[]{:S(2)}, u32[]{:S(2)}) collective-permute-start(bf16[2,256,512]{2,1,0:T(8,128)(2,1)S(1)} %copy-done.4), channel_id=1, source_target_pairs={{0,1},{1,0},{2,3},{3,2},{4,5},{5,4},{6,7},{7,6},{8,9},{9,8},{10,11... | collective-permute-start | bytes 1572872 | tf_op jit(solution)/shard_map/ppermute | solution.py:31
  101.0 0.5 collective-permute-done.17
  101.5 2.8 %collective-permute-start.18 = (bf16[2,256,512]{2,1,0:T(8,128)(2,1)S(1)}, bf16[2,256,512]{2,1,0:T(8,128)(2,1)S(1)}, u32[]{:S(2)}, u32[]{:S(2)}) collective-permute-start(bf16[2,256,512]{2,1,0:T(8,128)(2,1)S(1)} %collective-permute-done.9.far), channel_id=1, source_target_pairs={{0,1},{1,0},{2,3},{3,2},{4,5},{5,4},{6,7},{7,6},{8,9},{9,8},{10,11... | collective-permute-start | bytes 1572872 | tf_op jit(solution)/shard_map/ppermute | solution.py:31
  104.3 1.2 collective-permute-start.22
  105.5 2.6 %collective-permute-start.21 = (bf16[16,1024]{1,0:T(8,128)(2,1)S(1)}, bf16[16,1024]{1,0:T(8,128)(2,1)S(1)}, u32[]{:S(2)}, u32[]{:S(2)}) collective-permute-start(bf16[16,1024]{1,0:T(8,128)(2,1)S(1)} %add_convert_fusion.part), channel_id=1, source_target_pairs={{0,128},{64,192},{128,0},{192,64},{1,129},{65,193},{129,1},{193,65... | collective-permute-start | bytes 98312 | tf_op jit(solution)/shard_map/ppermute | solution.py:365
  108.1 2.4 %collective-permute-start.20 = (bf16[16,1024]{1,0:T(8,128)(2,1)S(1)}, bf16[16,1024]{1,0:T(8,128)(2,1)S(1)}, u32[]{:S(2)}, u32[]{:S(2)}) collective-permute-start(bf16[16,1024]{1,0:T(8,128)(2,1)S(1)} %add_convert_fusion.part), channel_id=1, source_target_pairs={{0,64},{64,128},{128,192},{192,0},{1,65},{65,129},{129,193},{193,1... | collective-permute-start | bytes 98312 | tf_op jit(solution)/shard_map/ppermute | solution.py:365
  110.5 3.0 %step.3.a_in = f32[256,512]{1,0:T(8,128)S(1)} custom-call(f32[256,512]{1,0:T(8,128)S(1)} %step.2.a_in), custom_call_target="tpu_custom_call", output_to_operand_aliasing={{}: (0, {})} | custom-call | flops 300000000 | bytes 1048576 | tf_op jit(solution)/shard_map/step/pallas_call | solution.py:292
  113.5 0.8 copy-done.11
  114.3 0.9 spread.3
  115.2 3.6 %all-to-all-start.3 = ((bf16[16,16,1024]{2,1,0:T(8,128)(2,1)}), bf16[16,16,1024]{2,1,0:T(8,128)(2,1)S(1)}, u32[]{:S(2)}, u32[]{:S(2)}) async-start(bf16[16,16,1024]{2,1,0:T(8,128)(2,1)} %spread.3), calls=%async_computation.3 | async-start | bytes 1048576 | tf_op jit(solution)/shard_map/all_to_all | solution.py:377
  118.8 3.6 %basis.1 = (f32[256,256]{1,0:T(8,128)S(1)}, bf16[512,256]{1,0:T(8,128)(2,1)S(1)}) custom-call(s32[2]{0:T(128)S(1)} %pad_add_fusion.at, f32[256,512]{1,0:T(8,128)S(1)} %step.3.a_in, bf16[256,2048]{1,0:T(8,128)(2,1)S(1)} %get-tuple-element.67.left), custom_call_target="tpu_custom_call" | custom-call | flops 300000000 | bytes 2097160 | tf_op jit(solution)/shard_map/basis/pallas_call | solution.py:292
  122.4 0.7 copy-done.6
  123.1 33.7 %place.1 = bf16[256,2048]{1,0:T(8,128)(2,1)} custom-call(s32[2]{0:T(128)} %copy-done.7, bf16[256,512]{1,0:T(8,128)(2,1)} %get-tuple-element.54.own, bf16[256,512]{1,0:T(8,128)(2,1)} %copy-done.12, bf16[2,256,512]{2,1,0:T(8,128)(2,1)} %copy-done.10, bf16[2,256,512]{2,1,0:T(8,128)(2,1)} %copy-done.11), custom_call_target="tpu_custom_call" | custom-call | bytes 2097152 | tf_op jit(solution)/shard_map/place/pallas_call | solution.py:484
  156.8 1.0 collective-permute-start.23
  157.8 1.2 begin.1
  159.0 0.3 collective-permute-done.23.other
  159.3 6.9 %last.1 = (f32[512,2048]{1,0:T(8,128)}, f32[512,256]{1,0:T(8,128)}) custom-call(s32[2]{0:T(128)S(1)} %copy-done.8, bf16[16,16,1024]{2,1,0:T(8,128)(2,1)S(1)} %collective-permute-done.23.other, f32[256,256]{1,0:T(8,128)S(1)} %get-tuple-element.74.inverse, bf16[512,256]{1,0:T(8,128)(2,1)} %copy-done.6, f32[256,2048]{1,0:T(8,128)S(1)} %get-tuple-element.75.begun, ...), custom_call_target="tpu_custom_call" | custom-call | flops 2000000000 | bytes 14680072 | tf_op jit(solution)/shard_map/last/pallas_call | solution.py:317
  (40 shorter events, 0.1 us)
Async XLA Ops:
  0.6 4.7 %collective-permute-start.1 = (bf16[512,256]{1,0:T(8,128)(2,1)}, bf16[512,256]{1,0:T(8,128)(2,1)S(1)}, u32[]{:S(2)}, u32[]{:S(2)}) collective-permute-start(bf16[512,256]{1,0:T(8,128)(2,1)} %w0.1), channel_id=1, source_target_pairs={{0,1},{1,0},{2,3},{3,2},{4,5},{5,4},{6,7},{7,6},{8,9},{9,8},{10,11... | collective-permute-start | bytes 786440 | tf_op jit(solution)/shard_map/ppermute | solution.py:31
  4.0 8.1 %collective-permute-start = (bf16[512,256]{1,0:T(8,128)(2,1)}, bf16[512,256]{1,0:T(8,128)(2,1)S(1)}, u32[]{:S(2)}, u32[]{:S(2)}) collective-permute-start(bf16[512,256]{1,0:T(8,128)(2,1)} %w0.1), channel_id=1, source_target_pairs={{0,2},{2,0},{1,3},{3,1},{4,6},{6,4},{5,7},{7,5},{8,10},{10,8},{9,1... | collective-permute-start | bytes 786440 | tf_op jit(solution)/shard_map/ppermute | solution.py:31
  4.0 114.7 %copy-start.7 = (s32[2]{0:T(128)}, s32[2]{0:T(128)S(1)}, u32[]{:S(2)}) copy-start(s32[2]{0:T(128)S(1)} %pad_add_fusion.at) | copy-start | bytes 28
  5.3 7.6 %copy-start.1 = (bf16[256,2048]{1,0:T(8,128)(2,1)S(1)}, bf16[256,2048]{1,0:T(8,128)(2,1)}, u32[]{:S(2)}) copy-start(bf16[256,2048]{1,0:T(8,128)(2,1)} %og.3) | copy-start | bytes 3145732
  5.3 8.7 %copy-start = (bf16[256,2048]{1,0:T(8,128)(2,1)S(1)}, bf16[256,2048]{1,0:T(8,128)(2,1)}, u32[]{:S(2)}) copy-start(bf16[256,2048]{1,0:T(8,128)(2,1)} %ctx.7) | copy-start | bytes 3145732
  5.3 8.7 %copy-start.9 = (bf16[512,256]{1,0:T(8,128)(2,1)S(1)}, bf16[512,256]{1,0:T(8,128)(2,1)}, u32[]{:S(2)}) copy-start(bf16[512,256]{1,0:T(8,128)(2,1)} %w0.1) | copy-start | bytes 786436
  10.2 3.0 %collective-permute-start.4 = (bf16[256,512]{1,0:T(8,128)(2,1)}, bf16[256,512]{1,0:T(8,128)(2,1)S(1)}, u32[]{:S(2)}, u32[]{:S(2)}) collective-permute-start(bf16[256,512]{1,0:T(8,128)(2,1)} %get-tuple-element.46), channel_id=1, source_target_pairs={{0,1},{1,0},{2,3},{3,2},{4,5},{5,4},{6,7},{7,6},{8,9},{9,8},{10,11... | collective-permute-start | bytes 786440 | tf_op jit(solution)/shard_map/ppermute | solution.py:31
  12.0 2.0 %collective-permute-start.5 = (bf16[512,256]{1,0:T(8,128)(2,1)S(1)}, bf16[512,256]{1,0:T(8,128)(2,1)S(1)}, u32[]{:S(2)}, u32[]{:S(2)}) collective-permute-start(bf16[512,256]{1,0:T(8,128)(2,1)S(1)} %collective-permute-done.w2), channel_id=1, source_target_pairs={{0,1},{1,0},{2,3},{3,2},{4,5},{5,4},{6,7},{7,6},{8,9},{9,8},{10,11... | collective-permute-start | bytes 786440 | tf_op jit(solution)/shard_map/ppermute | solution.py:31
  12.9 24.9 %collective-permute-start.3 = (bf16[256,2048]{1,0:T(8,128)(2,1)S(1)}, bf16[256,2048]{1,0:T(8,128)(2,1)}, u32[]{:S(2)}, u32[]{:S(2)}) collective-permute-start(bf16[256,2048]{1,0:T(8,128)(2,1)S(1)} %copy-done.1), channel_id=1, source_target_pairs={{0,2},{2,0},{1,3},{3,1},{4,6},{6,4},{5,7},{7,5},{8,10},{10,8},{9,1... | collective-permute-start | bytes 3145736 | tf_op jit(solution)/shard_map/ppermute | solution.py:31
  12.9 12.3 %collective-permute-start.2 = (bf16[256,2048]{1,0:T(8,128)(2,1)S(1)}, bf16[256,2048]{1,0:T(8,128)(2,1)}, u32[]{:S(2)}, u32[]{:S(2)}) collective-permute-start(bf16[256,2048]{1,0:T(8,128)(2,1)S(1)} %copy-done.1), channel_id=1, source_target_pairs={{0,1},{1,0},{2,3},{3,2},{4,5},{5,4},{6,7},{7,6},{8,9},{9,8},{10,11... | collective-permute-start | bytes 3145736 | tf_op jit(solution)/shard_map/ppermute | solution.py:31
  16.5 8.7 %copy-start.5 = (bf16[256,512]{1,0:T(8,128)(2,1)S(1)}, bf16[256,512]{1,0:T(8,128)(2,1)}, u32[]{:S(2)}) copy-start(bf16[256,512]{1,0:T(8,128)(2,1)} %get-tuple-element.51.c0) | copy-start | bytes 786436
  16.5 2.0 %collective-permute-start.6 = (bf16[16,16,1024]{2,1,0:T(8,128)(2,1)S(1)}, bf16[16,16,1024]{2,1,0:T(8,128)(2,1)S(1)}, u32[]{:S(2)}, u32[]{:S(2)}) collective-permute-start(bf16[16,16,1024]{2,1,0:T(8,128)(2,1)S(1)} %get-tuple-element.50), channel_id=1, source_target_pairs={{0,1},{1,0},{2,3},{3,2},{4,5},{5,4},{6,7},{7,6},{8,9},{9,8},{10,11... | collective-permute-start | bytes 1572872 | tf_op jit(solution)/shard_map/ppermute | solution.py:31
  19.4 16.6 %all-to-all-start = ((bf16[16,16,1024]{2,1,0:T(8,128)(2,1)}), bf16[16,16,1024]{2,1,0:T(8,128)(2,1)S(1)}, u32[]{:S(2)}, u32[]{:S(2)}) async-start(bf16[16,16,1024]{2,1,0:T(8,128)(2,1)} %add.14), calls=%async_computation | async-start | bytes 1048576 | tf_op jit(solution)/shard_map/all_to_all | solution.py:356
  37.8 24.0 %collective-permute-start.7 = (bf16[256,2048]{1,0:T(8,128)(2,1)}, bf16[256,2048]{1,0:T(8,128)(2,1)}, u32[]{:S(2)}, u32[]{:S(2)}) collective-permute-start(bf16[256,2048]{1,0:T(8,128)(2,1)} %collective-permute-done.3.h2.g2), channel_id=1, source_target_pairs={{0,1},{1,0},{2,3},{3,2},{4,5},{5,4},{6,7},{7,6},{8,9},{9,8},{10,11... | collective-permute-start | bytes 3145736 | tf_op jit(solution)/shard_map/ppermute | solution.py:31
  38.6 3.7 %collective-permute-start.10 = (f32[16,1024]{1,0:T(8,128)S(1)}, f32[16,1024]{1,0:T(8,128)S(1)}, u32[]{:S(2)}, u32[]{:S(2)}) collective-permute-start(f32[16,1024]{1,0:T(8,128)S(1)} %sum.2), channel_id=1, source_target_pairs={{0,2},{2,0},{1,3},{3,1},{4,6},{6,4},{5,7},{7,5},{8,10},{10,8},{9,1... | collective-permute-start | bytes 196616 | tf_op jit(solution)/shard_map/ppermute | solution.py:31
  42.3 7.8 %collective-permute-start.13 = (bf16[16,1024]{1,0:T(8,128)(2,1)S(1)}, bf16[16,1024]{1,0:T(8,128)(2,1)S(1)}, u32[]{:S(2)}, u32[]{:S(2)}) collective-permute-start(bf16[16,1024]{1,0:T(8,128)(2,1)S(1)} %add_convert_fusion.1.part), channel_id=1, source_target_pairs={{0,192},{64,0},{128,64},{192,128},{1,193},{65,1},{129,65},{193,129... | collective-permute-start | bytes 98312 | tf_op jit(solution)/shard_map/ppermute | solution.py:365
  46.9 6.7 %collective-permute-start.12 = (bf16[16,1024]{1,0:T(8,128)(2,1)S(1)}, bf16[16,1024]{1,0:T(8,128)(2,1)S(1)}, u32[]{:S(2)}, u32[]{:S(2)}) collective-permute-start(bf16[16,1024]{1,0:T(8,128)(2,1)S(1)} %add_convert_fusion.1.part), channel_id=1, source_target_pairs={{0,128},{64,192},{128,0},{192,64},{1,129},{65,193},{129,1},{193,65... | collective-permute-start | bytes 98312 | tf_op jit(solution)/shard_map/ppermute | solution.py:365
  47.9 5.7 %collective-permute-start.11 = (bf16[16,1024]{1,0:T(8,128)(2,1)S(1)}, bf16[16,1024]{1,0:T(8,128)(2,1)S(1)}, u32[]{:S(2)}, u32[]{:S(2)}) collective-permute-start(bf16[16,1024]{1,0:T(8,128)(2,1)S(1)} %add_convert_fusion.1.part), channel_id=1, source_target_pairs={{0,64},{64,128},{128,192},{192,0},{1,65},{65,129},{129,193},{193,1... | collective-permute-start | bytes 98312 | tf_op jit(solution)/shard_map/ppermute | solution.py:365
  53.5 17.3 %collective-permute-start.14 = (bf16[2,256,512]{2,1,0:T(8,128)(2,1)}, bf16[2,256,512]{2,1,0:T(8,128)(2,1)S(1)}, u32[]{:S(2)}, u32[]{:S(2)}) collective-permute-start(bf16[2,256,512]{2,1,0:T(8,128)(2,1)} %get-tuple-element.62), channel_id=1, source_target_pairs={{0,2},{2,0},{1,3},{3,1},{4,6},{6,4},{5,7},{7,5},{8,10},{10,8},{9,1... | collective-permute-start | bytes 1572872 | tf_op jit(solution)/shard_map/ppermute | solution.py:31
  55.2 15.7 %all-to-all-start.1 = ((bf16[16,16,1024]{2,1,0:T(8,128)(2,1)}), bf16[16,16,1024]{2,1,0:T(8,128)(2,1)S(1)}, u32[]{:S(2)}, u32[]{:S(2)}) async-start(bf16[16,16,1024]{2,1,0:T(8,128)(2,1)} %spread.2), calls=%async_computation.1 | async-start | bytes 1048576 | tf_op jit(solution)/shard_map/all_to_all | solution.py:377
  61.8 14.5 %copy-start.2 = (bf16[256,2048]{1,0:T(8,128)(2,1)S(1)}, bf16[256,2048]{1,0:T(8,128)(2,1)}, u32[]{:S(2)}) copy-start(bf16[256,2048]{1,0:T(8,128)(2,1)} %og.3) | copy-start | bytes 3145732
  70.8 5.4 %copy-start.3 = (bf16[2,256,512]{2,1,0:T(8,128)(2,1)}, bf16[2,256,512]{2,1,0:T(8,128)(2,1)S(1)}, u32[]{:S(2)}) copy-start(bf16[2,256,512]{2,1,0:T(8,128)(2,1)S(1)} %collective-permute-done.14.c2) | copy-start | bytes 1572868
  70.8 5.4 %collective-permute-start.15 = (bf16[16,16,1024]{2,1,0:T(8,128)(2,1)S(1)}, bf16[16,16,1024]{2,1,0:T(8,128)(2,1)S(1)}, u32[]{:S(2)}, u32[]{:S(2)}) collective-permute-start(bf16[16,16,1024]{2,1,0:T(8,128)(2,1)S(1)} %all-to-all-done.1.mine), channel_id=1, source_target_pairs={{0,1},{1,0},{2,3},{3,2},{4,5},{5,4},{6,7},{7,6},{8,9},{9,8},{10,11... | collective-permute-start | bytes 1572872 | tf_op jit(solution)/shard_map/ppermute | solution.py:31
  80.7 2.0 %collective-permute-start.16 = (bf16[16,16,1024]{2,1,0:T(8,128)(2,1)S(1)}, bf16[16,16,1024]{2,1,0:T(8,128)(2,1)S(1)}, u32[]{:S(2)}, u32[]{:S(2)}) collective-permute-start(bf16[16,16,1024]{2,1,0:T(8,128)(2,1)S(1)} %get-tuple-element.66), channel_id=1, source_target_pairs={{0,1},{1,0},{2,3},{3,2},{4,5},{5,4},{6,7},{7,6},{8,9},{9,8},{10,11... | collective-permute-start | bytes 1572872 | tf_op jit(solution)/shard_map/ppermute | solution.py:31
  81.1 17.1 %collective-permute-start.9 = (bf16[2,256,512]{2,1,0:T(8,128)(2,1)}, bf16[2,256,512]{2,1,0:T(8,128)(2,1)S(1)}, u32[]{:S(2)}, u32[]{:S(2)}) collective-permute-start(bf16[2,256,512]{2,1,0:T(8,128)(2,1)} %get-tuple-element.56), channel_id=1, source_target_pairs={{0,2},{2,0},{1,3},{3,1},{4,6},{6,4},{5,7},{7,5},{8,10},{10,8},{9,1... | collective-permute-start | bytes 1572872 | tf_op jit(solution)/shard_map/ppermute | solution.py:31
  83.5 15.6 %copy-start.4 = (bf16[2,256,512]{2,1,0:T(8,128)(2,1)S(1)}, bf16[2,256,512]{2,1,0:T(8,128)(2,1)}, u32[]{:S(2)}) copy-start(bf16[2,256,512]{2,1,0:T(8,128)(2,1)} %copy-done.3) | copy-start | bytes 1572868
  83.5 14.6 %all-to-all-start.2 = ((bf16[16,16,1024]{2,1,0:T(8,128)(2,1)}), bf16[16,16,1024]{2,1,0:T(8,128)(2,1)S(1)}, u32[]{:S(2)}, u32[]{:S(2)}) async-start(bf16[16,16,1024]{2,1,0:T(8,128)(2,1)} %add.15), calls=%async_computation.2 | async-start | bytes 1048576 | tf_op jit(solution)/shard_map/all_to_all | solution.py:356
  87.3 11.0 %collective-permute-start.8 = (bf16[256,512]{1,0:T(8,128)(2,1)}, bf16[256,512]{1,0:T(8,128)(2,1)S(1)}, u32[]{:S(2)}, u32[]{:S(2)}) collective-permute-start(bf16[256,512]{1,0:T(8,128)(2,1)} %get-tuple-element.55), channel_id=1, source_target_pairs={{0,1},{1,0},{2,3},{3,2},{4,5},{5,4},{6,7},{7,6},{8,9},{9,8},{10,11... | collective-permute-start | bytes 786440 | tf_op jit(solution)/shard_map/ppermute | solution.py:31
  98.2 16.9 %copy-start.12 = (bf16[256,512]{1,0:T(8,128)(2,1)}, bf16[256,512]{1,0:T(8,128)(2,1)S(1)}, u32[]{:S(2)}) copy-start(bf16[256,512]{1,0:T(8,128)(2,1)S(1)} %collective-permute-done.8.near) | copy-start | bytes 786436
  98.3 16.9 %copy-start.10 = (bf16[2,256,512]{2,1,0:T(8,128)(2,1)}, bf16[2,256,512]{2,1,0:T(8,128)(2,1)S(1)}, u32[]{:S(2)}) copy-start(bf16[2,256,512]{2,1,0:T(8,128)(2,1)S(1)} %collective-permute-done.9.far) | copy-start | bytes 1572868
  98.3 3.2 %collective-permute-start.17 = (f32[16,1024]{1,0:T(8,128)S(1)}, f32[16,1024]{1,0:T(8,128)S(1)}, u32[]{:S(2)}, u32[]{:S(2)}) collective-permute-start(f32[16,1024]{1,0:T(8,128)S(1)} %sum.3), channel_id=1, source_target_pairs={{0,2},{2,0},{1,3},{3,1},{4,6},{6,4},{5,7},{7,5},{8,10},{10,8},{9,1... | collective-permute-start | bytes 196616 | tf_op jit(solution)/shard_map/ppermute | solution.py:31
  99.1 14.4 %collective-permute-start.19 = (bf16[2,256,512]{2,1,0:T(8,128)(2,1)S(1)}, bf16[2,256,512]{2,1,0:T(8,128)(2,1)S(1)}, u32[]{:S(2)}, u32[]{:S(2)}) collective-permute-start(bf16[2,256,512]{2,1,0:T(8,128)(2,1)S(1)} %copy-done.4), channel_id=1, source_target_pairs={{0,1},{1,0},{2,3},{3,2},{4,5},{5,4},{6,7},{7,6},{8,9},{9,8},{10,11... | collective-permute-start | bytes 1572872 | tf_op jit(solution)/shard_map/ppermute | solution.py:31
  101.5 12.0 %collective-permute-start.18 = (bf16[2,256,512]{2,1,0:T(8,128)(2,1)S(1)}, bf16[2,256,512]{2,1,0:T(8,128)(2,1)S(1)}, u32[]{:S(2)}, u32[]{:S(2)}) collective-permute-start(bf16[2,256,512]{2,1,0:T(8,128)(2,1)S(1)} %collective-permute-done.9.far), channel_id=1, source_target_pairs={{0,1},{1,0},{2,3},{3,2},{4,5},{5,4},{6,7},{7,6},{8,9},{9,8},{10,11... | collective-permute-start | bytes 1572872 | tf_op jit(solution)/shard_map/ppermute | solution.py:31
  104.3 9.3 %collective-permute-start.22 = (bf16[16,1024]{1,0:T(8,128)(2,1)S(1)}, bf16[16,1024]{1,0:T(8,128)(2,1)S(1)}, u32[]{:S(2)}, u32[]{:S(2)}) collective-permute-start(bf16[16,1024]{1,0:T(8,128)(2,1)S(1)} %add_convert_fusion.part), channel_id=1, source_target_pairs={{0,192},{64,0},{128,64},{192,128},{1,193},{65,1},{129,65},{193,129... | collective-permute-start | bytes 98312 | tf_op jit(solution)/shard_map/ppermute | solution.py:365
  105.5 8.1 %collective-permute-start.21 = (bf16[16,1024]{1,0:T(8,128)(2,1)S(1)}, bf16[16,1024]{1,0:T(8,128)(2,1)S(1)}, u32[]{:S(2)}, u32[]{:S(2)}) collective-permute-start(bf16[16,1024]{1,0:T(8,128)(2,1)S(1)} %add_convert_fusion.part), channel_id=1, source_target_pairs={{0,128},{64,192},{128,0},{192,64},{1,129},{65,193},{129,1},{193,65... | collective-permute-start | bytes 98312 | tf_op jit(solution)/shard_map/ppermute | solution.py:365
  108.1 6.2 %collective-permute-start.20 = (bf16[16,1024]{1,0:T(8,128)(2,1)S(1)}, bf16[16,1024]{1,0:T(8,128)(2,1)S(1)}, u32[]{:S(2)}, u32[]{:S(2)}) collective-permute-start(bf16[16,1024]{1,0:T(8,128)(2,1)S(1)} %add_convert_fusion.part), channel_id=1, source_target_pairs={{0,64},{64,128},{128,192},{192,0},{1,65},{65,129},{129,193},{193,1... | collective-permute-start | bytes 98312 | tf_op jit(solution)/shard_map/ppermute | solution.py:365
  113.5 0.8 copy-start.11
  115.2 41.6 %all-to-all-start.3 = ((bf16[16,16,1024]{2,1,0:T(8,128)(2,1)}), bf16[16,16,1024]{2,1,0:T(8,128)(2,1)S(1)}, u32[]{:S(2)}, u32[]{:S(2)}) async-start(bf16[16,16,1024]{2,1,0:T(8,128)(2,1)} %spread.3), calls=%async_computation.3 | async-start | bytes 1048576 | tf_op jit(solution)/shard_map/all_to_all | solution.py:377
  122.4 0.7 copy-start.6
  123.1 34.7 %copy-start.8 = (s32[2]{0:T(128)S(1)}, s32[2]{0:T(128)}, u32[]{:S(2)}) copy-start(s32[2]{0:T(128)} %copy-done.7) | copy-start | bytes 28
  156.8 2.5 %collective-permute-start.23 = (bf16[16,16,1024]{2,1,0:T(8,128)(2,1)S(1)}, bf16[16,16,1024]{2,1,0:T(8,128)(2,1)S(1)}, u32[]{:S(2)}, u32[]{:S(2)}) collective-permute-start(bf16[16,16,1024]{2,1,0:T(8,128)(2,1)S(1)} %all-to-all-done.3.chunks), channel_id=1, source_target_pairs={{0,1},{1,0},{2,3},{3,2},{4,5},{5,4},{6,7},{7,6},{8,9},{9,8},{10,11... | collective-permute-start | bytes 1572872 | tf_op jit(solution)/shard_map/ppermute | solution.py:31

commit v5 on v4

--- a/solution.py
+++ b/solution.py
@@ -231,11 +231,19 @@
     out[...] = err[...] + total * scale
 
 
-def place_kernel(at, own, near, far, diag, out, sems):
-    zl, core = at[0], at[1]
-    where = (block(zl, core), block(zl, 1 - core), block(1 - zl, core), block(1 - zl, 1 - core))
-    for copy in fetch((own, near, far.at[0], diag.at[1]), [out.at[:, cols] for cols in where], sems):
-        copy.wait()
+def place_kernel(at, own, near, far, diag, out):
+    step = pl.program_id(0)
+    same_zl, same_core = step // 2 == at[0], step % 2 == at[1]
+    for piece, here in (
+        (own, same_zl & same_core),
+        (near, same_zl & jnp.logical_not(same_core)),
+        (far, jnp.logical_not(same_zl) & same_core),
+        (diag, jnp.logical_not(same_zl) & jnp.logical_not(same_core)),
+    ):
+
+        @pl.when(here)
+        def _(piece=piece):
+            out[...] = piece[...]
 
 
 def columns_of(inverse, half):
@@ -444,7 +452,7 @@
         free=True,
         sems=5,
     )
-    other = swap(tied(mine, i_own, c_far), "core")
+    other = swap(tied(mine, i_own), "core")
     i_far = swap(i_far, "zl")
     i_near = swap(i_near, "core")
 
@@ -455,7 +463,7 @@
         150_000_000,
         "early",
     )
-    other = tied(other, proj)
+    other = tied(other, proj, c_far)
     keep, send, left = call(
         functools.partial(right_kernel, scale),
         [(CHUNKED, F32), (CHUNKED, BF16), ((RANK, FEAT), BF16)],
@@ -476,20 +484,23 @@
     part = tied(part, i_far, i_near)
     c_diag = swap(c_far, "core")
     zs = across_z(part)
-    i_diag = swap(tied(i_far, zs[0]), "core")
+    i_diag = swap(i_far, "core")
     (a,) = call(
         functools.partial(step_kernel, 2 * PART), [table], (a,), 300_000_000, "step", alias={0: 0}
     )
     mine = back_over_plane(*zs, beside=(a, c_diag, i_diag))
-    in_grad = pl.pallas_call(
+    block_in = whole(TOK, ROWS)
+    first = pl.BlockSpec((None, TOK, ROWS), lambda j: (0, 0, 0))
+    second = pl.BlockSpec((None, TOK, ROWS), lambda j: (1, 0, 0))
+    (in_grad,) = call_grid(
         place_kernel,
-        out_shape=pltpu.HBM((TOK, FEAT), BF16),
-        in_specs=[SMEM] + [ANY] * 4,
-        out_specs=ANY,
-        scratch_shapes=[pltpu.SemaphoreType.DMA((4,))],
-        cost_estimate=pl.CostEstimate(flops=0, bytes_accessed=2**21, transcendentals=0),
-        name="place",
-    )(at, *(in_hbm(x) for x in (i_own, i_near, i_far, i_diag)))
+        4,
+        [((TOK, FEAT), BF16, column(TOK))],
+        [SMEM, block_in, block_in, first, second],
+        (at, i_own, i_near, i_far, i_diag),
+        1_000_000,
+        "place",
+    )
     inverse, basis = call(
         basis_kernel,
         [((RANK, RANK), F32), ((ROWS, RANK), BF16)],

time: 167 us -> 146 us (0.87)
  Pallas kernels: 83.6 us -> 52.7 us
  waiting for transfers between devices: 27.5 us -> 33 us
  starting transfers between devices: 52.7 us -> 57.6 us
    pallas_call x1 -> x0, Pallas kernels: 33.7 us -> none  [on_device(): pl.pallas_call(place_kernel, out_shape=pltpu.HBM((TOK, FEAT), BF16), in_s...]
    ppermute x18, waiting for transfers between devices: 13.1 us -> 19.4 us  [swap(): return lax.ppermute(x, axis, [(0, 1), (1, 0)])]
    all_to_all x2, waiting for transfers between devices: 8.31 us -> 4.93 us  [across_plane(): parts = tied(lax.all_to_all(half, ('y', 'x'), 0, 0), *beside)]
    all_to_all x2, starting transfers between devices: 10.2 us -> 13.2 us  [back_over_plane(): return lax.all_to_all(whole, ('y', 'x'), 0, 0)]
    all_to_all x2, starting transfers between devices: 9.49 us -> 12.4 us  [across_plane(): parts = tied(lax.all_to_all(half, ('y', 'x'), 0, 0), *beside)]
    pallas_call x3 -> x4, Pallas kernels: 17.7 us -> 20.5 us  [call_grid(): pl.pallas_call(kernel, grid=(steps,), out_shape=[(jax.ShapeDtypeStruct if...]
    all_to_all x2, waiting for transfers between devices: 2.65 us -> 4.7 us  [back_over_plane(): return lax.all_to_all(whole, ('y', 'x'), 0, 0)]
  transfers between devices with their start and end apart: 28 -> 28, of which waited for: 14 -> 16; matrix products, arithmetic and copies ran while one was open for 0% -> 0% of each run, Pallas kernels for 43% -> 28%
where the time goes in v5:
time: 146 us; the launch traced here: 145 us
  starting transfers between devices  57.6 us (39%)
  Pallas kernels  52.7 us (36%)
  waiting for transfers between devices  33 us (23%)
    pallas_call x15, Pallas kernels, call(): pl.pallas_call(kernel, out_shape=[(pltpu.HBM if free else jax.ShapeDtypeS...  32.2 us
    pallas_call x4, Pallas kernels, call_grid(): pl.pallas_call(kernel, grid=(steps,), out_shape=[(jax.ShapeDtypeStruct if...  20.5 us
    ppermute x18, waiting for transfers between devices, swap(): return lax.ppermute(x, axis, [(0, 1), (1, 0)])  19.4 us
    ppermute x18, starting transfers between devices, swap(): return lax.ppermute(x, axis, [(0, 1), (1, 0)])  18.1 us
    ppermute x6, starting transfers between devices, across_z(): lax.ppermute(part, 'zh', [(i, (i + step) % 4) for i in range(4)])  13.9 us
    all_to_all x2, starting transfers between devices, back_over_plane(): return lax.all_to_all(whole, ('y', 'x'), 0, 0)  13.2 us
    all_to_all x2, starting transfers between devices, across_plane(): parts = tied(lax.all_to_all(half, ('y', 'x'), 0, 0), *beside)  12.4 us
    all_to_all x2, waiting for transfers between devices, across_plane(): parts = tied(lax.all_to_all(half, ('y', 'x'), 0, 0), *beside)  4.93 us
  transfers between devices with their start and end apart: 28, of which 16 were waited for; matrix products, arithmetic and copies ran while one was open for 0% of the time, Pallas kernels for 28%

profile of v5, /device:TPU:1, one launch (start us, length us, event | category | flops | bytes accessed | tf_op | source)
XLA Modules:
  0.0 145.0 jit_solution(7734199959184979812)
XLA Ops:
  0.6 3.3 %collective-permute-start.1 = (bf16[512,256]{1,0:T(8,128)(2,1)}, bf16[512,256]{1,0:T(8,128)(2,1)S(1)}, u32[]{:S(2)}, u32[]{:S(2)}) collective-permute-start(bf16[512,256]{1,0:T(8,128)(2,1)} %w0.1), channel_id=1, source_target_pairs={{0,1},{1,0},{2,3},{3,2},{4,5},{5,4},{6,7},{7,6},{8,9},{9,8},{10,11... | collective-permute-start | bytes 786440 | tf_op jit(solution)/shard_map/ppermute | solution.py:31
  4.0 0.1 pad_add_fusion.at
  4.0 1.3 collective-permute-done.1.w1
  5.3 4.9 %prepare.1 = (bf16[256,512]{1,0:T(8,128)(2,1)}, bf16[256,512]{1,0:T(8,128)(2,1)}, bf16[2,256,512]{2,1,0:T(8,128)(2,1)}, bf16[512,2048]{1,0:T(8,128)(2,1)S(1)}, bf16[512,2048]{1,0:T(8,128)(2,1)}) custom-call(s32[2]{0:T(128)S(1)} %pad_add_fusion.at, bf16[256,2048]{1,0:T(8,128)(2,1)} %ctx.7, f32[512,2048]{1,0:T(8,128)} %bitcast.4), custom_call_target="tpu_custom_call" | custom-call | flops 4000000 | bytes 10485768 | tf_op jit(solution)/shard_map/prepare/pallas_call | solution.py:325
  10.2 0.4 collective-permute-start.4
  10.6 1.5 %collective-permute-done.w2 = bf16[512,256]{1,0:T(8,128)(2,1)S(1)} collective-permute-done((bf16[512,256]{1,0:T(8,128)(2,1)}, bf16[512,256]{1,0:T(8,128)(2,1)S(1)}, u32[]{:S(2)}, u32[]{:S(2)}) %collective-permute-start) | collective-permute-done | bytes 262176 | tf_op jit(solution)/shard_map/ppermute | solution.py:31
  12.0 0.9 collective-permute-start.5
  12.9 0.3 collective-permute-start.2
  13.2 0.9 collective-permute-done.5.w3
  14.1 2.4 %left.1 = (f32[16,16,1024]{2,1,0:T(8,128)S(1)}, bf16[16,16,1024]{2,1,0:T(8,128)(2,1)S(1)}) custom-call(s32[2]{0:T(128)S(1)} %pad_add_fusion.at, bf16[256,2048]{1,0:T(8,128)(2,1)S(1)} %copy-done.1, bf16[256,2048]{1,0:T(8,128)(2,1)S(1)} %copy-done, bf16[512,2048]{1,0:T(8,128)(2,1)S(1)} %get-tuple-element.46.low, bf16[512,256]{1,0:T(8,128)(2,1)S(1)} %copy-done.7, ...), custom_call_target="tpu_custom_call" | custom-call | flops 2000000000 | bytes 6815752 | tf_op jit(solution)/shard_map/left/pallas_call | solution.py:300
  16.5 0.5 collective-permute-start.6
  17.0 1.5 %collective-permute-done.6.got = bf16[16,16,1024]{2,1,0:T(8,128)(2,1)S(1)} collective-permute-done((bf16[16,16,1024]{2,1,0:T(8,128)(2,1)S(1)}, bf16[16,16,1024]{2,1,0:T(8,128)(2,1)S(1)}, u32[]{:S(2)}, u32[]{:S(2)}) %collective-permute-start.6) | collective-permute-done | bytes 524320 | tf_op jit(solution)/shard_map/ppermute | solution.py:31
  18.5 0.9 add.14
  19.4 5.8 %all-to-all-start = ((bf16[16,16,1024]{2,1,0:T(8,128)(2,1)}), bf16[16,16,1024]{2,1,0:T(8,128)(2,1)S(1)}, u32[]{:S(2)}, u32[]{:S(2)}) async-start(bf16[16,16,1024]{2,1,0:T(8,128)(2,1)} %add.14), calls=%async_computation | async-start | bytes 1048576 | tf_op jit(solution)/shard_map/all_to_all | solution.py:364
  25.2 5.9 %merge.1.merged = f32[512,2048]{1,0:T(8,128)} custom-call(f32[512,2048]{1,0:T(8,128)} %bitcast.5, bf16[256,512]{1,0:T(8,128)(2,1)S(1)} %copy-done.5, bf16[256,512]{1,0:T(8,128)(2,1)S(1)} %collective-permute-done.4.c1, bf16[256,2048]{1,0:T(8,128)(2,1)S(1)} %copy-done.1, bf16[256,2048]{1,0:T(8,128)(2,1)} %collective-permute-done.2.g1.h1), custom_call_target="tpu_custom_call" | custom-call | flops 1100000000 | bytes 11010048 | tf_op jit(solution)/shard_map/merge/pallas_call | solution.py:325
  31.1 4.9 %all-to-all-done.parts = bf16[16,16,1024]{2,1,0:T(8,128)(2,1)S(1)} async-done(((bf16[16,16,1024]{2,1,0:T(8,128)(2,1)}), bf16[16,16,1024]{2,1,0:T(8,128)(2,1)S(1)}, u32[]{:S(2)}, u32[]{:S(2)}) %all-to-all-start) | async-done | bytes 524320 | tf_op jit(solution)/shard_map/all_to_all | solution.py:364
  36.0 0.1 sum.2
  36.1 1.7 %collective-permute-done.3.h2.g2 = bf16[256,2048]{1,0:T(8,128)(2,1)} collective-permute-done((bf16[256,2048]{1,0:T(8,128)(2,1)S(1)}, bf16[256,2048]{1,0:T(8,128)(2,1)}, u32[]{:S(2)}, u32[]{:S(2)}) %collective-permute-start.3) | collective-permute-done | bytes 1048608 | tf_op jit(solution)/shard_map/ppermute | solution.py:31
  37.8 0.8 collective-permute-start.7
  38.6 0.2 collective-permute-start.11
  38.7 3.6 %collective-permute-done.11 = f32[16,1024]{1,0:T(8,128)S(1)} collective-permute-done((f32[16,1024]{1,0:T(8,128)S(1)}, f32[16,1024]{1,0:T(8,128)S(1)}, u32[]{:S(2)}, u32[]{:S(2)}) %collective-permute-start.11) | collective-permute-done | bytes 65568 | tf_op jit(solution)/shard_map/ppermute | solution.py:31
  42.3 4.5 %collective-permute-start.14 = (bf16[16,1024]{1,0:T(8,128)(2,1)S(1)}, bf16[16,1024]{1,0:T(8,128)(2,1)S(1)}, u32[]{:S(2)}, u32[]{:S(2)}) collective-permute-start(bf16[16,1024]{1,0:T(8,128)(2,1)S(1)} %add_convert_fusion.1.part), channel_id=1, source_target_pairs={{0,192},{64,0},{128,64},{192,128},{1,193},{65,1},{129,65},{193,129... | collective-permute-start | bytes 98312 | tf_op jit(solution)/shard_map/ppermute | solution.py:373
  46.9 1.0 collective-permute-start.13
  47.9 2.2 %collective-permute-start.12 = (bf16[16,1024]{1,0:T(8,128)(2,1)S(1)}, bf16[16,1024]{1,0:T(8,128)(2,1)S(1)}, u32[]{:S(2)}, u32[]{:S(2)}) collective-permute-start(bf16[16,1024]{1,0:T(8,128)(2,1)S(1)} %add_convert_fusion.1.part), channel_id=1, source_target_pairs={{0,64},{64,128},{128,192},{192,0},{1,65},{65,129},{129,193},{193,1... | collective-permute-start | bytes 98312 | tf_op jit(solution)/shard_map/ppermute | solution.py:373
  50.1 3.4 %collective-permute-done.13.opposite = bf16[16,1024]{1,0:T(8,128)(2,1)S(1)} collective-permute-done((bf16[16,1024]{1,0:T(8,128)(2,1)S(1)}, bf16[16,1024]{1,0:T(8,128)(2,1)S(1)}, u32[]{:S(2)}, u32[]{:S(2)}) %collective-permute-start.13) | collective-permute-done | bytes 32800 | tf_op jit(solution)/shard_map/ppermute | solution.py:373
  53.5 0.9 spread.2
  54.5 6.6 %all-to-all-start.1 = ((bf16[16,16,1024]{2,1,0:T(8,128)(2,1)}), bf16[16,16,1024]{2,1,0:T(8,128)(2,1)S(1)}, u32[]{:S(2)}, u32[]{:S(2)}) async-start(bf16[16,16,1024]{2,1,0:T(8,128)(2,1)} %spread.2), calls=%async_computation.1 | async-start | bytes 1048576 | tf_op jit(solution)/shard_map/all_to_all | solution.py:385
  61.0 0.0 copy-start.2
  61.1 1.0 collective-permute-start.16
  62.1 6.4 %grad.1 = (bf16[256,512]{1,0:T(8,128)(2,1)}, bf16[256,512]{1,0:T(8,128)(2,1)}, bf16[2,256,512]{2,1,0:T(8,128)(2,1)}) custom-call(bf16[256,2048]{1,0:T(8,128)(2,1)} %og.3, bf16[256,2048]{1,0:T(8,128)(2,1)} %collective-permute-done.2.g1.h1, bf16[256,2048]{1,0:T(8,128)(2,1)} %collective-permute-done.3.h2.g2, bf16[256,2048]{1,0:T(8,128)(2,1)} %collective-permute-done.7.h3.g3, ...), custom_call_target="tpu_custom_call" | custom-call | flops 2200000000 | bytes 7340032 | tf_op jit(solution)/shard_map/grad/pallas_call | solution.py:300
  68.4 1.9 %all-to-all-done.1.mine = bf16[16,16,1024]{2,1,0:T(8,128)(2,1)S(1)} async-done(((bf16[16,16,1024]{2,1,0:T(8,128)(2,1)}), bf16[16,16,1024]{2,1,0:T(8,128)(2,1)S(1)}, u32[]{:S(2)}, u32[]{:S(2)}) %all-to-all-start.1) | async-done | bytes 524320 | tf_op jit(solution)/shard_map/all_to_all | solution.py:385
  70.3 3.3 %collective-permute-start.15 = (bf16[16,16,1024]{2,1,0:T(8,128)(2,1)S(1)}, bf16[16,16,1024]{2,1,0:T(8,128)(2,1)S(1)}, u32[]{:S(2)}, u32[]{:S(2)}) collective-permute-start(bf16[16,16,1024]{2,1,0:T(8,128)(2,1)S(1)} %all-to-all-done.1.mine), channel_id=1, source_target_pairs={{0,1},{1,0},{2,3},{3,2},{4,5},{5,4},{6,7},{7,6},{8,9},{9,8},{10,11... | collective-permute-start | bytes 1572872 | tf_op jit(solution)/shard_map/ppermute | solution.py:31
  73.7 0.5 early.1
  74.2 1.0 collective-permute-done.15.other
  75.2 4.4 %right.1 = (f32[16,16,1024]{2,1,0:T(8,128)S(1)}, bf16[16,16,1024]{2,1,0:T(8,128)(2,1)S(1)}, bf16[256,2048]{1,0:T(8,128)(2,1)S(1)}) custom-call(s32[2]{0:T(128)S(1)} %pad_add_fusion.at, bf16[256,2048]{1,0:T(8,128)(2,1)S(1)} %copy-done, bf16[256,2048]{1,0:T(8,128)(2,1)S(1)} %copy-done.2, bf16[512,2048]{1,0:T(8,128)(2,1)} %get-tuple-element.56.low_hbm, ...), custom_call_target="tpu_custom_call" | custom-call | flops 2000000000 | bytes 7995400 | tf_op jit(solution)/shard_map/right/pallas_call | solution.py:300
  79.7 1.5 %collective-permute-start.17 = (bf16[16,16,1024]{2,1,0:T(8,128)(2,1)S(1)}, bf16[16,16,1024]{2,1,0:T(8,128)(2,1)S(1)}, u32[]{:S(2)}, u32[]{:S(2)}) collective-permute-start(bf16[16,16,1024]{2,1,0:T(8,128)(2,1)S(1)} %get-tuple-element.65), channel_id=1, source_target_pairs={{0,1},{1,0},{2,3},{3,2},{4,5},{5,4},{6,7},{7,6},{8,9},{9,8},{10,11... | collective-permute-start | bytes 1572872 | tf_op jit(solution)/shard_map/ppermute | solution.py:31
  81.2 0.8 collective-permute-start.9
  82.0 0.8 collective-permute-done.17.got
  82.8 0.9 add.15
  83.6 6.6 %all-to-all-start.2 = ((bf16[16,16,1024]{2,1,0:T(8,128)(2,1)}), bf16[16,16,1024]{2,1,0:T(8,128)(2,1)S(1)}, u32[]{:S(2)}, u32[]{:S(2)}) async-start(bf16[16,16,1024]{2,1,0:T(8,128)(2,1)} %add.15), calls=%async_computation.2 | async-start | bytes 1048576 | tf_op jit(solution)/shard_map/all_to_all | solution.py:364
  90.3 0.7 collective-permute-start.8
  91.1 0.1 collective-permute-start.19
  91.2 3.9 %collective-permute-done.9.far = bf16[2,256,512]{2,1,0:T(8,128)(2,1)} collective-permute-done((bf16[2,256,512]{2,1,0:T(8,128)(2,1)}, bf16[2,256,512]{2,1,0:T(8,128)(2,1)}, u32[]{:S(2)}, u32[]{:S(2)}) %collective-permute-start.9) | collective-permute-done | bytes 524320 | tf_op jit(solution)/shard_map/ppermute | solution.py:31
  95.0 0.9 collective-permute-start.10
  95.9 4.0 %gram.1.a_in = f32[256,512]{1,0:T(8,128)S(1)} custom-call(bf16[256,2048]{1,0:T(8,128)(2,1)S(1)} %get-tuple-element.66.left), custom_call_target="tpu_custom_call" | custom-call | flops 300000000 | bytes 1572864 | tf_op jit(solution)/shard_map/gram/pallas_call | solution.py:300
  99.9 3.1 %step.2.a_in = f32[256,512]{1,0:T(8,128)S(1)} custom-call(f32[256,512]{1,0:T(8,128)S(1)} %gram.1.a_in), custom_call_target="tpu_custom_call", output_to_operand_aliasing={{}: (0, {})} | custom-call | flops 300000000 | bytes 1048576 | tf_op jit(solution)/shard_map/step/pallas_call | solution.py:300
  103.0 0.1 sum.3
  103.0 0.8 collective-permute-start.18
  103.9 3.0 %collective-permute-done.18 = f32[16,1024]{1,0:T(8,128)S(1)} collective-permute-done((f32[16,1024]{1,0:T(8,128)S(1)}, f32[16,1024]{1,0:T(8,128)S(1)}, u32[]{:S(2)}, u32[]{:S(2)}) %collective-permute-start.18) | collective-permute-done | bytes 65568 | tf_op jit(solution)/shard_map/ppermute | solution.py:31
  106.9 1.6 %collective-permute-start.22 = (bf16[16,1024]{1,0:T(8,128)(2,1)S(1)}, bf16[16,1024]{1,0:T(8,128)(2,1)S(1)}, u32[]{:S(2)}, u32[]{:S(2)}) collective-permute-start(bf16[16,1024]{1,0:T(8,128)(2,1)S(1)} %add_convert_fusion.part), channel_id=1, source_target_pairs={{0,192},{64,0},{128,64},{192,128},{1,193},{65,1},{129,65},{193,129... | collective-permute-start | bytes 98312 | tf_op jit(solution)/shard_map/ppermute | solution.py:373
  108.5 2.2 %collective-permute-start.21 = (bf16[16,1024]{1,0:T(8,128)(2,1)S(1)}, bf16[16,1024]{1,0:T(8,128)(2,1)S(1)}, u32[]{:S(2)}, u32[]{:S(2)}) collective-permute-start(bf16[16,1024]{1,0:T(8,128)(2,1)S(1)} %add_convert_fusion.part), channel_id=1, source_target_pairs={{0,128},{64,192},{128,0},{192,64},{1,129},{65,193},{129,1},{193,65... | collective-permute-start | bytes 98312 | tf_op jit(solution)/shard_map/ppermute | solution.py:373
  110.7 2.3 %collective-permute-start.20 = (bf16[16,1024]{1,0:T(8,128)(2,1)S(1)}, bf16[16,1024]{1,0:T(8,128)(2,1)S(1)}, u32[]{:S(2)}, u32[]{:S(2)}) collective-permute-start(bf16[16,1024]{1,0:T(8,128)(2,1)S(1)} %add_convert_fusion.part), channel_id=1, source_target_pairs={{0,64},{64,128},{128,192},{192,0},{1,65},{65,129},{129,193},{193,1... | collective-permute-start | bytes 98312 | tf_op jit(solution)/shard_map/ppermute | solution.py:373
  112.9 3.0 %step.3.a_in = f32[256,512]{1,0:T(8,128)S(1)} custom-call(f32[256,512]{1,0:T(8,128)S(1)} %step.2.a_in), custom_call_target="tpu_custom_call", output_to_operand_aliasing={{}: (0, {})} | custom-call | flops 300000000 | bytes 1048576 | tf_op jit(solution)/shard_map/step/pallas_call | solution.py:300
  116.0 0.5 collective-permute-done.20.one
  116.5 0.9 spread.3
  117.3 6.6 %all-to-all-start.3 = ((bf16[16,16,1024]{2,1,0:T(8,128)(2,1)}), bf16[16,16,1024]{2,1,0:T(8,128)(2,1)S(1)}, u32[]{:S(2)}, u32[]{:S(2)}) async-start(bf16[16,16,1024]{2,1,0:T(8,128)(2,1)} %spread.3), calls=%async_computation.3 | async-start | bytes 1048576 | tf_op jit(solution)/shard_map/all_to_all | solution.py:385
  124.0 2.8 %place.1 = bf16[256,2048]{1,0:T(8,128)(2,1)} custom-call(s32[2]{0:T(128)S(1)} %pad_add_fusion.at, bf16[256,512]{1,0:T(8,128)(2,1)} %get-tuple-element.53.own, bf16[256,512]{1,0:T(8,128)(2,1)} %collective-permute-done.8.near, bf16[2,256,512]{2,1,0:T(8,128)(2,1)} %collective-permute-done.9.far, bf16[2,256,512]{2,1,0:T(8,128)(2,1)} %collective-permute-done.10.diag), custom_call_target="tpu_custom_call" | custom-call | flops 1000000 | bytes 2621448 | tf_op jit(solution)/shard_map/place/pallas_call | solution.py:325
  126.8 3.6 %basis.1 = (f32[256,256]{1,0:T(8,128)S(1)}, bf16[512,256]{1,0:T(8,128)(2,1)S(1)}) custom-call(s32[2]{0:T(128)S(1)} %pad_add_fusion.at, f32[256,512]{1,0:T(8,128)S(1)} %step.3.a_in, bf16[256,2048]{1,0:T(8,128)(2,1)S(1)} %get-tuple-element.66.left), custom_call_target="tpu_custom_call" | custom-call | flops 300000000 | bytes 2097160 | tf_op jit(solution)/shard_map/basis/pallas_call | solution.py:300
  130.4 0.7 copy-done.6
  131.1 2.8 %all-to-all-done.3.chunks = bf16[16,16,1024]{2,1,0:T(8,128)(2,1)S(1)} async-done(((bf16[16,16,1024]{2,1,0:T(8,128)(2,1)}), bf16[16,16,1024]{2,1,0:T(8,128)(2,1)S(1)}, u32[]{:S(2)}, u32[]{:S(2)}) %all-to-all-start.3) | async-done | bytes 524320 | tf_op jit(solution)/shard_map/all_to_all | solution.py:385
  133.9 2.6 %collective-permute-start.23 = (bf16[16,16,1024]{2,1,0:T(8,128)(2,1)S(1)}, bf16[16,16,1024]{2,1,0:T(8,128)(2,1)S(1)}, u32[]{:S(2)}, u32[]{:S(2)}) collective-permute-start(bf16[16,16,1024]{2,1,0:T(8,128)(2,1)S(1)} %all-to-all-done.3.chunks), channel_id=1, source_target_pairs={{0,1},{1,0},{2,3},{3,2},{4,5},{5,4},{6,7},{7,6},{8,9},{9,8},{10,11... | collective-permute-start | bytes 1572872 | tf_op jit(solution)/shard_map/ppermute | solution.py:31
  136.5 1.2 begin.1
  137.7 0.3 collective-permute-done.23.other
  138.0 6.9 %last.1 = (f32[512,2048]{1,0:T(8,128)}, f32[512,256]{1,0:T(8,128)}) custom-call(s32[2]{0:T(128)S(1)} %pad_add_fusion.at, bf16[16,16,1024]{2,1,0:T(8,128)(2,1)S(1)} %collective-permute-done.23.other, f32[256,256]{1,0:T(8,128)S(1)} %get-tuple-element.72.inverse, bf16[512,256]{1,0:T(8,128)(2,1)} %copy-done.6, f32[256,2048]{1,0:T(8,128)S(1)} %get-tuple-element.73.begun, ...), custom_call_target="tpu_custom_call" | custom-call | flops 2000000000 | bytes 14680072 | tf_op jit(solution)/shard_map/last/pallas_call | solution.py:325
  (32 shorter events, 0.1 us)
Async XLA Ops:
  0.6 4.7 %collective-permute-start.1 = (bf16[512,256]{1,0:T(8,128)(2,1)}, bf16[512,256]{1,0:T(8,128)(2,1)S(1)}, u32[]{:S(2)}, u32[]{:S(2)}) collective-permute-start(bf16[512,256]{1,0:T(8,128)(2,1)} %w0.1), channel_id=1, source_target_pairs={{0,1},{1,0},{2,3},{3,2},{4,5},{5,4},{6,7},{7,6},{8,9},{9,8},{10,11... | collective-permute-start | bytes 786440 | tf_op jit(solution)/shard_map/ppermute | solution.py:31
  4.0 8.1 %collective-permute-start = (bf16[512,256]{1,0:T(8,128)(2,1)}, bf16[512,256]{1,0:T(8,128)(2,1)S(1)}, u32[]{:S(2)}, u32[]{:S(2)}) collective-permute-start(bf16[512,256]{1,0:T(8,128)(2,1)} %w0.1), channel_id=1, source_target_pairs={{0,2},{2,0},{1,3},{3,1},{4,6},{6,4},{5,7},{7,5},{8,10},{10,8},{9,1... | collective-permute-start | bytes 786440 | tf_op jit(solution)/shard_map/ppermute | solution.py:31
  5.3 7.6 %copy-start.1 = (bf16[256,2048]{1,0:T(8,128)(2,1)S(1)}, bf16[256,2048]{1,0:T(8,128)(2,1)}, u32[]{:S(2)}) copy-start(bf16[256,2048]{1,0:T(8,128)(2,1)} %og.3) | copy-start | bytes 3145732
  5.3 8.7 %copy-start = (bf16[256,2048]{1,0:T(8,128)(2,1)S(1)}, bf16[256,2048]{1,0:T(8,128)(2,1)}, u32[]{:S(2)}) copy-start(bf16[256,2048]{1,0:T(8,128)(2,1)} %ctx.7) | copy-start | bytes 3145732
  5.3 8.7 %copy-start.7 = (bf16[512,256]{1,0:T(8,128)(2,1)S(1)}, bf16[512,256]{1,0:T(8,128)(2,1)}, u32[]{:S(2)}) copy-start(bf16[512,256]{1,0:T(8,128)(2,1)} %w0.1) | copy-start | bytes 786436
  10.2 3.0 %collective-permute-start.4 = (bf16[256,512]{1,0:T(8,128)(2,1)}, bf16[256,512]{1,0:T(8,128)(2,1)S(1)}, u32[]{:S(2)}, u32[]{:S(2)}) collective-permute-start(bf16[256,512]{1,0:T(8,128)(2,1)} %get-tuple-element.45), channel_id=1, source_target_pairs={{0,1},{1,0},{2,3},{3,2},{4,5},{5,4},{6,7},{7,6},{8,9},{9,8},{10,11... | collective-permute-start | bytes 786440 | tf_op jit(solution)/shard_map/ppermute | solution.py:31
  12.0 2.0 %collective-permute-start.5 = (bf16[512,256]{1,0:T(8,128)(2,1)S(1)}, bf16[512,256]{1,0:T(8,128)(2,1)S(1)}, u32[]{:S(2)}, u32[]{:S(2)}) collective-permute-start(bf16[512,256]{1,0:T(8,128)(2,1)S(1)} %collective-permute-done.w2), channel_id=1, source_target_pairs={{0,1},{1,0},{2,3},{3,2},{4,5},{5,4},{6,7},{7,6},{8,9},{9,8},{10,11... | collective-permute-start | bytes 786440 | tf_op jit(solution)/shard_map/ppermute | solution.py:31
  12.9 24.9 %collective-permute-start.3 = (bf16[256,2048]{1,0:T(8,128)(2,1)S(1)}, bf16[256,2048]{1,0:T(8,128)(2,1)}, u32[]{:S(2)}, u32[]{:S(2)}) collective-permute-start(bf16[256,2048]{1,0:T(8,128)(2,1)S(1)} %copy-done.1), channel_id=1, source_target_pairs={{0,2},{2,0},{1,3},{3,1},{4,6},{6,4},{5,7},{7,5},{8,10},{10,8},{9,1... | collective-permute-start | bytes 3145736 | tf_op jit(solution)/shard_map/ppermute | solution.py:31
  12.9 12.3 %collective-permute-start.2 = (bf16[256,2048]{1,0:T(8,128)(2,1)S(1)}, bf16[256,2048]{1,0:T(8,128)(2,1)}, u32[]{:S(2)}, u32[]{:S(2)}) collective-permute-start(bf16[256,2048]{1,0:T(8,128)(2,1)S(1)} %copy-done.1), channel_id=1, source_target_pairs={{0,1},{1,0},{2,3},{3,2},{4,5},{5,4},{6,7},{7,6},{8,9},{9,8},{10,11... | collective-permute-start | bytes 3145736 | tf_op jit(solution)/shard_map/ppermute | solution.py:31
  16.5 8.7 %copy-start.5 = (bf16[256,512]{1,0:T(8,128)(2,1)S(1)}, bf16[256,512]{1,0:T(8,128)(2,1)}, u32[]{:S(2)}) copy-start(bf16[256,512]{1,0:T(8,128)(2,1)} %get-tuple-element.50.c0) | copy-start | bytes 786436
  16.5 2.0 %collective-permute-start.6 = (bf16[16,16,1024]{2,1,0:T(8,128)(2,1)S(1)}, bf16[16,16,1024]{2,1,0:T(8,128)(2,1)S(1)}, u32[]{:S(2)}, u32[]{:S(2)}) collective-permute-start(bf16[16,16,1024]{2,1,0:T(8,128)(2,1)S(1)} %get-tuple-element.49), channel_id=1, source_target_pairs={{0,1},{1,0},{2,3},{3,2},{4,5},{5,4},{6,7},{7,6},{8,9},{9,8},{10,11... | collective-permute-start | bytes 1572872 | tf_op jit(solution)/shard_map/ppermute | solution.py:31
  19.4 16.6 %all-to-all-start = ((bf16[16,16,1024]{2,1,0:T(8,128)(2,1)}), bf16[16,16,1024]{2,1,0:T(8,128)(2,1)S(1)}, u32[]{:S(2)}, u32[]{:S(2)}) async-start(bf16[16,16,1024]{2,1,0:T(8,128)(2,1)} %add.14), calls=%async_computation | async-start | bytes 1048576 | tf_op jit(solution)/shard_map/all_to_all | solution.py:364
  37.8 24.3 %collective-permute-start.7 = (bf16[256,2048]{1,0:T(8,128)(2,1)}, bf16[256,2048]{1,0:T(8,128)(2,1)}, u32[]{:S(2)}, u32[]{:S(2)}) collective-permute-start(bf16[256,2048]{1,0:T(8,128)(2,1)} %collective-permute-done.3.h2.g2), channel_id=1, source_target_pairs={{0,1},{1,0},{2,3},{3,2},{4,5},{5,4},{6,7},{7,6},{8,9},{9,8},{10,11... | collective-permute-start | bytes 3145736 | tf_op jit(solution)/shard_map/ppermute | solution.py:31
  38.6 3.7 %collective-permute-start.11 = (f32[16,1024]{1,0:T(8,128)S(1)}, f32[16,1024]{1,0:T(8,128)S(1)}, u32[]{:S(2)}, u32[]{:S(2)}) collective-permute-start(f32[16,1024]{1,0:T(8,128)S(1)} %sum.2), channel_id=1, source_target_pairs={{0,2},{2,0},{1,3},{3,1},{4,6},{6,4},{5,7},{7,5},{8,10},{10,8},{9,1... | collective-permute-start | bytes 196616 | tf_op jit(solution)/shard_map/ppermute | solution.py:31
  42.3 7.8 %collective-permute-start.14 = (bf16[16,1024]{1,0:T(8,128)(2,1)S(1)}, bf16[16,1024]{1,0:T(8,128)(2,1)S(1)}, u32[]{:S(2)}, u32[]{:S(2)}) collective-permute-start(bf16[16,1024]{1,0:T(8,128)(2,1)S(1)} %add_convert_fusion.1.part), channel_id=1, source_target_pairs={{0,192},{64,0},{128,64},{192,128},{1,193},{65,1},{129,65},{193,129... | collective-permute-start | bytes 98312 | tf_op jit(solution)/shard_map/ppermute | solution.py:373
  46.9 6.7 %collective-permute-start.13 = (bf16[16,1024]{1,0:T(8,128)(2,1)S(1)}, bf16[16,1024]{1,0:T(8,128)(2,1)S(1)}, u32[]{:S(2)}, u32[]{:S(2)}) collective-permute-start(bf16[16,1024]{1,0:T(8,128)(2,1)S(1)} %add_convert_fusion.1.part), channel_id=1, source_target_pairs={{0,128},{64,192},{128,0},{192,64},{1,129},{65,193},{129,1},{193,65... | collective-permute-start | bytes 98312 | tf_op jit(solution)/shard_map/ppermute | solution.py:373
  47.9 5.7 %collective-permute-start.12 = (bf16[16,1024]{1,0:T(8,128)(2,1)S(1)}, bf16[16,1024]{1,0:T(8,128)(2,1)S(1)}, u32[]{:S(2)}, u32[]{:S(2)}) collective-permute-start(bf16[16,1024]{1,0:T(8,128)(2,1)S(1)} %add_convert_fusion.1.part), channel_id=1, source_target_pairs={{0,64},{64,128},{128,192},{192,0},{1,65},{65,129},{129,193},{193,1... | collective-permute-start | bytes 98312 | tf_op jit(solution)/shard_map/ppermute | solution.py:373
  54.5 15.9 %all-to-all-start.1 = ((bf16[16,16,1024]{2,1,0:T(8,128)(2,1)}), bf16[16,16,1024]{2,1,0:T(8,128)(2,1)S(1)}, u32[]{:S(2)}, u32[]{:S(2)}) async-start(bf16[16,16,1024]{2,1,0:T(8,128)(2,1)} %spread.2), calls=%async_computation.1 | async-start | bytes 1048576 | tf_op jit(solution)/shard_map/all_to_all | solution.py:385
  61.0 14.2 %copy-start.2 = (bf16[256,2048]{1,0:T(8,128)(2,1)S(1)}, bf16[256,2048]{1,0:T(8,128)(2,1)}, u32[]{:S(2)}) copy-start(bf16[256,2048]{1,0:T(8,128)(2,1)} %og.3) | copy-start | bytes 3145732
  61.1 13.1 %collective-permute-start.16 = (bf16[2,256,512]{2,1,0:T(8,128)(2,1)}, bf16[2,256,512]{2,1,0:T(8,128)(2,1)S(1)}, u32[]{:S(2)}, u32[]{:S(2)}) collective-permute-start(bf16[2,256,512]{2,1,0:T(8,128)(2,1)} %get-tuple-element.62), channel_id=1, source_target_pairs={{0,2},{2,0},{1,3},{3,1},{4,6},{6,4},{5,7},{7,5},{8,10},{10,8},{9,1... | collective-permute-start | bytes 1572872 | tf_op jit(solution)/shard_map/ppermute | solution.py:31
  70.3 4.9 %collective-permute-start.15 = (bf16[16,16,1024]{2,1,0:T(8,128)(2,1)S(1)}, bf16[16,16,1024]{2,1,0:T(8,128)(2,1)S(1)}, u32[]{:S(2)}, u32[]{:S(2)}) collective-permute-start(bf16[16,16,1024]{2,1,0:T(8,128)(2,1)S(1)} %all-to-all-done.1.mine), channel_id=1, source_target_pairs={{0,1},{1,0},{2,3},{3,2},{4,5},{5,4},{6,7},{7,6},{8,9},{9,8},{10,11... | collective-permute-start | bytes 1572872 | tf_op jit(solution)/shard_map/ppermute | solution.py:31
  74.2 1.0 copy-start.3
  79.7 10.6 %copy-start.8 = (bf16[256,512]{1,0:T(8,128)(2,1)S(1)}, bf16[256,512]{1,0:T(8,128)(2,1)}, u32[]{:S(2)}) copy-start(bf16[256,512]{1,0:T(8,128)(2,1)} %get-tuple-element.54) | copy-start | bytes 786436
  79.7 11.4 %copy-start.4 = (bf16[2,256,512]{2,1,0:T(8,128)(2,1)S(1)}, bf16[2,256,512]{2,1,0:T(8,128)(2,1)}, u32[]{:S(2)}) copy-start(bf16[2,256,512]{2,1,0:T(8,128)(2,1)} %copy-done.3) | copy-start | bytes 1572868
  79.7 3.1 %collective-permute-start.17 = (bf16[16,16,1024]{2,1,0:T(8,128)(2,1)S(1)}, bf16[16,16,1024]{2,1,0:T(8,128)(2,1)S(1)}, u32[]{:S(2)}, u32[]{:S(2)}) collective-permute-start(bf16[16,16,1024]{2,1,0:T(8,128)(2,1)S(1)} %get-tuple-element.65), channel_id=1, source_target_pairs={{0,1},{1,0},{2,3},{3,2},{4,5},{5,4},{6,7},{7,6},{8,9},{9,8},{10,11... | collective-permute-start | bytes 1572872 | tf_op jit(solution)/shard_map/ppermute | solution.py:31
  81.2 13.8 %collective-permute-start.9 = (bf16[2,256,512]{2,1,0:T(8,128)(2,1)}, bf16[2,256,512]{2,1,0:T(8,128)(2,1)}, u32[]{:S(2)}, u32[]{:S(2)}) collective-permute-start(bf16[2,256,512]{2,1,0:T(8,128)(2,1)} %get-tuple-element.55), channel_id=1, source_target_pairs={{0,2},{2,0},{1,3},{3,1},{4,6},{6,4},{5,7},{7,5},{8,10},{10,8},{9,1... | collective-permute-start | bytes 1572872 | tf_op jit(solution)/shard_map/ppermute | solution.py:31
  83.6 19.3 %all-to-all-start.2 = ((bf16[16,16,1024]{2,1,0:T(8,128)(2,1)}), bf16[16,16,1024]{2,1,0:T(8,128)(2,1)S(1)}, u32[]{:S(2)}, u32[]{:S(2)}) async-start(bf16[16,16,1024]{2,1,0:T(8,128)(2,1)} %add.15), calls=%async_computation.2 | async-start | bytes 1048576 | tf_op jit(solution)/shard_map/all_to_all | solution.py:364
  90.3 12.7 %collective-permute-start.8 = (bf16[256,512]{1,0:T(8,128)(2,1)S(1)}, bf16[256,512]{1,0:T(8,128)(2,1)}, u32[]{:S(2)}, u32[]{:S(2)}) collective-permute-start(bf16[256,512]{1,0:T(8,128)(2,1)S(1)} %copy-done.8), channel_id=1, source_target_pairs={{0,1},{1,0},{2,3},{3,2},{4,5},{5,4},{6,7},{7,6},{8,9},{9,8},{10,11... | collective-permute-start | bytes 786440 | tf_op jit(solution)/shard_map/ppermute | solution.py:31
  91.1 24.9 %collective-permute-start.19 = (bf16[2,256,512]{2,1,0:T(8,128)(2,1)S(1)}, bf16[2,256,512]{2,1,0:T(8,128)(2,1)S(1)}, u32[]{:S(2)}, u32[]{:S(2)}) collective-permute-start(bf16[2,256,512]{2,1,0:T(8,128)(2,1)S(1)} %copy-done.4), channel_id=1, source_target_pairs={{0,1},{1,0},{2,3},{3,2},{4,5},{5,4},{6,7},{7,6},{8,9},{9,8},{10,11... | collective-permute-start | bytes 1572872 | tf_op jit(solution)/shard_map/ppermute | solution.py:31
  95.0 20.9 %collective-permute-start.10 = (bf16[2,256,512]{2,1,0:T(8,128)(2,1)}, bf16[2,256,512]{2,1,0:T(8,128)(2,1)}, u32[]{:S(2)}, u32[]{:S(2)}) collective-permute-start(bf16[2,256,512]{2,1,0:T(8,128)(2,1)} %collective-permute-done.9.far), channel_id=1, source_target_pairs={{0,1},{1,0},{2,3},{3,2},{4,5},{5,4},{6,7},{7,6},{8,9},{9,8},{10,11... | collective-permute-start | bytes 1572872 | tf_op jit(solution)/shard_map/ppermute | solution.py:31
  103.0 3.8 %collective-permute-start.18 = (f32[16,1024]{1,0:T(8,128)S(1)}, f32[16,1024]{1,0:T(8,128)S(1)}, u32[]{:S(2)}, u32[]{:S(2)}) collective-permute-start(f32[16,1024]{1,0:T(8,128)S(1)} %sum.3), channel_id=1, source_target_pairs={{0,2},{2,0},{1,3},{3,1},{4,6},{6,4},{5,7},{7,5},{8,10},{10,8},{9,1... | collective-permute-start | bytes 196616 | tf_op jit(solution)/shard_map/ppermute | solution.py:31
  106.9 9.1 %collective-permute-start.22 = (bf16[16,1024]{1,0:T(8,128)(2,1)S(1)}, bf16[16,1024]{1,0:T(8,128)(2,1)S(1)}, u32[]{:S(2)}, u32[]{:S(2)}) collective-permute-start(bf16[16,1024]{1,0:T(8,128)(2,1)S(1)} %add_convert_fusion.part), channel_id=1, source_target_pairs={{0,192},{64,0},{128,64},{192,128},{1,193},{65,1},{129,65},{193,129... | collective-permute-start | bytes 98312 | tf_op jit(solution)/shard_map/ppermute | solution.py:373
  108.5 7.5 %collective-permute-start.21 = (bf16[16,1024]{1,0:T(8,128)(2,1)S(1)}, bf16[16,1024]{1,0:T(8,128)(2,1)S(1)}, u32[]{:S(2)}, u32[]{:S(2)}) collective-permute-start(bf16[16,1024]{1,0:T(8,128)(2,1)S(1)} %add_convert_fusion.part), channel_id=1, source_target_pairs={{0,128},{64,192},{128,0},{192,64},{1,129},{65,193},{129,1},{193,65... | collective-permute-start | bytes 98312 | tf_op jit(solution)/shard_map/ppermute | solution.py:373
  110.7 5.8 %collective-permute-start.20 = (bf16[16,1024]{1,0:T(8,128)(2,1)S(1)}, bf16[16,1024]{1,0:T(8,128)(2,1)S(1)}, u32[]{:S(2)}, u32[]{:S(2)}) collective-permute-start(bf16[16,1024]{1,0:T(8,128)(2,1)S(1)} %add_convert_fusion.part), channel_id=1, source_target_pairs={{0,64},{64,128},{128,192},{192,0},{1,65},{65,129},{129,193},{193,1... | collective-permute-start | bytes 98312 | tf_op jit(solution)/shard_map/ppermute | solution.py:373
  117.3 16.5 %all-to-all-start.3 = ((bf16[16,16,1024]{2,1,0:T(8,128)(2,1)}), bf16[16,16,1024]{2,1,0:T(8,128)(2,1)S(1)}, u32[]{:S(2)}, u32[]{:S(2)}) async-start(bf16[16,16,1024]{2,1,0:T(8,128)(2,1)} %spread.3), calls=%async_computation.3 | async-start | bytes 1048576 | tf_op jit(solution)/shard_map/all_to_all | solution.py:385
  130.4 0.7 copy-start.6
  133.9 4.2 %collective-permute-start.23 = (bf16[16,16,1024]{2,1,0:T(8,128)(2,1)S(1)}, bf16[16,16,1024]{2,1,0:T(8,128)(2,1)S(1)}, u32[]{:S(2)}, u32[]{:S(2)}) collective-permute-start(bf16[16,16,1024]{2,1,0:T(8,128)(2,1)S(1)} %all-to-all-done.3.chunks), channel_id=1, source_target_pairs={{0,1},{1,0},{2,3},{3,2},{4,5},{5,4},{6,7},{7,6},{8,9},{9,8},{10,11... | collective-permute-start | bytes 1572872 | tf_op jit(solution)/shard_map/ppermute | solution.py:31

commit v6 on v4

--- a/solution.py
+++ b/solution.py
@@ -211,12 +211,12 @@
     basis[...] = (mm(first, own, 1, 0) + mm(second, own, 1, 0)).astype(BF16).T
 
 
-def grad_kernel(h0, h1, h2, h3, weight_hbm, o0, o1, far, weight, g0, g1, g2, g3, sems):
-    copies = fetch((weight_hbm, h0, h1, h2, h3), (weight, g0, g1, g2, g3), sems)
+def grad_kernel(h0, h1, weight_hbm, out, weight, g0, g1, sems):
+    copies = fetch((weight_hbm, h0, h1), (weight, g0, g1), sems)
     copies[0].wait()
-    for g, o, copy in zip((g0, g1, g2, g3), (o0, o1, far.at[0], far.at[1]), copies[1:]):
-        copy.wait()
-        o[...] = mm(g[...], weight[...], 1, 1).astype(BF16)
+    for n, g in enumerate((g0, g1)):
+        copies[n + 1].wait()
+        out[n] = mm(g[...], weight[...], 1, 1).astype(BF16)
 
 
 def merge_kernel(scale, err, c0, c1, g0, g1, out, t0, t1):
@@ -231,11 +231,12 @@
     out[...] = err[...] + total * scale
 
 
-def place_kernel(at, own, near, far, diag, out, sems):
+def place_kernel(at, own, near, far, diag, out):
     zl, core = at[0], at[1]
-    where = (block(zl, core), block(zl, 1 - core), block(1 - zl, core), block(1 - zl, 1 - core))
-    for copy in fetch((own, near, far.at[0], diag.at[1]), [out.at[:, cols] for cols in where], sems):
-        copy.wait()
+    out[:, block(zl, core)] = own[...]
+    out[:, block(zl, 1 - core)] = near[...]
+    out[:, block(1 - zl, core)] = far[...]
+    out[:, block(1 - zl, 1 - core)] = diag[...]
 
 
 def columns_of(inverse, half):
@@ -414,7 +415,7 @@
         [((RANK, FEAT), F32)],
     )
     g_far = swap(tied(out_grad, warm_near), "zl")
-    g_near = swap(tied(out_grad, warm_far, low), "core")
+    g_near = in_hbm(swap(tied(out_grad, warm_far, low), "core"))
     turned = [((ROWS, TOK), BF16)] * 2
     (merged,) = call_grid(
         functools.partial(merge_kernel, scale),
@@ -425,28 +426,34 @@
         1_100_000_000,
         "merge",
         turned,
-        loose=(3, 4),
+        loose=(3,),
     )
     part = across_plane(keep, send, (merged,))
     g_diag = swap(tied(g_far, part), "core")
-    zs = across_z(tied(part, g_far))
+
+    def grad(g0, g1):
+        (out,) = call(
+            grad_kernel,
+            [pair],
+            (g0, g1, weight),
+            1_100_000_000,
+            "grad",
+            [big] + [((TOK, FEAT), BF16)] * 2,
+            held=range(3),
+            free=True,
+            sems=3,
+        )
+        return out
+
+    i_home = grad(out_grad, g_near)
+    zs = across_z(tied(part, g_far), (i_home,))
     c_far = swap(tied(c_far, *zs[1:]), "zl")
     mine = back_over_plane(*zs)
 
-    i_own, i_near, i_far = call(
-        grad_kernel,
-        [tokens] * 2 + [pair],
-        (out_grad, g_near, g_far, g_diag, weight),
-        2_200_000_000,
-        "grad",
-        [big] + [((TOK, FEAT), BF16)] * 4,
-        held=range(5),
-        free=True,
-        sems=5,
-    )
-    other = swap(tied(mine, i_own, c_far), "core")
+    i_far = grad(g_far, g_diag)
+    other = swap(tied(mine, i_far, c_far), "core")
     i_far = swap(i_far, "zl")
-    i_near = swap(i_near, "core")
+    i_near = swap(i_home, "core")
 
     mine_half, proj = call(
         early_kernel,
@@ -481,15 +488,17 @@
         functools.partial(step_kernel, 2 * PART), [table], (a,), 300_000_000, "step", alias={0: 0}
     )
     mine = back_over_plane(*zs, beside=(a, c_diag, i_diag))
-    in_grad = pl.pallas_call(
+    first = pl.BlockSpec((None, TOK, ROWS), lambda j: (0, 0, 0))
+    second = pl.BlockSpec((None, TOK, ROWS), lambda j: (1, 0, 0))
+    (in_grad,) = call_grid(
         place_kernel,
-        out_shape=pltpu.HBM((TOK, FEAT), BF16),
-        in_specs=[SMEM] + [ANY] * 4,
-        out_specs=ANY,
-        scratch_shapes=[pltpu.SemaphoreType.DMA((4,))],
-        cost_estimate=pl.CostEstimate(flops=0, bytes_accessed=2**21, transcendentals=0),
-        name="place",
-    )(at, *(in_hbm(x) for x in (i_own, i_near, i_far, i_diag)))
+        1,
+        [((TOK, FEAT), BF16, whole(TOK, FEAT))],
+        [SMEM, first, second, first, second],
+        (at, i_home, i_near, i_far, i_diag),
+        1_000_000,
+        "place",
+    )
     inverse, basis = call(
         basis_kernel,
         [((RANK, RANK), F32), ((ROWS, RANK), BF16)],

time: 167 us -> 142 us (0.85)
  Pallas kernels: 83.6 us -> 54.2 us
  waiting for transfers between devices: 27.5 us -> 31.1 us
    pallas_call x1 -> x0, Pallas kernels: 33.7 us -> none  [on_device(): pl.pallas_call(place_kernel, out_shape=pltpu.HBM((TOK, FEAT), BF16), in_s...]
    all_to_all x2, waiting for transfers between devices: 2.65 us -> 8.95 us  [back_over_plane(): return lax.all_to_all(whole, ('y', 'x'), 0, 0)]
    ppermute x18, waiting for transfers between devices: 13.1 us -> 9.28 us  [swap(): return lax.ppermute(x, axis, [(0, 1), (1, 0)])]
    pallas_call x3 -> x4, Pallas kernels: 17.7 us -> 19.9 us  [call_grid(): pl.pallas_call(kernel, grid=(steps,), out_shape=[(jax.ShapeDtypeStruct if...]
    pallas_call x15 -> x16, Pallas kernels: 32.2 us -> 34.2 us  [call(): pl.pallas_call(kernel, out_shape=[(pltpu.HBM if free else jax.ShapeDtypeS...]
  transfers between devices with their start and end apart: 28 -> 28, of which waited for: 14 -> 16; matrix products, arithmetic and copies ran while one was open for 0% -> 0% of each run, Pallas kernels for 43% -> 30%
where the time goes in v6:
time: 142 us; the launch traced here: 141 us
  Pallas kernels  54.2 us (38%)
  starting transfers between devices  53 us (37%)
  waiting for transfers between devices  31.1 us (22%)
  local copies, waits for them, and re-layouts  1.52 us (1%)
    pallas_call x16, Pallas kernels, call(): pl.pallas_call(kernel, out_shape=[(pltpu.HBM if free else jax.ShapeDtypeS...  34.2 us
    pallas_call x4, Pallas kernels, call_grid(): pl.pallas_call(kernel, grid=(steps,), out_shape=[(jax.ShapeDtypeStruct if...  19.9 us
    ppermute x18, starting transfers between devices, swap(): return lax.ppermute(x, axis, [(0, 1), (1, 0)])  18.9 us
    ppermute x6, starting transfers between devices, across_z(): lax.ppermute(part, 'zh', [(i, (i + step) % 4) for i in range(4)])  14.5 us
    all_to_all x2, starting transfers between devices, back_over_plane(): return lax.all_to_all(whole, ('y', 'x'), 0, 0)  10.1 us
    all_to_all x2, starting transfers between devices, across_plane(): parts = tied(lax.all_to_all(half, ('y', 'x'), 0, 0), *beside)  9.49 us
    ppermute x18, waiting for transfers between devices, swap(): return lax.ppermute(x, axis, [(0, 1), (1, 0)])  9.28 us
    all_to_all x2, waiting for transfers between devices, back_over_plane(): return lax.all_to_all(whole, ('y', 'x'), 0, 0)  8.95 us
  transfers between devices with their start and end apart: 28, of which 16 were waited for; matrix products, arithmetic and copies ran while one was open for 0% of the time, Pallas kernels for 30%

profile of v6, /device:TPU:1, one launch (start us, length us, event | category | flops | bytes accessed | tf_op | source)
XLA Modules:
  0.0 140.8 jit_solution(12399906035597777729)
XLA Ops:
  0.6 3.3 %collective-permute-start.1 = (bf16[512,256]{1,0:T(8,128)(2,1)}, bf16[512,256]{1,0:T(8,128)(2,1)S(1)}, u32[]{:S(2)}, u32[]{:S(2)}) collective-permute-start(bf16[512,256]{1,0:T(8,128)(2,1)} %w0.1), channel_id=1, source_target_pairs={{0,1},{1,0},{2,3},{3,2},{4,5},{5,4},{6,7},{7,6},{8,9},{9,8},{10,11... | collective-permute-start | bytes 786440 | tf_op jit(solution)/shard_map/ppermute | solution.py:31
  4.0 0.1 pad_add_fusion.at
  4.0 1.3 collective-permute-done.1.w1
  5.3 4.9 %prepare.1 = (bf16[256,512]{1,0:T(8,128)(2,1)}, bf16[256,512]{1,0:T(8,128)(2,1)}, bf16[2,256,512]{2,1,0:T(8,128)(2,1)}, bf16[512,2048]{1,0:T(8,128)(2,1)S(1)}, bf16[512,2048]{1,0:T(8,128)(2,1)}) custom-call(s32[2]{0:T(128)S(1)} %pad_add_fusion.at, bf16[256,2048]{1,0:T(8,128)(2,1)} %ctx.7, f32[512,2048]{1,0:T(8,128)} %bitcast.4), custom_call_target="tpu_custom_call" | custom-call | flops 4000000 | bytes 10485768 | tf_op jit(solution)/shard_map/prepare/pallas_call | solution.py:318
  10.2 0.4 collective-permute-start.5
  10.6 1.5 %collective-permute-done.w2 = bf16[512,256]{1,0:T(8,128)(2,1)S(1)} collective-permute-done((bf16[512,256]{1,0:T(8,128)(2,1)}, bf16[512,256]{1,0:T(8,128)(2,1)S(1)}, u32[]{:S(2)}, u32[]{:S(2)}) %collective-permute-start) | collective-permute-done | bytes 262176 | tf_op jit(solution)/shard_map/ppermute | solution.py:31
  12.0 0.9 collective-permute-start.6
  12.9 0.3 collective-permute-start.2
  13.2 0.9 collective-permute-done.6.w3
  14.1 2.4 %left.1 = (f32[16,16,1024]{2,1,0:T(8,128)S(1)}, bf16[16,16,1024]{2,1,0:T(8,128)(2,1)S(1)}) custom-call(s32[2]{0:T(128)S(1)} %pad_add_fusion.at, bf16[256,2048]{1,0:T(8,128)(2,1)S(1)} %copy-done.1, bf16[256,2048]{1,0:T(8,128)(2,1)S(1)} %copy-done, bf16[512,2048]{1,0:T(8,128)(2,1)S(1)} %get-tuple-element.45.low, bf16[512,256]{1,0:T(8,128)(2,1)S(1)} %copy-done.7, ...), custom_call_target="tpu_custom_call" | custom-call | flops 2000000000 | bytes 6815752 | tf_op jit(solution)/shard_map/left/pallas_call | solution.py:293
  16.5 0.5 collective-permute-start.7
  17.0 1.5 %collective-permute-done.7.got = bf16[16,16,1024]{2,1,0:T(8,128)(2,1)S(1)} collective-permute-done((bf16[16,16,1024]{2,1,0:T(8,128)(2,1)S(1)}, bf16[16,16,1024]{2,1,0:T(8,128)(2,1)S(1)}, u32[]{:S(2)}, u32[]{:S(2)}) %collective-permute-start.7) | collective-permute-done | bytes 524320 | tf_op jit(solution)/shard_map/ppermute | solution.py:31
  18.5 0.9 add.14
  19.4 5.8 %all-to-all-start = ((bf16[16,16,1024]{2,1,0:T(8,128)(2,1)}), bf16[16,16,1024]{2,1,0:T(8,128)(2,1)S(1)}, u32[]{:S(2)}, u32[]{:S(2)}) async-start(bf16[16,16,1024]{2,1,0:T(8,128)(2,1)} %add.14), calls=%async_computation | async-start | bytes 1048576 | tf_op jit(solution)/shard_map/all_to_all | solution.py:357
  25.2 5.9 %merge.1.merged = f32[512,2048]{1,0:T(8,128)} custom-call(f32[512,2048]{1,0:T(8,128)} %bitcast.5, bf16[256,512]{1,0:T(8,128)(2,1)S(1)} %copy-done.5, bf16[256,512]{1,0:T(8,128)(2,1)S(1)} %collective-permute-done.5.c1, bf16[256,2048]{1,0:T(8,128)(2,1)S(1)} %copy-done.1, bf16[256,2048]{1,0:T(8,128)(2,1)} %collective-permute-done.2.h1.g1), custom_call_target="tpu_custom_call" | custom-call | flops 1100000000 | bytes 11010048 | tf_op jit(solution)/shard_map/merge/pallas_call | solution.py:318
  31.1 4.9 %all-to-all-done.parts = bf16[16,16,1024]{2,1,0:T(8,128)(2,1)S(1)} async-done(((bf16[16,16,1024]{2,1,0:T(8,128)(2,1)}), bf16[16,16,1024]{2,1,0:T(8,128)(2,1)S(1)}, u32[]{:S(2)}, u32[]{:S(2)}) %all-to-all-start) | async-done | bytes 524320 | tf_op jit(solution)/shard_map/all_to_all | solution.py:357
  36.0 0.1 sum.2
  36.1 1.7 %collective-permute-done.4.h0.g2 = bf16[256,2048]{1,0:T(8,128)(2,1)} collective-permute-done((bf16[256,2048]{1,0:T(8,128)(2,1)S(1)}, bf16[256,2048]{1,0:T(8,128)(2,1)}, u32[]{:S(2)}, u32[]{:S(2)}) %collective-permute-start.4) | collective-permute-done | bytes 1048608 | tf_op jit(solution)/shard_map/ppermute | solution.py:31
  37.8 0.8 collective-permute-start.8
  38.6 0.1 collective-permute-start.10
  38.7 4.2 %grad.2.own = bf16[2,256,512]{2,1,0:T(8,128)(2,1)} custom-call(bf16[256,2048]{1,0:T(8,128)(2,1)} %og.3, bf16[256,2048]{1,0:T(8,128)(2,1)} %collective-permute-done.2.h1.g1, bf16[512,2048]{1,0:T(8,128)(2,1)} %weight_hbm.3), custom_call_target="tpu_custom_call" | custom-call | flops 1100000000 | bytes 4718592 | tf_op jit(solution)/shard_map/grad/pallas_call | solution.py:293
  42.9 5.2 %collective-permute-start.13 = (bf16[16,1024]{1,0:T(8,128)(2,1)S(1)}, bf16[16,1024]{1,0:T(8,128)(2,1)S(1)}, u32[]{:S(2)}, u32[]{:S(2)}) collective-permute-start(bf16[16,1024]{1,0:T(8,128)(2,1)S(1)} %add_convert_fusion.1.part), channel_id=1, source_target_pairs={{0,192},{64,0},{128,64},{192,128},{1,193},{65,1},{129,65},{193,129... | collective-permute-start | bytes 98312 | tf_op jit(solution)/shard_map/ppermute | solution.py:366
  48.1 1.2 collective-permute-start.12
  49.3 2.1 %collective-permute-start.11 = (bf16[16,1024]{1,0:T(8,128)(2,1)S(1)}, bf16[16,1024]{1,0:T(8,128)(2,1)S(1)}, u32[]{:S(2)}, u32[]{:S(2)}) collective-permute-start(bf16[16,1024]{1,0:T(8,128)(2,1)S(1)} %add_convert_fusion.1.part), channel_id=1, source_target_pairs={{0,64},{64,128},{128,192},{192,0},{1,65},{65,129},{129,193},{193,1... | collective-permute-start | bytes 98312 | tf_op jit(solution)/shard_map/ppermute | solution.py:366
  51.4 3.4 %collective-permute-done.12.opposite = bf16[16,1024]{1,0:T(8,128)(2,1)S(1)} collective-permute-done((bf16[16,1024]{1,0:T(8,128)(2,1)S(1)}, bf16[16,1024]{1,0:T(8,128)(2,1)S(1)}, u32[]{:S(2)}, u32[]{:S(2)}) %collective-permute-start.12) | collective-permute-done | bytes 32800 | tf_op jit(solution)/shard_map/ppermute | solution.py:366
  54.9 0.6 collective-permute-start.14
  55.5 0.8 spread.2
  56.4 6.5 %all-to-all-start.1 = ((bf16[16,16,1024]{2,1,0:T(8,128)(2,1)}), bf16[16,16,1024]{2,1,0:T(8,128)(2,1)S(1)}, u32[]{:S(2)}, u32[]{:S(2)}) async-start(bf16[16,16,1024]{2,1,0:T(8,128)(2,1)} %spread.2), calls=%async_computation.1 | async-start | bytes 1048576 | tf_op jit(solution)/shard_map/all_to_all | solution.py:378
  62.9 4.2 %grad.3 = bf16[2,256,512]{2,1,0:T(8,128)(2,1)} custom-call(bf16[256,2048]{1,0:T(8,128)(2,1)} %collective-permute-done.4.h0.g2, bf16[256,2048]{1,0:T(8,128)(2,1)} %collective-permute-done.8.h1.g3, bf16[512,2048]{1,0:T(8,128)(2,1)} %weight_hbm.3), custom_call_target="tpu_custom_call" | custom-call | flops 1100000000 | bytes 4718592 | tf_op jit(solution)/shard_map/grad/pallas_call | solution.py:293
  67.2 5.2 %all-to-all-done.1.mine = bf16[16,16,1024]{2,1,0:T(8,128)(2,1)S(1)} async-done(((bf16[16,16,1024]{2,1,0:T(8,128)(2,1)}), bf16[16,16,1024]{2,1,0:T(8,128)(2,1)S(1)}, u32[]{:S(2)}, u32[]{:S(2)}) %all-to-all-start.1) | async-done | bytes 524320 | tf_op jit(solution)/shard_map/all_to_all | solution.py:378
  72.3 3.1 %collective-permute-start.15 = (bf16[16,16,1024]{2,1,0:T(8,128)(2,1)S(1)}, bf16[16,16,1024]{2,1,0:T(8,128)(2,1)S(1)}, u32[]{:S(2)}, u32[]{:S(2)}) collective-permute-start(bf16[16,16,1024]{2,1,0:T(8,128)(2,1)S(1)} %all-to-all-done.1.mine), channel_id=1, source_target_pairs={{0,1},{1,0},{2,3},{3,2},{4,5},{5,4},{6,7},{7,6},{8,9},{9,8},{10,11... | collective-permute-start | bytes 1572872 | tf_op jit(solution)/shard_map/ppermute | solution.py:31
  75.4 0.5 early.1
  75.9 1.0 collective-permute-done.15.other
  77.0 4.4 %right.1 = (f32[16,16,1024]{2,1,0:T(8,128)S(1)}, bf16[16,16,1024]{2,1,0:T(8,128)(2,1)S(1)}, bf16[256,2048]{1,0:T(8,128)(2,1)S(1)}) custom-call(s32[2]{0:T(128)S(1)} %pad_add_fusion.at, bf16[256,2048]{1,0:T(8,128)(2,1)S(1)} %copy-done, bf16[256,2048]{1,0:T(8,128)(2,1)S(1)} %copy-done.2, bf16[512,2048]{1,0:T(8,128)(2,1)} %get-tuple-element.52.low_hbm, ...), custom_call_target="tpu_custom_call" | custom-call | flops 2000000000 | bytes 7995400 | tf_op jit(solution)/shard_map/right/pallas_call | solution.py:293
  81.4 0.5 collective-permute-start.16
  81.9 0.1 collective-permute-start.3
  82.0 0.9 collective-permute-start.9
  82.9 0.5 collective-permute-done.16.got
  83.4 0.9 add.15
  84.3 3.7 %all-to-all-start.2 = ((bf16[16,16,1024]{2,1,0:T(8,128)(2,1)}), bf16[16,16,1024]{2,1,0:T(8,128)(2,1)S(1)}, u32[]{:S(2)}, u32[]{:S(2)}) async-start(bf16[16,16,1024]{2,1,0:T(8,128)(2,1)} %add.15), calls=%async_computation.2 | async-start | bytes 1048576 | tf_op jit(solution)/shard_map/all_to_all | solution.py:357
  88.0 4.0 %gram.1.a_in = f32[256,512]{1,0:T(8,128)S(1)} custom-call(bf16[256,2048]{1,0:T(8,128)(2,1)S(1)} %get-tuple-element.63.left), custom_call_target="tpu_custom_call" | custom-call | flops 300000000 | bytes 1572864 | tf_op jit(solution)/shard_map/gram/pallas_call | solution.py:293
  92.0 3.1 %step.2.a_in = f32[256,512]{1,0:T(8,128)S(1)} custom-call(f32[256,512]{1,0:T(8,128)S(1)} %gram.1.a_in), custom_call_target="tpu_custom_call", output_to_operand_aliasing={{}: (0, {})} | custom-call | flops 300000000 | bytes 1048576 | tf_op jit(solution)/shard_map/step/pallas_call | solution.py:293
  95.1 3.9 %all-to-all-done.2.parts = bf16[16,16,1024]{2,1,0:T(8,128)(2,1)S(1)} async-done(((bf16[16,16,1024]{2,1,0:T(8,128)(2,1)}), bf16[16,16,1024]{2,1,0:T(8,128)(2,1)S(1)}, u32[]{:S(2)}, u32[]{:S(2)}) %all-to-all-start.2) | async-done | bytes 524320 | tf_op jit(solution)/shard_map/all_to_all | solution.py:357
  99.0 0.1 sum.3
  99.1 0.8 copy-done.8
  99.9 0.9 collective-permute-start.17
  100.7 1.8 %collective-permute-start.19 = (bf16[2,256,512]{2,1,0:T(8,128)(2,1)S(1)}, bf16[2,256,512]{2,1,0:T(8,128)(2,1)S(1)}, u32[]{:S(2)}, u32[]{:S(2)}) collective-permute-start(bf16[2,256,512]{2,1,0:T(8,128)(2,1)S(1)} %copy-done.4), channel_id=1, source_target_pairs={{0,1},{1,0},{2,3},{3,2},{4,5},{5,4},{6,7},{7,6},{8,9},{9,8},{10,11... | collective-permute-start | bytes 1572872 | tf_op jit(solution)/shard_map/ppermute | solution.py:31
  102.5 0.5 collective-permute-done.17
  103.0 2.7 %collective-permute-start.18 = (bf16[2,256,512]{2,1,0:T(8,128)(2,1)}, bf16[2,256,512]{2,1,0:T(8,128)(2,1)S(1)}, u32[]{:S(2)}, u32[]{:S(2)}) collective-permute-start(bf16[2,256,512]{2,1,0:T(8,128)(2,1)} %collective-permute-done.9.far), channel_id=1, source_target_pairs={{0,1},{1,0},{2,3},{3,2},{4,5},{5,4},{6,7},{7,6},{8,9},{9,8},{10,11... | collective-permute-start | bytes 1572872 | tf_op jit(solution)/shard_map/ppermute | solution.py:31
  105.7 1.3 collective-permute-start.22
  107.0 2.4 %collective-permute-start.21 = (bf16[16,1024]{1,0:T(8,128)(2,1)S(1)}, bf16[16,1024]{1,0:T(8,128)(2,1)S(1)}, u32[]{:S(2)}, u32[]{:S(2)}) collective-permute-start(bf16[16,1024]{1,0:T(8,128)(2,1)S(1)} %add_convert_fusion.part), channel_id=1, source_target_pairs={{0,128},{64,192},{128,0},{192,64},{1,129},{65,193},{129,1},{193,65... | collective-permute-start | bytes 98312 | tf_op jit(solution)/shard_map/ppermute | solution.py:366
  109.4 2.4 %collective-permute-start.20 = (bf16[16,1024]{1,0:T(8,128)(2,1)S(1)}, bf16[16,1024]{1,0:T(8,128)(2,1)S(1)}, u32[]{:S(2)}, u32[]{:S(2)}) collective-permute-start(bf16[16,1024]{1,0:T(8,128)(2,1)S(1)} %add_convert_fusion.part), channel_id=1, source_target_pairs={{0,64},{64,128},{128,192},{192,0},{1,65},{65,129},{129,193},{193,1... | collective-permute-start | bytes 98312 | tf_op jit(solution)/shard_map/ppermute | solution.py:366
  111.8 3.0 %step.3.a_in = f32[256,512]{1,0:T(8,128)S(1)} custom-call(f32[256,512]{1,0:T(8,128)S(1)} %step.2.a_in), custom_call_target="tpu_custom_call", output_to_operand_aliasing={{}: (0, {})} | custom-call | flops 300000000 | bytes 1048576 | tf_op jit(solution)/shard_map/step/pallas_call | solution.py:293
  114.8 0.5 collective-permute-done.20.one
  115.4 0.9 spread.3
  116.3 3.6 %all-to-all-start.3 = ((bf16[16,16,1024]{2,1,0:T(8,128)(2,1)}), bf16[16,16,1024]{2,1,0:T(8,128)(2,1)S(1)}, u32[]{:S(2)}, u32[]{:S(2)}) async-start(bf16[16,16,1024]{2,1,0:T(8,128)(2,1)} %spread.3), calls=%async_computation.3 | async-start | bytes 1048576 | tf_op jit(solution)/shard_map/all_to_all | solution.py:378
  119.9 3.6 %basis.1 = (f32[256,256]{1,0:T(8,128)S(1)}, bf16[512,256]{1,0:T(8,128)(2,1)S(1)}) custom-call(s32[2]{0:T(128)S(1)} %pad_add_fusion.at, f32[256,512]{1,0:T(8,128)S(1)} %step.3.a_in, bf16[256,2048]{1,0:T(8,128)(2,1)S(1)} %get-tuple-element.63.left), custom_call_target="tpu_custom_call" | custom-call | flops 300000000 | bytes 2097160 | tf_op jit(solution)/shard_map/basis/pallas_call | solution.py:293
  123.5 0.7 copy-done.6
  124.2 2.2 %place.1 = bf16[256,2048]{1,0:T(8,128)(2,1)} custom-call(s32[2]{0:T(128)S(1)} %pad_add_fusion.at, bf16[2,256,512]{2,1,0:T(8,128)(2,1)} %grad.2.own, bf16[2,256,512]{2,1,0:T(8,128)(2,1)} %copy-done.8, bf16[2,256,512]{2,1,0:T(8,128)(2,1)} %collective-permute-done.9.far, bf16[2,256,512]{2,1,0:T(8,128)(2,1)} %copy-done.9), custom_call_target="tpu_custom_call" | custom-call | flops 1000000 | bytes 3145736 | tf_op jit(solution)/shard_map/place/pallas_call | solution.py:318
  126.4 3.8 %all-to-all-done.3.chunks = bf16[16,16,1024]{2,1,0:T(8,128)(2,1)S(1)} async-done(((bf16[16,16,1024]{2,1,0:T(8,128)(2,1)}), bf16[16,16,1024]{2,1,0:T(8,128)(2,1)S(1)}, u32[]{:S(2)}, u32[]{:S(2)}) %all-to-all-start.3) | async-done | bytes 524320 | tf_op jit(solution)/shard_map/all_to_all | solution.py:378
  130.2 2.1 %collective-permute-start.23 = (bf16[16,16,1024]{2,1,0:T(8,128)(2,1)S(1)}, bf16[16,16,1024]{2,1,0:T(8,128)(2,1)S(1)}, u32[]{:S(2)}, u32[]{:S(2)}) collective-permute-start(bf16[16,16,1024]{2,1,0:T(8,128)(2,1)S(1)} %all-to-all-done.3.chunks), channel_id=1, source_target_pairs={{0,1},{1,0},{2,3},{3,2},{4,5},{5,4},{6,7},{7,6},{8,9},{9,8},{10,11... | collective-permute-start | bytes 1572872 | tf_op jit(solution)/shard_map/ppermute | solution.py:31
  132.3 1.2 begin.1
  133.5 0.3 collective-permute-done.23.other
  133.8 6.9 %last.1 = (f32[512,2048]{1,0:T(8,128)}, f32[512,256]{1,0:T(8,128)}) custom-call(s32[2]{0:T(128)S(1)} %pad_add_fusion.at, bf16[16,16,1024]{2,1,0:T(8,128)(2,1)S(1)} %collective-permute-done.23.other, f32[256,256]{1,0:T(8,128)S(1)} %get-tuple-element.70.inverse, bf16[512,256]{1,0:T(8,128)(2,1)} %copy-done.6, f32[256,2048]{1,0:T(8,128)S(1)} %get-tuple-element.71.begun, ...), custom_call_target="tpu_custom_call" | custom-call | flops 2000000000 | bytes 14680072 | tf_op jit(solution)/shard_map/last/pallas_call | solution.py:318
  (35 shorter events, 0.2 us)
Async XLA Ops:
  0.6 4.7 %collective-permute-start.1 = (bf16[512,256]{1,0:T(8,128)(2,1)}, bf16[512,256]{1,0:T(8,128)(2,1)S(1)}, u32[]{:S(2)}, u32[]{:S(2)}) collective-permute-start(bf16[512,256]{1,0:T(8,128)(2,1)} %w0.1), channel_id=1, source_target_pairs={{0,1},{1,0},{2,3},{3,2},{4,5},{5,4},{6,7},{7,6},{8,9},{9,8},{10,11... | collective-permute-start | bytes 786440 | tf_op jit(solution)/shard_map/ppermute | solution.py:31
  4.0 8.1 %collective-permute-start = (bf16[512,256]{1,0:T(8,128)(2,1)}, bf16[512,256]{1,0:T(8,128)(2,1)S(1)}, u32[]{:S(2)}, u32[]{:S(2)}) collective-permute-start(bf16[512,256]{1,0:T(8,128)(2,1)} %w0.1), channel_id=1, source_target_pairs={{0,2},{2,0},{1,3},{3,1},{4,6},{6,4},{5,7},{7,5},{8,10},{10,8},{9,1... | collective-permute-start | bytes 786440 | tf_op jit(solution)/shard_map/ppermute | solution.py:31
  5.3 7.6 %copy-start.1 = (bf16[256,2048]{1,0:T(8,128)(2,1)S(1)}, bf16[256,2048]{1,0:T(8,128)(2,1)}, u32[]{:S(2)}) copy-start(bf16[256,2048]{1,0:T(8,128)(2,1)} %og.3) | copy-start | bytes 3145732
  5.3 8.7 %copy-start = (bf16[256,2048]{1,0:T(8,128)(2,1)S(1)}, bf16[256,2048]{1,0:T(8,128)(2,1)}, u32[]{:S(2)}) copy-start(bf16[256,2048]{1,0:T(8,128)(2,1)} %ctx.7) | copy-start | bytes 3145732
  5.3 8.7 %copy-start.7 = (bf16[512,256]{1,0:T(8,128)(2,1)S(1)}, bf16[512,256]{1,0:T(8,128)(2,1)}, u32[]{:S(2)}) copy-start(bf16[512,256]{1,0:T(8,128)(2,1)} %w0.1) | copy-start | bytes 786436
  10.2 3.0 %collective-permute-start.5 = (bf16[256,512]{1,0:T(8,128)(2,1)}, bf16[256,512]{1,0:T(8,128)(2,1)S(1)}, u32[]{:S(2)}, u32[]{:S(2)}) collective-permute-start(bf16[256,512]{1,0:T(8,128)(2,1)} %get-tuple-element.44), channel_id=1, source_target_pairs={{0,1},{1,0},{2,3},{3,2},{4,5},{5,4},{6,7},{7,6},{8,9},{9,8},{10,11... | collective-permute-start | bytes 786440 | tf_op jit(solution)/shard_map/ppermute | solution.py:31
  12.0 2.0 %collective-permute-start.6 = (bf16[512,256]{1,0:T(8,128)(2,1)S(1)}, bf16[512,256]{1,0:T(8,128)(2,1)S(1)}, u32[]{:S(2)}, u32[]{:S(2)}) collective-permute-start(bf16[512,256]{1,0:T(8,128)(2,1)S(1)} %collective-permute-done.w2), channel_id=1, source_target_pairs={{0,1},{1,0},{2,3},{3,2},{4,5},{5,4},{6,7},{7,6},{8,9},{9,8},{10,11... | collective-permute-start | bytes 786440 | tf_op jit(solution)/shard_map/ppermute | solution.py:31
  12.9 24.9 %collective-permute-start.4 = (bf16[256,2048]{1,0:T(8,128)(2,1)S(1)}, bf16[256,2048]{1,0:T(8,128)(2,1)}, u32[]{:S(2)}, u32[]{:S(2)}) collective-permute-start(bf16[256,2048]{1,0:T(8,128)(2,1)S(1)} %copy-done.1), channel_id=1, source_target_pairs={{0,2},{2,0},{1,3},{3,1},{4,6},{6,4},{5,7},{7,5},{8,10},{10,8},{9,1... | collective-permute-start | bytes 3145736 | tf_op jit(solution)/shard_map/ppermute | solution.py:31
  12.9 12.3 %collective-permute-start.2 = (bf16[256,2048]{1,0:T(8,128)(2,1)S(1)}, bf16[256,2048]{1,0:T(8,128)(2,1)}, u32[]{:S(2)}, u32[]{:S(2)}) collective-permute-start(bf16[256,2048]{1,0:T(8,128)(2,1)S(1)} %copy-done.1), channel_id=1, source_target_pairs={{0,1},{1,0},{2,3},{3,2},{4,5},{5,4},{6,7},{7,6},{8,9},{9,8},{10,11... | collective-permute-start | bytes 3145736 | tf_op jit(solution)/shard_map/ppermute | solution.py:31
  16.5 8.7 %copy-start.5 = (bf16[256,512]{1,0:T(8,128)(2,1)S(1)}, bf16[256,512]{1,0:T(8,128)(2,1)}, u32[]{:S(2)}) copy-start(bf16[256,512]{1,0:T(8,128)(2,1)} %get-tuple-element.49.c0) | copy-start | bytes 786436
  16.5 2.0 %collective-permute-start.7 = (bf16[16,16,1024]{2,1,0:T(8,128)(2,1)S(1)}, bf16[16,16,1024]{2,1,0:T(8,128)(2,1)S(1)}, u32[]{:S(2)}, u32[]{:S(2)}) collective-permute-start(bf16[16,16,1024]{2,1,0:T(8,128)(2,1)S(1)} %get-tuple-element.48), channel_id=1, source_target_pairs={{0,1},{1,0},{2,3},{3,2},{4,5},{5,4},{6,7},{7,6},{8,9},{9,8},{10,11... | collective-permute-start | bytes 1572872 | tf_op jit(solution)/shard_map/ppermute | solution.py:31
  19.4 16.6 %all-to-all-start = ((bf16[16,16,1024]{2,1,0:T(8,128)(2,1)}), bf16[16,16,1024]{2,1,0:T(8,128)(2,1)S(1)}, u32[]{:S(2)}, u32[]{:S(2)}) async-start(bf16[16,16,1024]{2,1,0:T(8,128)(2,1)} %add.14), calls=%async_computation | async-start | bytes 1048576 | tf_op jit(solution)/shard_map/all_to_all | solution.py:357
  37.8 25.1 %collective-permute-start.8 = (bf16[256,2048]{1,0:T(8,128)(2,1)}, bf16[256,2048]{1,0:T(8,128)(2,1)}, u32[]{:S(2)}, u32[]{:S(2)}) collective-permute-start(bf16[256,2048]{1,0:T(8,128)(2,1)} %collective-permute-done.4.h0.g2), channel_id=1, source_target_pairs={{0,1},{1,0},{2,3},{3,2},{4,5},{5,4},{6,7},{7,6},{8,9},{9,8},{10,11... | collective-permute-start | bytes 3145736 | tf_op jit(solution)/shard_map/ppermute | solution.py:31
  38.6 4.3 %collective-permute-start.10 = (f32[16,1024]{1,0:T(8,128)S(1)}, f32[16,1024]{1,0:T(8,128)S(1)}, u32[]{:S(2)}, u32[]{:S(2)}) collective-permute-start(f32[16,1024]{1,0:T(8,128)S(1)} %sum.2), channel_id=1, source_target_pairs={{0,2},{2,0},{1,3},{3,1},{4,6},{6,4},{5,7},{7,5},{8,10},{10,8},{9,1... | collective-permute-start | bytes 196616 | tf_op jit(solution)/shard_map/ppermute | solution.py:31
  42.9 8.5 %collective-permute-start.13 = (bf16[16,1024]{1,0:T(8,128)(2,1)S(1)}, bf16[16,1024]{1,0:T(8,128)(2,1)S(1)}, u32[]{:S(2)}, u32[]{:S(2)}) collective-permute-start(bf16[16,1024]{1,0:T(8,128)(2,1)S(1)} %add_convert_fusion.1.part), channel_id=1, source_target_pairs={{0,192},{64,0},{128,64},{192,128},{1,193},{65,1},{129,65},{193,129... | collective-permute-start | bytes 98312 | tf_op jit(solution)/shard_map/ppermute | solution.py:366
  48.1 6.7 %collective-permute-start.12 = (bf16[16,1024]{1,0:T(8,128)(2,1)S(1)}, bf16[16,1024]{1,0:T(8,128)(2,1)S(1)}, u32[]{:S(2)}, u32[]{:S(2)}) collective-permute-start(bf16[16,1024]{1,0:T(8,128)(2,1)S(1)} %add_convert_fusion.1.part), channel_id=1, source_target_pairs={{0,128},{64,192},{128,0},{192,64},{1,129},{65,193},{129,1},{193,65... | collective-permute-start | bytes 98312 | tf_op jit(solution)/shard_map/ppermute | solution.py:366
  49.3 5.6 %collective-permute-start.11 = (bf16[16,1024]{1,0:T(8,128)(2,1)S(1)}, bf16[16,1024]{1,0:T(8,128)(2,1)S(1)}, u32[]{:S(2)}, u32[]{:S(2)}) collective-permute-start(bf16[16,1024]{1,0:T(8,128)(2,1)S(1)} %add_convert_fusion.1.part), channel_id=1, source_target_pairs={{0,64},{64,128},{128,192},{192,0},{1,65},{65,129},{129,193},{193,1... | collective-permute-start | bytes 98312 | tf_op jit(solution)/shard_map/ppermute | solution.py:366
  54.9 17.5 %collective-permute-start.14 = (bf16[2,256,512]{2,1,0:T(8,128)(2,1)}, bf16[2,256,512]{2,1,0:T(8,128)(2,1)S(1)}, u32[]{:S(2)}, u32[]{:S(2)}) collective-permute-start(bf16[2,256,512]{2,1,0:T(8,128)(2,1)} %get-tuple-element.58), channel_id=1, source_target_pairs={{0,2},{2,0},{1,3},{3,1},{4,6},{6,4},{5,7},{7,5},{8,10},{10,8},{9,1... | collective-permute-start | bytes 1572872 | tf_op jit(solution)/shard_map/ppermute | solution.py:31
  56.4 16.0 %all-to-all-start.1 = ((bf16[16,16,1024]{2,1,0:T(8,128)(2,1)}), bf16[16,16,1024]{2,1,0:T(8,128)(2,1)S(1)}, u32[]{:S(2)}, u32[]{:S(2)}) async-start(bf16[16,16,1024]{2,1,0:T(8,128)(2,1)} %spread.2), calls=%async_computation.1 | async-start | bytes 1048576 | tf_op jit(solution)/shard_map/all_to_all | solution.py:378
  62.9 14.1 %copy-start.2 = (bf16[256,2048]{1,0:T(8,128)(2,1)S(1)}, bf16[256,2048]{1,0:T(8,128)(2,1)}, u32[]{:S(2)}) copy-start(bf16[256,2048]{1,0:T(8,128)(2,1)} %og.3) | copy-start | bytes 3145732
  72.3 4.6 %copy-start.3 = (bf16[2,256,512]{2,1,0:T(8,128)(2,1)}, bf16[2,256,512]{2,1,0:T(8,128)(2,1)S(1)}, u32[]{:S(2)}) copy-start(bf16[2,256,512]{2,1,0:T(8,128)(2,1)S(1)} %collective-permute-done.14.c2) | copy-start | bytes 1572868
  72.3 4.6 %collective-permute-start.15 = (bf16[16,16,1024]{2,1,0:T(8,128)(2,1)S(1)}, bf16[16,16,1024]{2,1,0:T(8,128)(2,1)S(1)}, u32[]{:S(2)}, u32[]{:S(2)}) collective-permute-start(bf16[16,16,1024]{2,1,0:T(8,128)(2,1)S(1)} %all-to-all-done.1.mine), channel_id=1, source_target_pairs={{0,1},{1,0},{2,3},{3,2},{4,5},{5,4},{6,7},{7,6},{8,9},{9,8},{10,11... | collective-permute-start | bytes 1572872 | tf_op jit(solution)/shard_map/ppermute | solution.py:31
  81.4 2.0 %collective-permute-start.16 = (bf16[16,16,1024]{2,1,0:T(8,128)(2,1)S(1)}, bf16[16,16,1024]{2,1,0:T(8,128)(2,1)S(1)}, u32[]{:S(2)}, u32[]{:S(2)}) collective-permute-start(bf16[16,16,1024]{2,1,0:T(8,128)(2,1)S(1)} %get-tuple-element.62), channel_id=1, source_target_pairs={{0,1},{1,0},{2,3},{3,2},{4,5},{5,4},{6,7},{7,6},{8,9},{9,8},{10,11... | collective-permute-start | bytes 1572872 | tf_op jit(solution)/shard_map/ppermute | solution.py:31
  81.9 17.2 %collective-permute-start.3 = (bf16[2,256,512]{2,1,0:T(8,128)(2,1)}, bf16[2,256,512]{2,1,0:T(8,128)(2,1)S(1)}, u32[]{:S(2)}, u32[]{:S(2)}) collective-permute-start(bf16[2,256,512]{2,1,0:T(8,128)(2,1)} %grad.2.own), channel_id=1, source_target_pairs={{0,1},{1,0},{2,3},{3,2},{4,5},{5,4},{6,7},{7,6},{8,9},{9,8},{10,11... | collective-permute-start | bytes 1572872 | tf_op jit(solution)/shard_map/ppermute | solution.py:31
  82.0 17.1 %collective-permute-start.9 = (bf16[2,256,512]{2,1,0:T(8,128)(2,1)}, bf16[2,256,512]{2,1,0:T(8,128)(2,1)}, u32[]{:S(2)}, u32[]{:S(2)}) collective-permute-start(bf16[2,256,512]{2,1,0:T(8,128)(2,1)} %grad.3), channel_id=1, source_target_pairs={{0,2},{2,0},{1,3},{3,1},{4,6},{6,4},{5,7},{7,5},{8,10},{10,8},{9,1... | collective-permute-start | bytes 1572872 | tf_op jit(solution)/shard_map/ppermute | solution.py:31
  84.3 16.4 %copy-start.4 = (bf16[2,256,512]{2,1,0:T(8,128)(2,1)S(1)}, bf16[2,256,512]{2,1,0:T(8,128)(2,1)}, u32[]{:S(2)}) copy-start(bf16[2,256,512]{2,1,0:T(8,128)(2,1)} %copy-done.3) | copy-start | bytes 1572868
  84.3 14.7 %all-to-all-start.2 = ((bf16[16,16,1024]{2,1,0:T(8,128)(2,1)}), bf16[16,16,1024]{2,1,0:T(8,128)(2,1)S(1)}, u32[]{:S(2)}, u32[]{:S(2)}) async-start(bf16[16,16,1024]{2,1,0:T(8,128)(2,1)} %add.15), calls=%async_computation.2 | async-start | bytes 1048576 | tf_op jit(solution)/shard_map/all_to_all | solution.py:357
  99.1 0.8 copy-start.8
  99.9 3.1 %collective-permute-start.17 = (f32[16,1024]{1,0:T(8,128)S(1)}, f32[16,1024]{1,0:T(8,128)S(1)}, u32[]{:S(2)}, u32[]{:S(2)}) collective-permute-start(f32[16,1024]{1,0:T(8,128)S(1)} %sum.3), channel_id=1, source_target_pairs={{0,2},{2,0},{1,3},{3,1},{4,6},{6,4},{5,7},{7,5},{8,10},{10,8},{9,1... | collective-permute-start | bytes 196616 | tf_op jit(solution)/shard_map/ppermute | solution.py:31
  100.7 14.1 %collective-permute-start.19 = (bf16[2,256,512]{2,1,0:T(8,128)(2,1)S(1)}, bf16[2,256,512]{2,1,0:T(8,128)(2,1)S(1)}, u32[]{:S(2)}, u32[]{:S(2)}) collective-permute-start(bf16[2,256,512]{2,1,0:T(8,128)(2,1)S(1)} %copy-done.4), channel_id=1, source_target_pairs={{0,1},{1,0},{2,3},{3,2},{4,5},{5,4},{6,7},{7,6},{8,9},{9,8},{10,11... | collective-permute-start | bytes 1572872 | tf_op jit(solution)/shard_map/ppermute | solution.py:31
  103.0 11.8 %collective-permute-start.18 = (bf16[2,256,512]{2,1,0:T(8,128)(2,1)}, bf16[2,256,512]{2,1,0:T(8,128)(2,1)S(1)}, u32[]{:S(2)}, u32[]{:S(2)}) collective-permute-start(bf16[2,256,512]{2,1,0:T(8,128)(2,1)} %collective-permute-done.9.far), channel_id=1, source_target_pairs={{0,1},{1,0},{2,3},{3,2},{4,5},{5,4},{6,7},{7,6},{8,9},{9,8},{10,11... | collective-permute-start | bytes 1572872 | tf_op jit(solution)/shard_map/ppermute | solution.py:31
  105.7 9.1 %collective-permute-start.22 = (bf16[16,1024]{1,0:T(8,128)(2,1)S(1)}, bf16[16,1024]{1,0:T(8,128)(2,1)S(1)}, u32[]{:S(2)}, u32[]{:S(2)}) collective-permute-start(bf16[16,1024]{1,0:T(8,128)(2,1)S(1)} %add_convert_fusion.part), channel_id=1, source_target_pairs={{0,192},{64,0},{128,64},{192,128},{1,193},{65,1},{129,65},{193,129... | collective-permute-start | bytes 98312 | tf_op jit(solution)/shard_map/ppermute | solution.py:366
  107.0 7.8 %collective-permute-start.21 = (bf16[16,1024]{1,0:T(8,128)(2,1)S(1)}, bf16[16,1024]{1,0:T(8,128)(2,1)S(1)}, u32[]{:S(2)}, u32[]{:S(2)}) collective-permute-start(bf16[16,1024]{1,0:T(8,128)(2,1)S(1)} %add_convert_fusion.part), channel_id=1, source_target_pairs={{0,128},{64,192},{128,0},{192,64},{1,129},{65,193},{129,1},{193,65... | collective-permute-start | bytes 98312 | tf_op jit(solution)/shard_map/ppermute | solution.py:366
  109.4 6.0 %collective-permute-start.20 = (bf16[16,1024]{1,0:T(8,128)(2,1)S(1)}, bf16[16,1024]{1,0:T(8,128)(2,1)S(1)}, u32[]{:S(2)}, u32[]{:S(2)}) collective-permute-start(bf16[16,1024]{1,0:T(8,128)(2,1)S(1)} %add_convert_fusion.part), channel_id=1, source_target_pairs={{0,64},{64,128},{128,192},{192,0},{1,65},{65,129},{129,193},{193,1... | collective-permute-start | bytes 98312 | tf_op jit(solution)/shard_map/ppermute | solution.py:366
  114.8 1.5 %copy-start.9 = (bf16[2,256,512]{2,1,0:T(8,128)(2,1)}, bf16[2,256,512]{2,1,0:T(8,128)(2,1)S(1)}, u32[]{:S(2)}) copy-start(bf16[2,256,512]{2,1,0:T(8,128)(2,1)S(1)} %collective-permute-done.18.diag) | copy-start | bytes 1572868
  116.3 13.9 %all-to-all-start.3 = ((bf16[16,16,1024]{2,1,0:T(8,128)(2,1)}), bf16[16,16,1024]{2,1,0:T(8,128)(2,1)S(1)}, u32[]{:S(2)}, u32[]{:S(2)}) async-start(bf16[16,16,1024]{2,1,0:T(8,128)(2,1)} %spread.3), calls=%async_computation.3 | async-start | bytes 1048576 | tf_op jit(solution)/shard_map/all_to_all | solution.py:378
  123.4 0.7 copy-start.6
  130.2 3.7 %collective-permute-start.23 = (bf16[16,16,1024]{2,1,0:T(8,128)(2,1)S(1)}, bf16[16,16,1024]{2,1,0:T(8,128)(2,1)S(1)}, u32[]{:S(2)}, u32[]{:S(2)}) collective-permute-start(bf16[16,16,1024]{2,1,0:T(8,128)(2,1)S(1)} %all-to-all-done.3.chunks), channel_id=1, source_target_pairs={{0,1},{1,0},{2,3},{3,2},{4,5},{5,4},{6,7},{7,6},{8,9},{9,8},{10,11... | collective-permute-start | bytes 1572872 | tf_op jit(solution)/shard_map/ppermute | solution.py:31

commit v7 on v6

--- a/solution.py
+++ b/solution.py
@@ -128,15 +128,13 @@
     out[...] = (keep[...] + got[...].astype(F32)).astype(BF16)
 
 
-def sum_kernel(parts, out):
-    out[...] = parts[...].astype(F32).sum(0)
-
-
-def spread_kernel(part, one, opposite, three, out):
-    part, one, opposite, three = (x[...].astype(F32) for x in (part, one, opposite, three))
-    whole = ((part + opposite) + (one + three)).astype(BF16)
-    for n in range(CHUNKS):
-        out[n] = whole
+def spread_kernel(parts, out):
+    total = parts[0].astype(F32)
+    for n in range(1, parts.shape[0]):
+        total += parts[n].astype(F32)
+    total = total.astype(BF16)
+    for n in range(out.shape[0]):
+        out[n] = total
 
 
 def row_of(x, k):
@@ -351,31 +349,24 @@
     return lax.optimization_barrier((x,) + others)[0]
 
 
+def spread(parts, times):
+    (out,) = call(spread_kernel, [((times,) + CHUNK, BF16)], (parts,), 1_000_000, "spread")
+    return out
+
+
 def across_plane(keep, send, beside=()):
     got = swap(send, "core")
     (half,) = call(add_kernel, [(CHUNKED, BF16)], (keep, got), 1_000_000, "add")
     parts = tied(lax.all_to_all(half, ("y", "x"), 0, 0), *beside)
-    (part,) = call(sum_kernel, [(CHUNK, F32)], (parts,), 1_000_000, "sum")
-    return part
-
-
-def across_z(part, beside=()):
-    far = tied(swap(part, "zl"), *beside)
-    part = (part + far).astype(BF16)
-    return (part,) + tuple(
-        lax.ppermute(part, "zh", [(i, (i + step) % 4) for i in range(4)]) for step in (1, 2, 3)
-    )
-
-
-def back_over_plane(part, one, opposite, three, beside=()):
-    (whole,) = call(
-        spread_kernel,
-        [(CHUNKED, BF16)],
-        (tied(part, *beside), one, opposite, three),
-        1_000_000,
-        "spread",
-    )
-    return lax.all_to_all(whole, ("y", "x"), 0, 0)
+    return spread(parts, 8)
+
+
+def across_z(copies, beside=()):
+    return tied(lax.all_to_all(copies, ("zh", "zl"), 0, 0), *beside)
+
+
+def back_over_plane(parts, beside=()):
+    return lax.all_to_all(spread(tied(parts, *beside), CHUNKS), ("y", "x"), 0, 0)
 
 
 def on_device(context, out_grad, weight, error, warm):
@@ -447,8 +438,8 @@
 
     i_home = grad(out_grad, g_near)
     zs = across_z(tied(part, g_far), (i_home,))
-    c_far = swap(tied(c_far, *zs[1:]), "zl")
-    mine = back_over_plane(*zs)
+    c_far = swap(tied(c_far, zs), "zl")
+    mine = back_over_plane(zs)
 
     i_far = grad(g_far, g_diag)
     other = swap(tied(mine, i_far, c_far), "core")
@@ -482,12 +473,12 @@
     part = across_plane(keep, send, (a,))
     part = tied(part, i_far, i_near)
     c_diag = swap(c_far, "core")
-    zs = across_z(part)
-    i_diag = swap(tied(i_far, zs[0]), "core")
+    i_diag = swap(tied(i_far, part), "core")
     (a,) = call(
         functools.partial(step_kernel, 2 * PART), [table], (a,), 300_000_000, "step", alias={0: 0}
     )
-    mine = back_over_plane(*zs, beside=(a, c_diag, i_diag))
+    zs = across_z(part, (a,))
+    mine = back_over_plane(zs)
     first = pl.BlockSpec((None, TOK, ROWS), lambda j: (0, 0, 0))
     second = pl.BlockSpec((None, TOK, ROWS), lambda j: (1, 0, 0))
     (in_grad,) = call_grid(

time: 142 us -> 142 us (level)
  starting transfers between devices: 53 us -> 48.8 us
  waiting for transfers between devices: 31.1 us -> 35 us
    ppermute x6 -> x0, starting transfers between devices: 14.5 us -> none  [across_z(): lax.ppermute(part, 'zh', [(i, (i + step) % 4) for i in range(4)])]
    all_to_all x2 -> x4, starting transfers between devices: 10.1 us -> 20.7 us  [the longest x2 10.7 us: across_z(): return tied(lax.all_to_all(copies, ('zh', 'zl'), 0, 0), *beside)]
    all_to_all x2 -> x4, waiting for transfers between devices: 8.95 us -> 18.8 us  [the longest x2 12.8 us: across_z(): return tied(lax.all_to_all(copies, ('zh', 'zl'), 0, 0), *beside)]
    ppermute x6 -> x0, waiting for transfers between devices: 4.03 us -> none  [across_z(): lax.ppermute(part, 'zh', [(i, (i + step) % 4) for i in range(4)])]
    ppermute x18 -> x16, waiting for transfers between devices: 9.28 us -> 7.55 us  [swap(): return lax.ppermute(x, axis, [(0, 1), (1, 0)])]
    pallas_call x16, Pallas kernels: 34.2 us -> 35.7 us  [call(): pl.pallas_call(kernel, out_shape=[(pltpu.HBM if free else jax.ShapeDtypeS...]
    ppermute x18 -> x16, starting transfers between devices: 18.9 us -> 18.8 us  [swap(): return lax.ppermute(x, axis, [(0, 1), (1, 0)])]
  transfers between devices with their start and end apart: 28 -> 22, of which waited for: 16 -> 12; matrix products, arithmetic and copies ran while one was open for 0% -> 0% of each run, Pallas kernels for 30% -> 31%
where the time goes in v7:
time: 142 us; the launch traced here: 141 us
  Pallas kernels  55.6 us (39%)
  starting transfers between devices  48.8 us (34%)
  waiting for transfers between devices  35 us (25%)
    pallas_call x16, Pallas kernels, call(): pl.pallas_call(kernel, out_shape=[(pltpu.HBM if free else jax.ShapeDtypeS...  35.7 us
    pallas_call x4, Pallas kernels, call_grid(): pl.pallas_call(kernel, grid=(steps,), out_shape=[(jax.ShapeDtypeStruct if...  19.9 us
    ppermute x16, starting transfers between devices, swap(): return lax.ppermute(x, axis, [(0, 1), (1, 0)])  18.8 us
    all_to_all x2, waiting for transfers between devices, across_z(): return tied(lax.all_to_all(copies, ('zh', 'zl'), 0, 0), *beside)  12.8 us
    all_to_all x2, starting transfers between devices, across_z(): return tied(lax.all_to_all(copies, ('zh', 'zl'), 0, 0), *beside)  10.7 us
    all_to_all x2, starting transfers between devices, back_over_plane(): lax.all_to_all(spread(tied(parts, *beside), CHUNKS), ('y', 'x'), 0, 0)  9.95 us
    all_to_all x2, starting transfers between devices, across_plane(): parts = tied(lax.all_to_all(half, ('y', 'x'), 0, 0), *beside)  9.36 us
    all_to_all x2, waiting for transfers between devices, across_plane(): parts = tied(lax.all_to_all(half, ('y', 'x'), 0, 0), *beside)  8.57 us
  transfers between devices with their start and end apart: 22, of which 12 were waited for; matrix products, arithmetic and copies ran while one was open for 0% of the time, Pallas kernels for 31%

profile of v7, /device:TPU:1, one launch (start us, length us, event | category | flops | bytes accessed | tf_op | source)
XLA Modules:
  0.0 140.9 jit_solution(3586119547661754765)
XLA Ops:
  0.6 3.3 %collective-permute-start.1 = (bf16[512,256]{1,0:T(8,128)(2,1)}, bf16[512,256]{1,0:T(8,128)(2,1)S(1)}, u32[]{:S(2)}, u32[]{:S(2)}) collective-permute-start(bf16[512,256]{1,0:T(8,128)(2,1)} %w0.1), channel_id=1, source_target_pairs={{0,1},{1,0},{2,3},{3,2},{4,5},{5,4},{6,7},{7,6},{8,9},{9,8},{10,11... | collective-permute-start | bytes 786440 | tf_op jit(solution)/shard_map/ppermute | solution.py:31
  4.0 0.0 collective-permute-start
  4.0 0.1 pad_add_fusion.at
  4.0 1.3 collective-permute-done.1.w1
  5.3 4.9 %prepare.1 = (bf16[256,512]{1,0:T(8,128)(2,1)}, bf16[256,512]{1,0:T(8,128)(2,1)}, bf16[2,256,512]{2,1,0:T(8,128)(2,1)}, bf16[512,2048]{1,0:T(8,128)(2,1)S(1)}, bf16[512,2048]{1,0:T(8,128)(2,1)}) custom-call(s32[2]{0:T(128)S(1)} %pad_add_fusion.at, bf16[256,2048]{1,0:T(8,128)(2,1)} %ctx.7, f32[512,2048]{1,0:T(8,128)} %bitcast.4), custom_call_target="tpu_custom_call" | custom-call | flops 4000000 | bytes 10485768 | tf_op jit(solution)/shard_map/prepare/pallas_call | solution.py:316
  10.2 0.4 collective-permute-start.5
  10.6 1.5 %collective-permute-done.w2 = bf16[512,256]{1,0:T(8,128)(2,1)S(1)} collective-permute-done((bf16[512,256]{1,0:T(8,128)(2,1)}, bf16[512,256]{1,0:T(8,128)(2,1)S(1)}, u32[]{:S(2)}, u32[]{:S(2)}) %collective-permute-start) | collective-permute-done | bytes 262176 | tf_op jit(solution)/shard_map/ppermute | solution.py:31
  12.0 0.9 collective-permute-start.6
  12.9 0.0 collective-permute-start.4
  12.9 0.3 collective-permute-start.2
  13.2 0.0 collective-permute-done.5.c1
  13.2 0.9 collective-permute-done.6.w3
  14.1 2.4 %left.1 = (f32[16,16,1024]{2,1,0:T(8,128)S(1)}, bf16[16,16,1024]{2,1,0:T(8,128)(2,1)S(1)}) custom-call(s32[2]{0:T(128)S(1)} %pad_add_fusion.at, bf16[256,2048]{1,0:T(8,128)(2,1)S(1)} %copy-done.1, bf16[256,2048]{1,0:T(8,128)(2,1)S(1)} %copy-done, bf16[512,2048]{1,0:T(8,128)(2,1)S(1)} %get-tuple-element.45.low, bf16[512,256]{1,0:T(8,128)(2,1)S(1)} %copy-done.7, ...), custom_call_target="tpu_custom_call" | custom-call | flops 2000000000 | bytes 6815752 | tf_op jit(solution)/shard_map/left/pallas_call | solution.py:291
  16.5 0.0 copy-start.5
  16.5 0.5 collective-permute-start.7
  17.0 1.5 %collective-permute-done.7.got = bf16[16,16,1024]{2,1,0:T(8,128)(2,1)S(1)} collective-permute-done((bf16[16,16,1024]{2,1,0:T(8,128)(2,1)S(1)}, bf16[16,16,1024]{2,1,0:T(8,128)(2,1)S(1)}, u32[]{:S(2)}, u32[]{:S(2)}) %collective-permute-start.7) | collective-permute-done | bytes 524320 | tf_op jit(solution)/shard_map/ppermute | solution.py:31
  18.5 0.9 add.4
  19.4 5.8 %all-to-all-start = ((bf16[16,16,1024]{2,1,0:T(8,128)(2,1)}), bf16[16,16,1024]{2,1,0:T(8,128)(2,1)S(1)}, u32[]{:S(2)}, u32[]{:S(2)}) async-start(bf16[16,16,1024]{2,1,0:T(8,128)(2,1)} %add.4), calls=%async_computation | async-start | bytes 1048576 | tf_op jit(solution)/shard_map/all_to_all | solution.py:360
  25.2 0.0 collective-permute-done.2.h1.g1
  25.2 5.9 %merge.1.merged = f32[512,2048]{1,0:T(8,128)} custom-call(f32[512,2048]{1,0:T(8,128)} %bitcast.5, bf16[256,512]{1,0:T(8,128)(2,1)S(1)} %copy-done.5, bf16[256,512]{1,0:T(8,128)(2,1)S(1)} %collective-permute-done.5.c1, bf16[256,2048]{1,0:T(8,128)(2,1)S(1)} %copy-done.1, bf16[256,2048]{1,0:T(8,128)(2,1)} %collective-permute-done.2.h1.g1), custom_call_target="tpu_custom_call" | custom-call | flops 1100000000 | bytes 11010048 | tf_op jit(solution)/shard_map/merge/pallas_call | solution.py:316
  31.1 4.9 %all-to-all-done.parts = bf16[16,16,1024]{2,1,0:T(8,128)(2,1)S(1)} async-done(((bf16[16,16,1024]{2,1,0:T(8,128)(2,1)}), bf16[16,16,1024]{2,1,0:T(8,128)(2,1)S(1)}, u32[]{:S(2)}, u32[]{:S(2)}) %all-to-all-start) | async-done | bytes 524320 | tf_op jit(solution)/shard_map/all_to_all | solution.py:360
  36.0 0.8 spread.4
  36.8 1.0 collective-permute-done.4.h0.g2
  37.8 0.8 collective-permute-start.8
  38.6 7.3 %all-to-all-start.1 = ((bf16[8,16,1024]{2,1,0:T(8,128)(2,1)}), bf16[8,16,1024]{2,1,0:T(8,128)(2,1)S(1)}, u32[]{:S(2)}, u32[]{:S(2)}) async-start(bf16[8,16,1024]{2,1,0:T(8,128)(2,1)} %spread.4), calls=%async_computation.1 | async-start | bytes 524288 | tf_op jit(solution)/shard_map/all_to_all | solution.py:365
  45.9 4.2 %grad.2.own = bf16[2,256,512]{2,1,0:T(8,128)(2,1)} custom-call(bf16[256,2048]{1,0:T(8,128)(2,1)} %og.3, bf16[256,2048]{1,0:T(8,128)(2,1)} %collective-permute-done.2.h1.g1, bf16[512,2048]{1,0:T(8,128)(2,1)} %weight_hbm.3), custom_call_target="tpu_custom_call" | custom-call | flops 1100000000 | bytes 4718592 | tf_op jit(solution)/shard_map/grad/pallas_call | solution.py:291
  50.0 8.2 %all-to-all-done.1.parts = bf16[8,16,1024]{2,1,0:T(8,128)(2,1)S(1)} async-done(((bf16[8,16,1024]{2,1,0:T(8,128)(2,1)}), bf16[8,16,1024]{2,1,0:T(8,128)(2,1)S(1)}, u32[]{:S(2)}, u32[]{:S(2)}) %all-to-all-start.1) | async-done | bytes 262176 | tf_op jit(solution)/shard_map/all_to_all | solution.py:365
  58.2 0.0 collective-permute-start.10
  58.3 0.9 spread.5
  59.1 5.9 %all-to-all-start.2 = ((bf16[16,16,1024]{2,1,0:T(8,128)(2,1)}), bf16[16,16,1024]{2,1,0:T(8,128)(2,1)S(1)}, u32[]{:S(2)}, u32[]{:S(2)}) async-start(bf16[16,16,1024]{2,1,0:T(8,128)(2,1)} %spread.5), calls=%async_computation.2 | async-start | bytes 1048576 | tf_op jit(solution)/shard_map/all_to_all | solution.py:369
  65.0 0.0 copy-start.2
  65.1 0.0 collective-permute-done.8.h1.g3
  65.1 4.2 %grad.3 = bf16[2,256,512]{2,1,0:T(8,128)(2,1)} custom-call(bf16[256,2048]{1,0:T(8,128)(2,1)} %collective-permute-done.4.h0.g2, bf16[256,2048]{1,0:T(8,128)(2,1)} %collective-permute-done.8.h1.g3, bf16[512,2048]{1,0:T(8,128)(2,1)} %weight_hbm.3), custom_call_target="tpu_custom_call" | custom-call | flops 1100000000 | bytes 4718592 | tf_op jit(solution)/shard_map/grad/pallas_call | solution.py:291
  69.3 6.0 %all-to-all-done.2.mine = bf16[16,16,1024]{2,1,0:T(8,128)(2,1)S(1)} async-done(((bf16[16,16,1024]{2,1,0:T(8,128)(2,1)}), bf16[16,16,1024]{2,1,0:T(8,128)(2,1)S(1)}, u32[]{:S(2)}, u32[]{:S(2)}) %all-to-all-start.2) | async-done | bytes 524320 | tf_op jit(solution)/shard_map/all_to_all | solution.py:369
  75.3 0.0 collective-permute-done.10.c2
  75.4 2.2 %collective-permute-start.11 = (bf16[16,16,1024]{2,1,0:T(8,128)(2,1)S(1)}, bf16[16,16,1024]{2,1,0:T(8,128)(2,1)S(1)}, u32[]{:S(2)}, u32[]{:S(2)}) collective-permute-start(bf16[16,16,1024]{2,1,0:T(8,128)(2,1)S(1)} %all-to-all-done.2.mine), channel_id=1, source_target_pairs={{0,1},{1,0},{2,3},{3,2},{4,5},{5,4},{6,7},{7,6},{8,9},{9,8},{10,11... | collective-permute-start | bytes 1572872 | tf_op jit(solution)/shard_map/ppermute | solution.py:31
  77.5 0.5 early.1
  78.0 1.0 collective-permute-done.11.other
  79.1 4.4 %right.1 = (f32[16,16,1024]{2,1,0:T(8,128)S(1)}, bf16[16,16,1024]{2,1,0:T(8,128)(2,1)S(1)}, bf16[256,2048]{1,0:T(8,128)(2,1)S(1)}) custom-call(s32[2]{0:T(128)S(1)} %pad_add_fusion.at, bf16[256,2048]{1,0:T(8,128)(2,1)S(1)} %copy-done, bf16[256,2048]{1,0:T(8,128)(2,1)S(1)} %copy-done.2, bf16[512,2048]{1,0:T(8,128)(2,1)} %get-tuple-element.52.low_hbm, ...), custom_call_target="tpu_custom_call" | custom-call | flops 2000000000 | bytes 7995400 | tf_op jit(solution)/shard_map/right/pallas_call | solution.py:291
  83.5 0.5 collective-permute-start.12
  84.0 0.1 collective-permute-start.3
  84.1 1.5 %collective-permute-start.9 = (bf16[2,256,512]{2,1,0:T(8,128)(2,1)}, bf16[2,256,512]{2,1,0:T(8,128)(2,1)}, u32[]{:S(2)}, u32[]{:S(2)}) collective-permute-start(bf16[2,256,512]{2,1,0:T(8,128)(2,1)} %grad.3), channel_id=1, source_target_pairs={{0,2},{2,0},{1,3},{3,1},{4,6},{6,4},{5,7},{7,5},{8,10},{10,8},{9,1... | collective-permute-start | bytes 1572872 | tf_op jit(solution)/shard_map/ppermute | solution.py:31
  85.6 0.0 collective-permute-done.12.got
  85.6 0.9 add.5
  86.5 3.6 %all-to-all-start.3 = ((bf16[16,16,1024]{2,1,0:T(8,128)(2,1)}), bf16[16,16,1024]{2,1,0:T(8,128)(2,1)S(1)}, u32[]{:S(2)}, u32[]{:S(2)}) async-start(bf16[16,16,1024]{2,1,0:T(8,128)(2,1)} %add.5), calls=%async_computation.3 | async-start | bytes 1048576 | tf_op jit(solution)/shard_map/all_to_all | solution.py:360
  90.1 4.0 %gram.1.a_in = f32[256,512]{1,0:T(8,128)S(1)} custom-call(bf16[256,2048]{1,0:T(8,128)(2,1)S(1)} %get-tuple-element.63.left), custom_call_target="tpu_custom_call" | custom-call | flops 300000000 | bytes 1572864 | tf_op jit(solution)/shard_map/gram/pallas_call | solution.py:291
  94.0 3.1 %step.2.a_in = f32[256,512]{1,0:T(8,128)S(1)} custom-call(f32[256,512]{1,0:T(8,128)S(1)} %gram.1.a_in), custom_call_target="tpu_custom_call", output_to_operand_aliasing={{}: (0, {})} | custom-call | flops 300000000 | bytes 1048576 | tf_op jit(solution)/shard_map/step/pallas_call | solution.py:291
  97.1 3.6 %all-to-all-done.3.parts = bf16[16,16,1024]{2,1,0:T(8,128)(2,1)S(1)} async-done(((bf16[16,16,1024]{2,1,0:T(8,128)(2,1)}), bf16[16,16,1024]{2,1,0:T(8,128)(2,1)S(1)}, u32[]{:S(2)}, u32[]{:S(2)}) %all-to-all-start.3) | async-done | bytes 524320 | tf_op jit(solution)/shard_map/all_to_all | solution.py:360
  100.7 0.8 spread.6
  101.6 3.4 %all-to-all-start.4 = ((bf16[8,16,1024]{2,1,0:T(8,128)(2,1)}), bf16[8,16,1024]{2,1,0:T(8,128)(2,1)S(1)}, u32[]{:S(2)}, u32[]{:S(2)}) async-start(bf16[8,16,1024]{2,1,0:T(8,128)(2,1)} %spread.6), calls=%async_computation.4 | async-start | bytes 524288 | tf_op jit(solution)/shard_map/all_to_all | solution.py:365
  105.0 1.9 %collective-permute-start.13 = (bf16[2,256,512]{2,1,0:T(8,128)(2,1)}, bf16[2,256,512]{2,1,0:T(8,128)(2,1)}, u32[]{:S(2)}, u32[]{:S(2)}) collective-permute-start(bf16[2,256,512]{2,1,0:T(8,128)(2,1)} %collective-permute-done.9.far), channel_id=1, source_target_pairs={{0,1},{1,0},{2,3},{3,2},{4,5},{5,4},{6,7},{7,6},{8,9},{9,8},{10,11... | collective-permute-start | bytes 1572872 | tf_op jit(solution)/shard_map/ppermute | solution.py:31
  106.8 3.0 %step.3.a_in = f32[256,512]{1,0:T(8,128)S(1)} custom-call(f32[256,512]{1,0:T(8,128)S(1)} %step.2.a_in), custom_call_target="tpu_custom_call", output_to_operand_aliasing={{}: (0, {})} | custom-call | flops 300000000 | bytes 1048576 | tf_op jit(solution)/shard_map/step/pallas_call | solution.py:291
  109.9 4.6 %all-to-all-done.4.parts = bf16[8,16,1024]{2,1,0:T(8,128)(2,1)S(1)} async-done(((bf16[8,16,1024]{2,1,0:T(8,128)(2,1)}), bf16[8,16,1024]{2,1,0:T(8,128)(2,1)S(1)}, u32[]{:S(2)}, u32[]{:S(2)}) %all-to-all-start.4) | async-done | bytes 262176 | tf_op jit(solution)/shard_map/all_to_all | solution.py:365
  114.5 0.9 spread.7
  115.4 4.0 %all-to-all-start.5 = ((bf16[16,16,1024]{2,1,0:T(8,128)(2,1)}), bf16[16,16,1024]{2,1,0:T(8,128)(2,1)S(1)}, u32[]{:S(2)}, u32[]{:S(2)}) async-start(bf16[16,16,1024]{2,1,0:T(8,128)(2,1)} %spread.7), calls=%async_computation.5 | async-start | bytes 1048576 | tf_op jit(solution)/shard_map/all_to_all | solution.py:369
  119.4 3.3 %collective-permute-start.15 = (bf16[2,256,512]{2,1,0:T(8,128)(2,1)S(1)}, bf16[2,256,512]{2,1,0:T(8,128)(2,1)S(1)}, u32[]{:S(2)}, u32[]{:S(2)}) collective-permute-start(bf16[2,256,512]{2,1,0:T(8,128)(2,1)S(1)} %copy-done.4), channel_id=1, source_target_pairs={{0,1},{1,0},{2,3},{3,2},{4,5},{5,4},{6,7},{7,6},{8,9},{9,8},{10,11... | collective-permute-start | bytes 1572872 | tf_op jit(solution)/shard_map/ppermute | solution.py:31
  122.7 3.6 %basis.1 = (f32[256,256]{1,0:T(8,128)S(1)}, bf16[512,256]{1,0:T(8,128)(2,1)S(1)}) custom-call(s32[2]{0:T(128)S(1)} %pad_add_fusion.at, f32[256,512]{1,0:T(8,128)S(1)} %step.3.a_in, bf16[256,2048]{1,0:T(8,128)(2,1)S(1)} %get-tuple-element.63.left), custom_call_target="tpu_custom_call" | custom-call | flops 300000000 | bytes 2097160 | tf_op jit(solution)/shard_map/basis/pallas_call | solution.py:291
  126.3 0.7 copy-done.6
  126.9 2.2 %place.1 = bf16[256,2048]{1,0:T(8,128)(2,1)} custom-call(s32[2]{0:T(128)S(1)} %pad_add_fusion.at, bf16[2,256,512]{2,1,0:T(8,128)(2,1)} %grad.2.own, bf16[2,256,512]{2,1,0:T(8,128)(2,1)} %copy-done.8, bf16[2,256,512]{2,1,0:T(8,128)(2,1)} %collective-permute-done.9.far, bf16[2,256,512]{2,1,0:T(8,128)(2,1)} %collective-permute-done.13.diag), custom_call_target="tpu_custom_call" | custom-call | flops 1000000 | bytes 3145736 | tf_op jit(solution)/shard_map/place/pallas_call | solution.py:316
  129.2 0.0 all-to-all-done.5.chunks
  129.2 3.3 %collective-permute-start.14 = (bf16[16,16,1024]{2,1,0:T(8,128)(2,1)S(1)}, bf16[16,16,1024]{2,1,0:T(8,128)(2,1)S(1)}, u32[]{:S(2)}, u32[]{:S(2)}) collective-permute-start(bf16[16,16,1024]{2,1,0:T(8,128)(2,1)S(1)} %all-to-all-done.5.chunks), channel_id=1, source_target_pairs={{0,1},{1,0},{2,3},{3,2},{4,5},{5,4},{6,7},{7,6},{8,9},{9,8},{10,11... | collective-permute-start | bytes 1572872 | tf_op jit(solution)/shard_map/ppermute | solution.py:31
  132.5 1.2 begin.1
  133.7 0.3 collective-permute-done.14.other
  134.0 6.9 %last.1 = (f32[512,2048]{1,0:T(8,128)}, f32[512,256]{1,0:T(8,128)}) custom-call(s32[2]{0:T(128)S(1)} %pad_add_fusion.at, bf16[16,16,1024]{2,1,0:T(8,128)(2,1)S(1)} %collective-permute-done.14.other, f32[256,256]{1,0:T(8,128)S(1)} %get-tuple-element.70.inverse, bf16[512,256]{1,0:T(8,128)(2,1)} %copy-done.6, f32[256,2048]{1,0:T(8,128)S(1)} %get-tuple-element.71.begun, ...), custom_call_target="tpu_custom_call" | custom-call | flops 2000000000 | bytes 14680072 | tf_op jit(solution)/shard_map/last/pallas_call | solution.py:316
  (19 shorter events, 0.0 us)
Async XLA Ops:
  0.6 4.7 %collective-permute-start.1 = (bf16[512,256]{1,0:T(8,128)(2,1)}, bf16[512,256]{1,0:T(8,128)(2,1)S(1)}, u32[]{:S(2)}, u32[]{:S(2)}) collective-permute-start(bf16[512,256]{1,0:T(8,128)(2,1)} %w0.1), channel_id=1, source_target_pairs={{0,1},{1,0},{2,3},{3,2},{4,5},{5,4},{6,7},{7,6},{8,9},{9,8},{10,11... | collective-permute-start | bytes 786440 | tf_op jit(solution)/shard_map/ppermute | solution.py:31
  4.0 8.1 %collective-permute-start = (bf16[512,256]{1,0:T(8,128)(2,1)}, bf16[512,256]{1,0:T(8,128)(2,1)S(1)}, u32[]{:S(2)}, u32[]{:S(2)}) collective-permute-start(bf16[512,256]{1,0:T(8,128)(2,1)} %w0.1), channel_id=1, source_target_pairs={{0,2},{2,0},{1,3},{3,1},{4,6},{6,4},{5,7},{7,5},{8,10},{10,8},{9,1... | collective-permute-start | bytes 786440 | tf_op jit(solution)/shard_map/ppermute | solution.py:31
  5.3 7.6 %copy-start.1 = (bf16[256,2048]{1,0:T(8,128)(2,1)S(1)}, bf16[256,2048]{1,0:T(8,128)(2,1)}, u32[]{:S(2)}) copy-start(bf16[256,2048]{1,0:T(8,128)(2,1)} %og.3) | copy-start | bytes 3145732
  5.3 8.7 %copy-start = (bf16[256,2048]{1,0:T(8,128)(2,1)S(1)}, bf16[256,2048]{1,0:T(8,128)(2,1)}, u32[]{:S(2)}) copy-start(bf16[256,2048]{1,0:T(8,128)(2,1)} %ctx.7) | copy-start | bytes 3145732
  5.3 8.7 %copy-start.7 = (bf16[512,256]{1,0:T(8,128)(2,1)S(1)}, bf16[512,256]{1,0:T(8,128)(2,1)}, u32[]{:S(2)}) copy-start(bf16[512,256]{1,0:T(8,128)(2,1)} %w0.1) | copy-start | bytes 786436
  10.2 3.0 %collective-permute-start.5 = (bf16[256,512]{1,0:T(8,128)(2,1)}, bf16[256,512]{1,0:T(8,128)(2,1)S(1)}, u32[]{:S(2)}, u32[]{:S(2)}) collective-permute-start(bf16[256,512]{1,0:T(8,128)(2,1)} %get-tuple-element.44), channel_id=1, source_target_pairs={{0,1},{1,0},{2,3},{3,2},{4,5},{5,4},{6,7},{7,6},{8,9},{9,8},{10,11... | collective-permute-start | bytes 786440 | tf_op jit(solution)/shard_map/ppermute | solution.py:31
  12.0 2.0 %collective-permute-start.6 = (bf16[512,256]{1,0:T(8,128)(2,1)S(1)}, bf16[512,256]{1,0:T(8,128)(2,1)S(1)}, u32[]{:S(2)}, u32[]{:S(2)}) collective-permute-start(bf16[512,256]{1,0:T(8,128)(2,1)S(1)} %collective-permute-done.w2), channel_id=1, source_target_pairs={{0,1},{1,0},{2,3},{3,2},{4,5},{5,4},{6,7},{7,6},{8,9},{9,8},{10,11... | collective-permute-start | bytes 786440 | tf_op jit(solution)/shard_map/ppermute | solution.py:31
  12.9 24.9 %collective-permute-start.4 = (bf16[256,2048]{1,0:T(8,128)(2,1)S(1)}, bf16[256,2048]{1,0:T(8,128)(2,1)}, u32[]{:S(2)}, u32[]{:S(2)}) collective-permute-start(bf16[256,2048]{1,0:T(8,128)(2,1)S(1)} %copy-done.1), channel_id=1, source_target_pairs={{0,2},{2,0},{1,3},{3,1},{4,6},{6,4},{5,7},{7,5},{8,10},{10,8},{9,1... | collective-permute-start | bytes 3145736 | tf_op jit(solution)/shard_map/ppermute | solution.py:31
  12.9 12.3 %collective-permute-start.2 = (bf16[256,2048]{1,0:T(8,128)(2,1)S(1)}, bf16[256,2048]{1,0:T(8,128)(2,1)}, u32[]{:S(2)}, u32[]{:S(2)}) collective-permute-start(bf16[256,2048]{1,0:T(8,128)(2,1)S(1)} %copy-done.1), channel_id=1, source_target_pairs={{0,1},{1,0},{2,3},{3,2},{4,5},{5,4},{6,7},{7,6},{8,9},{9,8},{10,11... | collective-permute-start | bytes 3145736 | tf_op jit(solution)/shard_map/ppermute | solution.py:31
  16.5 8.7 %copy-start.5 = (bf16[256,512]{1,0:T(8,128)(2,1)S(1)}, bf16[256,512]{1,0:T(8,128)(2,1)}, u32[]{:S(2)}) copy-start(bf16[256,512]{1,0:T(8,128)(2,1)} %get-tuple-element.49.c0) | copy-start | bytes 786436
  16.5 2.0 %collective-permute-start.7 = (bf16[16,16,1024]{2,1,0:T(8,128)(2,1)S(1)}, bf16[16,16,1024]{2,1,0:T(8,128)(2,1)S(1)}, u32[]{:S(2)}, u32[]{:S(2)}) collective-permute-start(bf16[16,16,1024]{2,1,0:T(8,128)(2,1)S(1)} %get-tuple-element.48), channel_id=1, source_target_pairs={{0,1},{1,0},{2,3},{3,2},{4,5},{5,4},{6,7},{7,6},{8,9},{9,8},{10,11... | collective-permute-start | bytes 1572872 | tf_op jit(solution)/shard_map/ppermute | solution.py:31
  19.4 16.6 %all-to-all-start = ((bf16[16,16,1024]{2,1,0:T(8,128)(2,1)}), bf16[16,16,1024]{2,1,0:T(8,128)(2,1)S(1)}, u32[]{:S(2)}, u32[]{:S(2)}) async-start(bf16[16,16,1024]{2,1,0:T(8,128)(2,1)} %add.4), calls=%async_computation | async-start | bytes 1048576 | tf_op jit(solution)/shard_map/all_to_all | solution.py:360
  37.8 27.3 %collective-permute-start.8 = (bf16[256,2048]{1,0:T(8,128)(2,1)}, bf16[256,2048]{1,0:T(8,128)(2,1)}, u32[]{:S(2)}, u32[]{:S(2)}) collective-permute-start(bf16[256,2048]{1,0:T(8,128)(2,1)} %collective-permute-done.4.h0.g2), channel_id=1, source_target_pairs={{0,1},{1,0},{2,3},{3,2},{4,5},{5,4},{6,7},{7,6},{8,9},{9,8},{10,11... | collective-permute-start | bytes 3145736 | tf_op jit(solution)/shard_map/ppermute | solution.py:31
  38.6 19.7 %all-to-all-start.1 = ((bf16[8,16,1024]{2,1,0:T(8,128)(2,1)}), bf16[8,16,1024]{2,1,0:T(8,128)(2,1)S(1)}, u32[]{:S(2)}, u32[]{:S(2)}) async-start(bf16[8,16,1024]{2,1,0:T(8,128)(2,1)} %spread.4), calls=%async_computation.1 | async-start | bytes 524288 | tf_op jit(solution)/shard_map/all_to_all | solution.py:365
  58.2 17.1 %collective-permute-start.10 = (bf16[2,256,512]{2,1,0:T(8,128)(2,1)}, bf16[2,256,512]{2,1,0:T(8,128)(2,1)S(1)}, u32[]{:S(2)}, u32[]{:S(2)}) collective-permute-start(bf16[2,256,512]{2,1,0:T(8,128)(2,1)} %get-tuple-element.58), channel_id=1, source_target_pairs={{0,2},{2,0},{1,3},{3,1},{4,6},{6,4},{5,7},{7,5},{8,10},{10,8},{9,1... | collective-permute-start | bytes 1572872 | tf_op jit(solution)/shard_map/ppermute | solution.py:31
  59.1 16.2 %all-to-all-start.2 = ((bf16[16,16,1024]{2,1,0:T(8,128)(2,1)}), bf16[16,16,1024]{2,1,0:T(8,128)(2,1)S(1)}, u32[]{:S(2)}, u32[]{:S(2)}) async-start(bf16[16,16,1024]{2,1,0:T(8,128)(2,1)} %spread.5), calls=%async_computation.2 | async-start | bytes 1048576 | tf_op jit(solution)/shard_map/all_to_all | solution.py:369
  65.0 14.0 %copy-start.2 = (bf16[256,2048]{1,0:T(8,128)(2,1)S(1)}, bf16[256,2048]{1,0:T(8,128)(2,1)}, u32[]{:S(2)}) copy-start(bf16[256,2048]{1,0:T(8,128)(2,1)} %og.3) | copy-start | bytes 3145732
  75.3 3.7 %copy-start.3 = (bf16[2,256,512]{2,1,0:T(8,128)(2,1)}, bf16[2,256,512]{2,1,0:T(8,128)(2,1)S(1)}, u32[]{:S(2)}) copy-start(bf16[2,256,512]{2,1,0:T(8,128)(2,1)S(1)} %collective-permute-done.10.c2) | copy-start | bytes 1572868
  75.4 3.7 %collective-permute-start.11 = (bf16[16,16,1024]{2,1,0:T(8,128)(2,1)S(1)}, bf16[16,16,1024]{2,1,0:T(8,128)(2,1)S(1)}, u32[]{:S(2)}, u32[]{:S(2)}) collective-permute-start(bf16[16,16,1024]{2,1,0:T(8,128)(2,1)S(1)} %all-to-all-done.2.mine), channel_id=1, source_target_pairs={{0,1},{1,0},{2,3},{3,2},{4,5},{5,4},{6,7},{7,6},{8,9},{9,8},{10,11... | collective-permute-start | bytes 1572872 | tf_op jit(solution)/shard_map/ppermute | solution.py:31
  83.5 2.1 %collective-permute-start.12 = (bf16[16,16,1024]{2,1,0:T(8,128)(2,1)S(1)}, bf16[16,16,1024]{2,1,0:T(8,128)(2,1)S(1)}, u32[]{:S(2)}, u32[]{:S(2)}) collective-permute-start(bf16[16,16,1024]{2,1,0:T(8,128)(2,1)S(1)} %get-tuple-element.62), channel_id=1, source_target_pairs={{0,1},{1,0},{2,3},{3,2},{4,5},{5,4},{6,7},{7,6},{8,9},{9,8},{10,11... | collective-permute-start | bytes 1572872 | tf_op jit(solution)/shard_map/ppermute | solution.py:31
  84.0 17.6 %collective-permute-start.3 = (bf16[2,256,512]{2,1,0:T(8,128)(2,1)}, bf16[2,256,512]{2,1,0:T(8,128)(2,1)S(1)}, u32[]{:S(2)}, u32[]{:S(2)}) collective-permute-start(bf16[2,256,512]{2,1,0:T(8,128)(2,1)} %grad.2.own), channel_id=1, source_target_pairs={{0,1},{1,0},{2,3},{3,2},{4,5},{5,4},{6,7},{7,6},{8,9},{9,8},{10,11... | collective-permute-start | bytes 1572872 | tf_op jit(solution)/shard_map/ppermute | solution.py:31
  84.1 17.4 %collective-permute-start.9 = (bf16[2,256,512]{2,1,0:T(8,128)(2,1)}, bf16[2,256,512]{2,1,0:T(8,128)(2,1)}, u32[]{:S(2)}, u32[]{:S(2)}) collective-permute-start(bf16[2,256,512]{2,1,0:T(8,128)(2,1)} %grad.3), channel_id=1, source_target_pairs={{0,2},{2,0},{1,3},{3,1},{4,6},{6,4},{5,7},{7,5},{8,10},{10,8},{9,1... | collective-permute-start | bytes 1572872 | tf_op jit(solution)/shard_map/ppermute | solution.py:31
  86.5 14.3 %all-to-all-start.3 = ((bf16[16,16,1024]{2,1,0:T(8,128)(2,1)}), bf16[16,16,1024]{2,1,0:T(8,128)(2,1)S(1)}, u32[]{:S(2)}, u32[]{:S(2)}) async-start(bf16[16,16,1024]{2,1,0:T(8,128)(2,1)} %add.5), calls=%async_computation.3 | async-start | bytes 1048576 | tf_op jit(solution)/shard_map/all_to_all | solution.py:360
  97.1 22.3 %copy-start.4 = (bf16[2,256,512]{2,1,0:T(8,128)(2,1)S(1)}, bf16[2,256,512]{2,1,0:T(8,128)(2,1)}, u32[]{:S(2)}) copy-start(bf16[2,256,512]{2,1,0:T(8,128)(2,1)} %copy-done.3) | copy-start | bytes 1572868
  101.5 13.8 %copy-start.8 = (bf16[2,256,512]{2,1,0:T(8,128)(2,1)}, bf16[2,256,512]{2,1,0:T(8,128)(2,1)S(1)}, u32[]{:S(2)}) copy-start(bf16[2,256,512]{2,1,0:T(8,128)(2,1)S(1)} %collective-permute-done.3.near) | copy-start | bytes 1572868
  101.6 12.9 %all-to-all-start.4 = ((bf16[8,16,1024]{2,1,0:T(8,128)(2,1)}), bf16[8,16,1024]{2,1,0:T(8,128)(2,1)S(1)}, u32[]{:S(2)}, u32[]{:S(2)}) async-start(bf16[8,16,1024]{2,1,0:T(8,128)(2,1)} %spread.6), calls=%async_computation.4 | async-start | bytes 524288 | tf_op jit(solution)/shard_map/all_to_all | solution.py:365
  105.0 22.0 %collective-permute-start.13 = (bf16[2,256,512]{2,1,0:T(8,128)(2,1)}, bf16[2,256,512]{2,1,0:T(8,128)(2,1)}, u32[]{:S(2)}, u32[]{:S(2)}) collective-permute-start(bf16[2,256,512]{2,1,0:T(8,128)(2,1)} %collective-permute-done.9.far), channel_id=1, source_target_pairs={{0,1},{1,0},{2,3},{3,2},{4,5},{5,4},{6,7},{7,6},{8,9},{9,8},{10,11... | collective-permute-start | bytes 1572872 | tf_op jit(solution)/shard_map/ppermute | solution.py:31
  115.4 13.8 %all-to-all-start.5 = ((bf16[16,16,1024]{2,1,0:T(8,128)(2,1)}), bf16[16,16,1024]{2,1,0:T(8,128)(2,1)S(1)}, u32[]{:S(2)}, u32[]{:S(2)}) async-start(bf16[16,16,1024]{2,1,0:T(8,128)(2,1)} %spread.7), calls=%async_computation.5 | async-start | bytes 1048576 | tf_op jit(solution)/shard_map/all_to_all | solution.py:369
  119.4 13.1 %collective-permute-start.15 = (bf16[2,256,512]{2,1,0:T(8,128)(2,1)S(1)}, bf16[2,256,512]{2,1,0:T(8,128)(2,1)S(1)}, u32[]{:S(2)}, u32[]{:S(2)}) collective-permute-start(bf16[2,256,512]{2,1,0:T(8,128)(2,1)S(1)} %copy-done.4), channel_id=1, source_target_pairs={{0,1},{1,0},{2,3},{3,2},{4,5},{5,4},{6,7},{7,6},{8,9},{9,8},{10,11... | collective-permute-start | bytes 1572872 | tf_op jit(solution)/shard_map/ppermute | solution.py:31
  126.2 0.7 copy-start.6
  129.2 4.8 %collective-permute-start.14 = (bf16[16,16,1024]{2,1,0:T(8,128)(2,1)S(1)}, bf16[16,16,1024]{2,1,0:T(8,128)(2,1)S(1)}, u32[]{:S(2)}, u32[]{:S(2)}) collective-permute-start(bf16[16,16,1024]{2,1,0:T(8,128)(2,1)S(1)} %all-to-all-done.5.chunks), channel_id=1, source_target_pairs={{0,1},{1,0},{2,3},{3,2},{4,5},{5,4},{6,7},{7,6},{8,9},{9,8},{10,11... | collective-permute-start | bytes 1572872 | tf_op jit(solution)/shard_map/ppermute | solution.py:31

commit v8 on v7

--- a/solution.py
+++ b/solution.py
@@ -206,7 +206,7 @@
     inverse[...] = a[:, RANK:]
     first, second = two(a[:, RANK:])
     own = left[:, block(at[0], at[1])]
-    basis[...] = (mm(first, own, 1, 0) + mm(second, own, 1, 0)).astype(BF16).T
+    basis[...] = -(mm(first, own, 1, 0) + mm(second, own, 1, 0)).astype(BF16).T
 
 
 def grad_kernel(h0, h1, weight_hbm, out, weight, g0, g1, sems):
@@ -241,16 +241,16 @@
     return inverse[:, pl.ds(pl.multiple_of(half * HALF, HALF), HALF)]
 
 
-def begin_kernel(at, chunks, inverse, c2, c3, out, t2, t3, half):
-    t2[...] = c2[0].T
-    t3[...] = c3[1].T
+def begin_kernel(scale, at, chunks, inverse, c2, c3, out, turned, half):
+    turned[:, :TOK] = (c2[0].T * scale).astype(BF16)
+    turned[:, TOK:] = (c3[1].T * scale).astype(BF16)
     unchunk(chunks, half)
     first, second = two(columns_of(inverse, at[1]))
     out[...] = mm(first, half[...], 1, 0) + mm(second, half[...], 1, 0)
 
 
 def last_kernel(
-    share, scale, at, other, inverse, basis, begun, t2, t3, merged, g2, g3,
+    share, at, other, inverse, basis, begun, turned, merged, g2, g3,
     new_error, factor_q, half,
 ):
     step = pl.program_id(0)
@@ -264,8 +264,9 @@
     first, second = two(columns_of(inverse, 1 - core))
     q = mm(first, half[:, cols], 1, 0) + mm(second, half[:, cols], 1, 0)
     q = (begun[:, cols] + q) * share
-    total = mm(t2[...], g2[...], 1, 0) + mm(t3[...], g3[...], 1, 0)
-    new_error[...] = merged[...] + total * scale - mm(basis[...], q.astype(BF16), 1, 0)
+    lhs = jnp.concatenate([turned[...], basis[...]], 1)
+    rhs = jnp.concatenate([g2[...], g3[...], q.astype(BF16)], 0)
+    new_error[...] = merged[...] + mm(lhs, rhs, 1, 0)
 
     @pl.when(step == zl * 2 + core)
     def _():
@@ -471,13 +472,21 @@
         functools.partial(step_kernel, PART), [table], (a,), 300_000_000, "step", alias={0: 0}
     )
     part = across_plane(keep, send, (a,))
-    part = tied(part, i_far, i_near)
+    part = tied(part, i_far)
     c_diag = swap(c_far, "core")
     i_diag = swap(tied(i_far, part), "core")
     (a,) = call(
         functools.partial(step_kernel, 2 * PART), [table], (a,), 300_000_000, "step", alias={0: 0}
     )
-    zs = across_z(part, (a,))
+    inverse, basis = call(
+        basis_kernel,
+        [((RANK, RANK), F32), ((ROWS, RANK), BF16)],
+        (at, a, left),
+        300_000_000,
+        "basis",
+        [table],
+    )
+    zs = across_z(part, (basis,))
     mine = back_over_plane(zs)
     first = pl.BlockSpec((None, TOK, ROWS), lambda j: (0, 0, 0))
     second = pl.BlockSpec((None, TOK, ROWS), lambda j: (1, 0, 0))
@@ -490,18 +499,10 @@
         1_000_000,
         "place",
     )
-    inverse, basis = call(
-        basis_kernel,
-        [((RANK, RANK), F32), ((ROWS, RANK), BF16)],
-        (at, a, left),
-        300_000_000,
-        "basis",
-        [table],
-    )
-    other = swap(tied(mine, basis, in_grad), "core")
-    begun, t2, t3 = call(
-        begin_kernel,
-        [((RANK, FEAT), F32)] + turned,
+    other = swap(tied(mine, in_grad), "core")
+    begun, far_turned = call(
+        functools.partial(begin_kernel, scale),
+        [((RANK, FEAT), F32), ((ROWS, 2 * TOK), BF16)],
         (at, mine, inverse, c_far, c_diag),
         300_000_000,
         "begin",
@@ -510,15 +511,15 @@
     other = tied(other, begun)
 
     new_error, factor_q = call_grid(
-        functools.partial(last_kernel, 1.0 / (SIZES[0] * SIZES[1] * SIZES[2]), scale),
+        functools.partial(last_kernel, 1.0 / (SIZES[0] * SIZES[1] * SIZES[2])),
         4,
         [
             ((ROWS, FEAT), F32, column(ROWS)),
             ((ROWS, RANK), F32, whole(ROWS, RANK)),
         ],
-        [SMEM, VMEM, VMEM, whole(ROWS, RANK), VMEM, VMEM, VMEM]
+        [SMEM, VMEM, VMEM, whole(ROWS, RANK), VMEM, VMEM]
         + [column(ROWS), column(TOK), column(TOK)],
-        (at, other, inverse, basis, begun, t2, t3, merged, g_far, g_diag),
+        (at, other, inverse, basis, begun, far_turned, merged, g_far, g_diag),
         2_000_000_000,
         "last",
         [((HALF, FEAT), BF16)],

time: 142 us -> 143 us (level)
  waiting for transfers between devices: 35 us -> 37.4 us
  starting transfers between devices: 48.8 us -> 47 us
    all_to_all x2, waiting for transfers between devices: 6.03 us -> 11.9 us  [back_over_plane(): lax.all_to_all(spread(tied(parts, *beside), CHUNKS), ('y', 'x'), 0, 0)]
    all_to_all x2, waiting for transfers between devices: 12.8 us -> 8.96 us  [across_z(): return tied(lax.all_to_all(copies, ('zh', 'zl'), 0, 0), *beside)]
    ppermute x16, starting transfers between devices: 18.8 us -> 16.5 us  [swap(): return lax.ppermute(x, axis, [(0, 1), (1, 0)])]
  transfers between devices with their start and end apart: 22 -> 22, of which waited for: 12 -> 14; matrix products, arithmetic and copies ran while one was open for 0% -> 0% of each run, Pallas kernels for 31% -> 31%
where the time goes in v8:
time: 143 us; the launch traced here: 142 us
  Pallas kernels  55.5 us (39%)
  starting transfers between devices  47 us (33%)
  waiting for transfers between devices  37.4 us (26%)
    pallas_call x16, Pallas kernels, call(): pl.pallas_call(kernel, out_shape=[(pltpu.HBM if free else jax.ShapeDtypeS...  35.6 us
    pallas_call x4, Pallas kernels, call_grid(): pl.pallas_call(kernel, grid=(steps,), out_shape=[(jax.ShapeDtypeStruct if...  19.9 us
    ppermute x16, starting transfers between devices, swap(): return lax.ppermute(x, axis, [(0, 1), (1, 0)])  16.5 us
    all_to_all x2, waiting for transfers between devices, back_over_plane(): lax.all_to_all(spread(tied(parts, *beside), CHUNKS), ('y', 'x'), 0, 0)  11.9 us
    all_to_all x2, starting transfers between devices, across_z(): return tied(lax.all_to_all(copies, ('zh', 'zl'), 0, 0), *beside)  10.7 us
    all_to_all x2, starting transfers between devices, back_over_plane(): lax.all_to_all(spread(tied(parts, *beside), CHUNKS), ('y', 'x'), 0, 0)  10.4 us
    all_to_all x2, starting transfers between devices, across_plane(): parts = tied(lax.all_to_all(half, ('y', 'x'), 0, 0), *beside)  9.36 us
    all_to_all x2, waiting for transfers between devices, across_z(): return tied(lax.all_to_all(copies, ('zh', 'zl'), 0, 0), *beside)  8.96 us
  transfers between devices with their start and end apart: 22, of which 14 were waited for; matrix products, arithmetic and copies ran while one was open for 0% of the time, Pallas kernels for 31%

profile of v8, /device:TPU:1, one launch (start us, length us, event | category | flops | bytes accessed | tf_op | source)
XLA Modules:
  0.0 141.5 jit_solution(4215184912505496184)
XLA Ops:
  0.6 3.3 %collective-permute-start.1 = (bf16[512,256]{1,0:T(8,128)(2,1)}, bf16[512,256]{1,0:T(8,128)(2,1)S(1)}, u32[]{:S(2)}, u32[]{:S(2)}) collective-permute-start(bf16[512,256]{1,0:T(8,128)(2,1)} %w0.1), channel_id=1, source_target_pairs={{0,1},{1,0},{2,3},{3,2},{4,5},{5,4},{6,7},{7,6},{8,9},{9,8},{10,11... | collective-permute-start | bytes 786440 | tf_op jit(solution)/shard_map/ppermute | solution.py:31
  4.0 0.0 collective-permute-start
  4.0 0.1 pad_add_fusion.at
  4.0 1.3 collective-permute-done.1.w1
  5.3 4.9 %prepare.1 = (bf16[256,512]{1,0:T(8,128)(2,1)}, bf16[256,512]{1,0:T(8,128)(2,1)}, bf16[2,256,512]{2,1,0:T(8,128)(2,1)}, bf16[512,2048]{1,0:T(8,128)(2,1)S(1)}, bf16[512,2048]{1,0:T(8,128)(2,1)}) custom-call(s32[2]{0:T(128)S(1)} %pad_add_fusion.at, bf16[256,2048]{1,0:T(8,128)(2,1)} %ctx.7, f32[512,2048]{1,0:T(8,128)} %bitcast.4), custom_call_target="tpu_custom_call" | custom-call | flops 4000000 | bytes 10485768 | tf_op jit(solution)/shard_map/prepare/pallas_call | solution.py:317
  10.2 0.4 collective-permute-start.5
  10.6 1.5 %collective-permute-done.w2 = bf16[512,256]{1,0:T(8,128)(2,1)S(1)} collective-permute-done((bf16[512,256]{1,0:T(8,128)(2,1)}, bf16[512,256]{1,0:T(8,128)(2,1)S(1)}, u32[]{:S(2)}, u32[]{:S(2)}) %collective-permute-start) | collective-permute-done | bytes 262176 | tf_op jit(solution)/shard_map/ppermute | solution.py:31
  12.0 0.9 collective-permute-start.6
  12.9 0.0 collective-permute-start.4
  12.9 0.3 collective-permute-start.2
  13.2 0.0 collective-permute-done.5.c1
  13.2 0.9 collective-permute-done.6.w3
  14.1 2.4 %left.1 = (f32[16,16,1024]{2,1,0:T(8,128)S(1)}, bf16[16,16,1024]{2,1,0:T(8,128)(2,1)S(1)}) custom-call(s32[2]{0:T(128)S(1)} %pad_add_fusion.at, bf16[256,2048]{1,0:T(8,128)(2,1)S(1)} %copy-done.1, bf16[256,2048]{1,0:T(8,128)(2,1)S(1)} %copy-done, bf16[512,2048]{1,0:T(8,128)(2,1)S(1)} %get-tuple-element.44.low, bf16[512,256]{1,0:T(8,128)(2,1)S(1)} %copy-done.7, ...), custom_call_target="tpu_custom_call" | custom-call | flops 2000000000 | bytes 6815752 | tf_op jit(solution)/shard_map/left/pallas_call | solution.py:292
  16.5 0.0 copy-start.6
  16.5 0.5 collective-permute-start.7
  17.0 1.5 %collective-permute-done.7.got = bf16[16,16,1024]{2,1,0:T(8,128)(2,1)S(1)} collective-permute-done((bf16[16,16,1024]{2,1,0:T(8,128)(2,1)S(1)}, bf16[16,16,1024]{2,1,0:T(8,128)(2,1)S(1)}, u32[]{:S(2)}, u32[]{:S(2)}) %collective-permute-start.7) | collective-permute-done | bytes 524320 | tf_op jit(solution)/shard_map/ppermute | solution.py:31
  18.5 0.9 add.4
  19.4 5.8 %all-to-all-start = ((bf16[16,16,1024]{2,1,0:T(8,128)(2,1)}), bf16[16,16,1024]{2,1,0:T(8,128)(2,1)S(1)}, u32[]{:S(2)}, u32[]{:S(2)}) async-start(bf16[16,16,1024]{2,1,0:T(8,128)(2,1)} %add.4), calls=%async_computation | async-start | bytes 1048576 | tf_op jit(solution)/shard_map/all_to_all | solution.py:361
  25.2 0.0 collective-permute-done.2.h1.g1
  25.2 5.9 %merge.1.merged = f32[512,2048]{1,0:T(8,128)} custom-call(f32[512,2048]{1,0:T(8,128)} %bitcast.5, bf16[256,512]{1,0:T(8,128)(2,1)S(1)} %copy-done.6, bf16[256,512]{1,0:T(8,128)(2,1)S(1)} %collective-permute-done.5.c1, bf16[256,2048]{1,0:T(8,128)(2,1)S(1)} %copy-done.1, bf16[256,2048]{1,0:T(8,128)(2,1)} %collective-permute-done.2.h1.g1), custom_call_target="tpu_custom_call" | custom-call | flops 1100000000 | bytes 11010048 | tf_op jit(solution)/shard_map/merge/pallas_call | solution.py:317
  31.1 5.0 %all-to-all-done.parts = bf16[16,16,1024]{2,1,0:T(8,128)(2,1)S(1)} async-done(((bf16[16,16,1024]{2,1,0:T(8,128)(2,1)}), bf16[16,16,1024]{2,1,0:T(8,128)(2,1)S(1)}, u32[]{:S(2)}, u32[]{:S(2)}) %all-to-all-start) | async-done | bytes 524320 | tf_op jit(solution)/shard_map/all_to_all | solution.py:361
  36.0 0.8 spread.4
  36.8 1.0 collective-permute-done.4.h0.g2
  37.8 0.8 collective-permute-start.8
  38.6 7.3 %all-to-all-start.1 = ((bf16[8,16,1024]{2,1,0:T(8,128)(2,1)}), bf16[8,16,1024]{2,1,0:T(8,128)(2,1)S(1)}, u32[]{:S(2)}, u32[]{:S(2)}) async-start(bf16[8,16,1024]{2,1,0:T(8,128)(2,1)} %spread.4), calls=%async_computation.1 | async-start | bytes 524288 | tf_op jit(solution)/shard_map/all_to_all | solution.py:366
  45.9 4.2 %grad.2.own = bf16[2,256,512]{2,1,0:T(8,128)(2,1)} custom-call(bf16[256,2048]{1,0:T(8,128)(2,1)} %og.3, bf16[256,2048]{1,0:T(8,128)(2,1)} %collective-permute-done.2.h1.g1, bf16[512,2048]{1,0:T(8,128)(2,1)} %weight_hbm.3), custom_call_target="tpu_custom_call" | custom-call | flops 1100000000 | bytes 4718592 | tf_op jit(solution)/shard_map/grad/pallas_call | solution.py:292
  50.0 8.2 %all-to-all-done.1.parts = bf16[8,16,1024]{2,1,0:T(8,128)(2,1)S(1)} async-done(((bf16[8,16,1024]{2,1,0:T(8,128)(2,1)}), bf16[8,16,1024]{2,1,0:T(8,128)(2,1)S(1)}, u32[]{:S(2)}, u32[]{:S(2)}) %all-to-all-start.1) | async-done | bytes 262176 | tf_op jit(solution)/shard_map/all_to_all | solution.py:366
  58.2 0.0 collective-permute-start.10
  58.3 0.9 spread.5
  59.1 5.9 %all-to-all-start.2 = ((bf16[16,16,1024]{2,1,0:T(8,128)(2,1)}), bf16[16,16,1024]{2,1,0:T(8,128)(2,1)S(1)}, u32[]{:S(2)}, u32[]{:S(2)}) async-start(bf16[16,16,1024]{2,1,0:T(8,128)(2,1)} %spread.5), calls=%async_computation.2 | async-start | bytes 1048576 | tf_op jit(solution)/shard_map/all_to_all | solution.py:370
  65.0 0.0 copy-start.2
  65.1 0.0 collective-permute-done.8.h1.g3
  65.1 4.2 %grad.3 = bf16[2,256,512]{2,1,0:T(8,128)(2,1)} custom-call(bf16[256,2048]{1,0:T(8,128)(2,1)} %collective-permute-done.4.h0.g2, bf16[256,2048]{1,0:T(8,128)(2,1)} %collective-permute-done.8.h1.g3, bf16[512,2048]{1,0:T(8,128)(2,1)} %weight_hbm.3), custom_call_target="tpu_custom_call" | custom-call | flops 1100000000 | bytes 4718592 | tf_op jit(solution)/shard_map/grad/pallas_call | solution.py:292
  69.3 6.0 %all-to-all-done.2.mine = bf16[16,16,1024]{2,1,0:T(8,128)(2,1)S(1)} async-done(((bf16[16,16,1024]{2,1,0:T(8,128)(2,1)}), bf16[16,16,1024]{2,1,0:T(8,128)(2,1)S(1)}, u32[]{:S(2)}, u32[]{:S(2)}) %all-to-all-start.2) | async-done | bytes 524320 | tf_op jit(solution)/shard_map/all_to_all | solution.py:370
  75.4 2.2 %collective-permute-start.11 = (bf16[16,16,1024]{2,1,0:T(8,128)(2,1)S(1)}, bf16[16,16,1024]{2,1,0:T(8,128)(2,1)S(1)}, u32[]{:S(2)}, u32[]{:S(2)}) collective-permute-start(bf16[16,16,1024]{2,1,0:T(8,128)(2,1)S(1)} %all-to-all-done.2.mine), channel_id=1, source_target_pairs={{0,1},{1,0},{2,3},{3,2},{4,5},{5,4},{6,7},{7,6},{8,9},{9,8},{10,11... | collective-permute-start | bytes 1572872 | tf_op jit(solution)/shard_map/ppermute | solution.py:31
  77.5 0.5 early.1
  78.0 1.1 collective-permute-done.11.other
  79.1 4.4 %right.1 = (f32[16,16,1024]{2,1,0:T(8,128)S(1)}, bf16[16,16,1024]{2,1,0:T(8,128)(2,1)S(1)}, bf16[256,2048]{1,0:T(8,128)(2,1)S(1)}) custom-call(s32[2]{0:T(128)S(1)} %pad_add_fusion.at, bf16[256,2048]{1,0:T(8,128)(2,1)S(1)} %copy-done, bf16[256,2048]{1,0:T(8,128)(2,1)S(1)} %copy-done.2, bf16[512,2048]{1,0:T(8,128)(2,1)} %get-tuple-element.51.low_hbm, ...), custom_call_target="tpu_custom_call" | custom-call | flops 2000000000 | bytes 7995400 | tf_op jit(solution)/shard_map/right/pallas_call | solution.py:292
  83.5 0.5 collective-permute-start.12
  84.0 1.5 %collective-permute-start.9 = (bf16[2,256,512]{2,1,0:T(8,128)(2,1)}, bf16[2,256,512]{2,1,0:T(8,128)(2,1)}, u32[]{:S(2)}, u32[]{:S(2)}) collective-permute-start(bf16[2,256,512]{2,1,0:T(8,128)(2,1)} %grad.3), channel_id=1, source_target_pairs={{0,2},{2,0},{1,3},{3,1},{4,6},{6,4},{5,7},{7,5},{8,10},{10,8},{9,1... | collective-permute-start | bytes 1572872 | tf_op jit(solution)/shard_map/ppermute | solution.py:31
  85.4 0.1 collective-permute-done.12.got
  85.5 0.9 add.5
  86.4 3.6 %all-to-all-start.3 = ((bf16[16,16,1024]{2,1,0:T(8,128)(2,1)}), bf16[16,16,1024]{2,1,0:T(8,128)(2,1)S(1)}, u32[]{:S(2)}, u32[]{:S(2)}) async-start(bf16[16,16,1024]{2,1,0:T(8,128)(2,1)} %add.5), calls=%async_computation.3 | async-start | bytes 1048576 | tf_op jit(solution)/shard_map/all_to_all | solution.py:361
  90.0 4.0 %gram.1.a_in = f32[256,512]{1,0:T(8,128)S(1)} custom-call(bf16[256,2048]{1,0:T(8,128)(2,1)S(1)} %get-tuple-element.62.left), custom_call_target="tpu_custom_call" | custom-call | flops 300000000 | bytes 1572864 | tf_op jit(solution)/shard_map/gram/pallas_call | solution.py:292
  94.0 3.1 %step.2.a_in = f32[256,512]{1,0:T(8,128)S(1)} custom-call(f32[256,512]{1,0:T(8,128)S(1)} %gram.1.a_in), custom_call_target="tpu_custom_call", output_to_operand_aliasing={{}: (0, {})} | custom-call | flops 300000000 | bytes 1048576 | tf_op jit(solution)/shard_map/step/pallas_call | solution.py:292
  97.0 3.9 %all-to-all-done.3.parts = bf16[16,16,1024]{2,1,0:T(8,128)(2,1)S(1)} async-done(((bf16[16,16,1024]{2,1,0:T(8,128)(2,1)}), bf16[16,16,1024]{2,1,0:T(8,128)(2,1)S(1)}, u32[]{:S(2)}, u32[]{:S(2)}) %all-to-all-start.3) | async-done | bytes 524320 | tf_op jit(solution)/shard_map/all_to_all | solution.py:361
  100.9 0.8 spread.6
  101.7 0.0 collective-permute-done.9.far
  101.7 3.4 %all-to-all-start.4 = ((bf16[8,16,1024]{2,1,0:T(8,128)(2,1)}), bf16[8,16,1024]{2,1,0:T(8,128)(2,1)S(1)}, u32[]{:S(2)}, u32[]{:S(2)}) async-start(bf16[8,16,1024]{2,1,0:T(8,128)(2,1)} %spread.6), calls=%async_computation.4 | async-start | bytes 524288 | tf_op jit(solution)/shard_map/all_to_all | solution.py:366
  105.2 1.6 %collective-permute-start.3 = (bf16[2,256,512]{2,1,0:T(8,128)(2,1)}, bf16[2,256,512]{2,1,0:T(8,128)(2,1)}, u32[]{:S(2)}, u32[]{:S(2)}) collective-permute-start(bf16[2,256,512]{2,1,0:T(8,128)(2,1)} %grad.2.own), channel_id=1, source_target_pairs={{0,1},{1,0},{2,3},{3,2},{4,5},{5,4},{6,7},{7,6},{8,9},{9,8},{10,11... | collective-permute-start | bytes 1572872 | tf_op jit(solution)/shard_map/ppermute | solution.py:31
  106.7 0.3 collective-permute-start.13
  107.1 3.0 %step.3.a_in = f32[256,512]{1,0:T(8,128)S(1)} custom-call(f32[256,512]{1,0:T(8,128)S(1)} %step.2.a_in), custom_call_target="tpu_custom_call", output_to_operand_aliasing={{}: (0, {})} | custom-call | flops 300000000 | bytes 1048576 | tf_op jit(solution)/shard_map/step/pallas_call | solution.py:292
  110.1 3.6 %basis.1 = (f32[256,256]{1,0:T(8,128)S(1)}, bf16[512,256]{1,0:T(8,128)(2,1)S(1)}) custom-call(s32[2]{0:T(128)S(1)} %pad_add_fusion.at, f32[256,512]{1,0:T(8,128)S(1)} %step.3.a_in, bf16[256,2048]{1,0:T(8,128)(2,1)S(1)} %get-tuple-element.62.left), custom_call_target="tpu_custom_call" | custom-call | flops 300000000 | bytes 2097160 | tf_op jit(solution)/shard_map/basis/pallas_call | solution.py:292
  113.7 0.7 copy-done.5
  114.4 0.8 all-to-all-done.4.parts
  115.2 0.9 spread.7
  116.0 4.5 %all-to-all-start.5 = ((bf16[16,16,1024]{2,1,0:T(8,128)(2,1)}), bf16[16,16,1024]{2,1,0:T(8,128)(2,1)S(1)}, u32[]{:S(2)}, u32[]{:S(2)}) async-start(bf16[16,16,1024]{2,1,0:T(8,128)(2,1)} %spread.7), calls=%async_computation.5 | async-start | bytes 1048576 | tf_op jit(solution)/shard_map/all_to_all | solution.py:370
  120.6 1.9 %collective-permute-start.15 = (bf16[2,256,512]{2,1,0:T(8,128)(2,1)S(1)}, bf16[2,256,512]{2,1,0:T(8,128)(2,1)S(1)}, u32[]{:S(2)}, u32[]{:S(2)}) collective-permute-start(bf16[2,256,512]{2,1,0:T(8,128)(2,1)S(1)} %copy-done.4), channel_id=1, source_target_pairs={{0,1},{1,0},{2,3},{3,2},{4,5},{5,4},{6,7},{7,6},{8,9},{9,8},{10,11... | collective-permute-start | bytes 1572872 | tf_op jit(solution)/shard_map/ppermute | solution.py:31
  122.4 2.2 %place.1 = bf16[256,2048]{1,0:T(8,128)(2,1)} custom-call(s32[2]{0:T(128)S(1)} %pad_add_fusion.at, bf16[2,256,512]{2,1,0:T(8,128)(2,1)} %grad.2.own, bf16[2,256,512]{2,1,0:T(8,128)(2,1)} %collective-permute-done.3.near, bf16[2,256,512]{2,1,0:T(8,128)(2,1)} %collective-permute-done.9.far, bf16[2,256,512]{2,1,0:T(8,128)(2,1)} %collective-permute-done.13.diag), custom_call_target="tpu_custom_call" | custom-call | flops 1000000 | bytes 3145736 | tf_op jit(solution)/shard_map/place/pallas_call | solution.py:317
  124.7 5.9 %all-to-all-done.5.chunks = bf16[16,16,1024]{2,1,0:T(8,128)(2,1)S(1)} async-done(((bf16[16,16,1024]{2,1,0:T(8,128)(2,1)}), bf16[16,16,1024]{2,1,0:T(8,128)(2,1)S(1)}, u32[]{:S(2)}, u32[]{:S(2)}) %all-to-all-start.5) | async-done | bytes 524320 | tf_op jit(solution)/shard_map/all_to_all | solution.py:370
  130.6 2.5 %collective-permute-start.14 = (bf16[16,16,1024]{2,1,0:T(8,128)(2,1)S(1)}, bf16[16,16,1024]{2,1,0:T(8,128)(2,1)S(1)}, u32[]{:S(2)}, u32[]{:S(2)}) collective-permute-start(bf16[16,16,1024]{2,1,0:T(8,128)(2,1)S(1)} %all-to-all-done.5.chunks), channel_id=1, source_target_pairs={{0,1},{1,0},{2,3},{3,2},{4,5},{5,4},{6,7},{7,6},{8,9},{9,8},{10,11... | collective-permute-start | bytes 1572872 | tf_op jit(solution)/shard_map/ppermute | solution.py:31
  133.1 1.2 begin.1
  134.3 0.3 collective-permute-done.14.other
  134.6 6.9 %last.1 = (f32[512,2048]{1,0:T(8,128)}, f32[512,256]{1,0:T(8,128)}) custom-call(s32[2]{0:T(128)S(1)} %pad_add_fusion.at, bf16[16,16,1024]{2,1,0:T(8,128)(2,1)S(1)} %collective-permute-done.14.other, f32[256,256]{1,0:T(8,128)S(1)} %get-tuple-element.69.inverse, bf16[512,256]{1,0:T(8,128)(2,1)} %copy-done.5, f32[256,2048]{1,0:T(8,128)S(1)} %get-tuple-element.70.begun, ...), custom_call_target="tpu_custom_call" | custom-call | flops 2000000000 | bytes 14680072 | tf_op jit(solution)/shard_map/last/pallas_call | solution.py:317
  (17 shorter events, 0.0 us)
Async XLA Ops:
  0.6 4.7 %collective-permute-start.1 = (bf16[512,256]{1,0:T(8,128)(2,1)}, bf16[512,256]{1,0:T(8,128)(2,1)S(1)}, u32[]{:S(2)}, u32[]{:S(2)}) collective-permute-start(bf16[512,256]{1,0:T(8,128)(2,1)} %w0.1), channel_id=1, source_target_pairs={{0,1},{1,0},{2,3},{3,2},{4,5},{5,4},{6,7},{7,6},{8,9},{9,8},{10,11... | collective-permute-start | bytes 786440 | tf_op jit(solution)/shard_map/ppermute | solution.py:31
  4.0 8.1 %collective-permute-start = (bf16[512,256]{1,0:T(8,128)(2,1)}, bf16[512,256]{1,0:T(8,128)(2,1)S(1)}, u32[]{:S(2)}, u32[]{:S(2)}) collective-permute-start(bf16[512,256]{1,0:T(8,128)(2,1)} %w0.1), channel_id=1, source_target_pairs={{0,2},{2,0},{1,3},{3,1},{4,6},{6,4},{5,7},{7,5},{8,10},{10,8},{9,1... | collective-permute-start | bytes 786440 | tf_op jit(solution)/shard_map/ppermute | solution.py:31
  5.3 7.6 %copy-start.1 = (bf16[256,2048]{1,0:T(8,128)(2,1)S(1)}, bf16[256,2048]{1,0:T(8,128)(2,1)}, u32[]{:S(2)}) copy-start(bf16[256,2048]{1,0:T(8,128)(2,1)} %og.3) | copy-start | bytes 3145732
  5.3 8.7 %copy-start = (bf16[256,2048]{1,0:T(8,128)(2,1)S(1)}, bf16[256,2048]{1,0:T(8,128)(2,1)}, u32[]{:S(2)}) copy-start(bf16[256,2048]{1,0:T(8,128)(2,1)} %ctx.7) | copy-start | bytes 3145732
  5.3 8.7 %copy-start.7 = (bf16[512,256]{1,0:T(8,128)(2,1)S(1)}, bf16[512,256]{1,0:T(8,128)(2,1)}, u32[]{:S(2)}) copy-start(bf16[512,256]{1,0:T(8,128)(2,1)} %w0.1) | copy-start | bytes 786436
  10.2 3.0 %collective-permute-start.5 = (bf16[256,512]{1,0:T(8,128)(2,1)}, bf16[256,512]{1,0:T(8,128)(2,1)S(1)}, u32[]{:S(2)}, u32[]{:S(2)}) collective-permute-start(bf16[256,512]{1,0:T(8,128)(2,1)} %get-tuple-element.43), channel_id=1, source_target_pairs={{0,1},{1,0},{2,3},{3,2},{4,5},{5,4},{6,7},{7,6},{8,9},{9,8},{10,11... | collective-permute-start | bytes 786440 | tf_op jit(solution)/shard_map/ppermute | solution.py:31
  12.0 2.0 %collective-permute-start.6 = (bf16[512,256]{1,0:T(8,128)(2,1)S(1)}, bf16[512,256]{1,0:T(8,128)(2,1)S(1)}, u32[]{:S(2)}, u32[]{:S(2)}) collective-permute-start(bf16[512,256]{1,0:T(8,128)(2,1)S(1)} %collective-permute-done.w2), channel_id=1, source_target_pairs={{0,1},{1,0},{2,3},{3,2},{4,5},{5,4},{6,7},{7,6},{8,9},{9,8},{10,11... | collective-permute-start | bytes 786440 | tf_op jit(solution)/shard_map/ppermute | solution.py:31
  12.9 24.9 %collective-permute-start.4 = (bf16[256,2048]{1,0:T(8,128)(2,1)S(1)}, bf16[256,2048]{1,0:T(8,128)(2,1)}, u32[]{:S(2)}, u32[]{:S(2)}) collective-permute-start(bf16[256,2048]{1,0:T(8,128)(2,1)S(1)} %copy-done.1), channel_id=1, source_target_pairs={{0,2},{2,0},{1,3},{3,1},{4,6},{6,4},{5,7},{7,5},{8,10},{10,8},{9,1... | collective-permute-start | bytes 3145736 | tf_op jit(solution)/shard_map/ppermute | solution.py:31
  12.9 12.3 %collective-permute-start.2 = (bf16[256,2048]{1,0:T(8,128)(2,1)S(1)}, bf16[256,2048]{1,0:T(8,128)(2,1)}, u32[]{:S(2)}, u32[]{:S(2)}) collective-permute-start(bf16[256,2048]{1,0:T(8,128)(2,1)S(1)} %copy-done.1), channel_id=1, source_target_pairs={{0,1},{1,0},{2,3},{3,2},{4,5},{5,4},{6,7},{7,6},{8,9},{9,8},{10,11... | collective-permute-start | bytes 3145736 | tf_op jit(solution)/shard_map/ppermute | solution.py:31
  16.5 8.7 %copy-start.6 = (bf16[256,512]{1,0:T(8,128)(2,1)S(1)}, bf16[256,512]{1,0:T(8,128)(2,1)}, u32[]{:S(2)}) copy-start(bf16[256,512]{1,0:T(8,128)(2,1)} %get-tuple-element.48.c0) | copy-start | bytes 786436
  16.5 2.0 %collective-permute-start.7 = (bf16[16,16,1024]{2,1,0:T(8,128)(2,1)S(1)}, bf16[16,16,1024]{2,1,0:T(8,128)(2,1)S(1)}, u32[]{:S(2)}, u32[]{:S(2)}) collective-permute-start(bf16[16,16,1024]{2,1,0:T(8,128)(2,1)S(1)} %get-tuple-element.47), channel_id=1, source_target_pairs={{0,1},{1,0},{2,3},{3,2},{4,5},{5,4},{6,7},{7,6},{8,9},{9,8},{10,11... | collective-permute-start | bytes 1572872 | tf_op jit(solution)/shard_map/ppermute | solution.py:31
  19.4 16.6 %all-to-all-start = ((bf16[16,16,1024]{2,1,0:T(8,128)(2,1)}), bf16[16,16,1024]{2,1,0:T(8,128)(2,1)S(1)}, u32[]{:S(2)}, u32[]{:S(2)}) async-start(bf16[16,16,1024]{2,1,0:T(8,128)(2,1)} %add.4), calls=%async_computation | async-start | bytes 1048576 | tf_op jit(solution)/shard_map/all_to_all | solution.py:361
  37.8 27.3 %collective-permute-start.8 = (bf16[256,2048]{1,0:T(8,128)(2,1)}, bf16[256,2048]{1,0:T(8,128)(2,1)}, u32[]{:S(2)}, u32[]{:S(2)}) collective-permute-start(bf16[256,2048]{1,0:T(8,128)(2,1)} %collective-permute-done.4.h0.g2), channel_id=1, source_target_pairs={{0,1},{1,0},{2,3},{3,2},{4,5},{5,4},{6,7},{7,6},{8,9},{9,8},{10,11... | collective-permute-start | bytes 3145736 | tf_op jit(solution)/shard_map/ppermute | solution.py:31
  38.6 19.7 %all-to-all-start.1 = ((bf16[8,16,1024]{2,1,0:T(8,128)(2,1)}), bf16[8,16,1024]{2,1,0:T(8,128)(2,1)S(1)}, u32[]{:S(2)}, u32[]{:S(2)}) async-start(bf16[8,16,1024]{2,1,0:T(8,128)(2,1)} %spread.4), calls=%async_computation.1 | async-start | bytes 524288 | tf_op jit(solution)/shard_map/all_to_all | solution.py:366
  58.2 17.1 %collective-permute-start.10 = (bf16[2,256,512]{2,1,0:T(8,128)(2,1)}, bf16[2,256,512]{2,1,0:T(8,128)(2,1)S(1)}, u32[]{:S(2)}, u32[]{:S(2)}) collective-permute-start(bf16[2,256,512]{2,1,0:T(8,128)(2,1)} %get-tuple-element.57), channel_id=1, source_target_pairs={{0,2},{2,0},{1,3},{3,1},{4,6},{6,4},{5,7},{7,5},{8,10},{10,8},{9,1... | collective-permute-start | bytes 1572872 | tf_op jit(solution)/shard_map/ppermute | solution.py:31
  59.1 16.2 %all-to-all-start.2 = ((bf16[16,16,1024]{2,1,0:T(8,128)(2,1)}), bf16[16,16,1024]{2,1,0:T(8,128)(2,1)S(1)}, u32[]{:S(2)}, u32[]{:S(2)}) async-start(bf16[16,16,1024]{2,1,0:T(8,128)(2,1)} %spread.5), calls=%async_computation.2 | async-start | bytes 1048576 | tf_op jit(solution)/shard_map/all_to_all | solution.py:370
  65.0 14.0 %copy-start.2 = (bf16[256,2048]{1,0:T(8,128)(2,1)S(1)}, bf16[256,2048]{1,0:T(8,128)(2,1)}, u32[]{:S(2)}) copy-start(bf16[256,2048]{1,0:T(8,128)(2,1)} %og.3) | copy-start | bytes 3145732
  75.4 3.7 %copy-start.3 = (bf16[2,256,512]{2,1,0:T(8,128)(2,1)}, bf16[2,256,512]{2,1,0:T(8,128)(2,1)S(1)}, u32[]{:S(2)}) copy-start(bf16[2,256,512]{2,1,0:T(8,128)(2,1)S(1)} %collective-permute-done.10.c2) | copy-start | bytes 1572868
  75.4 3.7 %collective-permute-start.11 = (bf16[16,16,1024]{2,1,0:T(8,128)(2,1)S(1)}, bf16[16,16,1024]{2,1,0:T(8,128)(2,1)S(1)}, u32[]{:S(2)}, u32[]{:S(2)}) collective-permute-start(bf16[16,16,1024]{2,1,0:T(8,128)(2,1)S(1)} %all-to-all-done.2.mine), channel_id=1, source_target_pairs={{0,1},{1,0},{2,3},{3,2},{4,5},{5,4},{6,7},{7,6},{8,9},{9,8},{10,11... | collective-permute-start | bytes 1572872 | tf_op jit(solution)/shard_map/ppermute | solution.py:31
  83.5 2.0 %collective-permute-start.12 = (bf16[16,16,1024]{2,1,0:T(8,128)(2,1)S(1)}, bf16[16,16,1024]{2,1,0:T(8,128)(2,1)S(1)}, u32[]{:S(2)}, u32[]{:S(2)}) collective-permute-start(bf16[16,16,1024]{2,1,0:T(8,128)(2,1)S(1)} %get-tuple-element.61), channel_id=1, source_target_pairs={{0,1},{1,0},{2,3},{3,2},{4,5},{5,4},{6,7},{7,6},{8,9},{9,8},{10,11... | collective-permute-start | bytes 1572872 | tf_op jit(solution)/shard_map/ppermute | solution.py:31
  84.0 17.7 %collective-permute-start.9 = (bf16[2,256,512]{2,1,0:T(8,128)(2,1)}, bf16[2,256,512]{2,1,0:T(8,128)(2,1)}, u32[]{:S(2)}, u32[]{:S(2)}) collective-permute-start(bf16[2,256,512]{2,1,0:T(8,128)(2,1)} %grad.3), channel_id=1, source_target_pairs={{0,2},{2,0},{1,3},{3,1},{4,6},{6,4},{5,7},{7,5},{8,10},{10,8},{9,1... | collective-permute-start | bytes 1572872 | tf_op jit(solution)/shard_map/ppermute | solution.py:31
  86.4 14.5 %all-to-all-start.3 = ((bf16[16,16,1024]{2,1,0:T(8,128)(2,1)}), bf16[16,16,1024]{2,1,0:T(8,128)(2,1)S(1)}, u32[]{:S(2)}, u32[]{:S(2)}) async-start(bf16[16,16,1024]{2,1,0:T(8,128)(2,1)} %add.5), calls=%async_computation.3 | async-start | bytes 1048576 | tf_op jit(solution)/shard_map/all_to_all | solution.py:361
  101.7 13.4 %all-to-all-start.4 = ((bf16[8,16,1024]{2,1,0:T(8,128)(2,1)}), bf16[8,16,1024]{2,1,0:T(8,128)(2,1)S(1)}, u32[]{:S(2)}, u32[]{:S(2)}) async-start(bf16[8,16,1024]{2,1,0:T(8,128)(2,1)} %spread.6), calls=%async_computation.4 | async-start | bytes 524288 | tf_op jit(solution)/shard_map/all_to_all | solution.py:366
  105.2 15.4 %copy-start.4 = (bf16[2,256,512]{2,1,0:T(8,128)(2,1)S(1)}, bf16[2,256,512]{2,1,0:T(8,128)(2,1)}, u32[]{:S(2)}) copy-start(bf16[2,256,512]{2,1,0:T(8,128)(2,1)} %copy-done.3) | copy-start | bytes 1572868
  105.2 17.3 %collective-permute-start.3 = (bf16[2,256,512]{2,1,0:T(8,128)(2,1)}, bf16[2,256,512]{2,1,0:T(8,128)(2,1)}, u32[]{:S(2)}, u32[]{:S(2)}) collective-permute-start(bf16[2,256,512]{2,1,0:T(8,128)(2,1)} %grad.2.own), channel_id=1, source_target_pairs={{0,1},{1,0},{2,3},{3,2},{4,5},{5,4},{6,7},{7,6},{8,9},{9,8},{10,11... | collective-permute-start | bytes 1572872 | tf_op jit(solution)/shard_map/ppermute | solution.py:31
  106.7 15.7 %collective-permute-start.13 = (bf16[2,256,512]{2,1,0:T(8,128)(2,1)}, bf16[2,256,512]{2,1,0:T(8,128)(2,1)}, u32[]{:S(2)}, u32[]{:S(2)}) collective-permute-start(bf16[2,256,512]{2,1,0:T(8,128)(2,1)} %collective-permute-done.9.far), channel_id=1, source_target_pairs={{0,1},{1,0},{2,3},{3,2},{4,5},{5,4},{6,7},{7,6},{8,9},{9,8},{10,11... | collective-permute-start | bytes 1572872 | tf_op jit(solution)/shard_map/ppermute | solution.py:31
  113.7 0.7 copy-start.5
  116.0 14.6 %all-to-all-start.5 = ((bf16[16,16,1024]{2,1,0:T(8,128)(2,1)}), bf16[16,16,1024]{2,1,0:T(8,128)(2,1)S(1)}, u32[]{:S(2)}, u32[]{:S(2)}) async-start(bf16[16,16,1024]{2,1,0:T(8,128)(2,1)} %spread.7), calls=%async_computation.5 | async-start | bytes 1048576 | tf_op jit(solution)/shard_map/all_to_all | solution.py:370
  120.6 12.5 %collective-permute-start.15 = (bf16[2,256,512]{2,1,0:T(8,128)(2,1)S(1)}, bf16[2,256,512]{2,1,0:T(8,128)(2,1)S(1)}, u32[]{:S(2)}, u32[]{:S(2)}) collective-permute-start(bf16[2,256,512]{2,1,0:T(8,128)(2,1)S(1)} %copy-done.4), channel_id=1, source_target_pairs={{0,1},{1,0},{2,3},{3,2},{4,5},{5,4},{6,7},{7,6},{8,9},{9,8},{10,11... | collective-permute-start | bytes 1572872 | tf_op jit(solution)/shard_map/ppermute | solution.py:31
  130.6 4.0 %collective-permute-start.14 = (bf16[16,16,1024]{2,1,0:T(8,128)(2,1)S(1)}, bf16[16,16,1024]{2,1,0:T(8,128)(2,1)S(1)}, u32[]{:S(2)}, u32[]{:S(2)}) collective-permute-start(bf16[16,16,1024]{2,1,0:T(8,128)(2,1)S(1)} %all-to-all-done.5.chunks), channel_id=1, source_target_pairs={{0,1},{1,0},{2,3},{3,2},{4,5},{5,4},{6,7},{7,6},{8,9},{9,8},{10,11... | collective-permute-start | bytes 1572872 | tf_op jit(solution)/shard_map/ppermute | solution.py:31

commit v9 on v8

--- a/solution.py
+++ b/solution.py
@@ -126,6 +126,17 @@
 
 def add_kernel(keep, got, out):
     out[...] = (keep[...] + got[...].astype(F32)).astype(BF16)
+
+
+def sum_kernel(parts, out):
+    out[...] = parts[...].astype(F32).sum(0)
+
+
+def close_kernel(part, one, opposite, three, out):
+    part, one, opposite, three = (x[...].astype(F32) for x in (part, one, opposite, three))
+    whole = ((part + opposite) + (one + three)).astype(BF16)
+    for n in range(CHUNKS):
+        out[n] = whole
 
 
 def spread_kernel(parts, out):
@@ -250,27 +261,43 @@
 
 
 def last_kernel(
-    share, at, other, inverse, basis, begun, turned, merged, g2, g3,
-    new_error, factor_q, half,
+    share, at, other, inverse, basis, begun, turned, merged_hbm, g2_hbm, g3_hbm,
+    out_hbm, factor_q, half, held, g2, g3, sems_in, sems_out,
 ):
-    step = pl.program_id(0)
     zl, core = at[0], at[1]
-
-    @pl.when(step == 0)
-    def _():
-        unchunk(other, half)
-
-    cols = pl.ds(pl.multiple_of(step * ROWS, ROWS), ROWS)
+    steps = FEAT // ROWS
+    blocks = [pl.ds(n * ROWS, ROWS) for n in range(steps)]
+    tops = [pl.ds(n * TOK, TOK) for n in range(ROWS // TOK)]
+    arriving, leaving = [], []
+    for n, cols in enumerate(blocks):
+        pairs = [(g2_hbm.at[:, cols], g2.at[:, cols]), (g3_hbm.at[:, cols], g3.at[:, cols])]
+        pairs += [(merged_hbm.at[r, cols], held.at[r, cols]) for r in tops]
+        arriving.append(
+            [pltpu.make_async_copy(*pair, sems_in.at[n, m]) for m, pair in enumerate(pairs)]
+        )
+        for copy in arriving[n]:
+            copy.start()
+    unchunk(other, half)
     first, second = two(columns_of(inverse, 1 - core))
-    q = mm(first, half[:, cols], 1, 0) + mm(second, half[:, cols], 1, 0)
-    q = (begun[:, cols] + q) * share
-    lhs = jnp.concatenate([turned[...], basis[...]], 1)
-    rhs = jnp.concatenate([g2[...], g3[...], q.astype(BF16)], 0)
-    new_error[...] = merged[...] + mm(lhs, rhs, 1, 0)
-
-    @pl.when(step == zl * 2 + core)
-    def _():
-        factor_q[...] = q.T
+    for n, cols in enumerate(blocks):
+        q = mm(first, half[:, cols], 1, 0) + mm(second, half[:, cols], 1, 0)
+        q = (begun[:, cols] + q) * share
+
+        @pl.when(zl * 2 + core == n)
+        def _(q=q):
+            factor_q[...] = q.T
+
+        for copy in arriving[n]:
+            copy.wait()
+        lhs = jnp.concatenate([turned[...], basis[...]], 1)
+        rhs = jnp.concatenate([g2[:, cols], g3[:, cols], q.astype(BF16)], 0)
+        held[:, cols] = held[:, cols] + mm(lhs, rhs, 1, 0)
+        for m, r in enumerate(tops):
+            copy = pltpu.make_async_copy(held.at[r, cols], out_hbm.at[r, cols], sems_out.at[n, m])
+            copy.start()
+            leaving.append(copy)
+    for copy in leaving:
+        copy.wait()
 
 
 def size(shape, dtype):
@@ -355,11 +382,22 @@
     return out
 
 
-def across_plane(keep, send, beside=()):
+def across_plane(keep, send, beside=(), copies=8):
     got = swap(send, "core")
     (half,) = call(add_kernel, [(CHUNKED, BF16)], (keep, got), 1_000_000, "add")
     parts = tied(lax.all_to_all(half, ("y", "x"), 0, 0), *beside)
-    return spread(parts, 8)
+    if copies:
+        return spread(parts, copies)
+    (part,) = call(sum_kernel, [(CHUNK, F32)], (parts,), 1_000_000, "sum")
+    return part
+
+
+def across_z_by_steps(part, beside=()):
+    far = tied(swap(part, "zl"), *beside)
+    part = (part + far).astype(BF16)
+    return (part,) + tuple(
+        lax.ppermute(part, "zh", [(i, (i + step) % 4) for i in range(4)]) for step in (1, 2, 3)
+    )
 
 
 def across_z(copies, beside=()):
@@ -420,7 +458,7 @@
         turned,
         loose=(3,),
     )
-    part = across_plane(keep, send, (merged,))
+    part = across_plane(keep, send, (merged,), 0)
     g_diag = swap(tied(g_far, part), "core")
 
     def grad(g0, g1):
@@ -438,9 +476,10 @@
         return out
 
     i_home = grad(out_grad, g_near)
-    zs = across_z(tied(part, g_far), (i_home,))
-    c_far = swap(tied(c_far, zs), "zl")
-    mine = back_over_plane(zs)
+    zs = across_z_by_steps(tied(part, g_far), (i_home,))
+    c_far = swap(tied(c_far, *zs[1:]), "zl")
+    (whole_part,) = call(close_kernel, [(CHUNKED, BF16)], zs, 1_000_000, "close")
+    mine = lax.all_to_all(whole_part, ("y", "x"), 0, 0)
 
     i_far = grad(g_far, g_diag)
     other = swap(tied(mine, i_far, c_far), "core")
@@ -510,19 +549,27 @@
     )
     other = tied(other, begun)
 
-    new_error, factor_q = call_grid(
+    new_error, factor_q = pl.pallas_call(
         functools.partial(last_kernel, 1.0 / (SIZES[0] * SIZES[1] * SIZES[2])),
-        4,
-        [
-            ((ROWS, FEAT), F32, column(ROWS)),
-            ((ROWS, RANK), F32, whole(ROWS, RANK)),
+        out_shape=[pltpu.HBM((ROWS, FEAT), F32), jax.ShapeDtypeStruct((ROWS, RANK), F32)],
+        in_specs=[SMEM, VMEM, VMEM, VMEM, VMEM, VMEM, ANY, ANY, ANY],
+        out_specs=[ANY, VMEM],
+        scratch_shapes=[
+            pltpu.VMEM((HALF, FEAT), BF16),
+            pltpu.VMEM((ROWS, FEAT), F32),
+            pltpu.VMEM((TOK, FEAT), BF16),
+            pltpu.VMEM((TOK, FEAT), BF16),
+            pltpu.SemaphoreType.DMA((4, 4)),
+            pltpu.SemaphoreType.DMA((4, 2)),
         ],
-        [SMEM, VMEM, VMEM, whole(ROWS, RANK), VMEM, VMEM]
-        + [column(ROWS), column(TOK), column(TOK)],
-        (at, other, inverse, basis, begun, far_turned, merged, g_far, g_diag),
-        2_000_000_000,
-        "last",
-        [((HALF, FEAT), BF16)],
+        compiler_params=pltpu.CompilerParams(vmem_limit_bytes=20 * 2**20),
+        cost_estimate=pl.CostEstimate(
+            flops=2_000_000_000, bytes_accessed=10_000_000, transcendentals=0
+        ),
+        name="last",
+    )(
+        at, other, inverse, basis, begun, far_turned,
+        in_hbm(merged), in_hbm(g_far), in_hbm(g_diag),
     )
     return in_grad, new_error[None], factor_q
 

time: 143 us -> 141 us (0.986)
  starting transfers between devices: 47 us -> 53.7 us
  waiting for transfers between devices: 37.4 us -> 30.9 us
    ppermute x0 -> x3, starting transfers between devices: none -> 8.45 us  [across_z_by_steps(): lax.ppermute(part, 'zh', [(i, (i + step) % 4) for i in range(4)])]
    all_to_all x2 -> x1, waiting for transfers between devices: 11.9 us -> 3.71 us  [back_over_plane(): lax.all_to_all(spread(tied(parts, *beside), CHUNKS), ('y', 'x'), 0, 0)]
    all_to_all x2 -> x1, waiting for transfers between devices: 8.96 us -> 0.76 us  [across_z(): return tied(lax.all_to_all(copies, ('zh', 'zl'), 0, 0), *beside)]
    pallas_call x4 -> x3, Pallas kernels: 19.9 us -> 13 us  [call_grid(): pl.pallas_call(kernel, grid=(steps,), out_shape=[(jax.ShapeDtypeStruct if...]
    pallas_call x0 -> x1, Pallas kernels: none -> 6.83 us  [on_device(): pl.pallas_call(functools.partial(last_kernel, 1.0 / (SIZES[0] * SIZES[1]...]
    all_to_all x2 -> x1, starting transfers between devices: 10.4 us -> 3.92 us  [back_over_plane(): lax.all_to_all(spread(tied(parts, *beside), CHUNKS), ('y', 'x'), 0, 0)]
    all_to_all x0 -> x1, starting transfers between devices: none -> 6.52 us  [on_device(): mine = lax.all_to_all(whole_part, ('y', 'x'), 0, 0)]
    all_to_all x2 -> x1, starting transfers between devices: 10.7 us -> 4.96 us  [across_z(): return tied(lax.all_to_all(copies, ('zh', 'zl'), 0, 0), *beside)]
  transfers between devices with their start and end apart: 22 -> 25, of which waited for: 14 -> 15; matrix products, arithmetic and copies ran while one was open for 0% -> 0% of each run, Pallas kernels for 31% -> 31%
where the time goes in v9:
time: 141 us
  Pallas kernels  54.7 us (39%)
  starting transfers between devices  53.7 us (38%)
  waiting for transfers between devices  30.9 us (22%)
    pallas_call x16, Pallas kernels, call(): pl.pallas_call(kernel, out_shape=[(pltpu.HBM if free else jax.ShapeDtypeS...  34.9 us
    ppermute x17, starting transfers between devices, swap(): return lax.ppermute(x, axis, [(0, 1), (1, 0)])  20.5 us
    pallas_call x3, Pallas kernels, call_grid(): pl.pallas_call(kernel, grid=(steps,), out_shape=[(jax.ShapeDtypeStruct if...  13 us
    all_to_all x2, starting transfers between devices, across_plane(): parts = tied(lax.all_to_all(half, ('y', 'x'), 0, 0), *beside)  9.36 us
    ppermute x17, waiting for transfers between devices, swap(): return lax.ppermute(x, axis, [(0, 1), (1, 0)])  8.94 us
    all_to_all x2, waiting for transfers between devices, across_plane(): parts = tied(lax.all_to_all(half, ('y', 'x'), 0, 0), *beside)  8.86 us
    ppermute x3, starting transfers between devices, across_z_by_steps(): lax.ppermute(part, 'zh', [(i, (i + step) % 4) for i in range(4)])  8.45 us
    pallas_call x1, Pallas kernels, on_device(): pl.pallas_call(functools.partial(last_kernel, 1.0 / (SIZES[0] * SIZES[1]...  6.83 us
  transfers between devices with their start and end apart: 25, of which 15 were waited for; matrix products, arithmetic and copies ran while one was open for 0% of the time, Pallas kernels for 31%

profile of v9, /device:TPU:1, one launch (start us, length us, event | category | flops | bytes accessed | tf_op | source)
XLA Modules:
  0.0 140.5 jit_solution(15970404082420129572)
XLA Ops:
  0.6 3.3 %collective-permute-start.1 = (bf16[512,256]{1,0:T(8,128)(2,1)}, bf16[512,256]{1,0:T(8,128)(2,1)S(1)}, u32[]{:S(2)}, u32[]{:S(2)}) collective-permute-start(bf16[512,256]{1,0:T(8,128)(2,1)} %w0.1), channel_id=1, source_target_pairs={{0,1},{1,0},{2,3},{3,2},{4,5},{5,4},{6,7},{7,6},{8,9},{9,8},{10,11... | collective-permute-start | bytes 786440 | tf_op jit(solution)/shard_map/ppermute | solution.py:31
  4.0 0.1 pad_add_fusion.at
  4.0 1.3 collective-permute-done.1.w1
  5.3 4.9 %prepare.1 = (bf16[256,512]{1,0:T(8,128)(2,1)}, bf16[256,512]{1,0:T(8,128)(2,1)}, bf16[2,256,512]{2,1,0:T(8,128)(2,1)}, bf16[512,2048]{1,0:T(8,128)(2,1)S(1)}, bf16[512,2048]{1,0:T(8,128)(2,1)}) custom-call(s32[2]{0:T(128)S(1)} %pad_add_fusion.at, bf16[256,2048]{1,0:T(8,128)(2,1)} %ctx.7, f32[512,2048]{1,0:T(8,128)} %bitcast.4), custom_call_target="tpu_custom_call" | custom-call | flops 4000000 | bytes 10485768 | tf_op jit(solution)/shard_map/prepare/pallas_call | solution.py:344
  10.2 0.4 collective-permute-start.5
  10.6 1.5 %collective-permute-done.w2 = bf16[512,256]{1,0:T(8,128)(2,1)S(1)} collective-permute-done((bf16[512,256]{1,0:T(8,128)(2,1)}, bf16[512,256]{1,0:T(8,128)(2,1)S(1)}, u32[]{:S(2)}, u32[]{:S(2)}) %collective-permute-start) | collective-permute-done | bytes 262176 | tf_op jit(solution)/shard_map/ppermute | solution.py:31
  12.0 0.9 collective-permute-start.6
  12.9 0.3 collective-permute-start.2
  13.2 0.0 collective-permute-done.5.c1
  13.2 0.9 collective-permute-done.6.w3
  14.1 2.4 %left.1 = (f32[16,16,1024]{2,1,0:T(8,128)S(1)}, bf16[16,16,1024]{2,1,0:T(8,128)(2,1)S(1)}) custom-call(s32[2]{0:T(128)S(1)} %pad_add_fusion.at, bf16[256,2048]{1,0:T(8,128)(2,1)S(1)} %copy-done.1, bf16[256,2048]{1,0:T(8,128)(2,1)S(1)} %copy-done, bf16[512,2048]{1,0:T(8,128)(2,1)S(1)} %get-tuple-element.44.low, bf16[512,256]{1,0:T(8,128)(2,1)S(1)} %copy-done.6, ...), custom_call_target="tpu_custom_call" | custom-call | flops 2000000000 | bytes 6815752 | tf_op jit(solution)/shard_map/left/pallas_call | solution.py:319
  16.5 0.0 copy-start.5
  16.5 0.5 collective-permute-start.7
  17.0 1.5 %collective-permute-done.7.got = bf16[16,16,1024]{2,1,0:T(8,128)(2,1)S(1)} collective-permute-done((bf16[16,16,1024]{2,1,0:T(8,128)(2,1)S(1)}, bf16[16,16,1024]{2,1,0:T(8,128)(2,1)S(1)}, u32[]{:S(2)}, u32[]{:S(2)}) %collective-permute-start.7) | collective-permute-done | bytes 524320 | tf_op jit(solution)/shard_map/ppermute | solution.py:31
  18.5 0.9 add.9
  19.4 5.8 %all-to-all-start = ((bf16[16,16,1024]{2,1,0:T(8,128)(2,1)}), bf16[16,16,1024]{2,1,0:T(8,128)(2,1)S(1)}, u32[]{:S(2)}, u32[]{:S(2)}) async-start(bf16[16,16,1024]{2,1,0:T(8,128)(2,1)} %add.9), calls=%async_computation | async-start | bytes 1048576 | tf_op jit(solution)/shard_map/all_to_all | solution.py:388
  25.2 5.9 %merge.1.merged_hbm = f32[512,2048]{1,0:T(8,128)} custom-call(f32[512,2048]{1,0:T(8,128)} %bitcast.5, bf16[256,512]{1,0:T(8,128)(2,1)S(1)} %copy-done.5, bf16[256,512]{1,0:T(8,128)(2,1)S(1)} %collective-permute-done.5.c1, bf16[256,2048]{1,0:T(8,128)(2,1)S(1)} %copy-done.1, bf16[256,2048]{1,0:T(8,128)(2,1)} %collective-permute-done.2.h1.g1), custom_call_target="tpu_custom_call" | custom-call | flops 1100000000 | bytes 11010048 | tf_op jit(solution)/shard_map/merge/pallas_call | solution.py:344
  31.1 4.9 %all-to-all-done.parts = bf16[16,16,1024]{2,1,0:T(8,128)(2,1)S(1)} async-done(((bf16[16,16,1024]{2,1,0:T(8,128)(2,1)}), bf16[16,16,1024]{2,1,0:T(8,128)(2,1)S(1)}, u32[]{:S(2)}, u32[]{:S(2)}) %all-to-all-start) | async-done | bytes 524320 | tf_op jit(solution)/shard_map/all_to_all | solution.py:388
  36.0 0.1 sum.1
  36.1 1.7 %collective-permute-done.4.h0.g2_hbm = bf16[256,2048]{1,0:T(8,128)(2,1)} collective-permute-done((bf16[256,2048]{1,0:T(8,128)(2,1)S(1)}, bf16[256,2048]{1,0:T(8,128)(2,1)}, u32[]{:S(2)}, u32[]{:S(2)}) %collective-permute-start.4) | collective-permute-done | bytes 1048608 | tf_op jit(solution)/shard_map/ppermute | solution.py:31
  37.8 0.8 collective-permute-start.8
  38.6 0.1 collective-permute-start.10
  38.7 4.2 %grad.2.own = bf16[2,256,512]{2,1,0:T(8,128)(2,1)} custom-call(bf16[256,2048]{1,0:T(8,128)(2,1)} %og.3, bf16[256,2048]{1,0:T(8,128)(2,1)} %collective-permute-done.2.h1.g1, bf16[512,2048]{1,0:T(8,128)(2,1)} %weight_hbm.3), custom_call_target="tpu_custom_call" | custom-call | flops 1100000000 | bytes 4718592 | tf_op jit(solution)/shard_map/grad/pallas_call | solution.py:319
  42.9 0.0 collective-permute-done.10
  42.9 5.2 %collective-permute-start.13 = (bf16[16,1024]{1,0:T(8,128)(2,1)S(1)}, bf16[16,1024]{1,0:T(8,128)(2,1)S(1)}, u32[]{:S(2)}, u32[]{:S(2)}) collective-permute-start(bf16[16,1024]{1,0:T(8,128)(2,1)S(1)} %add_convert_fusion.part), channel_id=1, source_target_pairs={{0,192},{64,0},{128,64},{192,128},{1,193},{65,1},{129,65},{193,129... | collective-permute-start | bytes 98312 | tf_op jit(solution)/shard_map/ppermute | solution.py:399
  48.1 1.2 collective-permute-start.12
  49.3 2.1 %collective-permute-start.11 = (bf16[16,1024]{1,0:T(8,128)(2,1)S(1)}, bf16[16,1024]{1,0:T(8,128)(2,1)S(1)}, u32[]{:S(2)}, u32[]{:S(2)}) collective-permute-start(bf16[16,1024]{1,0:T(8,128)(2,1)S(1)} %add_convert_fusion.part), channel_id=1, source_target_pairs={{0,64},{64,128},{128,192},{192,0},{1,65},{65,129},{129,193},{193,1... | collective-permute-start | bytes 98312 | tf_op jit(solution)/shard_map/ppermute | solution.py:399
  51.4 0.0 collective-permute-done.13.three
  51.4 3.4 %collective-permute-done.12.opposite = bf16[16,1024]{1,0:T(8,128)(2,1)S(1)} collective-permute-done((bf16[16,1024]{1,0:T(8,128)(2,1)S(1)}, bf16[16,1024]{1,0:T(8,128)(2,1)S(1)}, u32[]{:S(2)}, u32[]{:S(2)}) %collective-permute-start.12) | collective-permute-done | bytes 32800 | tf_op jit(solution)/shard_map/ppermute | solution.py:399
  54.8 0.1 collective-permute-done.11.one
  54.9 0.6 collective-permute-start.14
  55.5 0.9 close.1
  56.4 6.5 %all-to-all-start.1 = ((bf16[16,16,1024]{2,1,0:T(8,128)(2,1)}), bf16[16,16,1024]{2,1,0:T(8,128)(2,1)S(1)}, u32[]{:S(2)}, u32[]{:S(2)}) async-start(bf16[16,16,1024]{2,1,0:T(8,128)(2,1)} %close.1), calls=%async_computation.1 | async-start | bytes 1048576 | tf_op jit(solution)/shard_map/all_to_all | solution.py:482
  62.9 0.0 copy-start.2
  62.9 4.2 %grad.3 = bf16[2,256,512]{2,1,0:T(8,128)(2,1)} custom-call(bf16[256,2048]{1,0:T(8,128)(2,1)} %collective-permute-done.4.h0.g2_hbm, bf16[256,2048]{1,0:T(8,128)(2,1)} %collective-permute-done.8.h1.g3_hbm, bf16[512,2048]{1,0:T(8,128)(2,1)} %weight_hbm.3), custom_call_target="tpu_custom_call" | custom-call | flops 1100000000 | bytes 4718592 | tf_op jit(solution)/shard_map/grad/pallas_call | solution.py:319
  67.2 5.2 %all-to-all-done.1.mine = bf16[16,16,1024]{2,1,0:T(8,128)(2,1)S(1)} async-done(((bf16[16,16,1024]{2,1,0:T(8,128)(2,1)}), bf16[16,16,1024]{2,1,0:T(8,128)(2,1)S(1)}, u32[]{:S(2)}, u32[]{:S(2)}) %all-to-all-start.1) | async-done | bytes 524320 | tf_op jit(solution)/shard_map/all_to_all | solution.py:482
  72.4 3.1 %collective-permute-start.15 = (bf16[16,16,1024]{2,1,0:T(8,128)(2,1)S(1)}, bf16[16,16,1024]{2,1,0:T(8,128)(2,1)S(1)}, u32[]{:S(2)}, u32[]{:S(2)}) collective-permute-start(bf16[16,16,1024]{2,1,0:T(8,128)(2,1)S(1)} %all-to-all-done.1.mine), channel_id=1, source_target_pairs={{0,1},{1,0},{2,3},{3,2},{4,5},{5,4},{6,7},{7,6},{8,9},{9,8},{10,11... | collective-permute-start | bytes 1572872 | tf_op jit(solution)/shard_map/ppermute | solution.py:31
  75.5 0.5 early.1
  75.9 1.0 collective-permute-done.15.other
  77.0 4.4 %right.1 = (f32[16,16,1024]{2,1,0:T(8,128)S(1)}, bf16[16,16,1024]{2,1,0:T(8,128)(2,1)S(1)}, bf16[256,2048]{1,0:T(8,128)(2,1)S(1)}) custom-call(s32[2]{0:T(128)S(1)} %pad_add_fusion.at, bf16[256,2048]{1,0:T(8,128)(2,1)S(1)} %copy-done, bf16[256,2048]{1,0:T(8,128)(2,1)S(1)} %copy-done.2, bf16[512,2048]{1,0:T(8,128)(2,1)} %get-tuple-element.51.low_hbm, ...), custom_call_target="tpu_custom_call" | custom-call | flops 2000000000 | bytes 7995400 | tf_op jit(solution)/shard_map/right/pallas_call | solution.py:319
  81.4 0.5 collective-permute-start.16
  81.9 0.9 collective-permute-start.9
  82.7 0.7 collective-permute-done.16.got
  83.4 0.9 add.10
  84.3 3.6 %all-to-all-start.2 = ((bf16[16,16,1024]{2,1,0:T(8,128)(2,1)}), bf16[16,16,1024]{2,1,0:T(8,128)(2,1)S(1)}, u32[]{:S(2)}, u32[]{:S(2)}) async-start(bf16[16,16,1024]{2,1,0:T(8,128)(2,1)} %add.10), calls=%async_computation.2 | async-start | bytes 1048576 | tf_op jit(solution)/shard_map/all_to_all | solution.py:388
  87.9 4.0 %gram.1.a_in = f32[256,512]{1,0:T(8,128)S(1)} custom-call(bf16[256,2048]{1,0:T(8,128)(2,1)S(1)} %get-tuple-element.62.left), custom_call_target="tpu_custom_call" | custom-call | flops 300000000 | bytes 1572864 | tf_op jit(solution)/shard_map/gram/pallas_call | solution.py:319
  91.9 3.1 %step.2.a_in = f32[256,512]{1,0:T(8,128)S(1)} custom-call(f32[256,512]{1,0:T(8,128)S(1)} %gram.1.a_in), custom_call_target="tpu_custom_call", output_to_operand_aliasing={{}: (0, {})} | custom-call | flops 300000000 | bytes 1048576 | tf_op jit(solution)/shard_map/step/pallas_call | solution.py:319
  94.9 3.9 %all-to-all-done.2.parts = bf16[16,16,1024]{2,1,0:T(8,128)(2,1)S(1)} async-done(((bf16[16,16,1024]{2,1,0:T(8,128)(2,1)}), bf16[16,16,1024]{2,1,0:T(8,128)(2,1)S(1)}, u32[]{:S(2)}, u32[]{:S(2)}) %all-to-all-start.2) | async-done | bytes 524320 | tf_op jit(solution)/shard_map/all_to_all | solution.py:388
  98.9 0.8 spread.2
  99.6 5.0 %all-to-all-start.3 = ((bf16[8,16,1024]{2,1,0:T(8,128)(2,1)}), bf16[8,16,1024]{2,1,0:T(8,128)(2,1)S(1)}, u32[]{:S(2)}, u32[]{:S(2)}) async-start(bf16[8,16,1024]{2,1,0:T(8,128)(2,1)} %spread.2), calls=%async_computation.3 | async-start | bytes 524288 | tf_op jit(solution)/shard_map/all_to_all | solution.py:404
  104.6 1.9 %collective-permute-start.3 = (bf16[2,256,512]{2,1,0:T(8,128)(2,1)}, bf16[2,256,512]{2,1,0:T(8,128)(2,1)}, u32[]{:S(2)}, u32[]{:S(2)}) collective-permute-start(bf16[2,256,512]{2,1,0:T(8,128)(2,1)} %grad.2.own), channel_id=1, source_target_pairs={{0,1},{1,0},{2,3},{3,2},{4,5},{5,4},{6,7},{7,6},{8,9},{9,8},{10,11... | collective-permute-start | bytes 1572872 | tf_op jit(solution)/shard_map/ppermute | solution.py:31
  106.5 0.3 collective-permute-start.17
  106.8 3.0 %step.3.a_in = f32[256,512]{1,0:T(8,128)S(1)} custom-call(f32[256,512]{1,0:T(8,128)S(1)} %step.2.a_in), custom_call_target="tpu_custom_call", output_to_operand_aliasing={{}: (0, {})} | custom-call | flops 300000000 | bytes 1048576 | tf_op jit(solution)/shard_map/step/pallas_call | solution.py:319
  109.8 3.6 %basis.1 = (f32[256,256]{1,0:T(8,128)S(1)}, bf16[512,256]{1,0:T(8,128)(2,1)S(1)}) custom-call(s32[2]{0:T(128)S(1)} %pad_add_fusion.at, f32[256,512]{1,0:T(8,128)S(1)} %step.3.a_in, bf16[256,2048]{1,0:T(8,128)(2,1)S(1)} %get-tuple-element.62.left), custom_call_target="tpu_custom_call" | custom-call | flops 300000000 | bytes 2097160 | tf_op jit(solution)/shard_map/basis/pallas_call | solution.py:319
  113.4 0.8 all-to-all-done.3.parts
  114.2 0.9 spread.3
  115.0 3.9 %all-to-all-start.4 = ((bf16[16,16,1024]{2,1,0:T(8,128)(2,1)}), bf16[16,16,1024]{2,1,0:T(8,128)(2,1)S(1)}, u32[]{:S(2)}, u32[]{:S(2)}) async-start(bf16[16,16,1024]{2,1,0:T(8,128)(2,1)} %spread.3), calls=%async_computation.4 | async-start | bytes 1048576 | tf_op jit(solution)/shard_map/all_to_all | solution.py:408
  119.0 3.0 %collective-permute-start.19 = (bf16[2,256,512]{2,1,0:T(8,128)(2,1)S(1)}, bf16[2,256,512]{2,1,0:T(8,128)(2,1)S(1)}, u32[]{:S(2)}, u32[]{:S(2)}) collective-permute-start(bf16[2,256,512]{2,1,0:T(8,128)(2,1)S(1)} %copy-done.4), channel_id=1, source_target_pairs={{0,1},{1,0},{2,3},{3,2},{4,5},{5,4},{6,7},{7,6},{8,9},{9,8},{10,11... | collective-permute-start | bytes 1572872 | tf_op jit(solution)/shard_map/ppermute | solution.py:31
  122.0 2.2 %place.1 = bf16[256,2048]{1,0:T(8,128)(2,1)} custom-call(s32[2]{0:T(128)S(1)} %pad_add_fusion.at, bf16[2,256,512]{2,1,0:T(8,128)(2,1)} %grad.2.own, bf16[2,256,512]{2,1,0:T(8,128)(2,1)} %collective-permute-done.3.near, bf16[2,256,512]{2,1,0:T(8,128)(2,1)} %collective-permute-done.9.far, bf16[2,256,512]{2,1,0:T(8,128)(2,1)} %collective-permute-done.17.diag), custom_call_target="tpu_custom_call" | custom-call | flops 1000000 | bytes 3145736 | tf_op jit(solution)/shard_map/place/pallas_call | solution.py:344
  124.2 3.7 %all-to-all-done.4.chunks = bf16[16,16,1024]{2,1,0:T(8,128)(2,1)S(1)} async-done(((bf16[16,16,1024]{2,1,0:T(8,128)(2,1)}), bf16[16,16,1024]{2,1,0:T(8,128)(2,1)S(1)}, u32[]{:S(2)}, u32[]{:S(2)}) %all-to-all-start.4) | async-done | bytes 524320 | tf_op jit(solution)/shard_map/all_to_all | solution.py:408
  127.9 4.0 %collective-permute-start.18 = (bf16[16,16,1024]{2,1,0:T(8,128)(2,1)S(1)}, bf16[16,16,1024]{2,1,0:T(8,128)(2,1)S(1)}, u32[]{:S(2)}, u32[]{:S(2)}) collective-permute-start(bf16[16,16,1024]{2,1,0:T(8,128)(2,1)S(1)} %all-to-all-done.4.chunks), channel_id=1, source_target_pairs={{0,1},{1,0},{2,3},{3,2},{4,5},{5,4},{6,7},{7,6},{8,9},{9,8},{10,11... | collective-permute-start | bytes 1572872 | tf_op jit(solution)/shard_map/ppermute | solution.py:31
  132.0 1.2 begin.1
  133.2 0.3 collective-permute-done.18.other
  133.5 6.8 %last.1 = (f32[512,2048]{1,0:T(8,128)}, f32[512,256]{1,0:T(8,128)}) custom-call(s32[2]{0:T(128)S(1)} %pad_add_fusion.at, bf16[16,16,1024]{2,1,0:T(8,128)(2,1)S(1)} %collective-permute-done.18.other, f32[256,256]{1,0:T(8,128)S(1)} %get-tuple-element.69.inverse, bf16[512,256]{1,0:T(8,128)(2,1)S(1)} %get-tuple-element.66.basis, ...), custom_call_target="tpu_custom_call" | custom-call | flops 2000000000 | bytes 10000000 | tf_op jit(solution)/shard_map/last/pallas_call | solution.py:552
  (22 shorter events, 0.1 us)
Async XLA Ops:
  0.6 4.7 %collective-permute-start.1 = (bf16[512,256]{1,0:T(8,128)(2,1)}, bf16[512,256]{1,0:T(8,128)(2,1)S(1)}, u32[]{:S(2)}, u32[]{:S(2)}) collective-permute-start(bf16[512,256]{1,0:T(8,128)(2,1)} %w0.1), channel_id=1, source_target_pairs={{0,1},{1,0},{2,3},{3,2},{4,5},{5,4},{6,7},{7,6},{8,9},{9,8},{10,11... | collective-permute-start | bytes 786440 | tf_op jit(solution)/shard_map/ppermute | solution.py:31
  4.0 8.1 %collective-permute-start = (bf16[512,256]{1,0:T(8,128)(2,1)}, bf16[512,256]{1,0:T(8,128)(2,1)S(1)}, u32[]{:S(2)}, u32[]{:S(2)}) collective-permute-start(bf16[512,256]{1,0:T(8,128)(2,1)} %w0.1), channel_id=1, source_target_pairs={{0,2},{2,0},{1,3},{3,1},{4,6},{6,4},{5,7},{7,5},{8,10},{10,8},{9,1... | collective-permute-start | bytes 786440 | tf_op jit(solution)/shard_map/ppermute | solution.py:31
  5.3 7.6 %copy-start.1 = (bf16[256,2048]{1,0:T(8,128)(2,1)S(1)}, bf16[256,2048]{1,0:T(8,128)(2,1)}, u32[]{:S(2)}) copy-start(bf16[256,2048]{1,0:T(8,128)(2,1)} %og.3) | copy-start | bytes 3145732
  5.3 8.7 %copy-start = (bf16[256,2048]{1,0:T(8,128)(2,1)S(1)}, bf16[256,2048]{1,0:T(8,128)(2,1)}, u32[]{:S(2)}) copy-start(bf16[256,2048]{1,0:T(8,128)(2,1)} %ctx.7) | copy-start | bytes 3145732
  5.3 8.7 %copy-start.6 = (bf16[512,256]{1,0:T(8,128)(2,1)S(1)}, bf16[512,256]{1,0:T(8,128)(2,1)}, u32[]{:S(2)}) copy-start(bf16[512,256]{1,0:T(8,128)(2,1)} %w0.1) | copy-start | bytes 786436
  10.2 3.0 %collective-permute-start.5 = (bf16[256,512]{1,0:T(8,128)(2,1)}, bf16[256,512]{1,0:T(8,128)(2,1)S(1)}, u32[]{:S(2)}, u32[]{:S(2)}) collective-permute-start(bf16[256,512]{1,0:T(8,128)(2,1)} %get-tuple-element.43), channel_id=1, source_target_pairs={{0,1},{1,0},{2,3},{3,2},{4,5},{5,4},{6,7},{7,6},{8,9},{9,8},{10,11... | collective-permute-start | bytes 786440 | tf_op jit(solution)/shard_map/ppermute | solution.py:31
  12.0 2.0 %collective-permute-start.6 = (bf16[512,256]{1,0:T(8,128)(2,1)S(1)}, bf16[512,256]{1,0:T(8,128)(2,1)S(1)}, u32[]{:S(2)}, u32[]{:S(2)}) collective-permute-start(bf16[512,256]{1,0:T(8,128)(2,1)S(1)} %collective-permute-done.w2), channel_id=1, source_target_pairs={{0,1},{1,0},{2,3},{3,2},{4,5},{5,4},{6,7},{7,6},{8,9},{9,8},{10,11... | collective-permute-start | bytes 786440 | tf_op jit(solution)/shard_map/ppermute | solution.py:31
  12.9 24.9 %collective-permute-start.4 = (bf16[256,2048]{1,0:T(8,128)(2,1)S(1)}, bf16[256,2048]{1,0:T(8,128)(2,1)}, u32[]{:S(2)}, u32[]{:S(2)}) collective-permute-start(bf16[256,2048]{1,0:T(8,128)(2,1)S(1)} %copy-done.1), channel_id=1, source_target_pairs={{0,2},{2,0},{1,3},{3,1},{4,6},{6,4},{5,7},{7,5},{8,10},{10,8},{9,1... | collective-permute-start | bytes 3145736 | tf_op jit(solution)/shard_map/ppermute | solution.py:31
  12.9 12.3 %collective-permute-start.2 = (bf16[256,2048]{1,0:T(8,128)(2,1)S(1)}, bf16[256,2048]{1,0:T(8,128)(2,1)}, u32[]{:S(2)}, u32[]{:S(2)}) collective-permute-start(bf16[256,2048]{1,0:T(8,128)(2,1)S(1)} %copy-done.1), channel_id=1, source_target_pairs={{0,1},{1,0},{2,3},{3,2},{4,5},{5,4},{6,7},{7,6},{8,9},{9,8},{10,11... | collective-permute-start | bytes 3145736 | tf_op jit(solution)/shard_map/ppermute | solution.py:31
  16.5 8.7 %copy-start.5 = (bf16[256,512]{1,0:T(8,128)(2,1)S(1)}, bf16[256,512]{1,0:T(8,128)(2,1)}, u32[]{:S(2)}) copy-start(bf16[256,512]{1,0:T(8,128)(2,1)} %get-tuple-element.48.c0) | copy-start | bytes 786436
  16.5 2.0 %collective-permute-start.7 = (bf16[16,16,1024]{2,1,0:T(8,128)(2,1)S(1)}, bf16[16,16,1024]{2,1,0:T(8,128)(2,1)S(1)}, u32[]{:S(2)}, u32[]{:S(2)}) collective-permute-start(bf16[16,16,1024]{2,1,0:T(8,128)(2,1)S(1)} %get-tuple-element.47), channel_id=1, source_target_pairs={{0,1},{1,0},{2,3},{3,2},{4,5},{5,4},{6,7},{7,6},{8,9},{9,8},{10,11... | collective-permute-start | bytes 1572872 | tf_op jit(solution)/shard_map/ppermute | solution.py:31
  19.4 16.6 %all-to-all-start = ((bf16[16,16,1024]{2,1,0:T(8,128)(2,1)}), bf16[16,16,1024]{2,1,0:T(8,128)(2,1)S(1)}, u32[]{:S(2)}, u32[]{:S(2)}) async-start(bf16[16,16,1024]{2,1,0:T(8,128)(2,1)} %add.9), calls=%async_computation | async-start | bytes 1048576 | tf_op jit(solution)/shard_map/all_to_all | solution.py:388
  37.8 25.1 %collective-permute-start.8 = (bf16[256,2048]{1,0:T(8,128)(2,1)}, bf16[256,2048]{1,0:T(8,128)(2,1)}, u32[]{:S(2)}, u32[]{:S(2)}) collective-permute-start(bf16[256,2048]{1,0:T(8,128)(2,1)} %collective-permute-done.4.h0.g2_hbm), channel_id=1, source_target_pairs={{0,1},{1,0},{2,3},{3,2},{4,5},{5,4},{6,7},{7,6},{8,9},{9,8},{10,11... | collective-permute-start | bytes 3145736 | tf_op jit(solution)/shard_map/ppermute | solution.py:31
  38.6 4.3 %collective-permute-start.10 = (f32[16,1024]{1,0:T(8,128)S(1)}, f32[16,1024]{1,0:T(8,128)S(1)}, u32[]{:S(2)}, u32[]{:S(2)}) collective-permute-start(f32[16,1024]{1,0:T(8,128)S(1)} %sum.1), channel_id=1, source_target_pairs={{0,2},{2,0},{1,3},{3,1},{4,6},{6,4},{5,7},{7,5},{8,10},{10,8},{9,1... | collective-permute-start | bytes 196616 | tf_op jit(solution)/shard_map/ppermute | solution.py:31
  42.9 8.5 %collective-permute-start.13 = (bf16[16,1024]{1,0:T(8,128)(2,1)S(1)}, bf16[16,1024]{1,0:T(8,128)(2,1)S(1)}, u32[]{:S(2)}, u32[]{:S(2)}) collective-permute-start(bf16[16,1024]{1,0:T(8,128)(2,1)S(1)} %add_convert_fusion.part), channel_id=1, source_target_pairs={{0,192},{64,0},{128,64},{192,128},{1,193},{65,1},{129,65},{193,129... | collective-permute-start | bytes 98312 | tf_op jit(solution)/shard_map/ppermute | solution.py:399
  48.1 6.7 %collective-permute-start.12 = (bf16[16,1024]{1,0:T(8,128)(2,1)S(1)}, bf16[16,1024]{1,0:T(8,128)(2,1)S(1)}, u32[]{:S(2)}, u32[]{:S(2)}) collective-permute-start(bf16[16,1024]{1,0:T(8,128)(2,1)S(1)} %add_convert_fusion.part), channel_id=1, source_target_pairs={{0,128},{64,192},{128,0},{192,64},{1,129},{65,193},{129,1},{193,65... | collective-permute-start | bytes 98312 | tf_op jit(solution)/shard_map/ppermute | solution.py:399
  49.3 5.6 %collective-permute-start.11 = (bf16[16,1024]{1,0:T(8,128)(2,1)S(1)}, bf16[16,1024]{1,0:T(8,128)(2,1)S(1)}, u32[]{:S(2)}, u32[]{:S(2)}) collective-permute-start(bf16[16,1024]{1,0:T(8,128)(2,1)S(1)} %add_convert_fusion.part), channel_id=1, source_target_pairs={{0,64},{64,128},{128,192},{192,0},{1,65},{65,129},{129,193},{193,1... | collective-permute-start | bytes 98312 | tf_op jit(solution)/shard_map/ppermute | solution.py:399
  54.9 17.5 %collective-permute-start.14 = (bf16[2,256,512]{2,1,0:T(8,128)(2,1)}, bf16[2,256,512]{2,1,0:T(8,128)(2,1)S(1)}, u32[]{:S(2)}, u32[]{:S(2)}) collective-permute-start(bf16[2,256,512]{2,1,0:T(8,128)(2,1)} %get-tuple-element.57), channel_id=1, source_target_pairs={{0,2},{2,0},{1,3},{3,1},{4,6},{6,4},{5,7},{7,5},{8,10},{10,8},{9,1... | collective-permute-start | bytes 1572872 | tf_op jit(solution)/shard_map/ppermute | solution.py:31
  56.4 16.0 %all-to-all-start.1 = ((bf16[16,16,1024]{2,1,0:T(8,128)(2,1)}), bf16[16,16,1024]{2,1,0:T(8,128)(2,1)S(1)}, u32[]{:S(2)}, u32[]{:S(2)}) async-start(bf16[16,16,1024]{2,1,0:T(8,128)(2,1)} %close.1), calls=%async_computation.1 | async-start | bytes 1048576 | tf_op jit(solution)/shard_map/all_to_all | solution.py:482
  62.9 14.1 %copy-start.2 = (bf16[256,2048]{1,0:T(8,128)(2,1)S(1)}, bf16[256,2048]{1,0:T(8,128)(2,1)}, u32[]{:S(2)}) copy-start(bf16[256,2048]{1,0:T(8,128)(2,1)} %og.3) | copy-start | bytes 3145732
  72.4 4.6 %copy-start.3 = (bf16[2,256,512]{2,1,0:T(8,128)(2,1)}, bf16[2,256,512]{2,1,0:T(8,128)(2,1)S(1)}, u32[]{:S(2)}) copy-start(bf16[2,256,512]{2,1,0:T(8,128)(2,1)S(1)} %collective-permute-done.14.c2) | copy-start | bytes 1572868
  72.4 4.6 %collective-permute-start.15 = (bf16[16,16,1024]{2,1,0:T(8,128)(2,1)S(1)}, bf16[16,16,1024]{2,1,0:T(8,128)(2,1)S(1)}, u32[]{:S(2)}, u32[]{:S(2)}) collective-permute-start(bf16[16,16,1024]{2,1,0:T(8,128)(2,1)S(1)} %all-to-all-done.1.mine), channel_id=1, source_target_pairs={{0,1},{1,0},{2,3},{3,2},{4,5},{5,4},{6,7},{7,6},{8,9},{9,8},{10,11... | collective-permute-start | bytes 1572872 | tf_op jit(solution)/shard_map/ppermute | solution.py:31
  81.4 2.0 %collective-permute-start.16 = (bf16[16,16,1024]{2,1,0:T(8,128)(2,1)S(1)}, bf16[16,16,1024]{2,1,0:T(8,128)(2,1)S(1)}, u32[]{:S(2)}, u32[]{:S(2)}) collective-permute-start(bf16[16,16,1024]{2,1,0:T(8,128)(2,1)S(1)} %get-tuple-element.61), channel_id=1, source_target_pairs={{0,1},{1,0},{2,3},{3,2},{4,5},{5,4},{6,7},{7,6},{8,9},{9,8},{10,11... | collective-permute-start | bytes 1572872 | tf_op jit(solution)/shard_map/ppermute | solution.py:31
  81.9 17.8 %collective-permute-start.9 = (bf16[2,256,512]{2,1,0:T(8,128)(2,1)}, bf16[2,256,512]{2,1,0:T(8,128)(2,1)}, u32[]{:S(2)}, u32[]{:S(2)}) collective-permute-start(bf16[2,256,512]{2,1,0:T(8,128)(2,1)} %grad.3), channel_id=1, source_target_pairs={{0,2},{2,0},{1,3},{3,1},{4,6},{6,4},{5,7},{7,5},{8,10},{10,8},{9,1... | collective-permute-start | bytes 1572872 | tf_op jit(solution)/shard_map/ppermute | solution.py:31
  84.3 14.5 %all-to-all-start.2 = ((bf16[16,16,1024]{2,1,0:T(8,128)(2,1)}), bf16[16,16,1024]{2,1,0:T(8,128)(2,1)S(1)}, u32[]{:S(2)}, u32[]{:S(2)}) async-start(bf16[16,16,1024]{2,1,0:T(8,128)(2,1)} %add.10), calls=%async_computation.2 | async-start | bytes 1048576 | tf_op jit(solution)/shard_map/all_to_all | solution.py:388
  99.6 14.5 %all-to-all-start.3 = ((bf16[8,16,1024]{2,1,0:T(8,128)(2,1)}), bf16[8,16,1024]{2,1,0:T(8,128)(2,1)S(1)}, u32[]{:S(2)}, u32[]{:S(2)}) async-start(bf16[8,16,1024]{2,1,0:T(8,128)(2,1)} %spread.2), calls=%async_computation.3 | async-start | bytes 524288 | tf_op jit(solution)/shard_map/all_to_all | solution.py:404
  104.6 14.3 %copy-start.4 = (bf16[2,256,512]{2,1,0:T(8,128)(2,1)S(1)}, bf16[2,256,512]{2,1,0:T(8,128)(2,1)}, u32[]{:S(2)}) copy-start(bf16[2,256,512]{2,1,0:T(8,128)(2,1)} %copy-done.3) | copy-start | bytes 1572868
  104.6 17.4 %collective-permute-start.3 = (bf16[2,256,512]{2,1,0:T(8,128)(2,1)}, bf16[2,256,512]{2,1,0:T(8,128)(2,1)}, u32[]{:S(2)}, u32[]{:S(2)}) collective-permute-start(bf16[2,256,512]{2,1,0:T(8,128)(2,1)} %grad.2.own), channel_id=1, source_target_pairs={{0,1},{1,0},{2,3},{3,2},{4,5},{5,4},{6,7},{7,6},{8,9},{9,8},{10,11... | collective-permute-start | bytes 1572872 | tf_op jit(solution)/shard_map/ppermute | solution.py:31
  106.5 15.5 %collective-permute-start.17 = (bf16[2,256,512]{2,1,0:T(8,128)(2,1)}, bf16[2,256,512]{2,1,0:T(8,128)(2,1)}, u32[]{:S(2)}, u32[]{:S(2)}) collective-permute-start(bf16[2,256,512]{2,1,0:T(8,128)(2,1)} %collective-permute-done.9.far), channel_id=1, source_target_pairs={{0,1},{1,0},{2,3},{3,2},{4,5},{5,4},{6,7},{7,6},{8,9},{9,8},{10,11... | collective-permute-start | bytes 1572872 | tf_op jit(solution)/shard_map/ppermute | solution.py:31
  115.0 12.9 %all-to-all-start.4 = ((bf16[16,16,1024]{2,1,0:T(8,128)(2,1)}), bf16[16,16,1024]{2,1,0:T(8,128)(2,1)S(1)}, u32[]{:S(2)}, u32[]{:S(2)}) async-start(bf16[16,16,1024]{2,1,0:T(8,128)(2,1)} %spread.3), calls=%async_computation.4 | async-start | bytes 1048576 | tf_op jit(solution)/shard_map/all_to_all | solution.py:408
  119.0 13.0 %collective-permute-start.19 = (bf16[2,256,512]{2,1,0:T(8,128)(2,1)S(1)}, bf16[2,256,512]{2,1,0:T(8,128)(2,1)S(1)}, u32[]{:S(2)}, u32[]{:S(2)}) collective-permute-start(bf16[2,256,512]{2,1,0:T(8,128)(2,1)S(1)} %copy-done.4), channel_id=1, source_target_pairs={{0,1},{1,0},{2,3},{3,2},{4,5},{5,4},{6,7},{7,6},{8,9},{9,8},{10,11... | collective-permute-start | bytes 1572872 | tf_op jit(solution)/shard_map/ppermute | solution.py:31
  127.9 5.6 %collective-permute-start.18 = (bf16[16,16,1024]{2,1,0:T(8,128)(2,1)S(1)}, bf16[16,16,1024]{2,1,0:T(8,128)(2,1)S(1)}, u32[]{:S(2)}, u32[]{:S(2)}) collective-permute-start(bf16[16,16,1024]{2,1,0:T(8,128)(2,1)S(1)} %all-to-all-done.4.chunks), channel_id=1, source_target_pairs={{0,1},{1,0},{2,3},{3,2},{4,5},{5,4},{6,7},{7,6},{8,9},{9,8},{10,11... | collective-permute-start | bytes 1572872 | tf_op jit(solution)/shard_map/ppermute | solution.py:31
